TPU v7x, 32 devices: a whole 2x2x4 slice. The times are simulated.
32 devices in a mesh: lon: 16 (over z, x, core), lat: 2 (over y).
Axes of the slice: x: 2, y: 2, z: 4, core: 2. Of those that a mesh axis runs over, the one named last changes fastest.
Arguments:
- initial_state: float32 [4, 10, 32, 2048], P(None, None, 'lat', 'lon'), may hold values from -6 to 6
- land_mask: int32 [10, 32, 2048], P(None, 'lat', 'lon'), may hold values from 0 to 1, as said below
- surface_flux: float32 [32, 2048], P('lat', 'lon'), may hold values from 0 to 10, as said below
- weight_in: float32 [40, 64], replicated, may hold values from -1 to 1
- bias_in: float32 [64], replicated, may hold values from -3 to 3
- weight_mid: float32 [64, 64], replicated, may hold values from -0.75 to 0.75
- bias_mid: float32 [64], replicated, may hold values from -3 to 3
- weight_out: float32 [64, 40], replicated, may hold values from -0.75 to 0.75
- bias_out: float32 [40], replicated, may hold values from -3 to 3
- cotangent: float32 [4, 10, 32, 2048], P(None, None, 'lat', 'lon'), may hold values from -6 to 6
Outputs:
- final_state: float32 [4, 10, 32, 2048], P(None, None, 'lat', 'lon')
- state_grad: float32 [4, 10, 32, 2048], P(None, None, 'lat', 'lon')
- grad_weight_in: float32 [40, 64], replicated
- grad_bias_in: float32 [64], replicated
- grad_weight_mid: float32 [64, 64], replicated
- grad_bias_mid: float32 [64], replicated
- grad_weight_out: float32 [64, 40], replicated
- grad_bias_out: float32 [40], replicated
Inputs may be any that keep to these rules, and one draw needn't show every extreme that they name: `land_mask`: at every cell the ocean levels are a run from level 0 down; at least one cell is ocean at every level. `surface_flux`: strictly positive.
All inputs are finite; a program needn't handle non-finite values.
Results may differ from a plain program's by a relative error of at most 0.00012.
Values sent between devices are 32-bit elements; how exact they have to be, the bound alone decides.
No kernel may reach another device: no remote copies, remote signals or barrier semaphores. Data moves between devices by JAX's collectives and lax.ppermute only.
A program may use at most 128 MiB of HBM per device.

v0:
```python
import math

import jax
import jax.numpy as jnp
from jax import lax
from jax.experimental import pallas as pl
from jax.experimental.pallas import tpu as pltpu
from jax.sharding import PartitionSpec as P

LAT_LIMIT = 1.2
CORIOLIS = 1.0
VISCOSITY = 0.15
DIFFUSIVITY = 0.1

ROWS = 16
COLS = 128
REACH = 11
CREACH = 6
PAD = 12
EXT = 40
WIDE = 2 * COLS
FEATS = 40
HID = 64
PACK = 56
SLOT = 16
F32 = jnp.float32
BF16 = jnp.bfloat16
VMEM = pl.BlockSpec(memory_space=pltpu.VMEM)
SMEM = pl.BlockSpec(memory_space=pltpu.SMEM)
PARAMS = pltpu.CompilerParams(vmem_limit_bytes=44 * 1024 * 1024)


def sds(*shape):
    return jax.ShapeDtypeStruct(shape, F32)


def sub_index(width):
    return lax.broadcasted_iota(jnp.int32, (8, width), 0)


def tile(ref, row, number):
    return ref[row, 8 * number : 8 * number + 8, :]


def slot_pack(pieces, shift_of, width):
    lane = lax.broadcasted_iota(jnp.int32, (8, COLS), 1)
    packed = None
    for slot, piece in enumerate(pieces):
        turned = pltpu.roll(piece, shift_of(slot) % COLS, 1)
        if packed is None:
            packed = turned
        else:
            packed = jnp.where((lane >= slot * width) & (lane < (slot + 1) * width), turned, packed)
    return packed


def pack_kernel(sides, scal, x, mask, flux, cot, *outs):
    own, cown, sums, east, west = outs[:5]
    per_side = [outs[5 + 4 * i : 9 + 4 * i] for i in range(len(sides))]
    for r in range(ROWS):
        first = mask[pl.ds(r, 8, stride=ROWS), :].astype(F32)
        m8 = mask[8 * ROWS + r : 8 * ROWS + r + 1, :].astype(F32)
        m9 = mask[9 * ROWS + r : 9 * ROWS + r + 1, :].astype(F32)
        for t in range(4):
            own[r, 8 * t : 8 * t + 8, :] = x[pl.ds(t * 10 * ROWS + r, 8, stride=ROWS), :] * first
            cown[r, 8 * t : 8 * t + 8, :] = cot[pl.ds(t * 10 * ROWS + r, 8, stride=ROWS), :]
        for level, m in ((8, m8), (9, m9)):
            at = 32 + 4 * (level - 8)
            own[r, at : at + 4, :] = x[pl.ds(level * ROWS + r, 4, stride=10 * ROWS), :] * m
            cown[r, at : at + 4, :] = cot[pl.ds(level * ROWS + r, 4, stride=10 * ROWS), :]
        own[r, 40:48, :] = first
        own[r, 48:49, :] = m8
        own[r, 49:50, :] = m9
        own[r, 50:51, :] = flux[r : r + 1, :]
        own[r, 51:56, :] = jnp.zeros((5, COLS), F32)
    top = mask[0:ROWS, :].astype(F32)
    total = jnp.sum(jnp.sum(top * flux[...], axis=1, keepdims=True), axis=0, keepdims=True)
    count = jnp.sum(jnp.sum(top, axis=1, keepdims=True), axis=0, keepdims=True)
    sums[...] = jnp.where(sub_index(COLS) == 0, total, jnp.where(sub_index(COLS) == 1, count, 0.0))
    for half in range(2):
        for t in range(7):
            rows = [own[8 * half + s, 8 * t : 8 * t + 8, :] for s in range(8)]
            at = half * PACK + 8 * t
            east[at : at + 8, :] = slot_pack(rows, lambda s: SLOT * (s + 1), SLOT)
            west[at : at + 8, :] = slot_pack(rows, lambda s: SLOT * s, SLOT)
    for t in range(5):
        rows = [cown[s, 8 * t : 8 * t + 8, :] for s in range(ROWS)]
        at = 2 * PACK + 8 * t
        east[at : at + 8, :] = slot_pack(rows, lambda s: 8 * (s + 1), 8)
        west[at : at + 8, :] = slot_pack(rows, lambda s: 8 * s, 8)
    for side, (lat_x, lat_c, diag_e, diag_w) in zip(sides, per_side):
        start = {"swap": scal[0], "north": ROWS - REACH, "south": 0}[side]
        cstart = {"swap": scal[1], "north": ROWS - CREACH, "south": 0}[side]
        for n in range(REACH):
            lat_x[n] = own[start + n]
        for n in range(CREACH):
            lat_c[n] = cown[cstart + n]
        for t in range(7):
            rows = [own[start + n, 8 * t : 8 * t + 8, :] for n in range(REACH)]
            diag_e[8 * t : 8 * t + 8, :] = slot_pack(rows, lambda s: REACH * (s + 1), REACH)
            diag_w[8 * t : 8 * t + 8, :] = slot_pack(rows, lambda s: REACH * s, REACH)
        diag_e[PACK : PACK + 40, :] = east[2 * PACK : 2 * PACK + 40, :]
        diag_w[PACK : PACK + 40, :] = west[2 * PACK : 2 * PACK + 40, :]


def split(values):
    high = values.astype(BF16)
    return high, (values - high.astype(F32)).astype(BF16)


def stacked_weights(ref):
    values = ref[...]
    third = values.shape[1] // 3
    high, low = split(values)
    lane = lax.broadcasted_iota(jnp.int32, values.shape, 1)
    return jnp.where(lane < 2 * third, high.astype(F32), low.astype(F32)).astype(BF16)


def product(weights, high, low):
    return jnp.dot(weights, jnp.concatenate([high, low, high], axis=0), preferred_element_type=F32)


def across(a, b):
    dims = (((1,), (1,)), ((), ()))
    dot = lambda p, q: lax.dot_general(p, q, dims, preferred_element_type=F32)
    return dot(a[0], b[0]) + dot(a[0], b[1]) + dot(a[1], b[0])


def to_48(columns):
    return jnp.concatenate([columns, jnp.zeros((8, columns.shape[1]), F32)], axis=0)


def hidden_layers(z, w1, b1, w2, b2):
    h1 = jnp.tanh(product(w1, *z) + b1)
    h1s = split(h1)
    h2 = jnp.tanh(product(w2, *h1s) + b2)
    return h1, h1s, h2


def add_weight_terms(acc, z, h1s, h2s, g1s, g2s, gos):
    ones = jnp.ones((16, z[0].shape[1]), BF16)
    acc[0:48, 0:HID] += across(z, g1s)
    acc[48:112, 0:HID] += across(h1s, g2s)
    acc[112:160, 0:HID] += across(gos, h2s)
    acc[160:176, 0:HID] += ones_rows(ones, g1s)
    acc[176:192, 0:HID] += ones_rows(ones, g2s)
    acc[192:208, 0:48] += ones_rows(ones, gos)


def ones_rows(ones, g):
    dims = (((1,), (1,)), ((), ()))
    dot = lambda q: lax.dot_general(ones, q, dims, preferred_element_type=F32)
    return dot(g[0]) + dot(g[1])


def own_closure_kernel(own, w1, b1, w2, b2, w3, b3, out, h1_out, h2_out):
    k1, k2, k3 = stacked_weights(w1), stacked_weights(w2), stacked_weights(w3)

    def chunk(i, _):
        r = 4 * i
        z = split(to_48(jnp.concatenate([own[r + n, 0:FEATS, :] for n in range(4)], axis=1)))
        h1, h1s, h2 = hidden_layers(z, k1, b1[...], k2, b2[...])
        o = product(k3, *split(h2))[0:FEATS] + b3[...]
        for n in range(4):
            at = slice(n * COLS, (n + 1) * COLS)
            out[r + n] = o[:, at]
            h1_out[r + n] = h1[:, at]
            h2_out[r + n] = h2[:, at]
        return 0

    lax.fori_loop(0, ROWS // 4, chunk, 0)


class Row:
    def __init__(self, width):
        sub = sub_index(width)
        group = sub % 4
        self.sub = sub
        self.is_t = group == 0
        self.is_s = group == 1
        self.is_u = group == 2
        self.is_v = group == 3
        self.low = sub >= 4
        self.k4 = jnp.where(group < 2, DIFFUSIVITY, VISCOSITY).astype(F32)


def derived(k, temp, salt, mixed):
    zero = jnp.zeros_like(temp)
    press = 0.4 * salt - 0.1 * temp
    for by in (1, 2, 4):
        press = press + jnp.where(k.sub >= by, pltpu.roll(press, by, 0), zero)
    deep = jnp.where(k.is_t, 0.4 * pltpu.roll(mixed, 7, 0) - 0.1 * mixed, zero)
    deep = deep + jnp.where(k.low, pltpu.roll(deep, 4, 0), zero)
    deep = deep + pltpu.roll(deep, 1, 0)
    deep = deep + pltpu.roll(deep, 2, 0) + press[7:8, :]
    u4, v4 = deep_velocity(k, mixed)
    return press, deep, u4, v4


def deep_velocity(k, mixed):
    zero = jnp.zeros_like(mixed)
    u4 = jnp.where(k.is_u, mixed, zero)
    u4 = u4 + pltpu.roll(u4, 1, 0)
    u4 = u4 + pltpu.roll(u4, 6, 0)
    v4 = jnp.where(k.is_v, mixed, zero)
    v4 = v4 + pltpu.roll(v4, 7, 0)
    v4 = v4 + pltpu.roll(v4, 6, 0)
    return u4, v4


def put_state(k, ref, row, tiles):
    for t in range(5):
        ref[row, 8 * t : 8 * t + 8, :] = tiles[t]
    for t, values in enumerate(derived(k, tiles[0], tiles[1], tiles[4])):
        ref[row, 40 + 8 * t : 48 + 8 * t, :] = values


def east_of(q):
    return pltpu.roll(q, q.shape[1] - 1, 1)


def west_of(q):
    return pltpu.roll(q, 1, 1)


def tendency_row(k, ref, row, c, f):
    half = 0.5 * c
    c2 = c * c
    u, v = tile(ref, row, 2), tile(ref, row, 3)
    u4, v4 = tile(ref, row, 7), tile(ref, row, 8)
    uh, vh = u * half, v * 0.5
    u4h, v4h = u4 * half, v4 * 0.5
    change = []
    for t in range(5):
        q = tile(ref, row, t)
        e, w = east_of(q), west_of(q)
        n, s = tile(ref, row + 1, t), tile(ref, row - 1, t)
        lap = c2 * (e + w) + (n + s) - (2.0 * c2 + 2.0) * q
        gain = k.k4 if t == 4 else (DIFFUSIVITY if t < 2 else VISCOSITY)
        au, av = (u4h, v4h) if t == 4 else (uh, vh)
        change.append(gain * lap - (au * (e - w) + av * (n - s)))
    p = tile(ref, row, 5)
    change[2] = change[2] + (f * v - half * (east_of(p) - west_of(p)))
    change[3] = change[3] - (f * u + 0.5 * (tile(ref, row + 1, 5) - tile(ref, row - 1, 5)))
    p4 = tile(ref, row, 6)
    zero = jnp.zeros_like(p4)
    fx = f * v4 - half * (east_of(p4) - west_of(p4))
    fy = f * u4 + 0.5 * (tile(ref, row + 1, 6) - tile(ref, row - 1, 6))
    change[4] = change[4] + jnp.where(k.is_u, fx, jnp.where(k.is_v, -fy, zero))
    return change


def adjoint_row(k, ref, aref, row, c, f):
    half = 0.5 * c
    c2 = c * c
    u4 = tile(ref, row, 7)
    qe = [east_of(tile(ref, row, t)) for t in range(5)]
    qw = [west_of(tile(ref, row, t)) for t in range(5)]
    u4e, u4w = east_of(u4), west_of(u4)
    out = []
    to_u = to_v = None
    for t in range(5):
        a = tile(aref, row, t)
        ae, aw = east_of(a), west_of(a)
        an, as_ = tile(aref, row + 1, t), tile(aref, row - 1, t)
        gain = k.k4 if t == 4 else (DIFFUSIVITY if t < 2 else VISCOSITY)
        ue, uw = (u4e, u4w) if t == 4 else (qe[2], qw[2])
        which = 8 if t == 4 else 3
        vn, vs = tile(ref, row + 1, which), tile(ref, row - 1, which)
        lap = c2 * (ae + aw) + (an + as_) - (2.0 * c2 + 2.0) * a
        out.append(gain * lap + half * (ue * ae - uw * aw) + 0.5 * (vn * an - vs * as_))
        px = a * (qe[t] - qw[t])
        py = a * (tile(ref, row + 1, t) - tile(ref, row - 1, t))
        if t < 4:
            to_u = px if to_u is None else to_u + px
            to_v = py if to_v is None else to_v + py
        if t == 2:
            a2, bx = a, half * (ae - aw)
        if t == 3:
            a3, by = a, 0.5 * (an - as_)
        if t == 4:
            a4 = a
            deep_bx, deep_by = half * (ae - aw), 0.5 * (an - as_)
            px4, py4 = px * half, py * 0.5
    out[2] = out[2] - half * to_u - f * a3
    out[3] = out[3] - 0.5 * to_v + f * a2
    zero = jnp.zeros_like(a4)
    sx = px4 + pltpu.roll(px4, 7, 0)
    sx = sx + pltpu.roll(sx, 2, 0)
    sy = py4 + pltpu.roll(py4, 1, 0)
    sy = sy + pltpu.roll(sy, 2, 0)
    at_u = -sx - f * pltpu.roll(a4, 7, 0)
    at_v = f * pltpu.roll(a4, 1, 0) - sy
    deep = jnp.where(k.is_t, pltpu.roll(deep_bx, 6, 0) + pltpu.roll(deep_by, 5, 0), zero)
    deep = deep + jnp.where(k.low, zero, pltpu.roll(deep, 4, 0))
    press = bx + by
    for shift in (1, 2, 4):
        press = press + jnp.where(k.sub < 8 - shift, pltpu.roll(press, 8 - shift, 0), zero)
    press = press + deep[0:1, :]
    out[0] = out[0] - 0.1 * press
    out[1] = out[1] + 0.4 * press
    out[4] = out[4] + jnp.where(
        k.is_t,
        -0.1 * deep,
        jnp.where(k.is_s, 0.4 * pltpu.roll(deep, 1, 0), jnp.where(k.is_u, at_u, at_v)),
    )
    return out


def mask_tile(ref, row, t):
    return tile(ref, row, 1 if t == 4 else 0)


def adjoint_sections(k, cs, fs, bounds, states, masks, abuf, bbuf, hold, store, top):
    state_1, state_2, state_3 = states

    def third(r, _):
        d = adjoint_row(k, state_3, abuf, r, cs[r], fs[r])
        for t in range(5):
            ts = (2.0 / 3.0) * top(r, t) + d[t]
            hold[r, 8 * t : 8 * t + 8, :] = ts
            bbuf[r, 8 * t : 8 * t + 8, :] = 0.0625 * mask_tile(masks, r, t) * ts
        return 0

    def second(r, _):
        d = adjoint_row(k, state_2, bbuf, r, cs[r], fs[r])
        for t in range(5):
            ts = tile(hold, r, t)
            tf = 0.25 * ts + d[t]
            hold[r, 8 * t : 8 * t + 8, :] = (1.0 / 3.0) * top(r, t) + 0.75 * ts + tf
            abuf[r, 8 * t : 8 * t + 8, :] = 0.25 * mask_tile(masks, r, t) * tf
        return 0

    def first(r, _):
        d = adjoint_row(k, state_1, abuf, r, cs[r], fs[r])
        store(r, [tile(hold, r, t) + d[t] for t in range(5)])
        return 0

    lax.fori_loop(*bounds[0], third, 0)
    lax.fori_loop(*bounds[1], second, 0)
    lax.fori_loop(*bounds[2], first, 0)


def unpack(packed, slot_shift, keep):
    turned = pltpu.roll(packed, slot_shift % COLS, 1)
    return jnp.where(keep, turned, 0.0)


def edges(reach):
    lane = lax.broadcasted_iota(jnp.int32, (8, COLS), 1)
    return lane < reach, lane >= COLS - reach


def main_kernel(sides, scal, cs, fs, sums, own, cown, own_m, own_h1, own_h2, east, west, *rest):
    n = len(sides)
    side_refs = [rest[4 * i : 4 * i + 4] for i in range(n)]
    (w1, b1, w2, b2, w3, b3, v1, v2, v3), rest = rest[4 * n : 4 * n + 9], rest[4 * n + 9 :]
    final, grads, lam, from_closure, keep_1, keep_2, keep_3, keep_mask = rest[:8]
    s0, s1, s2, s3, s4, masks, fluxes, cot, outs, gz, abuf, bbuf, hold, acc = rest[8:]
    k = Row(WIDE)
    has_south, has_north = scal[2], scal[3]
    lo = lambda h: PAD - h * has_south
    hi = lambda h: PAD + ROWS + h * has_north

    for ref in (s0, s1, s2, s3, s4, abuf, bbuf):
        for row in (PAD - 1, PAD + ROWS):
            ref[row] = jnp.zeros(ref.shape[1:], F32)

    near_e, near_w = edges(REACH)
    cnear_e, cnear_w = edges(CREACH)

    def put_packed(row, core, halo):
        both = lambda t: jnp.concatenate([core(t), halo(t)], axis=1)
        put_state(k, s0, row, [both(t) for t in range(5)])
        masks[row, 0:8, :] = both(5)
        last = both(6)
        masks[row, 8:16, :] = jnp.where(k.low, last[1:2, :], last[0:1, :])
        fluxes[row] = last

    for r in range(ROWS):
        at = (r // 8) * PACK
        turn = SLOT * (r % 8)

        def halo(t):
            from_e = pltpu.roll(west[at + 8 * t : at + 8 * t + 8, :], -turn % COLS, 1)
            from_w = pltpu.roll(east[at + 8 * t : at + 8 * t + 8, :], -(turn + SLOT) % COLS, 1)
            return jnp.where(near_e, from_e, jnp.where(near_w, from_w, 0.0))

        put_packed(PAD + r, lambda t: own[r, 8 * t : 8 * t + 8, :], halo)
        for t in range(5):
            rows = slice(2 * PACK + 8 * t, 2 * PACK + 8 * t + 8)
            from_e = pltpu.roll(west[rows, :], -8 * r % COLS, 1)
            from_w = pltpu.roll(east[rows, :], -8 * (r + 1) % COLS, 1)
            side = jnp.where(cnear_e, from_e, jnp.where(cnear_w, from_w, 0.0))
            cot[PAD + r, 8 * t : 8 * t + 8, :] = jnp.concatenate(
                [cown[r, 8 * t : 8 * t + 8, :], side], axis=1
            )
    for side, (lat_x, lat_c, diag_e, diag_w) in zip(sides, side_refs):
        base = {"swap": scal[4], "north": 1, "south": PAD + ROWS}[side]
        cbase = {"swap": scal[5], "north": PAD - CREACH, "south": PAD + ROWS}[side]
        crow = {"swap": scal[6], "north": ROWS - CREACH, "south": 0}[side]
        for r in range(REACH):

            def halo(t):
                rows = slice(8 * t, 8 * t + 8)
                from_e = pltpu.roll(diag_w[rows, :], -REACH * r % COLS, 1)
                from_w = pltpu.roll(diag_e[rows, :], -REACH * (r + 1) % COLS, 1)
                return jnp.where(near_e, from_e, jnp.where(near_w, from_w, 0.0))

            put_packed(base + r, lambda t: lat_x[r, 8 * t : 8 * t + 8, :], halo)
        for r in range(CREACH):
            turn = lax.rem(2 * COLS - 8 * (crow + r), COLS)
            turn_w = lax.rem(2 * COLS - 8 * (crow + r + 1), COLS)
            for t in range(5):
                rows = slice(PACK + 8 * t, PACK + 8 * t + 8)
                from_e = pltpu.roll(diag_w[rows, :], turn, 1)
                from_w = pltpu.roll(diag_e[rows, :], turn_w, 1)
                part = jnp.where(cnear_e, from_e, jnp.where(cnear_w, from_w, 0.0))
                cot[cbase + r, 8 * t : 8 * t + 8, :] = jnp.concatenate(
                    [lat_c[r, 8 * t : 8 * t + 8, :], part], axis=1
                )

    k1, k2, k3 = stacked_weights(w1), stacked_weights(w2), stacked_weights(w3)
    q1, q2, q3 = stacked_weights(v1), stacked_weights(v2), stacked_weights(v3)

    def wide_pack(ref, base):
        parts = []
        for t in range(5):
            rows = [ref[base + s, 8 * t : 8 * t + 8, COLS:WIDE] for s in range(8)]
            parts.append(slot_pack(rows, lambda s: 8 + SLOT * s, SLOT))
        return jnp.concatenate(parts, axis=0)

    def wide_unpack(ref, base, values):
        for s in range(8):
            ref[base + s, 0:FEATS, COLS:WIDE] = pltpu.roll(values, -(8 + SLOT * s) % COLS, 1)

    for r in range(ROWS):
        outs[PAD + r, :, 0:COLS] = own_m[r]

    def closure_of(columns):
        z = split(to_48(columns))
        _, _, h2 = hidden_layers(z, k1, b1[...], k2, b2[...])
        return product(k3, *split(h2))[0:FEATS] + b3[...]

    def halo_rows(first):
        o = closure_of(jnp.concatenate([s0[first + i, 0:FEATS, 0:COLS] for i in range(4)], axis=1))
        for i in range(4):
            outs[first + i, :, 0:COLS] = o[:, i * COLS : (i + 1) * COLS]

    @pl.when(has_south == 1)
    def _():
        halo_rows(PAD - 8)
        halo_rows(PAD - 4)

    @pl.when(has_north == 1)
    def _():
        halo_rows(PAD + ROWS)
        halo_rows(PAD + ROWS + 4)

    groups = 3 if sides == ["swap"] else 4
    first = PAD - 8 * has_south
    o = closure_of(jnp.concatenate([wide_pack(s0, first + 8 * g) for g in range(groups)], axis=1))
    for g in range(groups):
        wide_unpack(outs, first + 8 * g, o[:, g * COLS : (g + 1) * COLS])

    def section_1(src, dst):
        def body(r, _):
            d = tendency_row(k, src, r, cs[r], fs[r])
            put_state(
                k, dst, r,
                [tile(src, r, t) + 0.25 * mask_tile(masks, r, t) * d[t] for t in range(5)],
            )
            return 0
        return body

    def section_2(src, mid, dst):
        def body(r, _):
            d = tendency_row(k, mid, r, cs[r], fs[r])
            put_state(
                k, dst, r,
                [
                    0.75 * tile(src, r, t) + 0.25 * tile(mid, r, t)
                    + 0.0625 * mask_tile(masks, r, t) * d[t]
                    for t in range(5)
                ],
            )
            return 0
        return body

    total = jnp.zeros((8, COLS), F32)
    for i in range(sums.shape[0] // 8):
        total = total + sums[8 * i : 8 * i + 8, :]
    mean = total[0:1, 0:1] / total[1:2, 0:1]

    def section_3(src, mid, r):
        d = tendency_row(k, mid, r, cs[r], fs[r])
        new = []
        for t in range(5):
            m = mask_tile(masks, r, t)
            o = tile(outs, r, t)
            if t == 1:
                force = 2.0 * (mean - fluxes[r, 2:3, :])
                o = o + jnp.where(k.sub == 0, force, 0.0)
            new.append(
                (1.0 / 3.0) * tile(src, r, t) + (2.0 / 3.0) * tile(mid, r, t)
                + m * ((1.0 / 6.0) * d[t] + 0.25 * o)
            )
        return new

    def step_1_end(r, _):
        put_state(k, s3, r, section_3(s0, s2, r))
        return 0

    lax.fori_loop(lo(10), hi(10), section_1(s0, s1), 0)
    lax.fori_loop(lo(9), hi(9), section_2(s0, s1, s2), 0)
    lax.fori_loop(lo(8), hi(8), step_1_end, 0)
    for i in range(24):
        at = lo(4) + i
        keep_1[i] = s0[at, 0:FEATS, :]
        keep_2[i] = s1[at, 0:FEATS, :]
        keep_3[i] = s2[at, 0:FEATS, :]
        keep_mask[i] = masks[at]

    acc[...] = jnp.zeros(acc.shape, F32)

    def closure_adjoint(z, h1, h1s, h2, go, with_weights):
        gos = split(to_48(go))
        g2 = product(q3, *gos) * (1.0 - h2 * h2)
        g2s = split(g2)
        g1 = product(q2, *g2s) * (1.0 - h1 * h1)
        g1s = split(g1)
        if with_weights:
            add_weight_terms(acc, z, h1s, split(h2), g1s, g2s, gos)
        return product(q1, *g1s)[0:FEATS]

    def both_ways(columns, go, with_weights):
        z = split(to_48(columns))
        h1, h1s, h2 = hidden_layers(z, k1, b1[...], k2, b2[...])
        o = product(k3, *split(h2))[0:FEATS] + b3[...] if with_weights else None
        return o, closure_adjoint(z, h1, h1s, h2, go, with_weights)

    def masked_core(ref, r):
        m0, m4 = masks[r, 0:8, 0:COLS], masks[r, 8:16, 0:COLS]
        parts = [
            0.25 * (m4 if t == 4 else m0) * ref[r, 8 * t : 8 * t + 8, 0:COLS] for t in range(5)
        ]
        return jnp.concatenate(parts, axis=0)

    def mask_cot(r, _):
        for t in range(5):
            bbuf[r, 8 * t : 8 * t + 8, :] = 0.25 * mask_tile(masks, r, t) * tile(cot, r, t)
            abuf[r, 8 * t : 8 * t + 8, :] = (1.0 / 6.0) * mask_tile(masks, r, t) * tile(cot, r, t)
        return 0

    lax.fori_loop(lo(6), hi(6), mask_cot, 0)

    def core_rows(first, with_weights):
        z = jnp.concatenate([s3[first + i, 0:FEATS, 0:COLS] for i in range(4)], axis=1)
        go = jnp.concatenate([bbuf[first + i, 0:FEATS, 0:COLS] for i in range(4)], axis=1)
        o, back = both_ways(z, go, with_weights)
        for i in range(4):
            at = slice(i * COLS, (i + 1) * COLS)
            if with_weights:
                outs[first + i, :, 0:COLS] = o[:, at]
            gz[first + i, :, 0:COLS] = back[:, at]

    lax.fori_loop(0, ROWS // 4, lambda i, _: (core_rows(PAD + 4 * i, True), 0)[1], 0)

    @pl.when(has_south == 1)
    def _():
        core_rows(PAD - 4, False)

    @pl.when(has_north == 1)
    def _():
        core_rows(PAD + ROWS, False)

    first = lo(4)
    z = jnp.concatenate([wide_pack(s3, first + 8 * g) for g in range(3)], axis=1)
    go = jnp.concatenate([wide_pack(bbuf, first + 8 * g) for g in range(3)], axis=1)
    _, back = both_ways(z, go, False)
    for g in range(3):
        wide_unpack(gz, first + 8 * g, back[:, g * COLS : (g + 1) * COLS])

    lax.fori_loop(lo(7), hi(7), section_1(s3, s1), 0)
    lax.fori_loop(lo(6), hi(6), section_2(s3, s1, s2), 0)

    def last(r, _):
        new = section_3(s3, s2, r)
        put_result(final, r - PAD, [x[:, 0:COLS] for x in new])
        return 0

    lax.fori_loop(PAD, PAD + ROWS, last, 0)

    def store(r, tiles):
        for t in range(5):
            s4[r, 8 * t : 8 * t + 8, :] = tiles[t] + tile(gz, r, t)

    @pl.when(has_south == 0)
    def _():
        bbuf[PAD - 1] = jnp.zeros((FEATS, WIDE), F32)

    @pl.when(has_north == 0)
    def _():
        bbuf[PAD + ROWS] = jnp.zeros((FEATS, WIDE), F32)

    adjoint_sections(
        k, cs, fs, [(lo(h), hi(h)) for h in (5, 4, 3)], (s3, s1, s2), masks, abuf, bbuf, hold,
        store, lambda r, t: tile(cot, r, t),
    )

    def first_step(i, _):
        r = 4 * i
        side = lambda read: jnp.concatenate([read(r + j) for j in range(4)], axis=1)
        z = split(to_48(side(lambda j: own[j, 0:FEATS, :])))
        h1 = side(lambda j: own_h1[j])
        h2 = side(lambda j: own_h2[j])
        go = side(lambda j: masked_core(s4, PAD + j))
        back = closure_adjoint(z, h1, split(h1), h2, go, True)
        for j in range(4):
            from_closure[r + j] = back[:, j * COLS : (j + 1) * COLS]
        return 0

    lax.fori_loop(0, ROWS // 4, first_step, 0)
    for i in range(24):
        lam[i] = s4[lo(4) + i, 0:FEATS, :]
    grads[...] = jnp.zeros(grads.shape, F32)
    grads[0:40, 0:HID] = acc[0:40, 0:HID]
    grads[0:40, HID : 2 * HID] = acc[112:152, 0:HID]
    grads[40:72, 0:HID] = acc[48:80, 0:HID]
    grads[40:72, HID : 2 * HID] = acc[80:112, 0:HID]
    grads[72:73, 0:HID] = acc[160:161, 0:HID]
    grads[72:73, HID : 2 * HID] = acc[176:177, 0:HID]
    grads[73:74, 0:HID] = acc[192:193, 0:HID]


def put_result(ref, row, tiles):
    for t in range(4):
        ref[pl.ds(t * 10 * ROWS + row, 8, stride=ROWS), :] = tiles[t]
    ref[pl.ds(8 * ROWS + row, 4, stride=10 * ROWS), :] = tiles[4][0:4, :]
    ref[pl.ds(9 * ROWS + row, 4, stride=10 * ROWS), :] = tiles[4][4:8, :]


def back_kernel(scal, cs, fs, lam, from_closure, keep_1, keep_2, keep_3, keep_mask, grad, *scratch):
    s0, s1, s2, masks, top, abuf, bbuf, hold = scratch
    k = Row(WIDE)
    has_south, has_north = scal[2], scal[3]
    lo = lambda h: PAD - h * has_south
    hi = lambda h: PAD + ROWS + h * has_north
    for ref in (abuf, bbuf):
        for row in (PAD - 1, PAD + ROWS):
            ref[row] = jnp.zeros((FEATS, WIDE), F32)
    for ref in (s0, s1, s2):
        for row in (PAD - 1, PAD + ROWS):
            ref[row] = jnp.zeros(ref.shape[1:], F32)

    def fill(i, _):
        r = lo(4) + i
        masks[r] = keep_mask[i]
        for src, dst in ((keep_1, s0), (keep_2, s1), (keep_3, s2)):
            dst[r, 0:FEATS, :] = src[i]
            u4, v4 = deep_velocity(k, src[i, 32:40, :])
            dst[r, 56:64, :] = u4
            dst[r, 64:72, :] = v4
        top[r] = lam[i]
        return 0

    lax.fori_loop(0, hi(4) - lo(4), fill, 0)

    def mask_top(r, _):
        for t in range(5):
            abuf[r, 8 * t : 8 * t + 8, :] = (1.0 / 6.0) * mask_tile(masks, r, t) * tile(top, r, t)
        return 0

    lax.fori_loop(lo(3), hi(3), mask_top, 0)

    def store(r, tiles):
        done = []
        for t in range(5):
            m = masks[r, 8:16, 0:COLS] if t == 4 else masks[r, 0:8, 0:COLS]
            done.append(m * (tiles[t][:, 0:COLS] + from_closure[r - PAD, 8 * t : 8 * t + 8, :]))
        put_result(grad, r - PAD, done)

    adjoint_sections(
        k, cs, fs, [(lo(2), hi(2)), (lo(1), hi(1)), (PAD, PAD + ROWS)], (s0, s1, s2), masks,
        abuf, bbuf, hold, store, lambda r, t: tile(top, r, t),
    )


def sum_kernel(parts, scale, gathered, win, bin_, wmid, bmid, wout, bout):
    total = gathered[0:80, :]
    for i in range(1, parts):
        total = total + gathered[80 * i : 80 * i + 80, :]
    total = total * scale
    win[...] = total[0:40, 0:HID]
    wout[...] = total[0:40, HID : 2 * HID]
    wmid[0:32, :] = total[40:72, 0:HID]
    wmid[32:64, :] = total[40:72, HID : 2 * HID]
    bin_[...] = total[72:73, 0:HID]
    bmid[...] = total[72:73, HID : 2 * HID]
    bout[...] = total[73:74, 0:40]


def by_tile(weights):
    fields = weights.reshape(4, 10, -1)
    head = fields[:, :8].reshape(32, -1)
    return jnp.concatenate([head, fields[:, 8], fields[:, 9]], axis=0)


def from_tile(rows):
    head = rows[:32].reshape(4, 8, -1)
    tail = jnp.stack([rows[32:36], rows[36:40]], axis=1)
    return jnp.concatenate([head, tail], axis=1).reshape(40, -1)


def three(w):
    return jnp.concatenate([w, w, w], axis=1)


def pad_cols(w):
    return jnp.pad(w, ((0, 0), (0, 8)))


def latitude_terms(row_index, row_count):
    latitude = LAT_LIMIT * (2.0 * (jnp.clip(row_index, 0.0, row_count - 1.0) + 0.5) / row_count - 1.0)
    return 1.0 / jnp.cos(latitude), CORIOLIS * jnp.sin(latitude)


def on_device(
    initial_state, land_mask, surface_flux, weight_in, bias_in, weight_mid, bias_mid, weight_out, bias_out, cotangent
):
    lat_n, lon_n = lax.axis_size("lat"), lax.axis_size("lon")
    lat_i = lax.axis_index("lat")
    lat_total, lon_total = ROWS * lat_n, COLS * lon_n
    sides = ["swap"] if lat_n == 2 else ["north", "south"]
    is_low = (lat_i == 0).astype(jnp.int32)
    has_south = (lat_i > 0).astype(jnp.int32)
    has_north = (lat_i < lat_n - 1).astype(jnp.int32)
    scal = jnp.stack(
        [
            is_low * (ROWS - REACH),
            is_low * (ROWS - CREACH),
            has_south,
            has_north,
            jnp.where(is_low == 1, PAD + ROWS, 1),
            jnp.where(is_low == 1, PAD + ROWS, PAD - CREACH),
            jnp.where(is_low == 1, 0, ROWS - CREACH),
        ]
    ).astype(jnp.int32)
    rows = (lat_i * ROWS - PAD + jnp.arange(EXT, dtype=jnp.int32)).astype(F32)
    cs, fs = latitude_terms(rows, lat_total)

    packed = pl.pallas_call(
        lambda *refs: pack_kernel(sides, *refs),
        out_shape=[
            sds(ROWS, PACK, COLS), sds(ROWS, FEATS, COLS), sds(8, COLS),
            sds(2 * PACK + 40, COLS), sds(2 * PACK + 40, COLS),
        ]
        + [sds(REACH, PACK, COLS), sds(CREACH, FEATS, COLS), sds(PACK + 40, COLS), sds(PACK + 40, COLS)] * len(sides),
        in_specs=[SMEM] + [VMEM] * 4,
        out_specs=[VMEM] * (5 + 4 * len(sides)),
        compiler_params=PARAMS,
        name="pack_halos",
    )(
        scal,
        initial_state.reshape(40 * ROWS, COLS),
        land_mask.reshape(10 * ROWS, COLS),
        surface_flux,
        cotangent.reshape(40 * ROWS, COLS),
    )
    own, cown, sums, east_pay, west_pay = packed[:5]

    def lat_pairs(side):
        if side == "swap":
            return [(0, 1), (1, 0)]
        if side == "north":
            return [(i, i + 1) for i in range(lat_n - 1)]
        return [(i + 1, i) for i in range(lat_n - 1)]

    def diagonal(side, step):
        return [
            (i * lat_n + a, ((i + step) % lon_n) * lat_n + b)
            for i in range(lon_n)
            for a, b in lat_pairs(side)
        ]

    east_ring = [(i, (i + 1) % lon_n) for i in range(lon_n)]
    west_ring = [((i + 1) % lon_n, i) for i in range(lon_n)]
    received = []
    for i, side in enumerate(sides):
        lat_x, lat_c, diag_e, diag_w = packed[5 + 4 * i : 9 + 4 * i]
        received.append(
            [
                lax.ppermute(lat_x, "lat", lat_pairs(side)),
                lax.ppermute(lat_c, "lat", lat_pairs(side)),
                lax.ppermute(diag_e, ("lon", "lat"), diagonal(side, 1)),
                lax.ppermute(diag_w, ("lon", "lat"), diagonal(side, -1)),
            ]
        )
    from_west = lax.ppermute(east_pay, "lon", east_ring)
    from_east = lax.ppermute(west_pay, "lon", west_ring)
    all_sums = lax.all_gather(sums, ("lon", "lat"), tiled=True)

    w_in, w_out_t = by_tile(weight_in), by_tile(weight_out.T)
    col = lambda b: b.reshape(-1, 1)
    forward = [
        three(pad_cols(w_in.T)), col(bias_in), three(weight_mid.T), col(bias_mid), three(w_out_t), by_tile(col(bias_out)),
    ]
    forward[4] = jnp.pad(forward[4], ((0, 8), (0, 0)))
    backward = [jnp.pad(three(w_in), ((0, 8), (0, 0))), three(weight_mid), three(pad_cols(w_out_t.T))]

    own_m, own_h1, own_h2 = pl.pallas_call(
        own_closure_kernel,
        out_shape=[sds(ROWS, FEATS, COLS), sds(ROWS, HID, COLS), sds(ROWS, HID, COLS)],
        in_specs=[VMEM] * 7,
        out_specs=[VMEM] * 3,
        compiler_params=PARAMS,
        cost_estimate=pl.CostEstimate(flops=10**9, bytes_accessed=2 * 10**6, transcendentals=0),
        name="own_closure",
    )(own, *forward)

    state = pltpu.VMEM((EXT, 72, WIDE), F32)
    plain = pltpu.VMEM((EXT, FEATS, WIDE), F32)
    marks = pltpu.VMEM((EXT, 16, WIDE), F32)
    outs = pl.pallas_call(
        lambda *refs: main_kernel(sides, *refs),
        out_shape=[
            sds(40 * ROWS, COLS), sds(80, COLS), sds(24, FEATS, WIDE), sds(ROWS, FEATS, COLS),
            sds(24, FEATS, WIDE), sds(24, FEATS, WIDE), sds(24, FEATS, WIDE), sds(24, 16, WIDE),
        ],
        in_specs=[SMEM] * 3 + [VMEM] * (8 + 4 * len(sides) + 9),
        out_specs=[VMEM] * 8,
        scratch_shapes=[state] * 5
        + [marks, pltpu.VMEM((EXT, 8, WIDE), F32)]
        + [plain] * 6
        + [pltpu.VMEM((208, HID), F32)],
        compiler_params=PARAMS,
        cost_estimate=pl.CostEstimate(flops=5 * 10**9, bytes_accessed=10**7, transcendentals=0),
        name="steps_and_adjoint",
    )(
        scal, cs, fs, all_sums, own, cown, own_m, own_h1, own_h2, from_west, from_east,
        *[item for side in received for item in side], *forward, *backward,
    )
    final, grads, lam, from_closure, keep_1, keep_2, keep_3, keep_mask = outs
    gathered = lax.all_gather(grads, ("lon", "lat"), tiled=True)

    state_grad = pl.pallas_call(
        back_kernel,
        out_shape=sds(40 * ROWS, COLS),
        in_specs=[SMEM] * 3 + [VMEM] * 6,
        out_specs=VMEM,
        scratch_shapes=[state] * 3 + [marks] + [plain] * 4,
        compiler_params=PARAMS,
        cost_estimate=pl.CostEstimate(flops=3 * 10**9, bytes_accessed=10**7, transcendentals=0),
        name="first_step_adjoint",
    )(scal, cs, fs, lam, from_closure, keep_1, keep_2, keep_3, keep_mask)

    parts = lat_n * lon_n
    scale = 1.0 / math.sqrt(lat_total * lon_total)
    g_in, g_bin, g_mid, g_bmid, g_out, g_bout = pl.pallas_call(
        lambda *refs: sum_kernel(parts, scale, *refs),
        out_shape=[sds(40, HID), sds(1, HID), sds(HID, HID), sds(1, HID), sds(40, HID), sds(1, 40)],
        in_specs=[VMEM],
        out_specs=[VMEM] * 6,
        compiler_params=PARAMS,
        name="sum_weight_grads",
    )(gathered)
    shape = initial_state.shape
    return (
        final.reshape(shape),
        state_grad.reshape(shape),
        from_tile(g_in),
        g_bin.reshape(-1),
        g_mid,
        g_bmid.reshape(-1),
        from_tile(g_out).T,
        from_tile(g_bout.reshape(40, 1)).reshape(-1),
    )


def solution(mesh):
    split_state = P(None, None, "lat", "lon")
    return jax.shard_map(
        on_device,
        mesh=mesh,
        in_specs=(split_state, P(None, "lat", "lon"), P("lat", "lon"), P(), P(), P(), P(), P(), P(), split_state),
        out_specs=(split_state, split_state, P(), P(), P(), P(), P(), P()),
        check_vma=False,
    )
```

profile of v0, /device:TPU:0, one launch (start us, length us, event | category | flops | bytes accessed | tf_op | source)
XLA Modules:
  0.0 196.1 jit_solution(7750711956641882832)
XLA Ops:
  7.4 1.0 copy-done.1
  8.3 1.0 copy-done.2
  9.3 0.9 copy-done.3
  10.9 1.2 pack_halos.1
  12.1 2.5 %collective-permute-start.4 = (f32[96,128]{1,0:T(8,128)S(1)}, f32[96,128]{1,0:T(8,128)S(1)}, u32[]{:S(2)}, u32[]{:S(2)}) collective-permute-start(f32[96,128]{1,0:T(8,128)S(1)} %get-tuple-element.44), channel_id=1, source_target_pairs={{0,3},{1,2},{2,5},{3,4},{4,7},{5,6},{6,9},{7,8},{8,11},{9,10},{10,... | collective-permute-start | bytes 147464 | tf_op jit(solution)/shard_map/ppermute | solution.py:795
  14.5 1.6 collective-permute-start
  16.1 2.8 %collective-permute-start.1 = (f32[152,128]{1,0:T(8,128)S(1)}, f32[152,128]{1,0:T(8,128)S(1)}, u32[]{:S(2)}, u32[]{:S(2)}) collective-permute-start(f32[152,128]{1,0:T(8,128)S(1)} %get-tuple-element.41), channel_id=1, source_target_pairs={{2,0},{4,2},{6,4},{8,6},{10,8},{12,10},{14,12},{16,14},{18,16},{20... | collective-permute-start | bytes 233480 | tf_op jit(solution)/shard_map/ppermute | solution.py:800
  19.6 1.4 collective-permute-start.2
  21.7 0.7 reshape.87
  24.4 1.9 own_closure.1
  26.4 67.0 %all_gather.6.refs_3_ = f32[256,128]{1,0:T(8,128)S(1)} all-gather(f32[8,128]{1,0:T(8,128)S(1)} %get-tuple-element.34), channel_id=1, replica_groups=mesh['lon'=16,'lat'=2] {'lon','lat'}, dimensions={0}, use_global_device_ids=true | all-gather | bytes 135168 | tf_op jit(solution)/shard_map/all_gather | solution.py:801
  93.4 36.7 %steps_and_adjoint.1 = (f32[640,128]{1,0:T(8,128)}, f32[80,128]{1,0:T(8,128)}, f32[24,40,256]{2,1,0:T(8,128)S(1)}, f32[16,40,128]{2,1,0:T(8,128)S(1)}, f32[24,40...) custom-call(s32[7]{0:T(128)S(1)} %stack.57.refs_0_.scal, ...), custom_call_target="tpu_custom_call" | custom-call | flops 5000000000 | bytes 10000000 | tf_op jit(solution)/shard_map/steps_and_adjoint/pallas_call | solution.py:824
  130.1 1.0 copy-done.5
  131.0 1.0 copy-done.7
  132.0 1.0 copy-done.9
  132.9 0.8 copy-done.11
  134.5 1.2 copy-done.6
  135.7 1.2 copy-done.8
  136.9 1.2 copy-done.10
  138.1 1.0 copy-done.12
  139.1 1.0 copy-done.14
  140.0 8.4 %first_step_adjoint.1 = f32[640,128]{1,0:T(8,128)} custom-call(s32[7]{0:T(128)S(1)} %stack.57.refs_0_.scal, f32[40]{0:T(128)S(1)} %get-tuple-element.72.refs_1_.cs, f32[40]{0:T(128)S(1)} %get-tuple-element.73.refs_2_.fs, f32[24,40,256]{2,1,0:T(8,128)S(1)} %get-tuple-element.47.lam, f32[16,40,128]{2,1,0:T(8,128)S(1)} %copy-done.14, ...), custom_call_target="tpu_custom_call" | custom-call | flops 3000000000 | bytes 10000000 | tf_op jit(solution)/shard_map/first_step_adjoint/pallas_call | solution.py:846
  148.5 36.4 %all-gather.2.cloned.1.call-done.refs_0_ = f32[2560,128]{1,0:T(8,128)} async-done(((f32[80,128]{1,0:T(8,128)}), f32[2560,128]{1,0:T(8,128)}) %all-gather.2.cloned.1.call-update) | async-done | bytes 1310736 | tf_op jit(solution)/shard_map/all_gather | solution.py:844
  184.9 1.3 copy-done
  (80 shorter events, 7.9 us)
Async XLA Ops:
  7.2 15.8 %copy-start.18 = (f32[40]{0:T(128)S(1)}, f32[40]{0:T(128)}, u32[]{:S(2)}) copy-start(f32[40]{0:T(128)} %param.18) | copy-start | bytes 484
  7.2 16.7 %copy-start.16 = (f32[64]{0:T(128)S(1)}, f32[64]{0:T(128)}, u32[]{:S(2)}) copy-start(f32[64]{0:T(128)} %param.14) | copy-start | bytes 772
  7.2 16.8 %copy-start.17 = (f32[64]{0:T(128)S(1)}, f32[64]{0:T(128)}, u32[]{:S(2)}) copy-start(f32[64]{0:T(128)} %param.16) | copy-start | bytes 772
  7.2 16.9 %copy-start.15 = (f32[64,64]{1,0:T(8,128)S(1)}, f32[64,64]{1,0:T(8,128)}, u32[]{:S(2)}) copy-start(f32[64,64]{1,0:T(8,128)} %param.15) | copy-start | bytes 49156
  7.2 177.7 %all-gather.2.cloned.1.call-start = ((), (), s32[]{:S(2)}) async-start(), calls=%async_computation | async-start | bytes 1351680 | tf_op jit(solution)/shard_map/all_gather | solution.py:844
  7.4 1.0 copy-start.1
  8.3 1.0 copy-start.2
  9.3 0.9 copy-start.3
  12.1 14.3 %collective-permute-start.4 = (f32[96,128]{1,0:T(8,128)S(1)}, f32[96,128]{1,0:T(8,128)S(1)}, u32[]{:S(2)}, u32[]{:S(2)}) collective-permute-start(f32[96,128]{1,0:T(8,128)S(1)} %get-tuple-element.44), channel_id=1, source_target_pairs={{0,3},{1,2},{2,5},{3,4},{4,7},{5,6},{6,9},{7,8},{8,11},{9,10},{10,... | collective-permute-start | bytes 147464 | tf_op jit(solution)/shard_map/ppermute | solution.py:795
  14.5 78.8 %collective-permute-start = (f32[152,128]{1,0:T(8,128)S(1)}, f32[152,128]{1,0:T(8,128)S(1)}, u32[]{:S(2)}, u32[]{:S(2)}) collective-permute-start(f32[152,128]{1,0:T(8,128)S(1)} %get-tuple-element.40), channel_id=1, source_target_pairs={{0,2},{2,4},{4,6},{6,8},{8,10},{10,12},{12,14},{14,16},{16,18},{18... | collective-permute-start | bytes 233480 | tf_op jit(solution)/shard_map/ppermute | solution.py:799
  16.1 77.2 %collective-permute-start.1 = (f32[152,128]{1,0:T(8,128)S(1)}, f32[152,128]{1,0:T(8,128)S(1)}, u32[]{:S(2)}, u32[]{:S(2)}) collective-permute-start(f32[152,128]{1,0:T(8,128)S(1)} %get-tuple-element.41), channel_id=1, source_target_pairs={{2,0},{4,2},{6,4},{8,6},{10,8},{12,10},{14,12},{16,14},{18,16},{20... | collective-permute-start | bytes 233480 | tf_op jit(solution)/shard_map/ppermute | solution.py:800
  19.0 74.4 %collective-permute-start.3 = (f32[6,40,128]{2,1,0:T(8,128)S(1)}, f32[6,40,128]{2,1,0:T(8,128)S(1)}, u32[]{:S(2)}, u32[]{:S(2)}) collective-permute-start(f32[6,40,128]{2,1,0:T(8,128)S(1)} %get-tuple-element.43), channel_id=1, source_target_pairs={{0,1},{1,0},{2,3},{3,2},{4,5},{5,4},{6,7},{7,6},{8,9},{9,8},{10,11... | collective-permute-start | bytes 368648 | tf_op jit(solution)/shard_map/ppermute | solution.py:794
  19.6 73.8 %collective-permute-start.2 = (f32[11,56,128]{2,1,0:T(8,128)S(1)}, f32[11,56,128]{2,1,0:T(8,128)S(1)}, u32[]{:S(2)}, u32[]{:S(2)}) collective-permute-start(f32[11,56,128]{2,1,0:T(8,128)S(1)} %get-tuple-element.42), channel_id=1, source_target_pairs={{0,1},{1,0},{2,3},{3,2},{4,5},{5,4},{6,7},{7,6},{8,9},{9,8},{10,11... | collective-permute-start | bytes 946184 | tf_op jit(solution)/shard_map/ppermute | solution.py:793
  26.3 67.0 %collective-permute-start.5 = (f32[96,128]{1,0:T(8,128)S(1)}, f32[96,128]{1,0:T(8,128)S(1)}, u32[]{:S(2)}, u32[]{:S(2)}) collective-permute-start(f32[96,128]{1,0:T(8,128)S(1)} %get-tuple-element.45), channel_id=1, source_target_pairs={{0,31},{1,30},{2,1},{3,0},{4,3},{5,2},{6,5},{7,4},{8,7},{9,6},{10,... | collective-permute-start | bytes 147464 | tf_op jit(solution)/shard_map/ppermute | solution.py:796
  130.1 1.0 copy-start.5
  131.0 1.0 copy-start.7
  132.0 1.0 copy-start.9
  132.9 0.8 copy-start.11
  134.5 1.2 copy-start.6
  135.7 1.2 copy-start.8
  136.9 1.2 copy-start.10
  138.1 1.0 copy-start.12
  139.1 1.0 copy-start.14
  184.9 1.3 copy-start
  (2 other events, 1.4 us)
Sparse Core Ops, SparseCore 0:
  134.6 50.2 all-gather.1
where the time goes:
time: 197 us; the launch traced here: 196 us
  blocking collectives  67 us (34%)
  Pallas kernels  48.9 us (25%)
  waiting for transfers between devices  36.4 us (18%)
  local copies, waits for them, and re-layouts  19.7 us (10%)
  between operations  14.3 us (7%)
  starting transfers between devices  9.02 us (5%)
    all_gather x1, blocking collectives, on_device(): all_sums = lax.all_gather(sums, ('lon', 'lat'), tiled=True)  67 us
    pallas_call x1, Pallas kernels, on_device(): pl.pallas_call(lambda *refs: main_kernel(sides, *refs), out_shape=[sds(40...  36.7 us
    all_gather x1, waiting for transfers between devices, on_device(): gathered = lax.all_gather(grads, ('lon', 'lat'), tiled=True)  36.4 us
    unnamed x41, local copies, waits for them, and re-layouts  15.1 us
    pallas_call x1, Pallas kernels, on_device(): pl.pallas_call(back_kernel, out_shape=sds(40 * ROWS, COLS), in_specs=[SME...  8.43 us
  transfers between devices with their start and end apart: 7, of which 1 were waited for; matrix products, arithmetic and copies ran while one was open for 2% of the time, Pallas kernels for 5%

commit v1 on v0

--- a/solution.py
+++ b/solution.py
@@ -27,7 +27,10 @@
 BF16 = jnp.bfloat16
 VMEM = pl.BlockSpec(memory_space=pltpu.VMEM)
 SMEM = pl.BlockSpec(memory_space=pltpu.SMEM)
-PARAMS = pltpu.CompilerParams(vmem_limit_bytes=44 * 1024 * 1024)
+
+
+def params(megabytes):
+    return pltpu.CompilerParams(vmem_limit_bytes=megabytes * 1024 * 1024)
 
 
 def sds(*shape):
@@ -54,9 +57,16 @@
     return packed
 
 
-def pack_kernel(sides, scal, x, mask, flux, cot, *outs):
+def pack_kernel(sides, scal, x_hbm, mask_hbm, flux_hbm, cot_hbm, *outs):
+    x, mask, flux, cot, sems = outs[-5:]
     own, cown, sums, east, west = outs[:5]
     per_side = [outs[5 + 4 * i : 9 + 4 * i] for i in range(len(sides))]
+    pairs = ((mask_hbm, mask), (x_hbm, x), (flux_hbm, flux), (cot_hbm, cot))
+    copies = [pltpu.make_async_copy(a, b, sems.at[i]) for i, (a, b) in enumerate(pairs)]
+    for copy in copies:
+        copy.start()
+    for copy in copies:
+        copy.wait()
     for r in range(ROWS):
         first = mask[pl.ds(r, 8, stride=ROWS), :].astype(F32)
         m8 = mask[8 * ROWS + r : 8 * ROWS + r + 1, :].astype(F32)
@@ -311,39 +321,38 @@
     return tile(ref, row, 1 if t == 4 else 0)
 
 
-def adjoint_sections(k, cs, fs, bounds, states, masks, abuf, bbuf, hold, store, top):
-    state_1, state_2, state_3 = states
-
-    def third(r, _):
-        d = adjoint_row(k, state_3, abuf, r, cs[r], fs[r])
+def adjoint_third(k, cs, fs, bounds, state, masks, abuf, top, hold, bbuf):
+    def body(r, _):
+        d = adjoint_row(k, state, abuf, r, cs[r], fs[r])
         for t in range(5):
-            ts = (2.0 / 3.0) * top(r, t) + d[t]
+            ts = (2.0 / 3.0) * tile(top, r, t) + d[t]
             hold[r, 8 * t : 8 * t + 8, :] = ts
             bbuf[r, 8 * t : 8 * t + 8, :] = 0.0625 * mask_tile(masks, r, t) * ts
         return 0
 
-    def second(r, _):
-        d = adjoint_row(k, state_2, bbuf, r, cs[r], fs[r])
+    lax.fori_loop(*bounds, body, 0)
+
+
+def adjoint_second(k, cs, fs, bounds, state, masks, bbuf, top, hold, left, abuf):
+    def body(r, _):
+        d = adjoint_row(k, state, bbuf, r, cs[r], fs[r])
         for t in range(5):
             ts = tile(hold, r, t)
             tf = 0.25 * ts + d[t]
-            hold[r, 8 * t : 8 * t + 8, :] = (1.0 / 3.0) * top(r, t) + 0.75 * ts + tf
+            left[r, 8 * t : 8 * t + 8, :] = (1.0 / 3.0) * tile(top, r, t) + 0.75 * ts + tf
             abuf[r, 8 * t : 8 * t + 8, :] = 0.25 * mask_tile(masks, r, t) * tf
         return 0
 
-    def first(r, _):
-        d = adjoint_row(k, state_1, abuf, r, cs[r], fs[r])
-        store(r, [tile(hold, r, t) + d[t] for t in range(5)])
-        return 0
-
-    lax.fori_loop(*bounds[0], third, 0)
-    lax.fori_loop(*bounds[1], second, 0)
-    lax.fori_loop(*bounds[2], first, 0)
-
-
-def unpack(packed, slot_shift, keep):
-    turned = pltpu.roll(packed, slot_shift % COLS, 1)
-    return jnp.where(keep, turned, 0.0)
+    lax.fori_loop(*bounds, body, 0)
+
+
+def adjoint_first(k, cs, fs, bounds, state, abuf, left, store):
+    def body(r, _):
+        d = adjoint_row(k, state, abuf, r, cs[r], fs[r])
+        store(r, [tile(left, r, t) + d[t] for t in range(5)])
+        return 0
+
+    lax.fori_loop(*bounds, body, 0)
 
 
 def edges(reach):
@@ -351,18 +360,54 @@
     return lane < reach, lane >= COLS - reach
 
 
-def main_kernel(sides, scal, cs, fs, sums, own, cown, own_m, own_h1, own_h2, east, west, *rest):
+def wide_pack(ref, base):
+    parts = []
+    for t in range(5):
+        rows = [ref[base + s, 8 * t : 8 * t + 8, COLS:WIDE] for s in range(8)]
+        parts.append(slot_pack(rows, lambda s: 8 + SLOT * s, SLOT))
+    return jnp.concatenate(parts, axis=0)
+
+def wide_unpack(ref, base, values):
+    for s in range(8):
+        ref[base + s, 0:FEATS, COLS:WIDE] = pltpu.roll(values, -(8 + SLOT * s) % COLS, 1)
+
+
+def section_1(k, cs, fs, masks, src, dst):
+    def body(r, _):
+        d = tendency_row(k, src, r, cs[r], fs[r])
+        put_state(
+            k, dst, r,
+            [tile(src, r, t) + 0.25 * mask_tile(masks, r, t) * d[t] for t in range(5)],
+        )
+        return 0
+    return body
+
+def section_2(k, cs, fs, masks, src, mid, dst):
+    def body(r, _):
+        d = tendency_row(k, mid, r, cs[r], fs[r])
+        put_state(
+            k, dst, r,
+            [
+                0.75 * tile(src, r, t) + 0.25 * tile(mid, r, t)
+                + 0.0625 * mask_tile(masks, r, t) * d[t]
+                for t in range(5)
+            ],
+        )
+        return 0
+    return body
+
+
+def early_kernel(sides, scal, cs, fs, gate, own, cown, own_m, east, west, *rest):
     n = len(sides)
     side_refs = [rest[4 * i : 4 * i + 4] for i in range(n)]
-    (w1, b1, w2, b2, w3, b3, v1, v2, v3), rest = rest[4 * n : 4 * n + 9], rest[4 * n + 9 :]
-    final, grads, lam, from_closure, keep_1, keep_2, keep_3, keep_mask = rest[:8]
-    s0, s1, s2, s3, s4, masks, fluxes, cot, outs, gz, abuf, bbuf, hold, acc = rest[8:]
+    (w1, b1, w2, b2, w3, b3), rest = rest[4 * n : 4 * n + 6], rest[4 * n + 6 :]
+    s0, s1, s2, masks, fluxes, cot, outs = rest
     k = Row(WIDE)
     has_south, has_north = scal[2], scal[3]
     lo = lambda h: PAD - h * has_south
     hi = lambda h: PAD + ROWS + h * has_north
 
-    for ref in (s0, s1, s2, s3, s4, abuf, bbuf):
+    for ref in (s0, s1, s2):
         for row in (PAD - 1, PAD + ROWS):
             ref[row] = jnp.zeros(ref.shape[1:], F32)
 
@@ -421,18 +466,6 @@
                 )
 
     k1, k2, k3 = stacked_weights(w1), stacked_weights(w2), stacked_weights(w3)
-    q1, q2, q3 = stacked_weights(v1), stacked_weights(v2), stacked_weights(v3)
-
-    def wide_pack(ref, base):
-        parts = []
-        for t in range(5):
-            rows = [ref[base + s, 8 * t : 8 * t + 8, COLS:WIDE] for s in range(8)]
-            parts.append(slot_pack(rows, lambda s: 8 + SLOT * s, SLOT))
-        return jnp.concatenate(parts, axis=0)
-
-    def wide_unpack(ref, base, values):
-        for s in range(8):
-            ref[base + s, 0:FEATS, COLS:WIDE] = pltpu.roll(values, -(8 + SLOT * s) % COLS, 1)
 
     for r in range(ROWS):
         outs[PAD + r, :, 0:COLS] = own_m[r]
@@ -463,41 +496,34 @@
     for g in range(groups):
         wide_unpack(outs, first + 8 * g, o[:, g * COLS : (g + 1) * COLS])
 
-    def section_1(src, dst):
-        def body(r, _):
-            d = tendency_row(k, src, r, cs[r], fs[r])
-            put_state(
-                k, dst, r,
-                [tile(src, r, t) + 0.25 * mask_tile(masks, r, t) * d[t] for t in range(5)],
-            )
-            return 0
-        return body
-
-    def section_2(src, mid, dst):
-        def body(r, _):
-            d = tendency_row(k, mid, r, cs[r], fs[r])
-            put_state(
-                k, dst, r,
-                [
-                    0.75 * tile(src, r, t) + 0.25 * tile(mid, r, t)
-                    + 0.0625 * mask_tile(masks, r, t) * d[t]
-                    for t in range(5)
-                ],
-            )
-            return 0
-        return body
-
-    total = jnp.zeros((8, COLS), F32)
-    for i in range(sums.shape[0] // 8):
-        total = total + sums[8 * i : 8 * i + 8, :]
-    mean = total[0:1, 0:1] / total[1:2, 0:1]
-
-    def section_3(src, mid, r):
+    lax.fori_loop(lo(10), hi(10), section_1(k, cs, fs, masks, s0, s1), 0)
+    lax.fori_loop(lo(9), hi(9), section_2(k, cs, fs, masks, s0, s1, s2), 0)
+
+
+def late_kernel(
+    scal, cs, fs, sums, own, own_h1, own_h2, s0, s1, s2, masks, fluxes, cot, outs_in,
+    w1, b1, w2, b2, w3, b3, v1, v2, v3, final, grads, s4, abuf, from_closure, *scratch
+):
+    s3, t1, t2, outs, gz, bbuf, hold, acc = scratch
+    k = Row(WIDE)
+    has_south, has_north = scal[2], scal[3]
+    lo = lambda h: PAD - h * has_south
+    hi = lambda h: PAD + ROWS + h * has_north
+
+    for ref in (s3, t1, t2, abuf, bbuf):
+        for row in (PAD - 1, PAD + ROWS):
+            ref[row] = jnp.zeros(ref.shape[1:], F32)
+    k1, k2, k3 = stacked_weights(w1), stacked_weights(w2), stacked_weights(w3)
+    q1, q2, q3 = stacked_weights(v1), stacked_weights(v2), stacked_weights(v3)
+
+    mean = sums[0:1, 0:1] / sums[1:2, 0:1]
+
+    def section_3(src, mid, net, r):
         d = tendency_row(k, mid, r, cs[r], fs[r])
         new = []
         for t in range(5):
             m = mask_tile(masks, r, t)
-            o = tile(outs, r, t)
+            o = tile(net, r, t)
             if t == 1:
                 force = 2.0 * (mean - fluxes[r, 2:3, :])
                 o = o + jnp.where(k.sub == 0, force, 0.0)
@@ -511,15 +537,11 @@
         put_state(k, s3, r, section_3(s0, s2, r))
         return 0
 
-    lax.fori_loop(lo(10), hi(10), section_1(s0, s1), 0)
-    lax.fori_loop(lo(9), hi(9), section_2(s0, s1, s2), 0)
+    def step_1_end(r, _):
+        put_state(k, s3, r, section_3(s0, s2, outs_in, r))
+        return 0
+
     lax.fori_loop(lo(8), hi(8), step_1_end, 0)
-    for i in range(24):
-        at = lo(4) + i
-        keep_1[i] = s0[at, 0:FEATS, :]
-        keep_2[i] = s1[at, 0:FEATS, :]
-        keep_3[i] = s2[at, 0:FEATS, :]
-        keep_mask[i] = masks[at]
 
     acc[...] = jnp.zeros(acc.shape, F32)
 
@@ -581,11 +603,11 @@
     for g in range(3):
         wide_unpack(gz, first + 8 * g, back[:, g * COLS : (g + 1) * COLS])
 
-    lax.fori_loop(lo(7), hi(7), section_1(s3, s1), 0)
-    lax.fori_loop(lo(6), hi(6), section_2(s3, s1, s2), 0)
+    lax.fori_loop(lo(7), hi(7), section_1(k, cs, fs, masks, s3, t1), 0)
+    lax.fori_loop(lo(6), hi(6), section_2(k, cs, fs, masks, s3, t1, t2), 0)
 
     def last(r, _):
-        new = section_3(s3, s2, r)
+        new = section_3(s3, t2, outs, r)
         put_result(final, r - PAD, [x[:, 0:COLS] for x in new])
         return 0
 
@@ -595,18 +617,9 @@
         for t in range(5):
             s4[r, 8 * t : 8 * t + 8, :] = tiles[t] + tile(gz, r, t)
 
-    @pl.when(has_south == 0)
-    def _():
-        bbuf[PAD - 1] = jnp.zeros((FEATS, WIDE), F32)
-
-    @pl.when(has_north == 0)
-    def _():
-        bbuf[PAD + ROWS] = jnp.zeros((FEATS, WIDE), F32)
-
-    adjoint_sections(
-        k, cs, fs, [(lo(h), hi(h)) for h in (5, 4, 3)], (s3, s1, s2), masks, abuf, bbuf, hold,
-        store, lambda r, t: tile(cot, r, t),
-    )
+    adjoint_third(k, cs, fs, (lo(5), hi(5)), t2, masks, abuf, cot, hold, bbuf)
+    adjoint_second(k, cs, fs, (lo(4), hi(4)), t1, masks, bbuf, cot, hold, hold, abuf)
+    adjoint_first(k, cs, fs, (lo(3), hi(3)), s3, abuf, hold, store)
 
     def first_step(i, _):
         r = 4 * i
@@ -621,8 +634,15 @@
         return 0
 
     lax.fori_loop(0, ROWS // 4, first_step, 0)
-    for i in range(24):
-        lam[i] = s4[lo(4) + i, 0:FEATS, :]
+    for row in (PAD - 1, PAD + ROWS):
+        abuf[row] = jnp.zeros((FEATS, WIDE), F32)
+
+    def mask_top(r, _):
+        for t in range(5):
+            abuf[r, 8 * t : 8 * t + 8, :] = (1.0 / 6.0) * mask_tile(masks, r, t) * tile(s4, r, t)
+        return 0
+
+    lax.fori_loop(lo(3), hi(3), mask_top, 0)
     grads[...] = jnp.zeros(grads.shape, F32)
     grads[0:40, 0:HID] = acc[0:40, 0:HID]
     grads[0:40, HID : 2 * HID] = acc[112:152, 0:HID]
@@ -640,39 +660,23 @@
     ref[pl.ds(9 * ROWS + row, 4, stride=10 * ROWS), :] = tiles[4][4:8, :]
 
 
-def back_kernel(scal, cs, fs, lam, from_closure, keep_1, keep_2, keep_3, keep_mask, grad, *scratch):
-    s0, s1, s2, masks, top, abuf, bbuf, hold = scratch
-    k = Row(WIDE)
-    has_south, has_north = scal[2], scal[3]
-    lo = lambda h: PAD - h * has_south
-    hi = lambda h: PAD + ROWS + h * has_north
-    for ref in (abuf, bbuf):
-        for row in (PAD - 1, PAD + ROWS):
-            ref[row] = jnp.zeros((FEATS, WIDE), F32)
-    for ref in (s0, s1, s2):
-        for row in (PAD - 1, PAD + ROWS):
-            ref[row] = jnp.zeros(ref.shape[1:], F32)
-
-    def fill(i, _):
-        r = lo(4) + i
-        masks[r] = keep_mask[i]
-        for src, dst in ((keep_1, s0), (keep_2, s1), (keep_3, s2)):
-            dst[r, 0:FEATS, :] = src[i]
-            u4, v4 = deep_velocity(k, src[i, 32:40, :])
-            dst[r, 56:64, :] = u4
-            dst[r, 64:72, :] = v4
-        top[r] = lam[i]
-        return 0
-
-    lax.fori_loop(0, hi(4) - lo(4), fill, 0)
-
-    def mask_top(r, _):
-        for t in range(5):
-            abuf[r, 8 * t : 8 * t + 8, :] = (1.0 / 6.0) * mask_tile(masks, r, t) * tile(top, r, t)
-        return 0
-
-    lax.fori_loop(lo(3), hi(3), mask_top, 0)
-
+def limits(scal, reach):
+    return PAD - reach * scal[2], PAD + ROWS + reach * scal[3]
+
+
+def back_third_kernel(scal, cs, fs, state, masks, abuf, top, hold, bbuf):
+    for row in (PAD - 1, PAD + ROWS):
+        bbuf[row] = jnp.zeros((FEATS, WIDE), F32)
+    adjoint_third(Row(WIDE), cs, fs, limits(scal, 2), state, masks, abuf, top, hold, bbuf)
+
+
+def back_second_kernel(scal, cs, fs, gate, state, masks, bbuf, top, hold, left, abuf):
+    for row in (PAD - 1, PAD + ROWS):
+        abuf[row] = jnp.zeros((FEATS, WIDE), F32)
+    adjoint_second(Row(WIDE), cs, fs, limits(scal, 1), state, masks, bbuf, top, hold, left, abuf)
+
+
+def back_first_kernel(scal, cs, fs, gate, state, masks, abuf, left, from_closure, grad):
     def store(r, tiles):
         done = []
         for t in range(5):
@@ -680,36 +684,50 @@
             done.append(m * (tiles[t][:, 0:COLS] + from_closure[r - PAD, 8 * t : 8 * t + 8, :]))
         put_result(grad, r - PAD, done)
 
-    adjoint_sections(
-        k, cs, fs, [(lo(2), hi(2)), (lo(1), hi(1)), (PAD, PAD + ROWS)], (s0, s1, s2), masks,
-        abuf, bbuf, hold, store, lambda r, t: tile(top, r, t),
-    )
-
-
-def sum_kernel(parts, scale, gathered, win, bin_, wmid, bmid, wout, bout):
-    total = gathered[0:80, :]
-    for i in range(1, parts):
-        total = total + gathered[80 * i : 80 * i + 80, :]
-    total = total * scale
-    win[...] = total[0:40, 0:HID]
-    wout[...] = total[0:40, HID : 2 * HID]
-    wmid[0:32, :] = total[40:72, 0:HID]
-    wmid[32:64, :] = total[40:72, HID : 2 * HID]
-    bin_[...] = total[72:73, 0:HID]
-    bmid[...] = total[72:73, HID : 2 * HID]
-    bout[...] = total[73:74, 0:40]
+    adjoint_first(Row(WIDE), cs, fs, (PAD, PAD + ROWS), state, abuf, left, store)
+
+
+def unpack_kernel(scale, packed, win, bin_, wmid, bmid, wout, bout):
+    for ref, lanes in ((win, slice(0, HID)), (wout, slice(HID, 2 * HID))):
+        for t in range(4):
+            ref[10 * t : 10 * t + 8, :] = packed[8 * t : 8 * t + 8, lanes] * scale
+            ref[10 * t + 8 : 10 * t + 9, :] = packed[32 + t : 33 + t, lanes] * scale
+            ref[10 * t + 9 : 10 * t + 10, :] = packed[36 + t : 37 + t, lanes] * scale
+    wmid[0:32, :] = packed[40:72, 0:HID] * scale
+    wmid[32:64, :] = packed[40:72, HID : 2 * HID] * scale
+    bin_[...] = packed[72:73, 0:HID] * scale
+    bmid[...] = packed[72:73, HID : 2 * HID] * scale
+    for t in range(4):
+        bout[:, 10 * t : 10 * t + 8] = packed[73:74, 8 * t : 8 * t + 8] * scale
+        bout[:, 10 * t + 8 : 10 * t + 9] = packed[73:74, 32 + t : 33 + t] * scale
+        bout[:, 10 * t + 9 : 10 * t + 10] = packed[73:74, 36 + t : 37 + t] * scale
 
 
 def by_tile(weights):
-    fields = weights.reshape(4, 10, -1)
-    head = fields[:, :8].reshape(32, -1)
-    return jnp.concatenate([head, fields[:, 8], fields[:, 9]], axis=0)
-
-
-def from_tile(rows):
-    head = rows[:32].reshape(4, 8, -1)
-    tail = jnp.stack([rows[32:36], rows[36:40]], axis=1)
-    return jnp.concatenate([head, tail], axis=1).reshape(40, -1)
+    heads = [weights[10 * t : 10 * t + 8] for t in range(4)]
+    tails = [weights[10 * t + level : 10 * t + level + 1] for level in (8, 9) for t in range(4)]
+    return jnp.concatenate(heads + tails, axis=0)
+
+
+def tree_round(x, axis, count, stride):
+    group = 4 if (count // stride) % 4 == 0 else 2
+    got = [
+        lax.ppermute(x, axis, [(i, i ^ (j * stride)) for i in range(count)]) for j in range(1, group)
+    ]
+    x = x + got[0] if group == 2 else (x + got[0]) + (got[1] + got[2])
+    return x, stride * group
+
+
+def tree_rounds(x, axes):
+    for axis, count in axes:
+        if count & (count - 1):
+            x = lax.psum(x, axis)
+            yield x
+            continue
+        stride = 1
+        while stride < count:
+            x, stride = tree_round(x, axis, count, stride)
+            yield x
 
 
 def three(w):
@@ -756,9 +774,13 @@
             sds(2 * PACK + 40, COLS), sds(2 * PACK + 40, COLS),
         ]
         + [sds(REACH, PACK, COLS), sds(CREACH, FEATS, COLS), sds(PACK + 40, COLS), sds(PACK + 40, COLS)] * len(sides),
-        in_specs=[SMEM] + [VMEM] * 4,
+        in_specs=[SMEM] + [pl.BlockSpec(memory_space=pl.ANY)] * 4,
         out_specs=[VMEM] * (5 + 4 * len(sides)),
-        compiler_params=PARAMS,
+        scratch_shapes=[
+            pltpu.VMEM((40 * ROWS, COLS), F32), pltpu.VMEM((10 * ROWS, COLS), jnp.int32),
+            pltpu.VMEM((ROWS, COLS), F32), pltpu.VMEM((40 * ROWS, COLS), F32), pltpu.SemaphoreType.DMA((4,)),
+        ],
+        compiler_params=params(48),
         name="pack_halos",
     )(
         scal,
@@ -798,7 +820,8 @@
         )
     from_west = lax.ppermute(east_pay, "lon", east_ring)
     from_east = lax.ppermute(west_pay, "lon", west_ring)
-    all_sums = lax.all_gather(sums, ("lon", "lat"), tiled=True)
+    axes = (("lon", lon_n), ("lat", lat_n))
+    mean_rounds = list(tree_rounds(sums, axes))
 
     w_in, w_out_t = by_tile(weight_in), by_tile(weight_out.T)
     col = lambda b: b.reshape(-1, 1)
@@ -813,67 +836,76 @@
         out_shape=[sds(ROWS, FEATS, COLS), sds(ROWS, HID, COLS), sds(ROWS, HID, COLS)],
         in_specs=[VMEM] * 7,
         out_specs=[VMEM] * 3,
-        compiler_params=PARAMS,
+        compiler_params=params(12),
         cost_estimate=pl.CostEstimate(flops=10**9, bytes_accessed=2 * 10**6, transcendentals=0),
         name="own_closure",
     )(own, *forward)
 
-    state = pltpu.VMEM((EXT, 72, WIDE), F32)
-    plain = pltpu.VMEM((EXT, FEATS, WIDE), F32)
-    marks = pltpu.VMEM((EXT, 16, WIDE), F32)
-    outs = pl.pallas_call(
-        lambda *refs: main_kernel(sides, *refs),
-        out_shape=[
-            sds(40 * ROWS, COLS), sds(80, COLS), sds(24, FEATS, WIDE), sds(ROWS, FEATS, COLS),
-            sds(24, FEATS, WIDE), sds(24, FEATS, WIDE), sds(24, FEATS, WIDE), sds(24, 16, WIDE),
-        ],
-        in_specs=[SMEM] * 3 + [VMEM] * (8 + 4 * len(sides) + 9),
-        out_specs=[VMEM] * 8,
-        scratch_shapes=[state] * 5
-        + [marks, pltpu.VMEM((EXT, 8, WIDE), F32)]
-        + [plain] * 6
-        + [pltpu.VMEM((208, HID), F32)],
-        compiler_params=PARAMS,
-        cost_estimate=pl.CostEstimate(flops=5 * 10**9, bytes_accessed=10**7, transcendentals=0),
-        name="steps_and_adjoint",
-    )(
-        scal, cs, fs, all_sums, own, cown, own_m, own_h1, own_h2, from_west, from_east,
-        *[item for side in received for item in side], *forward, *backward,
+    geometry = (scal, cs, fs)
+    state = sds(EXT, 72, WIDE)
+    plain = sds(EXT, FEATS, WIDE)
+    marks = sds(EXT, 16, WIDE)
+    vmem = lambda shape: pltpu.VMEM(shape.shape, F32)
+
+    def call(kernel, name, out_shape, scratch, args, flops, limit):
+        single = not isinstance(out_shape, list)
+        return pl.pallas_call(
+            kernel,
+            out_shape=out_shape,
+            in_specs=[SMEM] * 3 + [VMEM] * len(args),
+            out_specs=VMEM if single else [VMEM] * len(out_shape),
+            scratch_shapes=scratch,
+            compiler_params=params(limit),
+            cost_estimate=pl.CostEstimate(flops=flops, bytes_accessed=10**7, transcendentals=0),
+            name=name,
+        )(*geometry, *args)
+
+    s0, s1, s2, masks, fluxes, cot, net = call(
+        lambda *refs: early_kernel(sides, *refs), "first_sections",
+        [state, state, state, marks, sds(EXT, 8, WIDE), plain, plain], [],
+        [mean_rounds[-2], own, cown, own_m, from_west, from_east]
+        + [item for side in received for item in side] + forward,
+        2 * 10**9, 8,
     )
-    final, grads, lam, from_closure, keep_1, keep_2, keep_3, keep_mask = outs
-    gathered = lax.all_gather(grads, ("lon", "lat"), tiled=True)
-
-    state_grad = pl.pallas_call(
-        back_kernel,
-        out_shape=sds(40 * ROWS, COLS),
-        in_specs=[SMEM] * 3 + [VMEM] * 6,
-        out_specs=VMEM,
-        scratch_shapes=[state] * 3 + [marks] + [plain] * 4,
-        compiler_params=PARAMS,
-        cost_estimate=pl.CostEstimate(flops=3 * 10**9, bytes_accessed=10**7, transcendentals=0),
-        name="first_step_adjoint",
-    )(scal, cs, fs, lam, from_closure, keep_1, keep_2, keep_3, keep_mask)
-
-    parts = lat_n * lon_n
+    final, grads, top, abuf, from_closure = call(
+        late_kernel, "steps_and_adjoint",
+        [sds(40 * ROWS, COLS), sds(80, COLS), plain, plain, sds(ROWS, FEATS, COLS)],
+        [vmem(state)] * 3 + [vmem(plain)] * 4 + [pltpu.VMEM((208, HID), F32)],
+        [mean_rounds[-1], own, own_h1, own_h2, s0, s1, s2, masks, fluxes, cot, net] + forward + backward,
+        4 * 10**9, 24,
+    )
+    rounds = list(tree_rounds(grads, axes))
+    hold, bbuf = call(
+        back_third_kernel, "adjoint_third_section", [plain, plain], [], [s2, masks, abuf, top], 10**9, 8
+    )
+    left, abuf = call(
+        back_second_kernel, "adjoint_second_section", [plain, plain], [],
+        [rounds[0], s1, masks, bbuf, top, hold], 10**9, 8,
+    )
+    state_grad = call(
+        back_first_kernel, "adjoint_first_section", sds(40 * ROWS, COLS), [],
+        [rounds[1], s0, masks, abuf, left, from_closure], 10**9, 8,
+    )
+
     scale = 1.0 / math.sqrt(lat_total * lon_total)
     g_in, g_bin, g_mid, g_bmid, g_out, g_bout = pl.pallas_call(
-        lambda *refs: sum_kernel(parts, scale, *refs),
+        lambda *refs: unpack_kernel(scale, *refs),
         out_shape=[sds(40, HID), sds(1, HID), sds(HID, HID), sds(1, HID), sds(40, HID), sds(1, 40)],
         in_specs=[VMEM],
         out_specs=[VMEM] * 6,
-        compiler_params=PARAMS,
-        name="sum_weight_grads",
-    )(gathered)
+        compiler_params=params(8),
+        name="unpack_weight_grads",
+    )(rounds[-1])
     shape = initial_state.shape
     return (
         final.reshape(shape),
         state_grad.reshape(shape),
-        from_tile(g_in),
+        g_in,
         g_bin.reshape(-1),
         g_mid,
         g_bmid.reshape(-1),
-        from_tile(g_out).T,
-        from_tile(g_bout.reshape(40, 1)).reshape(-1),
+        g_out.T,
+        g_bout.reshape(-1),
     )
 
 

time: 197 us -> 98.4 us (0.50)
  blocking collectives: 67 us -> 0 us
  waiting for transfers between devices: 36.4 us -> 2 us
  starting transfers between devices: 9.02 us -> 28.9 us
  between operations: 14.3 us -> 0.96 us
  local copies, waits for them, and re-layouts: 19.7 us -> 13.7 us
  Pallas kernels: 48.9 us -> 50.9 us
    all_gather x1 -> x0, blocking collectives: 67 us -> none  [on_device(): all_sums = lax.all_gather(sums, ('lon', 'lat'), tiled=True)]
    all_gather x1 -> x0, waiting for transfers between devices: 36.4 us -> none  [on_device(): gathered = lax.all_gather(grads, ('lon', 'lat'), tiled=True)]
    ppermute x0 -> x14, starting transfers between devices: none -> 16.5 us  [tree_round(): lax.ppermute(x, axis, [(i, i ^ j * stride) for i in range(count)])]
    unnamed x41 -> x16, local copies, waits for them, and re-layouts: 15.1 us -> 5.18 us
    concatenate x2 -> x5, local copies, waits for them, and re-layouts: 0.16 us -> 5.64 us  [by_tile(): return jnp.concatenate(heads + tails, axis=0)]
    ppermute x1, starting transfers between devices: 0.06 us -> 3.86 us  [on_device(): lax.ppermute(diag_w, ('lon', 'lat'), diagonal(side, -1))]
    reshape x11 -> x0, local copies, waits for them, and re-layouts: 2.94 us -> none  [the longest x2 1.46 us: by_tile(): fields = weights.reshape(4, 10, -1)]
    slice x6, local copies, waits for them, and re-layouts: 0.26 us -> 2.49 us  [the longest x3 1.55 us: by_tile(): weights[10 * t + level:10 * t + level + 1]]
  transfers between devices with their start and end apart: 7 -> 20, of which waited for: 1 -> 3; matrix products, arithmetic and copies ran while one was open for 2% -> 12% of each run, Pallas kernels for 5% -> 11%
where the time goes in v1:
time: 98.4 us; the launch traced here: 97.8 us
  Pallas kernels  50.9 us (52%)
  starting transfers between devices  28.9 us (29%)
  local copies, waits for them, and re-layouts  13.7 us (14%)
  waiting for transfers between devices  2 us (2%)
  other arithmetic  1.34 us (1%)
    pallas_call x5, Pallas kernels, call(): pl.pallas_call(kernel, out_shape=out_shape, in_specs=[SMEM] * 3 + [VMEM]...  46.5 us
    ppermute x14, starting transfers between devices, tree_round(): lax.ppermute(x, axis, [(i, i ^ j * stride) for i in range(count)])  16.5 us
    concatenate x5, local copies, waits for them, and re-layouts, by_tile(): return jnp.concatenate(heads + tails, axis=0)  5.64 us
    unnamed x16, local copies, waits for them, and re-layouts  5.18 us
    ppermute x1, starting transfers between devices, on_device(): from_east = lax.ppermute(west_pay, 'lon', west_ring)  4.42 us
    ppermute x1, starting transfers between devices, on_device(): lax.ppermute(diag_w, ('lon', 'lat'), diagonal(side, -1))  3.86 us
  transfers between devices with their start and end apart: 20, of which 3 were waited for; matrix products, arithmetic and copies ran while one was open for 12% of the time, Pallas kernels for 11%

profile of v1, /device:TPU:0, one launch (start us, length us, event | category | flops | bytes accessed | tf_op | source)
XLA Modules:
  0.0 97.8 jit_solution(14546259979521549165)
XLA Ops:
  0.8 1.0 copy-done
  1.7 1.0 copy-done.1
  4.3 1.8 %pack_halos.1 = (f32[16,56,128]{2,1,0:T(8,128)S(1)}, f32[16,40,128]{2,1,0:T(8,128)S(1)}, f32[8,128]{1,0:T(8,128)S(1)}, f32[152,128]{1,0:T(8,128)S(1)}, f32[152,1...) custom-call(s32[7]{0:T(128)S(1)} %stack.39.refs_0_.scal, ...), custom_call_target="tpu_custom_call" | custom-call | tf_op jit(solution)/shard_map/pack_halos/pallas_call | solution.py:770
  6.1 2.4 %collective-permute-start.2 = (f32[8,128]{1,0:T(8,128)S(1)}, f32[8,128]{1,0:T(8,128)S(1)}, u32[]{:S(2)}, u32[]{:S(2)}) collective-permute-start(f32[8,128]{1,0:T(8,128)S(1)} %get-tuple-element.42), channel_id=1, source_target_pairs={{0,6},{2,4},{4,2},{6,0},{8,14},{10,12},{12,10},{14,8},{16,22},{18,... | collective-permute-start | bytes 12296 | tf_op jit(solution)/shard_map/ppermute | solution.py:715
  9.2 1.6 %collective-permute-start.11 = (f32[96,128]{1,0:T(8,128)S(1)}, f32[96,128]{1,0:T(8,128)S(1)}, u32[]{:S(2)}, u32[]{:S(2)}) collective-permute-start(f32[96,128]{1,0:T(8,128)S(1)} %get-tuple-element.52), channel_id=1, source_target_pairs={{0,3},{1,2},{2,5},{3,4},{4,7},{5,6},{6,9},{7,8},{8,11},{9,10},{10,... | collective-permute-start | bytes 147464 | tf_op jit(solution)/shard_map/ppermute | solution.py:817
  10.8 3.9 %collective-permute-start.12 = (f32[96,128]{1,0:T(8,128)S(1)}, f32[96,128]{1,0:T(8,128)S(1)}, u32[]{:S(2)}, u32[]{:S(2)}) collective-permute-start(f32[96,128]{1,0:T(8,128)S(1)} %get-tuple-element.53), channel_id=1, source_target_pairs={{0,31},{1,30},{2,1},{3,0},{4,3},{5,2},{6,5},{7,4},{8,7},{9,6},{10,... | collective-permute-start | bytes 147464 | tf_op jit(solution)/shard_map/ppermute | solution.py:818
  17.1 1.0 pad_maximum_fusion.2.v2
  19.9 2.0 %collective-permute-start.5 = (f32[8,128]{1,0:T(8,128)S(1)}, f32[8,128]{1,0:T(8,128)S(1)}, u32[]{:S(2)}, u32[]{:S(2)}) collective-permute-start(f32[8,128]{1,0:T(8,128)S(1)} %add_add_fusion.3), channel_id=1, source_target_pairs={{0,24},{2,26},{4,28},{6,30},{8,16},{10,18},{12,20},{14,22},{16,8},... | collective-permute-start | bytes 12296 | tf_op jit(solution)/shard_map/ppermute | solution.py:715
  21.9 2.4 %collective-permute-start.3 = (f32[8,128]{1,0:T(8,128)S(1)}, f32[8,128]{1,0:T(8,128)S(1)}, u32[]{:S(2)}, u32[]{:S(2)}) collective-permute-start(f32[8,128]{1,0:T(8,128)S(1)} %add_add_fusion.3), channel_id=1, source_target_pairs={{0,8},{2,10},{4,12},{6,14},{8,0},{10,2},{12,4},{14,6},{16,24},{18,... | collective-permute-start | bytes 12296 | tf_op jit(solution)/shard_map/ppermute | solution.py:715
  25.4 1.6 %collective-permute-start.10 = (f32[6,40,128]{2,1,0:T(8,128)S(1)}, f32[6,40,128]{2,1,0:T(8,128)S(1)}, u32[]{:S(2)}, u32[]{:S(2)}) collective-permute-start(f32[6,40,128]{2,1,0:T(8,128)S(1)} %get-tuple-element.51), channel_id=1, source_target_pairs={{0,1},{1,0},{2,3},{3,2},{4,5},{5,4},{6,7},{7,6},{8,9},{9,8},{10,11... | collective-permute-start | bytes 368648 | tf_op jit(solution)/shard_map/ppermute | solution.py:816
  27.0 0.9 collective-permute-start.9
  27.9 1.2 %collective-permute-start.6 = (f32[8,128]{1,0:T(8,128)S(1)}, f32[8,128]{1,0:T(8,128)S(1)}, u32[]{:S(2)}, u32[]{:S(2)}) collective-permute-start(f32[8,128]{1,0:T(8,128)S(1)} %add_add_fusion.2.refs_3_), channel_id=1, source_target_pairs={{0,1},{1,0},{2,3},{3,2},{4,5},{5,4},{6,7},{7,6},{8,9},{9,8},{10,11... | collective-permute-start | bytes 12296 | tf_op jit(solution)/shard_map/ppermute | solution.py:715
  29.1 5.3 %concatenate.32 = f32[40,1]{0,1:T(1,128)S(1)} concatenate(f32[8,1]{0,1:T(1,128)S(1)} %get-tuple-element.111, f32[8,1]{0,1:T(1,128)S(1)} %get-tuple-element.110, f32[8,1]{0,1:T(1,128)S(1)} %get-tuple-element.109, f32[8,1]{0,1:T(1,128)S(1)} %get-tuple-element.108, f32[1,1]{0,1:T(1,128)} %bitcast.19, f32[1,1]{0,1:T(1,128)} %bitcast.20, f32[1,1]{0,1:T(1,128)} %bitcast.21, ...), dimensions={0} | concatenate | bytes 320 | tf_op jit(solution)/shard_map/concatenate | solution.py:709
  34.9 4.4 %collective-permute-start.8 = (f32[152,128]{1,0:T(8,128)S(1)}, f32[152,128]{1,0:T(8,128)S(1)}, u32[]{:S(2)}, u32[]{:S(2)}) collective-permute-start(f32[152,128]{1,0:T(8,128)S(1)} %get-tuple-element.49), channel_id=1, source_target_pairs={{2,0},{4,2},{6,4},{8,6},{10,8},{12,10},{14,12},{16,14},{18,16},{20... | collective-permute-start | bytes 233480 | tf_op jit(solution)/shard_map/ppermute | solution.py:822
  39.3 1.9 %own_closure.1 = (f32[16,40,128]{2,1,0:T(8,128)S(1)}, f32[16,64,128]{2,1,0:T(8,128)S(1)}, f32[16,64,128]{2,1,0:T(8,128)S(1)}) custom-call(f32[16,56,128]{2,1,0:T(8,128)S(1)} %get-tuple-element.43.own.refs_4_, f32[64,144]{1,0:T(8,128)S(1)} %copy.41.w1.refs_13_, f32[64,1]{1,0:T(8,128)S(1)} %copy.42.b1.refs_14_, f32[64,192]{1,0:T(8,128)S(1)} %pad_maximum_fusion.1.w2.refs_15_, ...), custom_call_target="tpu_custom_call" | custom-call | flops 1000000000 | bytes 2000000 | tf_op jit(solution)/shard_map/own_closure/pallas_call | solution.py:834
  41.4 8.9 %first_sections.1 = (f32[40,72,256]{2,1,0:T(8,128)S(1)}, f32[40,72,256]{2,1,0:T(8,128)S(1)}, f32[40,72,256]{2,1,0:T(8,128)S(1)}, f32[40,16,256]{2,1,0:T(8,128)S(...) custom-call(s32[7]{0:T(128)S(1)} %stack.39.refs_0_.scal, ...), custom_call_target="tpu_custom_call" | custom-call | flops 2000000000 | bytes 10000000 | tf_op jit(solution)/shard_map/first_sections/pallas_call | solution.py:852
  50.3 28.5 %steps_and_adjoint.1 = (f32[640,128]{1,0:T(8,128)}, f32[80,128]{1,0:T(8,128)S(1)}, f32[40,40,256]{2,1,0:T(8,128)S(1)}, f32[40,40,256]{2,1,0:T(8,128)S(1)}, f32[16,40,128]{2,1,0:T(8,128)S(1)}) custom-call(s32[7]{0:T(128)S(1)} %stack.39.refs_0_.scal, f32[40]{0:T(128)S(1)} %get-tuple-element.112.refs_1_.cs, f32[40]{0:T(128)S(1)} %get-tuple-element.113.refs_2_.fs, ...), custom_call_target="tpu_custom_call" | custom-call | flops 4000000000 | bytes 10000000 | tf_op jit(solution)/shard_map/steps_and_adjoint/pallas_call | solution.py:852
  78.8 1.9 %collective-permute-start.13 = (f32[80,128]{1,0:T(8,128)S(1)}, f32[80,128]{1,0:T(8,128)S(1)}, u32[]{:S(2)}, u32[]{:S(2)}) collective-permute-start(f32[80,128]{1,0:T(8,128)S(1)} %get-tuple-element.62), channel_id=1, source_target_pairs={{0,2},{2,0},{4,6},{6,4},{8,10},{10,8},{12,14},{14,12},{16,18},{18,... | collective-permute-start | bytes 122888 | tf_op jit(solution)/shard_map/ppermute | solution.py:715
  80.7 2.9 %adjoint_third_section.1 = (f32[40,40,256]{2,1,0:T(8,128)S(1)}, f32[40,40,256]{2,1,0:T(8,128)S(1)}) custom-call(s32[7]{0:T(128)S(1)} %stack.39.refs_0_.scal, f32[40]{0:T(128)S(1)} %get-tuple-element.112.refs_1_.cs, f32[40]{0:T(128)S(1)} %get-tuple-element.113.refs_2_.fs, f32[40,72,256]{2,1,0:T(8,128)S(1)} %get-tuple-element.56.s2.state, ...), custom_call_target="tpu_custom_call" | custom-call | flops 1000000000 | bytes 10000000 | tf_op jit(solution)/shard_map/adjoint_third_section/pallas_call | solution.py:852
  83.7 4.2 %collective-permute-start.18 = (f32[80,128]{1,0:T(8,128)S(1)}, f32[80,128]{1,0:T(8,128)S(1)}, u32[]{:S(2)}, u32[]{:S(2)}) collective-permute-start(f32[80,128]{1,0:T(8,128)S(1)} %add_add_fusion.1.gate), channel_id=1, source_target_pairs={{0,24},{2,26},{4,28},{6,30},{8,16},{10,18},{12,20},{14,22},{16,8},... | collective-permute-start | bytes 122888 | tf_op jit(solution)/shard_map/ppermute | solution.py:715
  88.5 2.8 %adjoint_second_section.1 = (f32[40,40,256]{2,1,0:T(8,128)S(1)}, f32[40,40,256]{2,1,0:T(8,128)S(1)}) custom-call(s32[7]{0:T(128)S(1)} %stack.39.refs_0_.scal, f32[40]{0:T(128)S(1)} %get-tuple-element.112.refs_1_.cs, f32[40]{0:T(128)S(1)} %get-tuple-element.113.refs_2_.fs, f32[80,128]{1,0:T(8,128)S(1)} %add_add_fusion.1.gate, ...), custom_call_target="tpu_custom_call" | custom-call | flops 1000000000 | bytes 10000000 | tf_op jit(solution)/shard_map/adjoint_second_section/pallas_call | solution.py:852
  91.4 1.4 %collective-permute-done.17 = f32[80,128]{1,0:T(8,128)S(1)} collective-permute-done((f32[80,128]{1,0:T(8,128)S(1)}, f32[80,128]{1,0:T(8,128)S(1)}, u32[]{:S(2)}, u32[]{:S(2)}) %collective-permute-start.17) | collective-permute-done | bytes 40992 | tf_op jit(solution)/shard_map/ppermute | solution.py:715
  92.8 1.0 collective-permute-start.19
  93.8 3.3 %adjoint_first_section.1 = f32[640,128]{1,0:T(8,128)} custom-call(s32[7]{0:T(128)S(1)} %stack.39.refs_0_.scal, f32[40]{0:T(128)S(1)} %get-tuple-element.112.refs_1_.cs, f32[40]{0:T(128)S(1)} %get-tuple-element.113.refs_2_.fs, f32[80,128]{1,0:T(8,128)S(1)} %add_add_fusion.gate, f32[40,72,256]{2,1,0:T(8,128)S(1)} %get-tuple-element.54.s0.state, ...), custom_call_target="tpu_custom_call" | custom-call | flops 1000000000 | bytes 10000000 | tf_op jit(solution)/shard_map/adjoint_first_section/pallas_call | solution.py:852
  (69 shorter events, 9.5 us)
Async XLA Ops:
  0.6 18.5 %copy-start.4 = (f32[40]{0:T(128)S(1)}, f32[40]{0:T(128)}, u32[]{:S(2)}) copy-start(f32[40]{0:T(128)} %param.18) | copy-start | bytes 484
  0.6 33.9 %copy-start.5 = (f32[64]{0:T(128)S(1)}, f32[64]{0:T(128)}, u32[]{:S(2)}) copy-start(f32[64]{0:T(128)} %param.14) | copy-start | bytes 772
  0.7 34.0 %copy-start.6 = (f32[64]{0:T(128)S(1)}, f32[64]{0:T(128)}, u32[]{:S(2)}) copy-start(f32[64]{0:T(128)} %param.16) | copy-start | bytes 772
  0.8 1.0 copy-start
  6.1 13.7 %collective-permute-start.2 = (f32[8,128]{1,0:T(8,128)S(1)}, f32[8,128]{1,0:T(8,128)S(1)}, u32[]{:S(2)}, u32[]{:S(2)}) collective-permute-start(f32[8,128]{1,0:T(8,128)S(1)} %get-tuple-element.42), channel_id=1, source_target_pairs={{0,6},{2,4},{4,2},{6,0},{8,14},{10,12},{12,10},{14,8},{16,22},{18,... | collective-permute-start | bytes 12296 | tf_op jit(solution)/shard_map/ppermute | solution.py:715
  8.5 11.3 %collective-permute-start.1 = (f32[8,128]{1,0:T(8,128)S(1)}, f32[8,128]{1,0:T(8,128)S(1)}, u32[]{:S(2)}, u32[]{:S(2)}) collective-permute-start(f32[8,128]{1,0:T(8,128)S(1)} %get-tuple-element.42), channel_id=1, source_target_pairs={{0,4},{2,6},{4,0},{6,2},{8,12},{10,14},{12,8},{14,10},{16,20},{18,... | collective-permute-start | bytes 12296 | tf_op jit(solution)/shard_map/ppermute | solution.py:715
  9.2 10.6 %collective-permute-start = (f32[8,128]{1,0:T(8,128)S(1)}, f32[8,128]{1,0:T(8,128)S(1)}, u32[]{:S(2)}, u32[]{:S(2)}) collective-permute-start(f32[8,128]{1,0:T(8,128)S(1)} %get-tuple-element.42), channel_id=1, source_target_pairs={{0,2},{2,0},{4,6},{6,4},{8,10},{10,8},{12,14},{14,12},{16,18},{18,... | collective-permute-start | bytes 12296 | tf_op jit(solution)/shard_map/ppermute | solution.py:715
  9.2 25.6 %collective-permute-start.11 = (f32[96,128]{1,0:T(8,128)S(1)}, f32[96,128]{1,0:T(8,128)S(1)}, u32[]{:S(2)}, u32[]{:S(2)}) collective-permute-start(f32[96,128]{1,0:T(8,128)S(1)} %get-tuple-element.52), channel_id=1, source_target_pairs={{0,3},{1,2},{2,5},{3,4},{4,7},{5,6},{6,9},{7,8},{8,11},{9,10},{10,... | collective-permute-start | bytes 147464 | tf_op jit(solution)/shard_map/ppermute | solution.py:817
  10.8 30.4 %collective-permute-start.12 = (f32[96,128]{1,0:T(8,128)S(1)}, f32[96,128]{1,0:T(8,128)S(1)}, u32[]{:S(2)}, u32[]{:S(2)}) collective-permute-start(f32[96,128]{1,0:T(8,128)S(1)} %get-tuple-element.53), channel_id=1, source_target_pairs={{0,31},{1,30},{2,1},{3,0},{4,3},{5,2},{6,5},{7,4},{8,7},{9,6},{10,... | collective-permute-start | bytes 147464 | tf_op jit(solution)/shard_map/ppermute | solution.py:818
  19.9 5.5 %collective-permute-start.5 = (f32[8,128]{1,0:T(8,128)S(1)}, f32[8,128]{1,0:T(8,128)S(1)}, u32[]{:S(2)}, u32[]{:S(2)}) collective-permute-start(f32[8,128]{1,0:T(8,128)S(1)} %add_add_fusion.3), channel_id=1, source_target_pairs={{0,24},{2,26},{4,28},{6,30},{8,16},{10,18},{12,20},{14,22},{16,8},... | collective-permute-start | bytes 12296 | tf_op jit(solution)/shard_map/ppermute | solution.py:715
  21.9 5.1 %collective-permute-start.4 = (f32[8,128]{1,0:T(8,128)S(1)}, f32[8,128]{1,0:T(8,128)S(1)}, u32[]{:S(2)}, u32[]{:S(2)}) collective-permute-start(f32[8,128]{1,0:T(8,128)S(1)} %add_add_fusion.3), channel_id=1, source_target_pairs={{0,16},{2,18},{4,20},{6,22},{8,24},{10,26},{12,28},{14,30},{16,0},... | collective-permute-start | bytes 12296 | tf_op jit(solution)/shard_map/ppermute | solution.py:715
  21.9 6.0 %collective-permute-start.3 = (f32[8,128]{1,0:T(8,128)S(1)}, f32[8,128]{1,0:T(8,128)S(1)}, u32[]{:S(2)}, u32[]{:S(2)}) collective-permute-start(f32[8,128]{1,0:T(8,128)S(1)} %add_add_fusion.3), channel_id=1, source_target_pairs={{0,8},{2,10},{4,12},{6,14},{8,0},{10,2},{12,4},{14,6},{16,24},{18,... | collective-permute-start | bytes 12296 | tf_op jit(solution)/shard_map/ppermute | solution.py:715
  25.4 16.0 %collective-permute-start.10 = (f32[6,40,128]{2,1,0:T(8,128)S(1)}, f32[6,40,128]{2,1,0:T(8,128)S(1)}, u32[]{:S(2)}, u32[]{:S(2)}) collective-permute-start(f32[6,40,128]{2,1,0:T(8,128)S(1)} %get-tuple-element.51), channel_id=1, source_target_pairs={{0,1},{1,0},{2,3},{3,2},{4,5},{5,4},{6,7},{7,6},{8,9},{9,8},{10,11... | collective-permute-start | bytes 368648 | tf_op jit(solution)/shard_map/ppermute | solution.py:816
  27.0 14.4 %collective-permute-start.9 = (f32[11,56,128]{2,1,0:T(8,128)S(1)}, f32[11,56,128]{2,1,0:T(8,128)S(1)}, u32[]{:S(2)}, u32[]{:S(2)}) collective-permute-start(f32[11,56,128]{2,1,0:T(8,128)S(1)} %get-tuple-element.50), channel_id=1, source_target_pairs={{0,1},{1,0},{2,3},{3,2},{4,5},{5,4},{6,7},{7,6},{8,9},{9,8},{10,11... | collective-permute-start | bytes 946184 | tf_op jit(solution)/shard_map/ppermute | solution.py:815
  27.9 6.9 %collective-permute-start.6 = (f32[8,128]{1,0:T(8,128)S(1)}, f32[8,128]{1,0:T(8,128)S(1)}, u32[]{:S(2)}, u32[]{:S(2)}) collective-permute-start(f32[8,128]{1,0:T(8,128)S(1)} %add_add_fusion.2.refs_3_), channel_id=1, source_target_pairs={{0,1},{1,0},{2,3},{3,2},{4,5},{5,4},{6,7},{7,6},{8,9},{9,8},{10,11... | collective-permute-start | bytes 12296 | tf_op jit(solution)/shard_map/ppermute | solution.py:715
  34.8 6.6 %collective-permute-start.7 = (f32[152,128]{1,0:T(8,128)S(1)}, f32[152,128]{1,0:T(8,128)S(1)}, u32[]{:S(2)}, u32[]{:S(2)}) collective-permute-start(f32[152,128]{1,0:T(8,128)S(1)} %get-tuple-element.48), channel_id=1, source_target_pairs={{0,2},{2,4},{4,6},{6,8},{8,10},{10,12},{12,14},{14,16},{16,18},{18... | collective-permute-start | bytes 233480 | tf_op jit(solution)/shard_map/ppermute | solution.py:821
  34.9 6.5 %collective-permute-start.8 = (f32[152,128]{1,0:T(8,128)S(1)}, f32[152,128]{1,0:T(8,128)S(1)}, u32[]{:S(2)}, u32[]{:S(2)}) collective-permute-start(f32[152,128]{1,0:T(8,128)S(1)} %get-tuple-element.49), channel_id=1, source_target_pairs={{2,0},{4,2},{6,4},{8,6},{10,8},{12,10},{14,12},{16,14},{18,16},{20... | collective-permute-start | bytes 233480 | tf_op jit(solution)/shard_map/ppermute | solution.py:822
  78.8 4.8 %collective-permute-start.15 = (f32[80,128]{1,0:T(8,128)S(1)}, f32[80,128]{1,0:T(8,128)S(1)}, u32[]{:S(2)}, u32[]{:S(2)}) collective-permute-start(f32[80,128]{1,0:T(8,128)S(1)} %get-tuple-element.62), channel_id=1, source_target_pairs={{0,6},{2,4},{4,2},{6,0},{8,14},{10,12},{12,10},{14,8},{16,22},{18,... | collective-permute-start | bytes 122888 | tf_op jit(solution)/shard_map/ppermute | solution.py:715
  78.8 4.8 %collective-permute-start.14 = (f32[80,128]{1,0:T(8,128)S(1)}, f32[80,128]{1,0:T(8,128)S(1)}, u32[]{:S(2)}, u32[]{:S(2)}) collective-permute-start(f32[80,128]{1,0:T(8,128)S(1)} %get-tuple-element.62), channel_id=1, source_target_pairs={{0,4},{2,6},{4,0},{6,2},{8,12},{10,14},{12,8},{14,10},{16,20},{18,... | collective-permute-start | bytes 122888 | tf_op jit(solution)/shard_map/ppermute | solution.py:715
  78.8 4.8 %collective-permute-start.13 = (f32[80,128]{1,0:T(8,128)S(1)}, f32[80,128]{1,0:T(8,128)S(1)}, u32[]{:S(2)}, u32[]{:S(2)}) collective-permute-start(f32[80,128]{1,0:T(8,128)S(1)} %get-tuple-element.62), channel_id=1, source_target_pairs={{0,2},{2,0},{4,6},{6,4},{8,10},{10,8},{12,14},{14,12},{16,18},{18,... | collective-permute-start | bytes 122888 | tf_op jit(solution)/shard_map/ppermute | solution.py:715
  83.7 7.7 %collective-permute-start.18 = (f32[80,128]{1,0:T(8,128)S(1)}, f32[80,128]{1,0:T(8,128)S(1)}, u32[]{:S(2)}, u32[]{:S(2)}) collective-permute-start(f32[80,128]{1,0:T(8,128)S(1)} %add_add_fusion.1.gate), channel_id=1, source_target_pairs={{0,24},{2,26},{4,28},{6,30},{8,16},{10,18},{12,20},{14,22},{16,8},... | collective-permute-start | bytes 122888 | tf_op jit(solution)/shard_map/ppermute | solution.py:715
  87.9 4.9 %collective-permute-start.17 = (f32[80,128]{1,0:T(8,128)S(1)}, f32[80,128]{1,0:T(8,128)S(1)}, u32[]{:S(2)}, u32[]{:S(2)}) collective-permute-start(f32[80,128]{1,0:T(8,128)S(1)} %add_add_fusion.1.gate), channel_id=1, source_target_pairs={{0,16},{2,18},{4,20},{6,22},{8,24},{10,26},{12,28},{14,30},{16,0},... | collective-permute-start | bytes 122888 | tf_op jit(solution)/shard_map/ppermute | solution.py:715
  87.9 4.9 %collective-permute-start.16 = (f32[80,128]{1,0:T(8,128)S(1)}, f32[80,128]{1,0:T(8,128)S(1)}, u32[]{:S(2)}, u32[]{:S(2)}) collective-permute-start(f32[80,128]{1,0:T(8,128)S(1)} %add_add_fusion.1.gate), channel_id=1, source_target_pairs={{0,8},{2,10},{4,12},{6,14},{8,0},{10,2},{12,4},{14,6},{16,24},{18,... | collective-permute-start | bytes 122888 | tf_op jit(solution)/shard_map/ppermute | solution.py:715
  92.8 4.3 %collective-permute-start.19 = (f32[80,128]{1,0:T(8,128)S(1)}, f32[80,128]{1,0:T(8,128)S(1)}, u32[]{:S(2)}, u32[]{:S(2)}) collective-permute-start(f32[80,128]{1,0:T(8,128)S(1)} %add_add_fusion.gate), channel_id=1, source_target_pairs={{0,1},{1,0},{2,3},{3,2},{4,5},{5,4},{6,7},{7,6},{8,9},{9,8},{10,11... | collective-permute-start | bytes 122888 | tf_op jit(solution)/shard_map/ppermute | solution.py:715
  (3 other events, 2.6 us)

commit v2 on v1

--- a/solution.py
+++ b/solution.py
@@ -16,8 +16,9 @@
 COLS = 128
 REACH = 11
 CREACH = 6
-PAD = 12
-EXT = 40
+PAD = 16
+EXT = 48
+TURN = 4
 WIDE = 2 * COLS
 FEATS = 40
 HID = 64
@@ -166,19 +167,15 @@
 def own_closure_kernel(own, w1, b1, w2, b2, w3, b3, out, h1_out, h2_out):
     k1, k2, k3 = stacked_weights(w1), stacked_weights(w2), stacked_weights(w3)
 
-    def chunk(i, _):
-        r = 4 * i
-        z = split(to_48(jnp.concatenate([own[r + n, 0:FEATS, :] for n in range(4)], axis=1)))
+    for r in range(0, ROWS, 8):
+        z = split(to_48(jnp.concatenate([own[r + n, 0:FEATS, :] for n in range(8)], axis=1)))
         h1, h1s, h2 = hidden_layers(z, k1, b1[...], k2, b2[...])
         o = product(k3, *split(h2))[0:FEATS] + b3[...]
-        for n in range(4):
+        for n in range(8):
             at = slice(n * COLS, (n + 1) * COLS)
             out[r + n] = o[:, at]
             h1_out[r + n] = h1[:, at]
             h2_out[r + n] = h2[:, at]
-        return 0
-
-    lax.fori_loop(0, ROWS // 4, chunk, 0)
 
 
 class Row:
@@ -317,42 +314,52 @@
     return out
 
 
+def for_rows(scal, reach, body):
+    low, high = PAD - reach * scal[2], PAD + ROWS + reach * scal[3]
+    turns = lax.div(high - low + TURN - 1, TURN)
+    first = jnp.where(scal[3] == 1, low, high - TURN * turns)
+
+    def turn(i, _):
+        for j in range(TURN):
+            body(first + TURN * i + j)
+        return 0
+
+    lax.fori_loop(0, turns, turn, 0)
+
+
 def mask_tile(ref, row, t):
     return tile(ref, row, 1 if t == 4 else 0)
 
 
-def adjoint_third(k, cs, fs, bounds, state, masks, abuf, top, hold, bbuf):
-    def body(r, _):
+def adjoint_third(k, scal, cs, fs, reach, state, masks, abuf, top, hold, bbuf):
+    def body(r):
         d = adjoint_row(k, state, abuf, r, cs[r], fs[r])
         for t in range(5):
             ts = (2.0 / 3.0) * tile(top, r, t) + d[t]
             hold[r, 8 * t : 8 * t + 8, :] = ts
             bbuf[r, 8 * t : 8 * t + 8, :] = 0.0625 * mask_tile(masks, r, t) * ts
-        return 0
-
-    lax.fori_loop(*bounds, body, 0)
-
-
-def adjoint_second(k, cs, fs, bounds, state, masks, bbuf, top, hold, left, abuf):
-    def body(r, _):
+
+    for_rows(scal, reach, body)
+
+
+def adjoint_second(k, scal, cs, fs, reach, state, masks, bbuf, top, hold, left, abuf):
+    def body(r):
         d = adjoint_row(k, state, bbuf, r, cs[r], fs[r])
         for t in range(5):
             ts = tile(hold, r, t)
             tf = 0.25 * ts + d[t]
             left[r, 8 * t : 8 * t + 8, :] = (1.0 / 3.0) * tile(top, r, t) + 0.75 * ts + tf
             abuf[r, 8 * t : 8 * t + 8, :] = 0.25 * mask_tile(masks, r, t) * tf
-        return 0
-
-    lax.fori_loop(*bounds, body, 0)
-
-
-def adjoint_first(k, cs, fs, bounds, state, abuf, left, store):
-    def body(r, _):
+
+    for_rows(scal, reach, body)
+
+
+def adjoint_first(k, scal, cs, fs, reach, state, abuf, left, store):
+    def body(r):
         d = adjoint_row(k, state, abuf, r, cs[r], fs[r])
         store(r, [tile(left, r, t) + d[t] for t in range(5)])
-        return 0
-
-    lax.fori_loop(*bounds, body, 0)
+
+    for_rows(scal, reach, body)
 
 
 def edges(reach):
@@ -373,17 +380,16 @@
 
 
 def section_1(k, cs, fs, masks, src, dst):
-    def body(r, _):
+    def body(r):
         d = tendency_row(k, src, r, cs[r], fs[r])
         put_state(
             k, dst, r,
             [tile(src, r, t) + 0.25 * mask_tile(masks, r, t) * d[t] for t in range(5)],
         )
-        return 0
     return body
 
 def section_2(k, cs, fs, masks, src, mid, dst):
-    def body(r, _):
+    def body(r):
         d = tendency_row(k, mid, r, cs[r], fs[r])
         put_state(
             k, dst, r,
@@ -393,7 +399,6 @@
                 for t in range(5)
             ],
         )
-        return 0
     return body
 
 
@@ -441,7 +446,7 @@
                 [cown[r, 8 * t : 8 * t + 8, :], side], axis=1
             )
     for side, (lat_x, lat_c, diag_e, diag_w) in zip(sides, side_refs):
-        base = {"swap": scal[4], "north": 1, "south": PAD + ROWS}[side]
+        base = {"swap": scal[4], "north": PAD - REACH, "south": PAD + ROWS}[side]
         cbase = {"swap": scal[5], "north": PAD - CREACH, "south": PAD + ROWS}[side]
         crow = {"swap": scal[6], "north": ROWS - CREACH, "south": 0}[side]
         for r in range(REACH):
@@ -476,32 +481,28 @@
         return product(k3, *split(h2))[0:FEATS] + b3[...]
 
     def halo_rows(first):
-        o = closure_of(jnp.concatenate([s0[first + i, 0:FEATS, 0:COLS] for i in range(4)], axis=1))
-        for i in range(4):
+        o = closure_of(jnp.concatenate([s0[first + i, 0:FEATS, 0:COLS] for i in range(8)], axis=1))
+        for i in range(8):
             outs[first + i, :, 0:COLS] = o[:, i * COLS : (i + 1) * COLS]
 
-    @pl.when(has_south == 1)
-    def _():
+    if sides == ["swap"]:
+        groups = 3
+        halo_rows(jnp.where(has_south == 1, PAD - 8, PAD + ROWS))
+    else:
+        groups = 4
         halo_rows(PAD - 8)
-        halo_rows(PAD - 4)
-
-    @pl.when(has_north == 1)
-    def _():
         halo_rows(PAD + ROWS)
-        halo_rows(PAD + ROWS + 4)
-
-    groups = 3 if sides == ["swap"] else 4
-    first = PAD - 8 * has_south
+    first = lo(8)
     o = closure_of(jnp.concatenate([wide_pack(s0, first + 8 * g) for g in range(groups)], axis=1))
     for g in range(groups):
         wide_unpack(outs, first + 8 * g, o[:, g * COLS : (g + 1) * COLS])
 
-    lax.fori_loop(lo(10), hi(10), section_1(k, cs, fs, masks, s0, s1), 0)
-    lax.fori_loop(lo(9), hi(9), section_2(k, cs, fs, masks, s0, s1, s2), 0)
+    for_rows(scal, 10, section_1(k, cs, fs, masks, s0, s1))
+    for_rows(scal, 9, section_2(k, cs, fs, masks, s0, s1, s2))
 
 
 def late_kernel(
-    scal, cs, fs, sums, own, own_h1, own_h2, s0, s1, s2, masks, fluxes, cot, outs_in,
+    sides, scal, cs, fs, sums, own, own_h1, own_h2, s0, s1, s2, masks, fluxes, cot, outs_in,
     w1, b1, w2, b2, w3, b3, v1, v2, v3, final, grads, s4, abuf, from_closure, *scratch
 ):
     s3, t1, t2, outs, gz, bbuf, hold, acc = scratch
@@ -533,15 +534,13 @@
             )
         return new
 
-    def step_1_end(r, _):
+    def step_1_end(r):
         put_state(k, s3, r, section_3(s0, s2, r))
-        return 0
-
-    def step_1_end(r, _):
+
+    def step_1_end(r):
         put_state(k, s3, r, section_3(s0, s2, outs_in, r))
-        return 0
-
-    lax.fori_loop(lo(8), hi(8), step_1_end, 0)
+
+    for_rows(scal, 8, step_1_end)
 
     acc[...] = jnp.zeros(acc.shape, F32)
 
@@ -568,81 +567,72 @@
         ]
         return jnp.concatenate(parts, axis=0)
 
-    def mask_cot(r, _):
+    def mask_cot(r):
         for t in range(5):
             bbuf[r, 8 * t : 8 * t + 8, :] = 0.25 * mask_tile(masks, r, t) * tile(cot, r, t)
             abuf[r, 8 * t : 8 * t + 8, :] = (1.0 / 6.0) * mask_tile(masks, r, t) * tile(cot, r, t)
-        return 0
-
-    lax.fori_loop(lo(6), hi(6), mask_cot, 0)
-
-    def core_rows(first, with_weights):
-        z = jnp.concatenate([s3[first + i, 0:FEATS, 0:COLS] for i in range(4)], axis=1)
-        go = jnp.concatenate([bbuf[first + i, 0:FEATS, 0:COLS] for i in range(4)], axis=1)
-        o, back = both_ways(z, go, with_weights)
-        for i in range(4):
+
+    for_rows(scal, 6, mask_cot)
+
+    for first in range(PAD, PAD + ROWS, 8):
+        z = jnp.concatenate([s3[first + i, 0:FEATS, 0:COLS] for i in range(8)], axis=1)
+        go = jnp.concatenate([bbuf[first + i, 0:FEATS, 0:COLS] for i in range(8)], axis=1)
+        o, back = both_ways(z, go, True)
+        for i in range(8):
             at = slice(i * COLS, (i + 1) * COLS)
-            if with_weights:
-                outs[first + i, :, 0:COLS] = o[:, at]
+            outs[first + i, :, 0:COLS] = o[:, at]
             gz[first + i, :, 0:COLS] = back[:, at]
 
-    lax.fori_loop(0, ROWS // 4, lambda i, _: (core_rows(PAD + 4 * i, True), 0)[1], 0)
-
-    @pl.when(has_south == 1)
-    def _():
-        core_rows(PAD - 4, False)
-
-    @pl.when(has_north == 1)
-    def _():
-        core_rows(PAD + ROWS, False)
-
     first = lo(4)
-    z = jnp.concatenate([wide_pack(s3, first + 8 * g) for g in range(3)], axis=1)
-    go = jnp.concatenate([wide_pack(bbuf, first + 8 * g) for g in range(3)], axis=1)
-    _, back = both_ways(z, go, False)
+    if sides == ["swap"]:
+        rows = [jnp.where(has_south == 1, PAD - 4, PAD + ROWS) + i for i in range(4)]
+    else:
+        rows = [PAD - 4 + i for i in range(4)] + [PAD + ROWS + i for i in range(4)]
+    beyond = lambda ref: jnp.concatenate(
+        [ref[r, 0:FEATS, 0:COLS] for r in rows] + [wide_pack(ref, first + 8 * g) for g in range(3)], axis=1
+    )
+    _, back = both_ways(beyond(s3), beyond(bbuf), False)
+    for i, r in enumerate(rows):
+        gz[r, :, 0:COLS] = back[:, i * COLS : (i + 1) * COLS]
     for g in range(3):
-        wide_unpack(gz, first + 8 * g, back[:, g * COLS : (g + 1) * COLS])
-
-    lax.fori_loop(lo(7), hi(7), section_1(k, cs, fs, masks, s3, t1), 0)
-    lax.fori_loop(lo(6), hi(6), section_2(k, cs, fs, masks, s3, t1, t2), 0)
-
-    def last(r, _):
+        at = (len(rows) + g) * COLS
+        wide_unpack(gz, first + 8 * g, back[:, at : at + COLS])
+
+    for_rows(scal, 7, section_1(k, cs, fs, masks, s3, t1))
+    for_rows(scal, 6, section_2(k, cs, fs, masks, s3, t1, t2))
+
+    def last(r):
         new = section_3(s3, t2, outs, r)
         put_result(final, r - PAD, [x[:, 0:COLS] for x in new])
-        return 0
-
-    lax.fori_loop(PAD, PAD + ROWS, last, 0)
+
+    for_rows(scal, 0, last)
 
     def store(r, tiles):
         for t in range(5):
             s4[r, 8 * t : 8 * t + 8, :] = tiles[t] + tile(gz, r, t)
 
-    adjoint_third(k, cs, fs, (lo(5), hi(5)), t2, masks, abuf, cot, hold, bbuf)
-    adjoint_second(k, cs, fs, (lo(4), hi(4)), t1, masks, bbuf, cot, hold, hold, abuf)
-    adjoint_first(k, cs, fs, (lo(3), hi(3)), s3, abuf, hold, store)
-
-    def first_step(i, _):
-        r = 4 * i
-        side = lambda read: jnp.concatenate([read(r + j) for j in range(4)], axis=1)
+    adjoint_third(k, scal, cs, fs, 5, t2, masks, abuf, cot, hold, bbuf)
+    adjoint_second(k, scal, cs, fs, 4, t1, masks, bbuf, cot, hold, t2, abuf)
+    adjoint_first(k, scal, cs, fs, 3, s3, abuf, t2, store)
+
+    for r in range(0, ROWS, 8):
+        side = lambda read: jnp.concatenate([read(r + j) for j in range(8)], axis=1)
         z = split(to_48(side(lambda j: own[j, 0:FEATS, :])))
         h1 = side(lambda j: own_h1[j])
         h2 = side(lambda j: own_h2[j])
         go = side(lambda j: masked_core(s4, PAD + j))
         back = closure_adjoint(z, h1, split(h1), h2, go, True)
-        for j in range(4):
+        for j in range(8):
             from_closure[r + j] = back[:, j * COLS : (j + 1) * COLS]
-        return 0
-
-    lax.fori_loop(0, ROWS // 4, first_step, 0)
+
     for row in (PAD - 1, PAD + ROWS):
         abuf[row] = jnp.zeros((FEATS, WIDE), F32)
 
-    def mask_top(r, _):
+    def mask_top(r):
         for t in range(5):
             abuf[r, 8 * t : 8 * t + 8, :] = (1.0 / 6.0) * mask_tile(masks, r, t) * tile(s4, r, t)
-        return 0
-
-    lax.fori_loop(lo(3), hi(3), mask_top, 0)
+
+    for_rows(scal, 3, mask_top)
     grads[...] = jnp.zeros(grads.shape, F32)
     grads[0:40, 0:HID] = acc[0:40, 0:HID]
     grads[0:40, HID : 2 * HID] = acc[112:152, 0:HID]
@@ -660,20 +650,16 @@
     ref[pl.ds(9 * ROWS + row, 4, stride=10 * ROWS), :] = tiles[4][4:8, :]
 
 
-def limits(scal, reach):
-    return PAD - reach * scal[2], PAD + ROWS + reach * scal[3]
-
-
 def back_third_kernel(scal, cs, fs, state, masks, abuf, top, hold, bbuf):
     for row in (PAD - 1, PAD + ROWS):
         bbuf[row] = jnp.zeros((FEATS, WIDE), F32)
-    adjoint_third(Row(WIDE), cs, fs, limits(scal, 2), state, masks, abuf, top, hold, bbuf)
+    adjoint_third(Row(WIDE), scal, cs, fs, 2, state, masks, abuf, top, hold, bbuf)
 
 
 def back_second_kernel(scal, cs, fs, gate, state, masks, bbuf, top, hold, left, abuf):
     for row in (PAD - 1, PAD + ROWS):
         abuf[row] = jnp.zeros((FEATS, WIDE), F32)
-    adjoint_second(Row(WIDE), cs, fs, limits(scal, 1), state, masks, bbuf, top, hold, left, abuf)
+    adjoint_second(Row(WIDE), scal, cs, fs, 1, state, masks, bbuf, top, hold, left, abuf)
 
 
 def back_first_kernel(scal, cs, fs, gate, state, masks, abuf, left, from_closure, grad):
@@ -684,7 +670,7 @@
             done.append(m * (tiles[t][:, 0:COLS] + from_closure[r - PAD, 8 * t : 8 * t + 8, :]))
         put_result(grad, r - PAD, done)
 
-    adjoint_first(Row(WIDE), cs, fs, (PAD, PAD + ROWS), state, abuf, left, store)
+    adjoint_first(Row(WIDE), scal, cs, fs, 0, state, abuf, left, store)
 
 
 def unpack_kernel(scale, packed, win, bin_, wmid, bmid, wout, bout):
@@ -759,7 +745,7 @@
             is_low * (ROWS - CREACH),
             has_south,
             has_north,
-            jnp.where(is_low == 1, PAD + ROWS, 1),
+            jnp.where(is_low == 1, PAD + ROWS, PAD - REACH),
             jnp.where(is_low == 1, PAD + ROWS, PAD - CREACH),
             jnp.where(is_low == 1, 0, ROWS - CREACH),
         ]
@@ -868,7 +854,7 @@
         2 * 10**9, 8,
     )
     final, grads, top, abuf, from_closure = call(
-        late_kernel, "steps_and_adjoint",
+        lambda *refs: late_kernel(sides, *refs), "steps_and_adjoint",
         [sds(40 * ROWS, COLS), sds(80, COLS), plain, plain, sds(ROWS, FEATS, COLS)],
         [vmem(state)] * 3 + [vmem(plain)] * 4 + [pltpu.VMEM((208, HID), F32)],
         [mean_rounds[-1], own, own_h1, own_h2, s0, s1, s2, masks, fluxes, cot, net] + forward + backward,

time: 98.4 us -> 84.1 us (0.85)
  Pallas kernels: 50.9 us -> 32.6 us
  waiting for transfers between devices: 2 us -> 4.67 us
    pallas_call x5, Pallas kernels: 46.5 us -> 29.2 us  [call(): pl.pallas_call(kernel, out_shape=out_shape, in_specs=[SMEM] * 3 + [VMEM]...]
    ppermute x14, waiting for transfers between devices: 1.88 us -> 3.54 us  [tree_round(): lax.ppermute(x, axis, [(i, i ^ j * stride) for i in range(count)])]
    ppermute x1, waiting for transfers between devices: 0.1 us -> 1.12 us  [on_device(): from_west = lax.ppermute(east_pay, 'lon', east_ring)]
    pallas_call x1, Pallas kernels: 1.94 us -> 0.92 us  [on_device(): pl.pallas_call(own_closure_kernel, out_shape=[sds(ROWS, FEATS, COLS), sds...]
  transfers between devices with their start and end apart: 20 -> 20, of which waited for: 3 -> 5; matrix products, arithmetic and copies ran while one was open for 12% -> 15% of each run, Pallas kernels for 11% -> 9%
where the time goes in v2:
time: 84.1 us; the launch traced here: 83.5 us
  Pallas kernels  32.6 us (39%)
  starting transfers between devices  29.4 us (35%)
  local copies, waits for them, and re-layouts  14.5 us (17%)
  waiting for transfers between devices  4.67 us (6%)
  other arithmetic  1.34 us (2%)
  between operations  0.93 us (1%)
    pallas_call x5, Pallas kernels, call(): pl.pallas_call(kernel, out_shape=out_shape, in_specs=[SMEM] * 3 + [VMEM]...  29.2 us
    ppermute x14, starting transfers between devices, tree_round(): lax.ppermute(x, axis, [(i, i ^ j * stride) for i in range(count)])  17 us
    concatenate x5, local copies, waits for them, and re-layouts, by_tile(): return jnp.concatenate(heads + tails, axis=0)  5.64 us
    unnamed x16, local copies, waits for them, and re-layouts  5.18 us
    ppermute x1, starting transfers between devices, on_device(): from_east = lax.ppermute(west_pay, 'lon', west_ring)  4.42 us
    ppermute x1, starting transfers between devices, on_device(): lax.ppermute(diag_w, ('lon', 'lat'), diagonal(side, -1))  3.86 us
    ppermute x14, waiting for transfers between devices, tree_round(): lax.ppermute(x, axis, [(i, i ^ j * stride) for i in range(count)])  3.54 us
    pallas_call x1, Pallas kernels, on_device(): pl.pallas_call(lambda *refs: pack_kernel(sides, *refs), out_shape=[sds(RO...  1.79 us
  transfers between devices with their start and end apart: 20, of which 5 were waited for; matrix products, arithmetic and copies ran while one was open for 15% of the time, Pallas kernels for 9%

profile of v2, /device:TPU:0, one launch (start us, length us, event | category | flops | bytes accessed | tf_op | source)
XLA Modules:
  0.0 83.5 jit_solution(16338970463989095628)
XLA Ops:
  0.8 1.0 %copy-done = f32[4,10,16,128]{3,2,1,0:T(8,128)S(1)} copy-done((f32[4,10,16,128]{3,2,1,0:T(8,128)S(1)}, f32[4,10,16,128]{3,2,1,0:T(8,128)}, u32[]{:S(2)}) %copy-start) | copy-done | bytes 327704
  1.8 1.0 %copy-done.1 = f32[4,10,16,128]{3,2,1,0:T(8,128)S(1)} copy-done((f32[4,10,16,128]{3,2,1,0:T(8,128)S(1)}, f32[4,10,16,128]{3,2,1,0:T(8,128)}, u32[]{:S(2)}) %copy-start.1) | copy-done | bytes 327704
  4.3 1.8 %pack_halos.1 = (f32[16,56,128]{2,1,0:T(8,128)S(1)}, f32[16,40,128]{2,1,0:T(8,128)S(1)}, f32[8,128]{1,0:T(8,128)S(1)}, f32[152,128]{1,0:T(8,128)S(1)}, f32[152,1...) custom-call(s32[7]{0:T(128)S(1)} %stack.39.refs_0_.scal, ...), custom_call_target="tpu_custom_call" | custom-call | tf_op jit(solution)/shard_map/pack_halos/pallas_call | solution.py:756
  6.1 2.4 %collective-permute-start.2 = (f32[8,128]{1,0:T(8,128)S(1)}, f32[8,128]{1,0:T(8,128)S(1)}, u32[]{:S(2)}, u32[]{:S(2)}) collective-permute-start(f32[8,128]{1,0:T(8,128)S(1)} %get-tuple-element.42), channel_id=1, source_target_pairs={{0,6},{2,4},{4,2},{6,0},{8,14},{10,12},{12,10},{14,8},{16,22},{18,... | collective-permute-start | bytes 12296 | tf_op jit(solution)/shard_map/ppermute | solution.py:701
  9.2 1.6 %collective-permute-start.11 = (f32[96,128]{1,0:T(8,128)S(1)}, f32[96,128]{1,0:T(8,128)S(1)}, u32[]{:S(2)}, u32[]{:S(2)}) collective-permute-start(f32[96,128]{1,0:T(8,128)S(1)} %get-tuple-element.52), channel_id=1, source_target_pairs={{0,3},{1,2},{2,5},{3,4},{4,7},{5,6},{6,9},{7,8},{8,11},{9,10},{10,... | collective-permute-start | bytes 147464 | tf_op jit(solution)/shard_map/ppermute | solution.py:803
  10.8 3.9 %collective-permute-start.12 = (f32[96,128]{1,0:T(8,128)S(1)}, f32[96,128]{1,0:T(8,128)S(1)}, u32[]{:S(2)}, u32[]{:S(2)}) collective-permute-start(f32[96,128]{1,0:T(8,128)S(1)} %get-tuple-element.53), channel_id=1, source_target_pairs={{0,31},{1,30},{2,1},{3,0},{4,3},{5,2},{6,5},{7,4},{8,7},{9,6},{10,... | collective-permute-start | bytes 147464 | tf_op jit(solution)/shard_map/ppermute | solution.py:804
  17.1 1.0 %pad_maximum_fusion.2.refs_21_ = f32[64,192]{1,0:T(8,128)S(1)} fusion(f32[64,64]{1,0:T(8,128)} %param.15), kind=kLoop, calls=%fused_computation.2 | loop fusion | flops 24576 | bytes 65536 | tf_op jit(solution)/shard_map/concatenate | solution.py:720
  20.7 2.0 %collective-permute-start.5 = (f32[8,128]{1,0:T(8,128)S(1)}, f32[8,128]{1,0:T(8,128)S(1)}, u32[]{:S(2)}, u32[]{:S(2)}) collective-permute-start(f32[8,128]{1,0:T(8,128)S(1)} %add_add_fusion.3), channel_id=1, source_target_pairs={{0,24},{2,26},{4,28},{6,30},{8,16},{10,18},{12,20},{14,22},{16,8},... | collective-permute-start | bytes 12296 | tf_op jit(solution)/shard_map/ppermute | solution.py:701
  22.7 2.4 %collective-permute-start.3 = (f32[8,128]{1,0:T(8,128)S(1)}, f32[8,128]{1,0:T(8,128)S(1)}, u32[]{:S(2)}, u32[]{:S(2)}) collective-permute-start(f32[8,128]{1,0:T(8,128)S(1)} %add_add_fusion.3), channel_id=1, source_target_pairs={{0,8},{2,10},{4,12},{6,14},{8,0},{10,2},{12,4},{14,6},{16,24},{18,... | collective-permute-start | bytes 12296 | tf_op jit(solution)/shard_map/ppermute | solution.py:701
  26.2 1.6 %collective-permute-start.10 = (f32[6,40,128]{2,1,0:T(8,128)S(1)}, f32[6,40,128]{2,1,0:T(8,128)S(1)}, u32[]{:S(2)}, u32[]{:S(2)}) collective-permute-start(f32[6,40,128]{2,1,0:T(8,128)S(1)} %get-tuple-element.51), channel_id=1, source_target_pairs={{0,1},{1,0},{2,3},{3,2},{4,5},{5,4},{6,7},{7,6},{8,9},{9,8},{10,11... | collective-permute-start | bytes 368648 | tf_op jit(solution)/shard_map/ppermute | solution.py:802
  28.7 1.2 %collective-permute-start.6 = (f32[8,128]{1,0:T(8,128)S(1)}, f32[8,128]{1,0:T(8,128)S(1)}, u32[]{:S(2)}, u32[]{:S(2)}) collective-permute-start(f32[8,128]{1,0:T(8,128)S(1)} %add_add_fusion.2.refs_3_), channel_id=1, source_target_pairs={{0,1},{1,0},{2,3},{3,2},{4,5},{5,4},{6,7},{7,6},{8,9},{9,8},{10,11... | collective-permute-start | bytes 12296 | tf_op jit(solution)/shard_map/ppermute | solution.py:701
  29.9 5.3 %concatenate.32 = f32[40,1]{0,1:T(1,128)S(1)} concatenate(f32[8,1]{0,1:T(1,128)S(1)} %get-tuple-element.111, f32[8,1]{0,1:T(1,128)S(1)} %get-tuple-element.110, f32[8,1]{0,1:T(1,128)S(1)} %get-tuple-element.109, f32[8,1]{0,1:T(1,128)S(1)} %get-tuple-element.108, f32[1,1]{0,1:T(1,128)} %bitcast.19, f32[1,1]{0,1:T(1,128)} %bitcast.20, f32[1,1]{0,1:T(1,128)} %bitcast.21, ...), dimensions={0} | concatenate | bytes 320 | tf_op jit(solution)/shard_map/concatenate | solution.py:695
  35.7 4.4 %collective-permute-start.8 = (f32[152,128]{1,0:T(8,128)S(1)}, f32[152,128]{1,0:T(8,128)S(1)}, u32[]{:S(2)}, u32[]{:S(2)}) collective-permute-start(f32[152,128]{1,0:T(8,128)S(1)} %get-tuple-element.49), channel_id=1, source_target_pairs={{2,0},{4,2},{6,4},{8,6},{10,8},{12,10},{14,12},{16,14},{18,16},{20... | collective-permute-start | bytes 233480 | tf_op jit(solution)/shard_map/ppermute | solution.py:808
  40.1 0.9 %own_closure.1 = (f32[16,40,128]{2,1,0:T(8,128)S(1)}, f32[16,64,128]{2,1,0:T(8,128)S(1)}, f32[16,64,128]{2,1,0:T(8,128)S(1)}) custom-call(f32[16,56,128]{2,1,0:T(8,128)S(1)} %get-tuple-element.43.own.refs_4_, f32[64,144]{1,0:T(8,128)S(1)} %copy.41.w1.refs_13_.refs_14_, f32[64,1]{1,0:T(8,128)S(1)} %copy.42.b1.refs_14_.refs_15_, ...), custom_call_target="tpu_custom_call" | custom-call | flops 1000000000 | bytes 2000000 | tf_op jit(solution)/shard_map/own_closure/pallas_call | solution.py:820
  41.1 1.1 %collective-permute-done.7.refs_7_ = f32[152,128]{1,0:T(8,128)S(1)} collective-permute-done((f32[152,128]{1,0:T(8,128)S(1)}, f32[152,128]{1,0:T(8,128)S(1)}, u32[]{:S(2)}, u32[]{:S(2)}) %collective-permute-start.7) | collective-permute-done | bytes 77856 | tf_op jit(solution)/shard_map/ppermute | solution.py:807
  42.2 5.5 %first_sections.1 = (f32[48,72,256]{2,1,0:T(8,128)S(1)}, f32[48,72,256]{2,1,0:T(8,128)S(1)}, f32[48,72,256]{2,1,0:T(8,128)S(1)}, f32[48,16,256]{2,1,0:T(8,128)S(...) custom-call(s32[7]{0:T(128)S(1)} %stack.39.refs_0_.scal, ...), custom_call_target="tpu_custom_call" | custom-call | flops 2000000000 | bytes 10000000 | tf_op jit(solution)/shard_map/first_sections/pallas_call | solution.py:838
  47.7 17.1 %steps_and_adjoint.1 = (f32[640,128]{1,0:T(8,128)}, f32[80,128]{1,0:T(8,128)S(1)}, f32[48,40,256]{2,1,0:T(8,128)S(1)}, f32[48,40,256]{2,1,0:T(8,128)S(1)}, f32[16,40,128]{2,1,0:T(8,128)S(1)}) custom-call(s32[7]{0:T(128)S(1)} %stack.39.refs_0_.scal, f32[48]{0:T(128)S(1)} %get-tuple-element.112.refs_1_.cs, f32[48]{0:T(128)S(1)} %get-tuple-element.113.refs_2_.fs, ...), custom_call_target="tpu_custom_call" | custom-call | flops 4000000000 | bytes 10000000 | tf_op jit(solution)/shard_map/steps_and_adjoint/pallas_call | solution.py:838
  64.7 1.9 %collective-permute-start.13 = (f32[80,128]{1,0:T(8,128)S(1)}, f32[80,128]{1,0:T(8,128)S(1)}, u32[]{:S(2)}, u32[]{:S(2)}) collective-permute-start(f32[80,128]{1,0:T(8,128)S(1)} %get-tuple-element.62), channel_id=1, source_target_pairs={{0,2},{2,0},{4,6},{6,4},{8,10},{10,8},{12,14},{14,12},{16,18},{18,... | collective-permute-start | bytes 122888 | tf_op jit(solution)/shard_map/ppermute | solution.py:701
  66.6 2.1 %adjoint_third_section.1 = (f32[48,40,256]{2,1,0:T(8,128)S(1)}, f32[48,40,256]{2,1,0:T(8,128)S(1)}) custom-call(s32[7]{0:T(128)S(1)} %stack.39.refs_0_.scal, f32[48]{0:T(128)S(1)} %get-tuple-element.112.refs_1_.cs, f32[48]{0:T(128)S(1)} %get-tuple-element.113.refs_2_.fs, f32[48,72,256]{2,1,0:T(8,128)S(1)} %get-tuple-element.56.refs_9_.state, ...), custom_call_target="tpu_custom_call" | custom-call | flops 1000000000 | bytes 10000000 | tf_op jit(solution)/shard_map/adjoint_third_section/pallas_call | solution.py:838
  69.0 4.7 %collective-permute-start.18 = (f32[80,128]{1,0:T(8,128)S(1)}, f32[80,128]{1,0:T(8,128)S(1)}, u32[]{:S(2)}, u32[]{:S(2)}) collective-permute-start(f32[80,128]{1,0:T(8,128)S(1)} %add_add_fusion.1.gate), channel_id=1, source_target_pairs={{0,24},{2,26},{4,28},{6,30},{8,16},{10,18},{12,20},{14,22},{16,8},... | collective-permute-start | bytes 122888 | tf_op jit(solution)/shard_map/ppermute | solution.py:701
  74.4 2.2 %adjoint_second_section.1 = (f32[48,40,256]{2,1,0:T(8,128)S(1)}, f32[48,40,256]{2,1,0:T(8,128)S(1)}) custom-call(s32[7]{0:T(128)S(1)} %stack.39.refs_0_.scal, f32[48]{0:T(128)S(1)} %get-tuple-element.112.refs_1_.cs, f32[48]{0:T(128)S(1)} %get-tuple-element.113.refs_2_.fs, f32[80,128]{1,0:T(8,128)S(1)} %add_add_fusion.1.gate, ...), custom_call_target="tpu_custom_call" | custom-call | flops 1000000000 | bytes 10000000 | tf_op jit(solution)/shard_map/adjoint_second_section/pallas_call | solution.py:838
  76.7 2.0 %collective-permute-done.17 = f32[80,128]{1,0:T(8,128)S(1)} collective-permute-done((f32[80,128]{1,0:T(8,128)S(1)}, f32[80,128]{1,0:T(8,128)S(1)}, u32[]{:S(2)}, u32[]{:S(2)}) %collective-permute-start.17) | collective-permute-done | bytes 40992 | tf_op jit(solution)/shard_map/ppermute | solution.py:701
  78.7 1.0 %collective-permute-start.19 = (f32[80,128]{1,0:T(8,128)S(1)}, f32[80,128]{1,0:T(8,128)S(1)}, u32[]{:S(2)}, u32[]{:S(2)}) collective-permute-start(f32[80,128]{1,0:T(8,128)S(1)} %add_add_fusion.gate), channel_id=1, source_target_pairs={{0,1},{1,0},{2,3},{3,2},{4,5},{5,4},{6,7},{7,6},{8,9},{9,8},{10,11... | collective-permute-start | bytes 122888 | tf_op jit(solution)/shard_map/ppermute | solution.py:701
  79.7 2.4 %adjoint_first_section.1 = f32[640,128]{1,0:T(8,128)} custom-call(s32[7]{0:T(128)S(1)} %stack.39.refs_0_.scal, f32[48]{0:T(128)S(1)} %get-tuple-element.112.refs_1_.cs, f32[48]{0:T(128)S(1)} %get-tuple-element.113.refs_2_.fs, f32[80,128]{1,0:T(8,128)S(1)} %add_add_fusion.gate, f32[48,72,256]{2,1,0:T(8,128)S(1)} %get-tuple-element.54.refs_7_.state, ...), custom_call_target="tpu_custom_call" | custom-call | flops 1000000000 | bytes 10000000 | tf_op jit(solution)/shard_map/adjoint_first_section/pallas_call | solution.py:838
  (69 shorter events, 12.2 us)
Async XLA Ops:
  0.6 24.5 %copy-start.4 = (f32[40]{0:T(128)S(1)}, f32[40]{0:T(128)}, u32[]{:S(2)}) copy-start(f32[40]{0:T(128)} %param.18) | copy-start | bytes 484
  0.6 34.7 %copy-start.5 = (f32[64]{0:T(128)S(1)}, f32[64]{0:T(128)}, u32[]{:S(2)}) copy-start(f32[64]{0:T(128)} %param.14) | copy-start | bytes 772
  0.7 34.8 %copy-start.6 = (f32[64]{0:T(128)S(1)}, f32[64]{0:T(128)}, u32[]{:S(2)}) copy-start(f32[64]{0:T(128)} %param.16) | copy-start | bytes 772
  0.8 1.0 %copy-start = (f32[4,10,16,128]{3,2,1,0:T(8,128)S(1)}, f32[4,10,16,128]{3,2,1,0:T(8,128)}, u32[]{:S(2)}) copy-start(f32[4,10,16,128]{3,2,1,0:T(8,128)} %param.10) | copy-start | bytes 983044
  6.1 14.5 %collective-permute-start.2 = (f32[8,128]{1,0:T(8,128)S(1)}, f32[8,128]{1,0:T(8,128)S(1)}, u32[]{:S(2)}, u32[]{:S(2)}) collective-permute-start(f32[8,128]{1,0:T(8,128)S(1)} %get-tuple-element.42), channel_id=1, source_target_pairs={{0,6},{2,4},{4,2},{6,0},{8,14},{10,12},{12,10},{14,8},{16,22},{18,... | collective-permute-start | bytes 12296 | tf_op jit(solution)/shard_map/ppermute | solution.py:701
  8.5 12.1 %collective-permute-start.1 = (f32[8,128]{1,0:T(8,128)S(1)}, f32[8,128]{1,0:T(8,128)S(1)}, u32[]{:S(2)}, u32[]{:S(2)}) collective-permute-start(f32[8,128]{1,0:T(8,128)S(1)} %get-tuple-element.42), channel_id=1, source_target_pairs={{0,4},{2,6},{4,0},{6,2},{8,12},{10,14},{12,8},{14,10},{16,20},{18,... | collective-permute-start | bytes 12296 | tf_op jit(solution)/shard_map/ppermute | solution.py:701
  9.2 11.4 %collective-permute-start = (f32[8,128]{1,0:T(8,128)S(1)}, f32[8,128]{1,0:T(8,128)S(1)}, u32[]{:S(2)}, u32[]{:S(2)}) collective-permute-start(f32[8,128]{1,0:T(8,128)S(1)} %get-tuple-element.42), channel_id=1, source_target_pairs={{0,2},{2,0},{4,6},{6,4},{8,10},{10,8},{12,14},{14,12},{16,18},{18,... | collective-permute-start | bytes 12296 | tf_op jit(solution)/shard_map/ppermute | solution.py:701
  9.2 26.4 %collective-permute-start.11 = (f32[96,128]{1,0:T(8,128)S(1)}, f32[96,128]{1,0:T(8,128)S(1)}, u32[]{:S(2)}, u32[]{:S(2)}) collective-permute-start(f32[96,128]{1,0:T(8,128)S(1)} %get-tuple-element.52), channel_id=1, source_target_pairs={{0,3},{1,2},{2,5},{3,4},{4,7},{5,6},{6,9},{7,8},{8,11},{9,10},{10,... | collective-permute-start | bytes 147464 | tf_op jit(solution)/shard_map/ppermute | solution.py:803
  10.8 30.2 %collective-permute-start.12 = (f32[96,128]{1,0:T(8,128)S(1)}, f32[96,128]{1,0:T(8,128)S(1)}, u32[]{:S(2)}, u32[]{:S(2)}) collective-permute-start(f32[96,128]{1,0:T(8,128)S(1)} %get-tuple-element.53), channel_id=1, source_target_pairs={{0,31},{1,30},{2,1},{3,0},{4,3},{5,2},{6,5},{7,4},{8,7},{9,6},{10,... | collective-permute-start | bytes 147464 | tf_op jit(solution)/shard_map/ppermute | solution.py:804
  20.7 5.5 %collective-permute-start.5 = (f32[8,128]{1,0:T(8,128)S(1)}, f32[8,128]{1,0:T(8,128)S(1)}, u32[]{:S(2)}, u32[]{:S(2)}) collective-permute-start(f32[8,128]{1,0:T(8,128)S(1)} %add_add_fusion.3), channel_id=1, source_target_pairs={{0,24},{2,26},{4,28},{6,30},{8,16},{10,18},{12,20},{14,22},{16,8},... | collective-permute-start | bytes 12296 | tf_op jit(solution)/shard_map/ppermute | solution.py:701
  22.7 5.1 %collective-permute-start.4 = (f32[8,128]{1,0:T(8,128)S(1)}, f32[8,128]{1,0:T(8,128)S(1)}, u32[]{:S(2)}, u32[]{:S(2)}) collective-permute-start(f32[8,128]{1,0:T(8,128)S(1)} %add_add_fusion.3), channel_id=1, source_target_pairs={{0,16},{2,18},{4,20},{6,22},{8,24},{10,26},{12,28},{14,30},{16,0},... | collective-permute-start | bytes 12296 | tf_op jit(solution)/shard_map/ppermute | solution.py:701
  22.7 6.0 %collective-permute-start.3 = (f32[8,128]{1,0:T(8,128)S(1)}, f32[8,128]{1,0:T(8,128)S(1)}, u32[]{:S(2)}, u32[]{:S(2)}) collective-permute-start(f32[8,128]{1,0:T(8,128)S(1)} %add_add_fusion.3), channel_id=1, source_target_pairs={{0,8},{2,10},{4,12},{6,14},{8,0},{10,2},{12,4},{14,6},{16,24},{18,... | collective-permute-start | bytes 12296 | tf_op jit(solution)/shard_map/ppermute | solution.py:701
  26.2 16.0 %collective-permute-start.10 = (f32[6,40,128]{2,1,0:T(8,128)S(1)}, f32[6,40,128]{2,1,0:T(8,128)S(1)}, u32[]{:S(2)}, u32[]{:S(2)}) collective-permute-start(f32[6,40,128]{2,1,0:T(8,128)S(1)} %get-tuple-element.51), channel_id=1, source_target_pairs={{0,1},{1,0},{2,3},{3,2},{4,5},{5,4},{6,7},{7,6},{8,9},{9,8},{10,11... | collective-permute-start | bytes 368648 | tf_op jit(solution)/shard_map/ppermute | solution.py:802
  27.8 14.4 %collective-permute-start.9 = (f32[11,56,128]{2,1,0:T(8,128)S(1)}, f32[11,56,128]{2,1,0:T(8,128)S(1)}, u32[]{:S(2)}, u32[]{:S(2)}) collective-permute-start(f32[11,56,128]{2,1,0:T(8,128)S(1)} %get-tuple-element.50), channel_id=1, source_target_pairs={{0,1},{1,0},{2,3},{3,2},{4,5},{5,4},{6,7},{7,6},{8,9},{9,8},{10,11... | collective-permute-start | bytes 946184 | tf_op jit(solution)/shard_map/ppermute | solution.py:801
  28.7 6.9 %collective-permute-start.6 = (f32[8,128]{1,0:T(8,128)S(1)}, f32[8,128]{1,0:T(8,128)S(1)}, u32[]{:S(2)}, u32[]{:S(2)}) collective-permute-start(f32[8,128]{1,0:T(8,128)S(1)} %add_add_fusion.2.refs_3_), channel_id=1, source_target_pairs={{0,1},{1,0},{2,3},{3,2},{4,5},{5,4},{6,7},{7,6},{8,9},{9,8},{10,11... | collective-permute-start | bytes 12296 | tf_op jit(solution)/shard_map/ppermute | solution.py:701
  35.6 6.6 %collective-permute-start.7 = (f32[152,128]{1,0:T(8,128)S(1)}, f32[152,128]{1,0:T(8,128)S(1)}, u32[]{:S(2)}, u32[]{:S(2)}) collective-permute-start(f32[152,128]{1,0:T(8,128)S(1)} %get-tuple-element.48), channel_id=1, source_target_pairs={{0,2},{2,4},{4,6},{6,8},{8,10},{10,12},{12,14},{14,16},{16,18},{18... | collective-permute-start | bytes 233480 | tf_op jit(solution)/shard_map/ppermute | solution.py:807
  35.7 6.5 %collective-permute-start.8 = (f32[152,128]{1,0:T(8,128)S(1)}, f32[152,128]{1,0:T(8,128)S(1)}, u32[]{:S(2)}, u32[]{:S(2)}) collective-permute-start(f32[152,128]{1,0:T(8,128)S(1)} %get-tuple-element.49), channel_id=1, source_target_pairs={{2,0},{4,2},{6,4},{8,6},{10,8},{12,10},{14,12},{16,14},{18,16},{20... | collective-permute-start | bytes 233480 | tf_op jit(solution)/shard_map/ppermute | solution.py:808
  64.7 4.0 %collective-permute-start.15 = (f32[80,128]{1,0:T(8,128)S(1)}, f32[80,128]{1,0:T(8,128)S(1)}, u32[]{:S(2)}, u32[]{:S(2)}) collective-permute-start(f32[80,128]{1,0:T(8,128)S(1)} %get-tuple-element.62), channel_id=1, source_target_pairs={{0,6},{2,4},{4,2},{6,0},{8,14},{10,12},{12,10},{14,8},{16,22},{18,... | collective-permute-start | bytes 122888 | tf_op jit(solution)/shard_map/ppermute | solution.py:701
  64.7 4.3 %collective-permute-start.14 = (f32[80,128]{1,0:T(8,128)S(1)}, f32[80,128]{1,0:T(8,128)S(1)}, u32[]{:S(2)}, u32[]{:S(2)}) collective-permute-start(f32[80,128]{1,0:T(8,128)S(1)} %get-tuple-element.62), channel_id=1, source_target_pairs={{0,4},{2,6},{4,0},{6,2},{8,12},{10,14},{12,8},{14,10},{16,20},{18,... | collective-permute-start | bytes 122888 | tf_op jit(solution)/shard_map/ppermute | solution.py:701
  64.7 4.3 %collective-permute-start.13 = (f32[80,128]{1,0:T(8,128)S(1)}, f32[80,128]{1,0:T(8,128)S(1)}, u32[]{:S(2)}, u32[]{:S(2)}) collective-permute-start(f32[80,128]{1,0:T(8,128)S(1)} %get-tuple-element.62), channel_id=1, source_target_pairs={{0,2},{2,0},{4,6},{6,4},{8,10},{10,8},{12,14},{14,12},{16,18},{18,... | collective-permute-start | bytes 122888 | tf_op jit(solution)/shard_map/ppermute | solution.py:701
  69.0 7.6 %collective-permute-start.18 = (f32[80,128]{1,0:T(8,128)S(1)}, f32[80,128]{1,0:T(8,128)S(1)}, u32[]{:S(2)}, u32[]{:S(2)}) collective-permute-start(f32[80,128]{1,0:T(8,128)S(1)} %add_add_fusion.1.gate), channel_id=1, source_target_pairs={{0,24},{2,26},{4,28},{6,30},{8,16},{10,18},{12,20},{14,22},{16,8},... | collective-permute-start | bytes 122888 | tf_op jit(solution)/shard_map/ppermute | solution.py:701
  73.8 4.9 %collective-permute-start.17 = (f32[80,128]{1,0:T(8,128)S(1)}, f32[80,128]{1,0:T(8,128)S(1)}, u32[]{:S(2)}, u32[]{:S(2)}) collective-permute-start(f32[80,128]{1,0:T(8,128)S(1)} %add_add_fusion.1.gate), channel_id=1, source_target_pairs={{0,16},{2,18},{4,20},{6,22},{8,24},{10,26},{12,28},{14,30},{16,0},... | collective-permute-start | bytes 122888 | tf_op jit(solution)/shard_map/ppermute | solution.py:701
  73.8 4.9 %collective-permute-start.16 = (f32[80,128]{1,0:T(8,128)S(1)}, f32[80,128]{1,0:T(8,128)S(1)}, u32[]{:S(2)}, u32[]{:S(2)}) collective-permute-start(f32[80,128]{1,0:T(8,128)S(1)} %add_add_fusion.1.gate), channel_id=1, source_target_pairs={{0,8},{2,10},{4,12},{6,14},{8,0},{10,2},{12,4},{14,6},{16,24},{18,... | collective-permute-start | bytes 122888 | tf_op jit(solution)/shard_map/ppermute | solution.py:701
  78.7 4.1 %collective-permute-start.19 = (f32[80,128]{1,0:T(8,128)S(1)}, f32[80,128]{1,0:T(8,128)S(1)}, u32[]{:S(2)}, u32[]{:S(2)}) collective-permute-start(f32[80,128]{1,0:T(8,128)S(1)} %add_add_fusion.gate), channel_id=1, source_target_pairs={{0,1},{1,0},{2,3},{3,2},{4,5},{5,4},{6,7},{7,6},{8,9},{9,8},{10,11... | collective-permute-start | bytes 122888 | tf_op jit(solution)/shard_map/ppermute | solution.py:701
  (3 other events, 2.6 us)

commit v3 on v2

--- a/solution.py
+++ b/solution.py
@@ -23,6 +23,7 @@
 FEATS = 40
 HID = 64
 PACK = 56
+SUMS = 51
 SLOT = 16
 F32 = jnp.float32
 BF16 = jnp.bfloat16
@@ -60,14 +61,18 @@
 
 def pack_kernel(sides, scal, x_hbm, mask_hbm, flux_hbm, cot_hbm, *outs):
     x, mask, flux, cot, sems = outs[-5:]
-    own, cown, sums, east, west = outs[:5]
-    per_side = [outs[5 + 4 * i : 9 + 4 * i] for i in range(len(sides))]
+    own, cown, east, west = outs[:4]
+    per_side = [outs[4 + 4 * i : 8 + 4 * i] for i in range(len(sides))]
     pairs = ((mask_hbm, mask), (x_hbm, x), (flux_hbm, flux), (cot_hbm, cot))
     copies = [pltpu.make_async_copy(a, b, sems.at[i]) for i, (a, b) in enumerate(pairs)]
     for copy in copies:
         copy.start()
     for copy in copies:
         copy.wait()
+    top = mask[0:ROWS, :].astype(F32)
+    total = jnp.sum(jnp.sum(top * flux[...], axis=1, keepdims=True), axis=0, keepdims=True)
+    count = jnp.sum(jnp.sum(top, axis=1, keepdims=True), axis=0, keepdims=True)
+    tail = jnp.where(sub_index(COLS) == 0, total, jnp.where(sub_index(COLS) == 1, count, 0.0))
     for r in range(ROWS):
         first = mask[pl.ds(r, 8, stride=ROWS), :].astype(F32)
         m8 = mask[8 * ROWS + r : 8 * ROWS + r + 1, :].astype(F32)
@@ -83,11 +88,7 @@
         own[r, 48:49, :] = m8
         own[r, 49:50, :] = m9
         own[r, 50:51, :] = flux[r : r + 1, :]
-        own[r, 51:56, :] = jnp.zeros((5, COLS), F32)
-    top = mask[0:ROWS, :].astype(F32)
-    total = jnp.sum(jnp.sum(top * flux[...], axis=1, keepdims=True), axis=0, keepdims=True)
-    count = jnp.sum(jnp.sum(top, axis=1, keepdims=True), axis=0, keepdims=True)
-    sums[...] = jnp.where(sub_index(COLS) == 0, total, jnp.where(sub_index(COLS) == 1, count, 0.0))
+        own[r, SUMS:56, :] = tail[0:5, :]
     for half in range(2):
         for t in range(7):
             rows = [own[8 * half + s, 8 * t : 8 * t + 8, :] for s in range(8)]
@@ -119,12 +120,21 @@
     return high, (values - high.astype(F32)).astype(BF16)
 
 
-def stacked_weights(ref):
-    values = ref[...]
-    third = values.shape[1] // 3
+def stack(out, values, buffer):
+    k = values.shape[1]
+    rows = slice(0, values.shape[0])
     high, low = split(values)
-    lane = lax.broadcasted_iota(jnp.int32, values.shape, 1)
-    return jnp.where(lane < 2 * third, high.astype(F32), low.astype(F32)).astype(BF16)
+    buffer[rows, 0:k] = high.astype(F32)
+    buffer[rows, k : 2 * k] = high.astype(F32)
+    buffer[rows, 2 * k : 3 * k] = low.astype(F32)
+    out[...] = buffer[rows, 0 : 3 * k].astype(BF16)
+
+
+def by_tile(dst, src, lanes):
+    for t in range(4):
+        dst[8 * t : 8 * t + 8, lanes] = src[10 * t : 10 * t + 8, lanes]
+        dst[32 + t : 33 + t, lanes] = src[10 * t + 8 : 10 * t + 9, lanes]
+        dst[36 + t : 37 + t, lanes] = src[10 * t + 9 : 10 * t + 10, lanes]
 
 
 def product(weights, high, low):
@@ -137,15 +147,25 @@
     return dot(a[0], b[0]) + dot(a[0], b[1]) + dot(a[1], b[0])
 
 
-def to_48(columns):
-    return jnp.concatenate([columns, jnp.zeros((8, columns.shape[1]), F32)], axis=0)
-
-
-def hidden_layers(z, w1, b1, w2, b2):
-    h1 = jnp.tanh(product(w1, *z) + b1)
+def to_48(columns, first=0.0):
+    more = jnp.where(sub_index(columns.shape[1]) == 0, first, 0.0).astype(F32)
+    return jnp.concatenate([columns, more], axis=0)
+
+
+def wide(bias, values):
+    return jnp.concatenate([bias[...]] * (values.shape[1] // COLS), axis=1)
+
+
+def hidden_layers(z, k1, k2, b2):
+    h1 = jnp.tanh(product(k1[...], *z))
     h1s = split(h1)
-    h2 = jnp.tanh(product(w2, *h1s) + b2)
-    return h1, h1s, h2
+    h2 = product(k2[...], *h1s)
+    return h1, h1s, jnp.tanh(h2 + wide(b2, h2))
+
+
+def last_layer(h2, k3, b3):
+    o = product(k3[...], *split(h2))[0:FEATS]
+    return o + wide(b3, o)
 
 
 def add_weight_terms(acc, z, h1s, h2s, g1s, g2s, gos):
@@ -153,9 +173,8 @@
     acc[0:48, 0:HID] += across(z, g1s)
     acc[48:112, 0:HID] += across(h1s, g2s)
     acc[112:160, 0:HID] += across(gos, h2s)
-    acc[160:176, 0:HID] += ones_rows(ones, g1s)
-    acc[176:192, 0:HID] += ones_rows(ones, g2s)
-    acc[192:208, 0:48] += ones_rows(ones, gos)
+    acc[160:176, 0:HID] += ones_rows(ones, g2s)
+    acc[176:192, 0:48] += ones_rows(ones, gos)
 
 
 def ones_rows(ones, g):
@@ -164,13 +183,42 @@
     return dot(g[0]) + dot(g[1])
 
 
-def own_closure_kernel(own, w1, b1, w2, b2, w3, b3, out, h1_out, h2_out):
-    k1, k2, k3 = stacked_weights(w1), stacked_weights(w2), stacked_weights(w3)
+def own_closure_kernel(own, *refs):
+    raw, (out, h1_out, h2_out, k1, k2, k3, q1, q2, q3, b2, b3) = refs[:6], refs[6:17]
+    w_in, w_mid, w_out, b_in, b_mid, b_out = refs[17:23]
+    buffer, spare, stacked, sems = refs[23:]
+    copies = [pltpu.make_async_copy(a, b, sems.at[i]) for i, (a, b) in enumerate(zip(raw, refs[17:23]))]
+    for copy in copies:
+        copy.start()
+    for copy in copies:
+        copy.wait()
+    buffer[...] = jnp.zeros(buffer.shape, F32)
+    by_tile(buffer, w_in, slice(0, HID))
+    buffer[40:41, 0:HID] = b_in[...]
+    stack(q1, buffer[0:48, 0:HID], stacked)
+    spare[...] = buffer[...].T
+    stack(k1, spare[0:HID, 0:48], stacked)
+    buffer[0:HID, 0:HID] = w_mid[...]
+    buffer[HID : HID + 1, 0:HID] = b_mid[...]
+    stack(q2, buffer[0:HID, 0:HID], stacked)
+    spare[...] = buffer[...].T
+    stack(k2, spare[0:HID, 0:HID], stacked)
+    b2[...] = jnp.broadcast_to(spare[0:HID, HID : HID + 1], (HID, COLS))
+    buffer[...] = jnp.zeros(buffer.shape, F32)
+    buffer[0:HID, 0:FEATS] = w_out[...]
+    buffer[HID : HID + 1, 0:FEATS] = b_out[...]
+    spare[...] = buffer[...].T
+    buffer[...] = jnp.zeros(buffer.shape, F32)
+    by_tile(buffer, spare, slice(0, COLS))
+    stack(k3, buffer[0:48, 0:HID], stacked)
+    b3[...] = jnp.broadcast_to(buffer[0:FEATS, HID : HID + 1], (FEATS, COLS))
+    spare[...] = buffer[...].T
+    stack(q3, spare[0:HID, 0:48], stacked)
 
     for r in range(0, ROWS, 8):
-        z = split(to_48(jnp.concatenate([own[r + n, 0:FEATS, :] for n in range(8)], axis=1)))
-        h1, h1s, h2 = hidden_layers(z, k1, b1[...], k2, b2[...])
-        o = product(k3, *split(h2))[0:FEATS] + b3[...]
+        z = split(to_48(jnp.concatenate([own[r + n, 0:FEATS, :] for n in range(8)], axis=1), 1.0))
+        h1, h1s, h2 = hidden_layers(z, k1, k2, b2)
+        o = last_layer(h2, k3, b3)
         for n in range(8):
             at = slice(n * COLS, (n + 1) * COLS)
             out[r + n] = o[:, at]
@@ -402,22 +450,39 @@
     return body
 
 
-def early_kernel(sides, scal, cs, fs, gate, own, cown, own_m, east, west, *rest):
+def section_3(k, cs, fs, masks, fluxes, mean, src, mid, net, r):
+    d = tendency_row(k, mid, r, cs[r], fs[r])
+    new = []
+    for t in range(5):
+        m = mask_tile(masks, r, t)
+        o = tile(net, r, t)
+        if t == 1:
+            force = 2.0 * (mean - fluxes[r, 2:3, :])
+            o = o + jnp.where(k.sub == 0, force, 0.0)
+        new.append(
+            (1.0 / 3.0) * tile(src, r, t) + (2.0 / 3.0) * tile(mid, r, t)
+            + m * ((1.0 / 6.0) * d[t] + 0.25 * o)
+        )
+    return new
+
+
+def zero_walls(ref):
+    for row in (PAD - 1, PAD + ROWS):
+        ref[row] = jnp.zeros(ref.shape[1:], F32)
+
+
+def assemble_kernel(sides, scal, cs, fs, own, own_m, east, west, *rest):
     n = len(sides)
-    side_refs = [rest[4 * i : 4 * i + 4] for i in range(n)]
-    (w1, b1, w2, b2, w3, b3), rest = rest[4 * n : 4 * n + 6], rest[4 * n + 6 :]
-    s0, s1, s2, masks, fluxes, cot, outs = rest
+    side_refs = [rest[3 * i : 3 * i + 3] for i in range(n)]
+    (k1, k2, k3, b2, b3), rest = rest[3 * n : 3 * n + 5], rest[3 * n + 5 :]
+    s0, masks, fluxes, outs, window = rest
     k = Row(WIDE)
-    has_south, has_north = scal[2], scal[3]
+    has_south = scal[2]
     lo = lambda h: PAD - h * has_south
-    hi = lambda h: PAD + ROWS + h * has_north
-
-    for ref in (s0, s1, s2):
-        for row in (PAD - 1, PAD + ROWS):
-            ref[row] = jnp.zeros(ref.shape[1:], F32)
+
+    zero_walls(s0)
 
     near_e, near_w = edges(REACH)
-    cnear_e, cnear_w = edges(CREACH)
 
     def put_packed(row, core, halo):
         both = lambda t: jnp.concatenate([core(t), halo(t)], axis=1)
@@ -437,6 +502,88 @@
             return jnp.where(near_e, from_e, jnp.where(near_w, from_w, 0.0))
 
         put_packed(PAD + r, lambda t: own[r, 8 * t : 8 * t + 8, :], halo)
+    for side, (lat_x, diag_e, diag_w) in zip(sides, side_refs):
+        base = {"swap": scal[4], "north": PAD - REACH, "south": PAD + ROWS}[side]
+        for r in range(REACH):
+
+            def halo(t):
+                rows = slice(8 * t, 8 * t + 8)
+                from_e = pltpu.roll(diag_w[rows, :], -REACH * r % COLS, 1)
+                from_w = pltpu.roll(diag_e[rows, :], -REACH * (r + 1) % COLS, 1)
+                return jnp.where(near_e, from_e, jnp.where(near_w, from_w, 0.0))
+
+            put_packed(base + r, lambda t: lat_x[r, 8 * t : 8 * t + 8, :], halo)
+
+    of = lambda ref: ref[SUMS : SUMS + 2, :]
+    sums = of(own.at[0]) + jnp.broadcast_to(of(east)[:, 0:1], (2, COLS))
+    if sides == ["swap"]:
+        lat_x, diag_e, _ = side_refs[0]
+        sums = sums + (of(lat_x.at[0]) + jnp.broadcast_to(of(diag_e)[:, 0:1], (2, COLS)))
+    window[...] = jnp.zeros((8, COLS), F32)
+    window[0:2, :] = sums
+
+    for r in range(ROWS):
+        outs[PAD + r, :, 0:COLS] = own_m[r]
+
+    def closure_of(columns):
+        _, _, h2 = hidden_layers(split(to_48(columns, 1.0)), k1, k2, b2)
+        return last_layer(h2, k3, b3)
+
+    def halo_rows(first):
+        o = closure_of(jnp.concatenate([s0[first + i, 0:FEATS, 0:COLS] for i in range(8)], axis=1))
+        for i in range(8):
+            outs[first + i, :, 0:COLS] = o[:, i * COLS : (i + 1) * COLS]
+
+    if sides == ["swap"]:
+        groups = 3
+        halo_rows(jnp.where(has_south == 1, PAD - 8, PAD + ROWS))
+    else:
+        groups = 4
+        halo_rows(PAD - 8)
+        halo_rows(PAD + ROWS)
+    first = lo(8)
+    o = closure_of(jnp.concatenate([wide_pack(s0, first + 8 * g) for g in range(groups)], axis=1))
+    for g in range(groups):
+        wide_unpack(outs, first + 8 * g, o[:, g * COLS : (g + 1) * COLS])
+
+
+def first_section_kernel(scal, cs, fs, s0, masks, s1):
+    zero_walls(s1)
+    for_rows(scal, 10, section_1(Row(WIDE), cs, fs, masks, s0, s1))
+
+
+def second_section_kernel(scal, cs, fs, gate, s0, s1, masks, s2):
+    zero_walls(s2)
+    for_rows(scal, 9, section_2(Row(WIDE), cs, fs, masks, s0, s1, s2))
+
+
+def last_section_kernel(scal, cs, fs, gate, sums, s3, t2, masks, fluxes, outs, final):
+    k = Row(WIDE)
+    mean = sums[0:1, 0:1] / sums[1:2, 0:1]
+
+    def last(r):
+        new = section_3(k, cs, fs, masks, fluxes, mean, s3, t2, outs, r)
+        put_result(final, r - PAD, [x[:, 0:COLS] for x in new])
+
+    for_rows(scal, 0, last)
+
+
+def late_kernel(
+    sides, scal, cs, fs, sums, own, cown, own_h1, own_h2, s0, s2, masks, fluxes, outs_in, east, west, *rest
+):
+    n = len(sides)
+    side_refs = [rest[3 * i : 3 * i + 3] for i in range(n)]
+    (k1, k2, k3, q1, q2, q3, b2, b3), rest = rest[3 * n : 3 * n + 8], rest[3 * n + 8 :]
+    grads, s4, abuf, from_closure, s3, t2, outs, t1, cot, gz, bbuf, hold, left, acc = rest
+    k = Row(WIDE)
+    has_south = scal[2]
+    lo = lambda h: PAD - h * has_south
+    for ref in (s3, t1, t2, abuf, bbuf):
+        zero_walls(ref)
+    mean = sums[0:1, 0:1] / sums[1:2, 0:1]
+
+    cnear_e, cnear_w = edges(CREACH)
+    for r in range(ROWS):
         for t in range(5):
             rows = slice(2 * PACK + 8 * t, 2 * PACK + 8 * t + 8)
             from_e = pltpu.roll(west[rows, :], -8 * r % COLS, 1)
@@ -445,19 +592,9 @@
             cot[PAD + r, 8 * t : 8 * t + 8, :] = jnp.concatenate(
                 [cown[r, 8 * t : 8 * t + 8, :], side], axis=1
             )
-    for side, (lat_x, lat_c, diag_e, diag_w) in zip(sides, side_refs):
-        base = {"swap": scal[4], "north": PAD - REACH, "south": PAD + ROWS}[side]
+    for side, (lat_c, diag_e, diag_w) in zip(sides, side_refs):
         cbase = {"swap": scal[5], "north": PAD - CREACH, "south": PAD + ROWS}[side]
         crow = {"swap": scal[6], "north": ROWS - CREACH, "south": 0}[side]
-        for r in range(REACH):
-
-            def halo(t):
-                rows = slice(8 * t, 8 * t + 8)
-                from_e = pltpu.roll(diag_w[rows, :], -REACH * r % COLS, 1)
-                from_w = pltpu.roll(diag_e[rows, :], -REACH * (r + 1) % COLS, 1)
-                return jnp.where(near_e, from_e, jnp.where(near_w, from_w, 0.0))
-
-            put_packed(base + r, lambda t: lat_x[r, 8 * t : 8 * t + 8, :], halo)
         for r in range(CREACH):
             turn = lax.rem(2 * COLS - 8 * (crow + r), COLS)
             turn_w = lax.rem(2 * COLS - 8 * (crow + r + 1), COLS)
@@ -470,75 +607,12 @@
                     [lat_c[r, 8 * t : 8 * t + 8, :], part], axis=1
                 )
 
-    k1, k2, k3 = stacked_weights(w1), stacked_weights(w2), stacked_weights(w3)
-
-    for r in range(ROWS):
-        outs[PAD + r, :, 0:COLS] = own_m[r]
-
-    def closure_of(columns):
-        z = split(to_48(columns))
-        _, _, h2 = hidden_layers(z, k1, b1[...], k2, b2[...])
-        return product(k3, *split(h2))[0:FEATS] + b3[...]
-
-    def halo_rows(first):
-        o = closure_of(jnp.concatenate([s0[first + i, 0:FEATS, 0:COLS] for i in range(8)], axis=1))
-        for i in range(8):
-            outs[first + i, :, 0:COLS] = o[:, i * COLS : (i + 1) * COLS]
-
-    if sides == ["swap"]:
-        groups = 3
-        halo_rows(jnp.where(has_south == 1, PAD - 8, PAD + ROWS))
-    else:
-        groups = 4
-        halo_rows(PAD - 8)
-        halo_rows(PAD + ROWS)
-    first = lo(8)
-    o = closure_of(jnp.concatenate([wide_pack(s0, first + 8 * g) for g in range(groups)], axis=1))
-    for g in range(groups):
-        wide_unpack(outs, first + 8 * g, o[:, g * COLS : (g + 1) * COLS])
-
-    for_rows(scal, 10, section_1(k, cs, fs, masks, s0, s1))
-    for_rows(scal, 9, section_2(k, cs, fs, masks, s0, s1, s2))
-
-
-def late_kernel(
-    sides, scal, cs, fs, sums, own, own_h1, own_h2, s0, s1, s2, masks, fluxes, cot, outs_in,
-    w1, b1, w2, b2, w3, b3, v1, v2, v3, final, grads, s4, abuf, from_closure, *scratch
-):
-    s3, t1, t2, outs, gz, bbuf, hold, acc = scratch
-    k = Row(WIDE)
-    has_south, has_north = scal[2], scal[3]
-    lo = lambda h: PAD - h * has_south
-    hi = lambda h: PAD + ROWS + h * has_north
-
-    for ref in (s3, t1, t2, abuf, bbuf):
-        for row in (PAD - 1, PAD + ROWS):
-            ref[row] = jnp.zeros(ref.shape[1:], F32)
-    k1, k2, k3 = stacked_weights(w1), stacked_weights(w2), stacked_weights(w3)
-    q1, q2, q3 = stacked_weights(v1), stacked_weights(v2), stacked_weights(v3)
-
-    mean = sums[0:1, 0:1] / sums[1:2, 0:1]
-
-    def section_3(src, mid, net, r):
-        d = tendency_row(k, mid, r, cs[r], fs[r])
-        new = []
-        for t in range(5):
-            m = mask_tile(masks, r, t)
-            o = tile(net, r, t)
-            if t == 1:
-                force = 2.0 * (mean - fluxes[r, 2:3, :])
-                o = o + jnp.where(k.sub == 0, force, 0.0)
-            new.append(
-                (1.0 / 3.0) * tile(src, r, t) + (2.0 / 3.0) * tile(mid, r, t)
-                + m * ((1.0 / 6.0) * d[t] + 0.25 * o)
-            )
-        return new
 
     def step_1_end(r):
         put_state(k, s3, r, section_3(s0, s2, r))
 
     def step_1_end(r):
-        put_state(k, s3, r, section_3(s0, s2, outs_in, r))
+        put_state(k, s3, r, section_3(k, cs, fs, masks, fluxes, mean, s0, s2, outs_in, r))
 
     for_rows(scal, 8, step_1_end)
 
@@ -546,18 +620,18 @@
 
     def closure_adjoint(z, h1, h1s, h2, go, with_weights):
         gos = split(to_48(go))
-        g2 = product(q3, *gos) * (1.0 - h2 * h2)
+        g2 = product(q3[...], *gos) * (1.0 - h2 * h2)
         g2s = split(g2)
-        g1 = product(q2, *g2s) * (1.0 - h1 * h1)
+        g1 = product(q2[...], *g2s) * (1.0 - h1 * h1)
         g1s = split(g1)
         if with_weights:
             add_weight_terms(acc, z, h1s, split(h2), g1s, g2s, gos)
-        return product(q1, *g1s)[0:FEATS]
+        return product(q1[...], *g1s)[0:FEATS]
 
     def both_ways(columns, go, with_weights):
-        z = split(to_48(columns))
-        h1, h1s, h2 = hidden_layers(z, k1, b1[...], k2, b2[...])
-        o = product(k3, *split(h2))[0:FEATS] + b3[...] if with_weights else None
+        z = split(to_48(columns, 1.0))
+        h1, h1s, h2 = hidden_layers(z, k1, k2, b2)
+        o = last_layer(h2, k3, b3) if with_weights else None
         return o, closure_adjoint(z, h1, h1s, h2, go, with_weights)
 
     def masked_core(ref, r):
@@ -601,23 +675,17 @@
     for_rows(scal, 7, section_1(k, cs, fs, masks, s3, t1))
     for_rows(scal, 6, section_2(k, cs, fs, masks, s3, t1, t2))
 
-    def last(r):
-        new = section_3(s3, t2, outs, r)
-        put_result(final, r - PAD, [x[:, 0:COLS] for x in new])
-
-    for_rows(scal, 0, last)
-
     def store(r, tiles):
         for t in range(5):
             s4[r, 8 * t : 8 * t + 8, :] = tiles[t] + tile(gz, r, t)
 
     adjoint_third(k, scal, cs, fs, 5, t2, masks, abuf, cot, hold, bbuf)
-    adjoint_second(k, scal, cs, fs, 4, t1, masks, bbuf, cot, hold, t2, abuf)
-    adjoint_first(k, scal, cs, fs, 3, s3, abuf, t2, store)
+    adjoint_second(k, scal, cs, fs, 4, t1, masks, bbuf, cot, hold, left, abuf)
+    adjoint_first(k, scal, cs, fs, 3, s3, abuf, left, store)
 
     for r in range(0, ROWS, 8):
         side = lambda read: jnp.concatenate([read(r + j) for j in range(8)], axis=1)
-        z = split(to_48(side(lambda j: own[j, 0:FEATS, :])))
+        z = split(to_48(side(lambda j: own[j, 0:FEATS, :]), 1.0))
         h1 = side(lambda j: own_h1[j])
         h2 = side(lambda j: own_h2[j])
         go = side(lambda j: masked_core(s4, PAD + j))
@@ -625,8 +693,7 @@
         for j in range(8):
             from_closure[r + j] = back[:, j * COLS : (j + 1) * COLS]
 
-    for row in (PAD - 1, PAD + ROWS):
-        abuf[row] = jnp.zeros((FEATS, WIDE), F32)
+    zero_walls(abuf)
 
     def mask_top(r):
         for t in range(5):
@@ -638,9 +705,9 @@
     grads[0:40, HID : 2 * HID] = acc[112:152, 0:HID]
     grads[40:72, 0:HID] = acc[48:80, 0:HID]
     grads[40:72, HID : 2 * HID] = acc[80:112, 0:HID]
-    grads[72:73, 0:HID] = acc[160:161, 0:HID]
-    grads[72:73, HID : 2 * HID] = acc[176:177, 0:HID]
-    grads[73:74, 0:HID] = acc[192:193, 0:HID]
+    grads[72:73, 0:HID] = acc[40:41, 0:HID]
+    grads[72:73, HID : 2 * HID] = acc[160:161, 0:HID]
+    grads[73:74, 0:HID] = acc[176:177, 0:HID]
 
 
 def put_result(ref, row, tiles):
@@ -651,14 +718,12 @@
 
 
 def back_third_kernel(scal, cs, fs, state, masks, abuf, top, hold, bbuf):
-    for row in (PAD - 1, PAD + ROWS):
-        bbuf[row] = jnp.zeros((FEATS, WIDE), F32)
+    zero_walls(bbuf)
     adjoint_third(Row(WIDE), scal, cs, fs, 2, state, masks, abuf, top, hold, bbuf)
 
 
 def back_second_kernel(scal, cs, fs, gate, state, masks, bbuf, top, hold, left, abuf):
-    for row in (PAD - 1, PAD + ROWS):
-        abuf[row] = jnp.zeros((FEATS, WIDE), F32)
+    zero_walls(abuf)
     adjoint_second(Row(WIDE), scal, cs, fs, 1, state, masks, bbuf, top, hold, left, abuf)
 
 
@@ -689,39 +754,28 @@
         bout[:, 10 * t + 9 : 10 * t + 10] = packed[73:74, 36 + t : 37 + t] * scale
 
 
-def by_tile(weights):
-    heads = [weights[10 * t : 10 * t + 8] for t in range(4)]
-    tails = [weights[10 * t + level : 10 * t + level + 1] for level in (8, 9) for t in range(4)]
-    return jnp.concatenate(heads + tails, axis=0)
-
-
-def tree_round(x, axis, count, stride):
-    group = 4 if (count // stride) % 4 == 0 else 2
-    got = [
-        lax.ppermute(x, axis, [(i, i ^ (j * stride)) for i in range(count)]) for j in range(1, group)
-    ]
-    x = x + got[0] if group == 2 else (x + got[0]) + (got[1] + got[2])
-    return x, stride * group
-
-
-def tree_rounds(x, axes):
+def pair_rounds(x, axes):
+    rounds = []
     for axis, count in axes:
         if count & (count - 1):
-            x = lax.psum(x, axis)
-            yield x
+            rounds.append(x := lax.psum(x, axis))
             continue
         stride = 1
         while stride < count:
-            x, stride = tree_round(x, axis, count, stride)
-            yield x
-
-
-def three(w):
-    return jnp.concatenate([w, w, w], axis=1)
-
-
-def pad_cols(w):
-    return jnp.pad(w, ((0, 0), (0, 8)))
+            x = x + lax.ppermute(x, axis, [(i, i ^ stride) for i in range(count)])
+            rounds.append(x)
+            stride *= 2
+    return rounds
+
+
+def window_rounds(x, axis, count):
+    rounds = [x]
+    width = 2
+    while width < count:
+        x = x + lax.ppermute(x, axis, [(i, (i + width) % count) for i in range(count)])
+        rounds.append(x)
+        width *= 2
+    return rounds
 
 
 def latitude_terms(row_index, row_count):
@@ -753,20 +807,20 @@
     rows = (lat_i * ROWS - PAD + jnp.arange(EXT, dtype=jnp.int32)).astype(F32)
     cs, fs = latitude_terms(rows, lat_total)
 
+    hbm = pl.BlockSpec(memory_space=pltpu.HBM)
     packed = pl.pallas_call(
         lambda *refs: pack_kernel(sides, *refs),
         out_shape=[
-            sds(ROWS, PACK, COLS), sds(ROWS, FEATS, COLS), sds(8, COLS),
-            sds(2 * PACK + 40, COLS), sds(2 * PACK + 40, COLS),
+            sds(ROWS, PACK, COLS), sds(ROWS, FEATS, COLS), sds(2 * PACK + 40, COLS), sds(2 * PACK + 40, COLS),
         ]
         + [sds(REACH, PACK, COLS), sds(CREACH, FEATS, COLS), sds(PACK + 40, COLS), sds(PACK + 40, COLS)] * len(sides),
-        in_specs=[SMEM] + [pl.BlockSpec(memory_space=pl.ANY)] * 4,
-        out_specs=[VMEM] * (5 + 4 * len(sides)),
+        in_specs=[SMEM] + [hbm] * 4,
+        out_specs=[VMEM] * (4 + 4 * len(sides)),
         scratch_shapes=[
             pltpu.VMEM((40 * ROWS, COLS), F32), pltpu.VMEM((10 * ROWS, COLS), jnp.int32),
             pltpu.VMEM((ROWS, COLS), F32), pltpu.VMEM((40 * ROWS, COLS), F32), pltpu.SemaphoreType.DMA((4,)),
         ],
-        compiler_params=params(48),
+        compiler_params=params(8),
         name="pack_halos",
     )(
         scal,
@@ -775,7 +829,7 @@
         surface_flux,
         cotangent.reshape(40 * ROWS, COLS),
     )
-    own, cown, sums, east_pay, west_pay = packed[:5]
+    own, cown, east_pay, west_pay = packed[:4]
 
     def lat_pairs(side):
         if side == "swap":
@@ -793,39 +847,39 @@
 
     east_ring = [(i, (i + 1) % lon_n) for i in range(lon_n)]
     west_ring = [((i + 1) % lon_n, i) for i in range(lon_n)]
-    received = []
+    lat_x, lat_c, diags = [], [], []
     for i, side in enumerate(sides):
-        lat_x, lat_c, diag_e, diag_w = packed[5 + 4 * i : 9 + 4 * i]
-        received.append(
+        pay_x, pay_c, diag_e, diag_w = packed[4 + 4 * i : 8 + 4 * i]
+        lat_x.append(lax.ppermute(pay_x, "lat", lat_pairs(side)))
+        diags.append(
             [
-                lax.ppermute(lat_x, "lat", lat_pairs(side)),
-                lax.ppermute(lat_c, "lat", lat_pairs(side)),
                 lax.ppermute(diag_e, ("lon", "lat"), diagonal(side, 1)),
                 lax.ppermute(diag_w, ("lon", "lat"), diagonal(side, -1)),
             ]
         )
+        lat_c.append(lax.ppermute(pay_c, "lat", lat_pairs(side)))
     from_west = lax.ppermute(east_pay, "lon", east_ring)
     from_east = lax.ppermute(west_pay, "lon", west_ring)
-    axes = (("lon", lon_n), ("lat", lat_n))
-    mean_rounds = list(tree_rounds(sums, axes))
-
-    w_in, w_out_t = by_tile(weight_in), by_tile(weight_out.T)
-    col = lambda b: b.reshape(-1, 1)
-    forward = [
-        three(pad_cols(w_in.T)), col(bias_in), three(weight_mid.T), col(bias_mid), three(w_out_t), by_tile(col(bias_out)),
-    ]
-    forward[4] = jnp.pad(forward[4], ((0, 8), (0, 0)))
-    backward = [jnp.pad(three(w_in), ((0, 8), (0, 0))), three(weight_mid), three(pad_cols(w_out_t.T))]
-
-    own_m, own_h1, own_h2 = pl.pallas_call(
+
+    row = lambda b: b.reshape(1, -1)
+    raw = (weight_in, weight_mid, weight_out, row(bias_in), row(bias_mid), row(bias_out))
+    half = lambda *shape: jax.ShapeDtypeStruct(shape, BF16)
+    own_m, own_h1, own_h2, k1, k2, k3, q1, q2, q3, b2, b3 = pl.pallas_call(
         own_closure_kernel,
-        out_shape=[sds(ROWS, FEATS, COLS), sds(ROWS, HID, COLS), sds(ROWS, HID, COLS)],
-        in_specs=[VMEM] * 7,
-        out_specs=[VMEM] * 3,
+        out_shape=[
+            sds(ROWS, FEATS, COLS), sds(ROWS, HID, COLS), sds(ROWS, HID, COLS),
+            half(HID, 144), half(HID, 192), half(48, 192), half(48, 192), half(HID, 192), half(HID, 144),
+            sds(HID, COLS), sds(FEATS, COLS),
+        ],
+        in_specs=[VMEM] + [hbm] * 6,
+        out_specs=[VMEM] * 11,
+        scratch_shapes=[pltpu.VMEM(w.shape, F32) for w in raw]
+        + [pltpu.VMEM((COLS, COLS), F32), pltpu.VMEM((COLS, COLS), F32), pltpu.VMEM((HID, WIDE), F32)]
+        + [pltpu.SemaphoreType.DMA((6,))],
         compiler_params=params(12),
         cost_estimate=pl.CostEstimate(flops=10**9, bytes_accessed=2 * 10**6, transcendentals=0),
         name="own_closure",
-    )(own, *forward)
+    )(own, *raw)
 
     geometry = (scal, cs, fs)
     state = sds(EXT, 72, WIDE)
@@ -846,21 +900,31 @@
             name=name,
         )(*geometry, *args)
 
-    s0, s1, s2, masks, fluxes, cot, net = call(
-        lambda *refs: early_kernel(sides, *refs), "first_sections",
-        [state, state, state, marks, sds(EXT, 8, WIDE), plain, plain], [],
-        [mean_rounds[-2], own, cown, own_m, from_west, from_east]
-        + [item for side in received for item in side] + forward,
+    s0, masks, fluxes, net, window = call(
+        lambda *refs: assemble_kernel(sides, *refs), "assemble",
+        [state, marks, sds(EXT, 8, WIDE), plain, sds(8, COLS)], [],
+        [own, own_m, from_west, from_east]
+        + [ref for x, diag in zip(lat_x, diags) for ref in (x, *diag)] + [k1, k2, k3, b2, b3],
         2 * 10**9, 8,
     )
-    final, grads, top, abuf, from_closure = call(
+    means = window_rounds(window, "lon", lon_n)
+    if sides != ["swap"]:
+        means += pair_rounds(means[-1], (("lat", lat_n),))
+    s1 = call(first_section_kernel, "first_section", state, [], [s0, masks], 10**9, 8)
+    s2 = call(second_section_kernel, "second_section", state, [], [means[min(1, len(means) - 1)], s0, s1, masks], 10**9, 8)
+    grads, top, abuf, from_closure, s3, t2, net_2 = call(
         lambda *refs: late_kernel(sides, *refs), "steps_and_adjoint",
-        [sds(40 * ROWS, COLS), sds(80, COLS), plain, plain, sds(ROWS, FEATS, COLS)],
-        [vmem(state)] * 3 + [vmem(plain)] * 4 + [pltpu.VMEM((208, HID), F32)],
-        [mean_rounds[-1], own, own_h1, own_h2, s0, s1, s2, masks, fluxes, cot, net] + forward + backward,
-        4 * 10**9, 24,
-    )
-    rounds = list(tree_rounds(grads, axes))
+        [sds(80, COLS), plain, plain, sds(ROWS, FEATS, COLS), state, state, plain],
+        [vmem(state)] + [vmem(plain)] * 5 + [pltpu.VMEM((192, HID), F32)],
+        [means[-1], own, cown, own_h1, own_h2, s0, s2, masks, fluxes, net, from_west, from_east]
+        + [ref for c, diag in zip(lat_c, diags) for ref in (c, *diag)] + [k1, k2, k3, q1, q2, q3, b2, b3],
+        4 * 10**9, 18,
+    )
+    rounds = pair_rounds(grads, (("lat", lat_n), ("lon", lon_n)))
+    final = call(
+        last_section_kernel, "last_section", sds(40 * ROWS, COLS), [],
+        [rounds[min(2, len(rounds) - 1)], means[-1], s3, t2, masks, fluxes, net_2], 10**9, 8,
+    )
     hold, bbuf = call(
         back_third_kernel, "adjoint_third_section", [plain, plain], [], [s2, masks, abuf, top], 10**9, 8
     )

time: 84.1 us -> 79.3 us (0.943)
  waiting for transfers between devices: 4.67 us -> 21.4 us
  starting transfers between devices: 29.4 us -> 13.9 us
  local copies, waits for them, and re-layouts: 14.5 us -> 7.87 us
  Pallas kernels: 32.6 us -> 34.7 us
  other arithmetic: 1.34 us -> 0.09 us
    ppermute x16 -> x10, waiting for transfers between devices: 3.55 us -> 21.4 us  [the longest x3 11.7 us: window_rounds(): lax.ppermute(x, axis, [(i, (i + width) % count) for i in range(count)])]
    ppermute x16 -> x10, starting transfers between devices: 19.5 us -> 4.09 us  [the longest x1 3.03 us: on_device(): lat_x.append(lax.ppermute(pay_x, 'lat', lat_pairs(side)))]
    concatenate x6 -> x0, local copies, waits for them, and re-layouts: 5.72 us -> none  [the longest x5 5.64 us: by_tile(): return jnp.concatenate(heads + tails, axis=0)]
    slice x6 -> x0, local copies, waits for them, and re-layouts: 3.29 us -> none  [the longest x3 1.75 us: by_tile(): heads = [weights[10 * t:10 * t + 8] for t in range(4)]]
    unnamed x16 -> x19, local copies, waits for them, and re-layouts: 5.18 us -> 7.78 us
    pallas_call x5 -> x8, Pallas kernels: 29.2 us -> 31 us  [call(): pl.pallas_call(kernel, out_shape=out_shape, in_specs=[SMEM] * 3 + [VMEM]...]
    ppermute x1, starting transfers between devices: 1.59 us -> 0.01 us  [on_device(): lax.ppermute(diag_e, ('lon', 'lat'), diagonal(side, 1))]
    ppermute x1, starting transfers between devices: 3.86 us -> 5.34 us  [on_device(): lax.ppermute(diag_w, ('lon', 'lat'), diagonal(side, -1))]
  transfers between devices with their start and end apart: 20 -> 14, of which waited for: 5 -> 7; matrix products, arithmetic and copies ran while one was open for 15% -> 1% of each run, Pallas kernels for 9% -> 18%
where the time goes in v3:
time: 79.3 us; the launch traced here: 78.8 us
  Pallas kernels  34.7 us (44%)
  waiting for transfers between devices  21.4 us (27%)
  starting transfers between devices  13.9 us (18%)
  local copies, waits for them, and re-layouts  7.87 us (10%)
  between operations  0.83 us (1%)
    pallas_call x8, Pallas kernels, call(): pl.pallas_call(kernel, out_shape=out_shape, in_specs=[SMEM] * 3 + [VMEM]...  31 us
    ppermute x3, waiting for transfers between devices, window_rounds(): lax.ppermute(x, axis, [(i, (i + width) % count) for i in range(count)])  11.7 us
    ppermute x5, waiting for transfers between devices, pair_rounds(): x = x + lax.ppermute(x, axis, [(i, i ^ stride) for i in range(count)])  9.78 us
    unnamed x19, local copies, waits for them, and re-layouts  7.78 us
    ppermute x1, starting transfers between devices, on_device(): lax.ppermute(diag_w, ('lon', 'lat'), diagonal(side, -1))  5.34 us
    ppermute x1, starting transfers between devices, on_device(): from_east = lax.ppermute(west_pay, 'lon', west_ring)  4.44 us
    ppermute x1, starting transfers between devices, on_device(): lat_x.append(lax.ppermute(pay_x, 'lat', lat_pairs(side)))  3.03 us
    pallas_call x1, Pallas kernels, on_device(): pl.pallas_call(lambda *refs: pack_kernel(sides, *refs), out_shape=[sds(RO...  1.68 us
  transfers between devices with their start and end apart: 14, of which 7 were waited for; matrix products, arithmetic and copies ran while one was open for 1% of the time, Pallas kernels for 18%

profile of v3, /device:TPU:0, one launch (start us, length us, event | category | flops | bytes accessed | tf_op | source)
XLA Modules:
  0.0 78.8 jit_solution(8859835672579696302)
XLA Ops:
  0.7 1.0 %copy-done = f32[4,10,16,128]{3,2,1,0:T(8,128)S(1)} copy-done((f32[4,10,16,128]{3,2,1,0:T(8,128)S(1)}, f32[4,10,16,128]{3,2,1,0:T(8,128)}, u32[]{:S(2)}) %copy-start) | copy-done | bytes 327704
  1.7 1.0 %copy-done.1 = f32[4,10,16,128]{3,2,1,0:T(8,128)S(1)} copy-done((f32[4,10,16,128]{3,2,1,0:T(8,128)S(1)}, f32[4,10,16,128]{3,2,1,0:T(8,128)}, u32[]{:S(2)}) %copy-start.1) | copy-done | bytes 327704
  2.7 0.9 %copy-done.2 = s32[10,16,128]{2,1,0:T(8,128)S(1)} copy-done((s32[10,16,128]{2,1,0:T(8,128)S(1)}, s32[10,16,128]{2,1,0:T(8,128)}, u32[]{:S(2)}) %copy-start.2) | copy-done | bytes 81944
  4.3 1.7 %pack_halos.1 = (f32[16,56,128]{2,1,0:T(8,128)S(1)}, f32[16,40,128]{2,1,0:T(8,128)S(1)}, f32[152,128]{1,0:T(8,128)S(1)}, f32[152,128]{1,0:T(8,128)S(1)}, f32[11,...) custom-call(s32[7]{0:T(128)S(1)} %stack.39.refs_0_.scal, ...), custom_call_target="tpu_custom_call" | custom-call | tf_op jit(solution)/shard_map/pack_halos/pallas_call | solution.py:811
  6.0 3.0 %collective-permute-start.2 = (f32[11,56,128]{2,1,0:T(8,128)S(1)}, f32[11,56,128]{2,1,0:T(8,128)S(1)}, u32[]{:S(2)}, u32[]{:S(2)}) collective-permute-start(f32[11,56,128]{2,1,0:T(8,128)S(1)} %get-tuple-element.53), channel_id=1, source_target_pairs={{0,1},{1,0},{2,3},{3,2},{4,5},{5,4},{6,7},{7,6},{8,9},{9,8},{10,11... | collective-permute-start | bytes 946184 | tf_op jit(solution)/shard_map/ppermute | solution.py:853
  9.0 5.3 %collective-permute-start.4 = (f32[96,128]{1,0:T(8,128)S(1)}, f32[96,128]{1,0:T(8,128)S(1)}, u32[]{:S(2)}, u32[]{:S(2)}) collective-permute-start(f32[96,128]{1,0:T(8,128)S(1)} %get-tuple-element.55), channel_id=1, source_target_pairs={{0,31},{1,30},{2,1},{3,0},{4,3},{5,2},{6,5},{7,4},{8,7},{9,6},{10,... | collective-permute-start | bytes 147464 | tf_op jit(solution)/shard_map/ppermute | solution.py:857
  14.3 4.4 %collective-permute-start.1 = (f32[152,128]{1,0:T(8,128)S(1)}, f32[152,128]{1,0:T(8,128)S(1)}, u32[]{:S(2)}, u32[]{:S(2)}) collective-permute-start(f32[152,128]{1,0:T(8,128)S(1)} %get-tuple-element.52), channel_id=1, source_target_pairs={{2,0},{4,2},{6,4},{8,6},{10,8},{12,10},{14,12},{16,14},{18,16},{20... | collective-permute-start | bytes 233480 | tf_op jit(solution)/shard_map/ppermute | solution.py:862
  18.8 0.8 %copy.18.refs_2_ = f32[64,40]{1,0:T(8,128)S(1)} copy(f32[64,40]{0,1:T(8,128)} %param.17) | data formatting | bytes 20480 | tf_op args[7]
  23.1 1.3 %own_closure.1 = (f32[16,40,128]{2,1,0:T(8,128)S(1)}, f32[16,64,128]{2,1,0:T(8,128)S(1)}, f32[16,64,128]{2,1,0:T(8,128)S(1)}, bf16[64,144]{1,0:T(8,128)(2,1)S(1)...) custom-call(f32[16,56,128]{2,1,0:T(8,128)S(1)} %get-tuple-element.49, ...), custom_call_target="tpu_custom_call" | custom-call | flops 1000000000 | bytes 2000000 | tf_op jit(solution)/shard_map/own_closure/pallas_call | solution.py:867
  24.4 2.1 %assemble.1 = (f32[48,72,256]{2,1,0:T(8,128)S(1)}, f32[48,16,256]{2,1,0:T(8,128)S(1)}, f32[48,8,256]{2,1,0:T(8,128)S(1)}, f32[48,40,256]{2,1,0:T(8,128)S(1)}, f32[8,128]{1,0:T(8,128)S(1)}) custom-call(s32[7]{0:T(128)S(1)} %stack.39.refs_0_.scal, f32[48]{0:T(128)S(1)} %get-tuple-element.90.refs_1_.cs, f32[48]{0:T(128)S(1)} %get-tuple-element.91.refs_2_.fs, ...), custom_call_target="tpu_custom_call" | custom-call | flops 2000000000 | bytes 10000000 | tf_op jit(solution)/shard_map/assemble/pallas_call | solution.py:892
  26.8 6.2 %collective-permute-done.5 = f32[8,128]{1,0:T(8,128)S(1)} collective-permute-done((f32[8,128]{1,0:T(8,128)S(1)}, f32[8,128]{1,0:T(8,128)S(1)}, u32[]{:S(2)}, u32[]{:S(2)}) %collective-permute-start.5) | collective-permute-done | bytes 4128 | tf_op jit(solution)/shard_map/ppermute | solution.py:775
  32.9 2.2 %first_section.1.s1.state = f32[48,72,256]{2,1,0:T(8,128)S(1)} custom-call(s32[7]{0:T(128)S(1)} %stack.39.refs_0_.scal, f32[48]{0:T(128)S(1)} %get-tuple-element.90.refs_1_.cs, f32[48]{0:T(128)S(1)} %get-tuple-element.91.refs_2_.fs, f32[48,72,256]{2,1,0:T(8,128)S(1)} %get-tuple-element.65.s0.refs_8_.state, f32[48,16,256]{2,1,0:T(8,128)S(1)} %get-tuple-element.66.masks.refs_10_), custom_call_target="tpu_custom_call" | custom-call | flops 1000000000 | bytes 10000000 | tf_op jit(solution)/shard_map/first_section/pallas_call | solution.py:892
  35.1 3.2 %collective-permute-done.6 = f32[8,128]{1,0:T(8,128)S(1)} collective-permute-done((f32[8,128]{1,0:T(8,128)S(1)}, f32[8,128]{1,0:T(8,128)S(1)}, u32[]{:S(2)}, u32[]{:S(2)}) %collective-permute-start.6) | collective-permute-done | bytes 4128 | tf_op jit(solution)/shard_map/ppermute | solution.py:775
  38.3 2.2 %second_section.1.refs_9_.state = f32[48,72,256]{2,1,0:T(8,128)S(1)} custom-call(s32[7]{0:T(128)S(1)} %stack.39.refs_0_.scal, f32[48]{0:T(128)S(1)} %get-tuple-element.90.refs_1_.cs, f32[48]{0:T(128)S(1)} %get-tuple-element.91.refs_2_.fs, f32[8,128]{1,0:T(8,128)S(1)} %add.42.gate, f32[48,72,256]{2,1,0:T(8,128)S(1)} %get-tuple-element.65.s0.refs_8_.state, ...), custom_call_target="tpu_custom_call" | custom-call | flops 1000000000 | bytes 10000000 | tf_op jit(solution)/shard_map/second_section/pallas_call | solution.py:892
  40.5 2.3 %collective-permute-done.7 = f32[8,128]{1,0:T(8,128)S(1)} collective-permute-done((f32[8,128]{1,0:T(8,128)S(1)}, f32[8,128]{1,0:T(8,128)S(1)}, u32[]{:S(2)}, u32[]{:S(2)}) %collective-permute-start.7) | collective-permute-done | bytes 4128 | tf_op jit(solution)/shard_map/ppermute | solution.py:775
  42.8 15.7 %steps_and_adjoint.1 = (f32[80,128]{1,0:T(8,128)S(1)}, f32[48,40,256]{2,1,0:T(8,128)S(1)}, f32[48,40,256]{2,1,0:T(8,128)S(1)}, f32[16,40,128]{2,1,0:T(8,128)S(1)...) custom-call(s32[7]{0:T(128)S(1)} %stack.39.refs_0_.scal, ...), custom_call_target="tpu_custom_call" | custom-call | flops 4000000000 | bytes 10000000 | tf_op jit(solution)/shard_map/steps_and_adjoint/pallas_call | solution.py:892
  58.6 3.9 %collective-permute-done.9 = f32[80,128]{1,0:T(8,128)S(1)} collective-permute-done((f32[80,128]{1,0:T(8,128)S(1)}, f32[80,128]{1,0:T(8,128)S(1)}, u32[]{:S(2)}, u32[]{:S(2)}) %collective-permute-start.9) | collective-permute-done | bytes 40992 | tf_op jit(solution)/shard_map/ppermute | solution.py:765
  62.6 2.1 %adjoint_third_section.1 = (f32[48,40,256]{2,1,0:T(8,128)S(1)}, f32[48,40,256]{2,1,0:T(8,128)S(1)}) custom-call(s32[7]{0:T(128)S(1)} %stack.39.refs_0_.scal, f32[48]{0:T(128)S(1)} %get-tuple-element.90.refs_1_.cs, f32[48]{0:T(128)S(1)} %get-tuple-element.91.refs_2_.fs, f32[48,72,256]{2,1,0:T(8,128)S(1)} %second_section.1.refs_9_.state, ...), custom_call_target="tpu_custom_call" | custom-call | flops 1000000000 | bytes 10000000 | tf_op jit(solution)/shard_map/adjoint_third_section/pallas_call | solution.py:892
  64.8 2.2 %adjoint_second_section.1 = (f32[48,40,256]{2,1,0:T(8,128)S(1)}, f32[48,40,256]{2,1,0:T(8,128)S(1)}) custom-call(s32[7]{0:T(128)S(1)} %stack.39.refs_0_.scal, f32[48]{0:T(128)S(1)} %get-tuple-element.90.refs_1_.cs, f32[48]{0:T(128)S(1)} %get-tuple-element.91.refs_2_.fs, f32[80,128]{1,0:T(8,128)S(1)} %add.45.gate, f32[48,72,256]{2,1,0:T(8,128)S(1)} %first_section.1.s1.state, ...), custom_call_target="tpu_custom_call" | custom-call | flops 1000000000 | bytes 10000000 | tf_op jit(solution)/shard_map/adjoint_second_section/pallas_call | solution.py:892
  67.0 1.8 %collective-permute-done.11 = f32[80,128]{1,0:T(8,128)S(1)} collective-permute-done((f32[80,128]{1,0:T(8,128)S(1)}, f32[80,128]{1,0:T(8,128)S(1)}, u32[]{:S(2)}, u32[]{:S(2)}) %collective-permute-start.11) | collective-permute-done | bytes 40992 | tf_op jit(solution)/shard_map/ppermute | solution.py:765
  68.8 2.4 %adjoint_first_section.1 = f32[640,128]{1,0:T(8,128)} custom-call(s32[7]{0:T(128)S(1)} %stack.39.refs_0_.scal, f32[48]{0:T(128)S(1)} %get-tuple-element.90.refs_1_.cs, f32[48]{0:T(128)S(1)} %get-tuple-element.91.refs_2_.fs, f32[80,128]{1,0:T(8,128)S(1)} %add.46.gate, f32[48,72,256]{2,1,0:T(8,128)S(1)} %get-tuple-element.65.s0.refs_8_.state, ...), custom_call_target="tpu_custom_call" | custom-call | flops 1000000000 | bytes 10000000 | tf_op jit(solution)/shard_map/adjoint_first_section/pallas_call | solution.py:892
  71.2 1.6 %collective-permute-done.12 = f32[80,128]{1,0:T(8,128)S(1)} collective-permute-done((f32[80,128]{1,0:T(8,128)S(1)}, f32[80,128]{1,0:T(8,128)S(1)}, u32[]{:S(2)}, u32[]{:S(2)}) %collective-permute-start.12) | collective-permute-done | bytes 40992 | tf_op jit(solution)/shard_map/ppermute | solution.py:765
  73.5 2.1 %last_section.1 = f32[640,128]{1,0:T(8,128)} custom-call(s32[7]{0:T(128)S(1)} %stack.39.refs_0_.scal, f32[48]{0:T(128)S(1)} %get-tuple-element.90.refs_1_.cs, f32[48]{0:T(128)S(1)} %get-tuple-element.91.refs_2_.fs, f32[80,128]{1,0:T(8,128)S(1)} %add.47.gate, f32[8,128]{1,0:T(8,128)S(1)} %add.44.refs_3_.sums, f32[48,72,256]{2,1,0:T(8,128)S(1)} %get-tuple-element.74.s3, ...), custom_call_target="tpu_custom_call" | custom-call | flops 1000000000 | bytes 10000000 | tf_op jit(solution)/shard_map/last_section/pallas_call | solution.py:892
  75.6 2.5 %collective-permute-done.13 = f32[80,128]{1,0:T(8,128)S(1)} collective-permute-done((f32[80,128]{1,0:T(8,128)S(1)}, f32[80,128]{1,0:T(8,128)S(1)}, u32[]{:S(2)}, u32[]{:S(2)}) %collective-permute-start.13) | collective-permute-done | bytes 40992 | tf_op jit(solution)/shard_map/ppermute | solution.py:765
  (44 shorter events, 6.1 us)
Async XLA Ops:
  0.7 1.0 %copy-start = (f32[4,10,16,128]{3,2,1,0:T(8,128)S(1)}, f32[4,10,16,128]{3,2,1,0:T(8,128)}, u32[]{:S(2)}) copy-start(f32[4,10,16,128]{3,2,1,0:T(8,128)} %param.10) | copy-start | bytes 983044
  1.7 1.0 %copy-start.1 = (f32[4,10,16,128]{3,2,1,0:T(8,128)S(1)}, f32[4,10,16,128]{3,2,1,0:T(8,128)}, u32[]{:S(2)}) copy-start(f32[4,10,16,128]{3,2,1,0:T(8,128)} %param.19) | copy-start | bytes 983044
  2.7 0.9 %copy-start.2 = (s32[10,16,128]{2,1,0:T(8,128)S(1)}, s32[10,16,128]{2,1,0:T(8,128)}, u32[]{:S(2)}) copy-start(s32[10,16,128]{2,1,0:T(8,128)} %param.11) | copy-start | bytes 245764
  3.6 0.7 copy-start.3
  6.0 18.4 %collective-permute-start.2 = (f32[11,56,128]{2,1,0:T(8,128)S(1)}, f32[11,56,128]{2,1,0:T(8,128)S(1)}, u32[]{:S(2)}, u32[]{:S(2)}) collective-permute-start(f32[11,56,128]{2,1,0:T(8,128)S(1)} %get-tuple-element.53), channel_id=1, source_target_pairs={{0,1},{1,0},{2,3},{3,2},{4,5},{5,4},{6,7},{7,6},{8,9},{9,8},{10,11... | collective-permute-start | bytes 946184 | tf_op jit(solution)/shard_map/ppermute | solution.py:853
  9.0 15.4 %collective-permute-start.3 = (f32[96,128]{1,0:T(8,128)S(1)}, f32[96,128]{1,0:T(8,128)S(1)}, u32[]{:S(2)}, u32[]{:S(2)}) collective-permute-start(f32[96,128]{1,0:T(8,128)S(1)} %get-tuple-element.54), channel_id=1, source_target_pairs={{0,3},{1,2},{2,5},{3,4},{4,7},{5,6},{6,9},{7,8},{8,11},{9,10},{10,... | collective-permute-start | bytes 147464 | tf_op jit(solution)/shard_map/ppermute | solution.py:856
  9.0 15.4 %collective-permute-start.4 = (f32[96,128]{1,0:T(8,128)S(1)}, f32[96,128]{1,0:T(8,128)S(1)}, u32[]{:S(2)}, u32[]{:S(2)}) collective-permute-start(f32[96,128]{1,0:T(8,128)S(1)} %get-tuple-element.55), channel_id=1, source_target_pairs={{0,31},{1,30},{2,1},{3,0},{4,3},{5,2},{6,5},{7,4},{8,7},{9,6},{10,... | collective-permute-start | bytes 147464 | tf_op jit(solution)/shard_map/ppermute | solution.py:857
  14.3 10.0 %collective-permute-start = (f32[152,128]{1,0:T(8,128)S(1)}, f32[152,128]{1,0:T(8,128)S(1)}, u32[]{:S(2)}, u32[]{:S(2)}) collective-permute-start(f32[152,128]{1,0:T(8,128)S(1)} %get-tuple-element.51), channel_id=1, source_target_pairs={{0,2},{2,4},{4,6},{6,8},{8,10},{10,12},{12,14},{14,16},{16,18},{18... | collective-permute-start | bytes 233480 | tf_op jit(solution)/shard_map/ppermute | solution.py:861
  14.3 10.1 %collective-permute-start.1 = (f32[152,128]{1,0:T(8,128)S(1)}, f32[152,128]{1,0:T(8,128)S(1)}, u32[]{:S(2)}, u32[]{:S(2)}) collective-permute-start(f32[152,128]{1,0:T(8,128)S(1)} %get-tuple-element.52), channel_id=1, source_target_pairs={{2,0},{4,2},{6,4},{8,6},{10,8},{12,10},{14,12},{16,14},{18,16},{20... | collective-permute-start | bytes 233480 | tf_op jit(solution)/shard_map/ppermute | solution.py:862
  19.6 0.8 copy-start.4
  20.4 0.7 copy-start.5
  21.1 0.7 copy-start.6
  21.8 0.7 copy-start.7
  22.4 0.7 copy-start.8
  26.6 6.4 %collective-permute-start.5 = (f32[8,128]{1,0:T(8,128)S(1)}, f32[8,128]{1,0:T(8,128)S(1)}, u32[]{:S(2)}, u32[]{:S(2)}) collective-permute-start(f32[8,128]{1,0:T(8,128)S(1)} %get-tuple-element.61), channel_id=1, source_target_pairs={{0,4},{2,6},{4,8},{6,10},{8,12},{10,14},{12,16},{14,18},{16,20},{1... | collective-permute-start | bytes 12296 | tf_op jit(solution)/shard_map/ppermute | solution.py:775
  26.6 16.2 %collective-permute-start.8 = (f32[6,40,128]{2,1,0:T(8,128)S(1)}, f32[6,40,128]{2,1,0:T(8,128)S(1)}, u32[]{:S(2)}, u32[]{:S(2)}) collective-permute-start(f32[6,40,128]{2,1,0:T(8,128)S(1)} %get-tuple-element.69), channel_id=1, source_target_pairs={{0,1},{1,0},{2,3},{3,2},{4,5},{5,4},{6,7},{7,6},{8,9},{9,8},{10,11... | collective-permute-start | bytes 368648 | tf_op jit(solution)/shard_map/ppermute | solution.py:860
  32.9 5.4 %collective-permute-start.6 = (f32[8,128]{1,0:T(8,128)S(1)}, f32[8,128]{1,0:T(8,128)S(1)}, u32[]{:S(2)}, u32[]{:S(2)}) collective-permute-start(f32[8,128]{1,0:T(8,128)S(1)} %add.42.gate), channel_id=1, source_target_pairs={{0,8},{2,10},{4,12},{6,14},{8,16},{10,18},{12,20},{14,22},{16,24},... | collective-permute-start | bytes 12296 | tf_op jit(solution)/shard_map/ppermute | solution.py:775
  38.3 4.5 %collective-permute-start.7 = (f32[8,128]{1,0:T(8,128)S(1)}, f32[8,128]{1,0:T(8,128)S(1)}, u32[]{:S(2)}, u32[]{:S(2)}) collective-permute-start(f32[8,128]{1,0:T(8,128)S(1)} %add.43), channel_id=1, source_target_pairs={{0,16},{2,18},{4,20},{6,22},{8,24},{10,26},{12,28},{14,30},{16,0},... | collective-permute-start | bytes 12296 | tf_op jit(solution)/shard_map/ppermute | solution.py:775
  58.5 4.0 %collective-permute-start.9 = (f32[80,128]{1,0:T(8,128)S(1)}, f32[80,128]{1,0:T(8,128)S(1)}, u32[]{:S(2)}, u32[]{:S(2)}) collective-permute-start(f32[80,128]{1,0:T(8,128)S(1)} %get-tuple-element.73), channel_id=1, source_target_pairs={{0,1},{1,0},{2,3},{3,2},{4,5},{5,4},{6,7},{7,6},{8,9},{9,8},{10,11... | collective-permute-start | bytes 122888 | tf_op jit(solution)/shard_map/ppermute | solution.py:765
  62.5 2.1 %collective-permute-start.10 = (f32[80,128]{1,0:T(8,128)S(1)}, f32[80,128]{1,0:T(8,128)S(1)}, u32[]{:S(2)}, u32[]{:S(2)}) collective-permute-start(f32[80,128]{1,0:T(8,128)S(1)} %add.45.gate), channel_id=1, source_target_pairs={{0,2},{2,0},{4,6},{6,4},{8,10},{10,8},{12,14},{14,12},{16,18},{18,... | collective-permute-start | bytes 122888 | tf_op jit(solution)/shard_map/ppermute | solution.py:765
  64.7 4.1 %collective-permute-start.11 = (f32[80,128]{1,0:T(8,128)S(1)}, f32[80,128]{1,0:T(8,128)S(1)}, u32[]{:S(2)}, u32[]{:S(2)}) collective-permute-start(f32[80,128]{1,0:T(8,128)S(1)} %add.46.gate), channel_id=1, source_target_pairs={{0,4},{2,6},{4,0},{6,2},{8,12},{10,14},{12,8},{14,10},{16,20},{18,... | collective-permute-start | bytes 122888 | tf_op jit(solution)/shard_map/ppermute | solution.py:765
  68.8 4.0 %collective-permute-start.12 = (f32[80,128]{1,0:T(8,128)S(1)}, f32[80,128]{1,0:T(8,128)S(1)}, u32[]{:S(2)}, u32[]{:S(2)}) collective-permute-start(f32[80,128]{1,0:T(8,128)S(1)} %add.47.gate), channel_id=1, source_target_pairs={{0,8},{2,10},{4,12},{6,14},{8,0},{10,2},{12,4},{14,6},{16,24},{18,... | collective-permute-start | bytes 122888 | tf_op jit(solution)/shard_map/ppermute | solution.py:765
  72.8 5.3 %collective-permute-start.13 = (f32[80,128]{1,0:T(8,128)S(1)}, f32[80,128]{1,0:T(8,128)S(1)}, u32[]{:S(2)}, u32[]{:S(2)}) collective-permute-start(f32[80,128]{1,0:T(8,128)S(1)} %add.48), channel_id=1, source_target_pairs={{0,16},{2,18},{4,20},{6,22},{8,24},{10,26},{12,28},{14,30},{16,0},... | collective-permute-start | bytes 122888 | tf_op jit(solution)/shard_map/ppermute | solution.py:765

commit v4 on v3

--- a/solution.py
+++ b/solution.py
@@ -23,7 +23,9 @@
 FEATS = 40
 HID = 64
 PACK = 56
-SUMS = 51
+STRIP = 2 * PACK + 40
+LAT_X = REACH * PACK
+LAT = LAT_X + CREACH * FEATS
 SLOT = 16
 F32 = jnp.float32
 BF16 = jnp.bfloat16
@@ -61,8 +63,8 @@
 
 def pack_kernel(sides, scal, x_hbm, mask_hbm, flux_hbm, cot_hbm, *outs):
     x, mask, flux, cot, sems = outs[-5:]
-    own, cown, east, west = outs[:4]
-    per_side = [outs[4 + 4 * i : 8 + 4 * i] for i in range(len(sides))]
+    own, cown, east, west, sums = outs[:5]
+    per_side = outs[5 : 5 + len(sides)]
     pairs = ((mask_hbm, mask), (x_hbm, x), (flux_hbm, flux), (cot_hbm, cot))
     copies = [pltpu.make_async_copy(a, b, sems.at[i]) for i, (a, b) in enumerate(pairs)]
     for copy in copies:
@@ -72,7 +74,7 @@
     top = mask[0:ROWS, :].astype(F32)
     total = jnp.sum(jnp.sum(top * flux[...], axis=1, keepdims=True), axis=0, keepdims=True)
     count = jnp.sum(jnp.sum(top, axis=1, keepdims=True), axis=0, keepdims=True)
-    tail = jnp.where(sub_index(COLS) == 0, total, jnp.where(sub_index(COLS) == 1, count, 0.0))
+    sums[...] = jnp.where(sub_index(COLS) == 0, total, jnp.where(sub_index(COLS) == 1, count, 0.0))
     for r in range(ROWS):
         first = mask[pl.ds(r, 8, stride=ROWS), :].astype(F32)
         m8 = mask[8 * ROWS + r : 8 * ROWS + r + 1, :].astype(F32)
@@ -88,7 +90,7 @@
         own[r, 48:49, :] = m8
         own[r, 49:50, :] = m9
         own[r, 50:51, :] = flux[r : r + 1, :]
-        own[r, SUMS:56, :] = tail[0:5, :]
+        own[r, 51:56, :] = jnp.zeros((5, COLS), F32)
     for half in range(2):
         for t in range(7):
             rows = [own[8 * half + s, 8 * t : 8 * t + 8, :] for s in range(8)]
@@ -100,19 +102,39 @@
         at = 2 * PACK + 8 * t
         east[at : at + 8, :] = slot_pack(rows, lambda s: 8 * (s + 1), 8)
         west[at : at + 8, :] = slot_pack(rows, lambda s: 8 * s, 8)
-    for side, (lat_x, lat_c, diag_e, diag_w) in zip(sides, per_side):
+    for side, lat in zip(sides, per_side):
         start = {"swap": scal[0], "north": ROWS - REACH, "south": 0}[side]
         cstart = {"swap": scal[1], "north": ROWS - CREACH, "south": 0}[side]
         for n in range(REACH):
-            lat_x[n] = own[start + n]
+            lat[PACK * n : PACK * (n + 1), :] = own[start + n]
         for n in range(CREACH):
-            lat_c[n] = cown[cstart + n]
-        for t in range(7):
-            rows = [own[start + n, 8 * t : 8 * t + 8, :] for n in range(REACH)]
-            diag_e[8 * t : 8 * t + 8, :] = slot_pack(rows, lambda s: REACH * (s + 1), REACH)
-            diag_w[8 * t : 8 * t + 8, :] = slot_pack(rows, lambda s: REACH * s, REACH)
-        diag_e[PACK : PACK + 40, :] = east[2 * PACK : 2 * PACK + 40, :]
-        diag_w[PACK : PACK + 40, :] = west[2 * PACK : 2 * PACK + 40, :]
+            lat[LAT_X + FEATS * n : LAT_X + FEATS * (n + 1), :] = cown[cstart + n]
+
+
+def corner_kernel(sides, scal, east, west, *outs):
+    for side, corner in zip(sides, outs):
+        start = {"swap": scal[0], "north": ROWS - REACH, "south": 0}[side]
+        for at, strip, near in ((0, east, 1), (PACK + 40, west, 0)):
+            for t in range(7):
+                rows = slice(at + 8 * t, at + 8 * t + 8)
+                corner[rows, :] = shift_rows(strip, t, start, near)
+            corner[at + PACK : at + PACK + 40, :] = strip[2 * PACK : 2 * PACK + 40, :]
+
+
+def shift_rows(strip, t, start, near):
+    lane = lax.broadcasted_iota(jnp.int32, (8, COLS), 1)
+    halves = [strip[8 * t : 8 * t + 8, :], strip[PACK + 8 * t : PACK + 8 * t + 8, :]]
+    if isinstance(start, int):
+        out = jnp.zeros((8, COLS), F32)
+        for n in range(REACH):
+            r = start + n
+            turn = REACH * n - (SLOT * (r % 8) + near * (SLOT - REACH))
+            turned = pltpu.roll(halves[r // 8], turn % COLS, 1)
+            out = jnp.where((lane >= REACH * n) & (lane < REACH * (n + 1)), turned, out)
+        return out
+    low = shift_rows(strip, t, 0, near)
+    high = shift_rows(strip, t, ROWS - REACH, near)
+    return jnp.where(start == 0, low, high)
 
 
 def split(values):
@@ -471,11 +493,11 @@
         ref[row] = jnp.zeros(ref.shape[1:], F32)
 
 
-def assemble_kernel(sides, scal, cs, fs, own, own_m, east, west, *rest):
+def assemble_kernel(sides, scal, cs, fs, gate, own, own_m, east, west, *rest):
     n = len(sides)
-    side_refs = [rest[3 * i : 3 * i + 3] for i in range(n)]
-    (k1, k2, k3, b2, b3), rest = rest[3 * n : 3 * n + 5], rest[3 * n + 5 :]
-    s0, masks, fluxes, outs, window = rest
+    side_refs = [rest[2 * i : 2 * i + 2] for i in range(n)]
+    (k1, k2, k3, b2, b3), rest = rest[2 * n : 2 * n + 5], rest[2 * n + 5 :]
+    s0, masks, fluxes, outs = rest
     k = Row(WIDE)
     has_south = scal[2]
     lo = lambda h: PAD - h * has_south
@@ -502,25 +524,18 @@
             return jnp.where(near_e, from_e, jnp.where(near_w, from_w, 0.0))
 
         put_packed(PAD + r, lambda t: own[r, 8 * t : 8 * t + 8, :], halo)
-    for side, (lat_x, diag_e, diag_w) in zip(sides, side_refs):
+    for side, (lat, corner) in zip(sides, side_refs):
         base = {"swap": scal[4], "north": PAD - REACH, "south": PAD + ROWS}[side]
         for r in range(REACH):
 
             def halo(t):
-                rows = slice(8 * t, 8 * t + 8)
-                from_e = pltpu.roll(diag_w[rows, :], -REACH * r % COLS, 1)
-                from_w = pltpu.roll(diag_e[rows, :], -REACH * (r + 1) % COLS, 1)
+                wrows = slice(8 * t, 8 * t + 8)
+                erows = slice(PACK + 40 + 8 * t, PACK + 48 + 8 * t)
+                from_e = pltpu.roll(corner[erows, :], -REACH * r % COLS, 1)
+                from_w = pltpu.roll(corner[wrows, :], -REACH * (r + 1) % COLS, 1)
                 return jnp.where(near_e, from_e, jnp.where(near_w, from_w, 0.0))
 
-            put_packed(base + r, lambda t: lat_x[r, 8 * t : 8 * t + 8, :], halo)
-
-    of = lambda ref: ref[SUMS : SUMS + 2, :]
-    sums = of(own.at[0]) + jnp.broadcast_to(of(east)[:, 0:1], (2, COLS))
-    if sides == ["swap"]:
-        lat_x, diag_e, _ = side_refs[0]
-        sums = sums + (of(lat_x.at[0]) + jnp.broadcast_to(of(diag_e)[:, 0:1], (2, COLS)))
-    window[...] = jnp.zeros((8, COLS), F32)
-    window[0:2, :] = sums
+            put_packed(base + r, lambda t: lat[PACK * r + 8 * t : PACK * r + 8 * t + 8, :], halo)
 
     for r in range(ROWS):
         outs[PAD + r, :, 0:COLS] = own_m[r]
@@ -552,7 +567,7 @@
     for_rows(scal, 10, section_1(Row(WIDE), cs, fs, masks, s0, s1))
 
 
-def second_section_kernel(scal, cs, fs, gate, s0, s1, masks, s2):
+def second_section_kernel(scal, cs, fs, s0, s1, masks, s2):
     zero_walls(s2)
     for_rows(scal, 9, section_2(Row(WIDE), cs, fs, masks, s0, s1, s2))
 
@@ -572,8 +587,8 @@
     sides, scal, cs, fs, sums, own, cown, own_h1, own_h2, s0, s2, masks, fluxes, outs_in, east, west, *rest
 ):
     n = len(sides)
-    side_refs = [rest[3 * i : 3 * i + 3] for i in range(n)]
-    (k1, k2, k3, q1, q2, q3, b2, b3), rest = rest[3 * n : 3 * n + 8], rest[3 * n + 8 :]
+    side_refs = [rest[2 * i : 2 * i + 2] for i in range(n)]
+    (k1, k2, k3, q1, q2, q3, b2, b3), rest = rest[2 * n : 2 * n + 8], rest[2 * n + 8 :]
     grads, s4, abuf, from_closure, s3, t2, outs, t1, cot, gz, bbuf, hold, left, acc = rest
     k = Row(WIDE)
     has_south = scal[2]
@@ -592,19 +607,20 @@
             cot[PAD + r, 8 * t : 8 * t + 8, :] = jnp.concatenate(
                 [cown[r, 8 * t : 8 * t + 8, :], side], axis=1
             )
-    for side, (lat_c, diag_e, diag_w) in zip(sides, side_refs):
+    for side, (lat, corner) in zip(sides, side_refs):
         cbase = {"swap": scal[5], "north": PAD - CREACH, "south": PAD + ROWS}[side]
         crow = {"swap": scal[6], "north": ROWS - CREACH, "south": 0}[side]
         for r in range(CREACH):
             turn = lax.rem(2 * COLS - 8 * (crow + r), COLS)
             turn_w = lax.rem(2 * COLS - 8 * (crow + r + 1), COLS)
             for t in range(5):
-                rows = slice(PACK + 8 * t, PACK + 8 * t + 8)
-                from_e = pltpu.roll(diag_w[rows, :], turn, 1)
-                from_w = pltpu.roll(diag_e[rows, :], turn_w, 1)
+                wrows = slice(PACK + 8 * t, PACK + 8 * t + 8)
+                erows = slice(2 * PACK + 40 + 8 * t, 2 * PACK + 48 + 8 * t)
+                from_e = pltpu.roll(corner[erows, :], turn, 1)
+                from_w = pltpu.roll(corner[wrows, :], turn_w, 1)
                 part = jnp.where(cnear_e, from_e, jnp.where(cnear_w, from_w, 0.0))
                 cot[cbase + r, 8 * t : 8 * t + 8, :] = jnp.concatenate(
-                    [lat_c[r, 8 * t : 8 * t + 8, :], part], axis=1
+                    [lat[LAT_X + FEATS * r + 8 * t : LAT_X + FEATS * r + 8 * t + 8, :], part], axis=1
                 )
 
 
@@ -765,16 +781,6 @@
             x = x + lax.ppermute(x, axis, [(i, i ^ stride) for i in range(count)])
             rounds.append(x)
             stride *= 2
-    return rounds
-
-
-def window_rounds(x, axis, count):
-    rounds = [x]
-    width = 2
-    while width < count:
-        x = x + lax.ppermute(x, axis, [(i, (i + width) % count) for i in range(count)])
-        rounds.append(x)
-        width *= 2
     return rounds
 
 
@@ -811,16 +817,17 @@
     packed = pl.pallas_call(
         lambda *refs: pack_kernel(sides, *refs),
         out_shape=[
-            sds(ROWS, PACK, COLS), sds(ROWS, FEATS, COLS), sds(2 * PACK + 40, COLS), sds(2 * PACK + 40, COLS),
+            sds(ROWS, PACK, COLS), sds(ROWS, FEATS, COLS), sds(STRIP, COLS), sds(STRIP, COLS), sds(8, COLS),
         ]
-        + [sds(REACH, PACK, COLS), sds(CREACH, FEATS, COLS), sds(PACK + 40, COLS), sds(PACK + 40, COLS)] * len(sides),
+        + [sds(LAT, COLS)] * len(sides),
         in_specs=[SMEM] + [hbm] * 4,
-        out_specs=[VMEM] * (4 + 4 * len(sides)),
+        out_specs=[VMEM] * (5 + len(sides)),
         scratch_shapes=[
             pltpu.VMEM((40 * ROWS, COLS), F32), pltpu.VMEM((10 * ROWS, COLS), jnp.int32),
             pltpu.VMEM((ROWS, COLS), F32), pltpu.VMEM((40 * ROWS, COLS), F32), pltpu.SemaphoreType.DMA((4,)),
         ],
-        compiler_params=params(8),
+        compiler_params=params(56),
+        cost_estimate=pl.CostEstimate(flops=10**9, bytes_accessed=3 * 10**6, transcendentals=0),
         name="pack_halos",
     )(
         scal,
@@ -829,7 +836,7 @@
         surface_flux,
         cotangent.reshape(40 * ROWS, COLS),
     )
-    own, cown, east_pay, west_pay = packed[:4]
+    own, cown, east_pay, west_pay, sums = packed[:5]
 
     def lat_pairs(side):
         if side == "swap":
@@ -838,28 +845,23 @@
             return [(i, i + 1) for i in range(lat_n - 1)]
         return [(i + 1, i) for i in range(lat_n - 1)]
 
-    def diagonal(side, step):
-        return [
-            (i * lat_n + a, ((i + step) % lon_n) * lat_n + b)
-            for i in range(lon_n)
-            for a, b in lat_pairs(side)
-        ]
-
     east_ring = [(i, (i + 1) % lon_n) for i in range(lon_n)]
     west_ring = [((i + 1) % lon_n, i) for i in range(lon_n)]
-    lat_x, lat_c, diags = [], [], []
-    for i, side in enumerate(sides):
-        pay_x, pay_c, diag_e, diag_w = packed[4 + 4 * i : 8 + 4 * i]
-        lat_x.append(lax.ppermute(pay_x, "lat", lat_pairs(side)))
-        diags.append(
-            [
-                lax.ppermute(diag_e, ("lon", "lat"), diagonal(side, 1)),
-                lax.ppermute(diag_w, ("lon", "lat"), diagonal(side, -1)),
-            ]
-        )
-        lat_c.append(lax.ppermute(pay_c, "lat", lat_pairs(side)))
+    lats = [lax.ppermute(pay, "lat", lat_pairs(side)) for side, pay in zip(sides, packed[5:])]
     from_west = lax.ppermute(east_pay, "lon", east_ring)
     from_east = lax.ppermute(west_pay, "lon", west_ring)
+    corner_pays = pl.pallas_call(
+        lambda *refs: corner_kernel(sides, *refs),
+        out_shape=[sds(2 * PACK + 80, COLS)] * len(sides),
+        in_specs=[SMEM, VMEM, VMEM],
+        out_specs=[VMEM] * len(sides),
+        compiler_params=params(8),
+        cost_estimate=pl.CostEstimate(flops=10**8, bytes_accessed=10**6, transcendentals=0),
+        name="pack_corners",
+    )(scal, from_west, from_east)
+    corners = [lax.ppermute(pay, "lat", lat_pairs(side)) for side, pay in zip(sides, corner_pays)]
+    received = [ref for pair in zip(lats, corners) for ref in pair]
+    means = pair_rounds(sums, (("lon", lon_n), ("lat", lat_n)))
 
     row = lambda b: b.reshape(1, -1)
     raw = (weight_in, weight_mid, weight_out, row(bias_in), row(bias_mid), row(bias_out))
@@ -900,24 +902,20 @@
             name=name,
         )(*geometry, *args)
 
-    s0, masks, fluxes, net, window = call(
+    s0, masks, fluxes, net = call(
         lambda *refs: assemble_kernel(sides, *refs), "assemble",
-        [state, marks, sds(EXT, 8, WIDE), plain, sds(8, COLS)], [],
-        [own, own_m, from_west, from_east]
-        + [ref for x, diag in zip(lat_x, diags) for ref in (x, *diag)] + [k1, k2, k3, b2, b3],
+        [state, marks, sds(EXT, 8, WIDE), plain], [],
+        [means[max(len(means) - 2, 0)], own, own_m, from_west, from_east] + received + [k1, k2, k3, b2, b3],
         2 * 10**9, 8,
     )
-    means = window_rounds(window, "lon", lon_n)
-    if sides != ["swap"]:
-        means += pair_rounds(means[-1], (("lat", lat_n),))
     s1 = call(first_section_kernel, "first_section", state, [], [s0, masks], 10**9, 8)
-    s2 = call(second_section_kernel, "second_section", state, [], [means[min(1, len(means) - 1)], s0, s1, masks], 10**9, 8)
+    s2 = call(second_section_kernel, "second_section", state, [], [s0, s1, masks], 10**9, 8)
     grads, top, abuf, from_closure, s3, t2, net_2 = call(
         lambda *refs: late_kernel(sides, *refs), "steps_and_adjoint",
         [sds(80, COLS), plain, plain, sds(ROWS, FEATS, COLS), state, state, plain],
         [vmem(state)] + [vmem(plain)] * 5 + [pltpu.VMEM((192, HID), F32)],
         [means[-1], own, cown, own_h1, own_h2, s0, s2, masks, fluxes, net, from_west, from_east]
-        + [ref for c, diag in zip(lat_c, diags) for ref in (c, *diag)] + [k1, k2, k3, q1, q2, q3, b2, b3],
+        + received + [k1, k2, k3, q1, q2, q3, b2, b3],
         4 * 10**9, 18,
     )
     rounds = pair_rounds(grads, (("lat", lat_n), ("lon", lon_n)))

time: 79.3 us -> 72.1 us (0.909)
  local copies, waits for them, and re-layouts: 7.87 us -> 1.8 us
  starting transfers between devices: 13.9 us -> 10.6 us
  Pallas kernels: 34.7 us -> 36.9 us
    ppermute x7 -> x2, waiting for transfers between devices: 11.7 us -> 0.01 us  [on_device(): lax.ppermute(pay, 'lat', lat_pairs(side))]
    ppermute x5 -> x10, waiting for transfers between devices: 9.78 us -> 20.9 us  [pair_rounds(): x = x + lax.ppermute(x, axis, [(i, i ^ stride) for i in range(count)])]
    unnamed x19 -> x21, local copies, waits for them, and re-layouts: 7.78 us -> 1.13 us
    ppermute x7 -> x2, starting transfers between devices: 8.57 us -> 3.6 us  [on_device(): lax.ppermute(pay, 'lat', lat_pairs(side))]
    ppermute x5 -> x10, starting transfers between devices: 0.86 us -> 2.52 us  [pair_rounds(): x = x + lax.ppermute(x, axis, [(i, i ^ stride) for i in range(count)])]
    pallas_call x1, Pallas kernels: 1.68 us -> 3.22 us  [on_device(): pl.pallas_call(lambda *refs: pack_kernel(sides, *refs), out_shape=[sds(RO...]
    pallas_call x0 -> x1, Pallas kernels: none -> 0.92 us  [on_device(): pl.pallas_call(lambda *refs: corner_kernel(sides, *refs), out_shape=[sds(...]
  transfers between devices with their start and end apart: 14 -> 14, of which waited for: 7 -> 9; matrix products, arithmetic and copies ran while one was open for 1% -> 1% of each run, Pallas kernels for 18% -> 15%
where the time goes in v4:
time: 72.1 us; the launch traced here: 71.9 us
  Pallas kernels  36.9 us (51%)
  waiting for transfers between devices  20.9 us (29%)
  starting transfers between devices  10.6 us (15%)
  local copies, waits for them, and re-layouts  1.8 us (2%)
  between operations  0.87 us (1%)
  other arithmetic  0.79 us (1%)
    pallas_call x8, Pallas kernels, call(): pl.pallas_call(kernel, out_shape=out_shape, in_specs=[SMEM] * 3 + [VMEM]...  30.8 us
    ppermute x10, waiting for transfers between devices, pair_rounds(): x = x + lax.ppermute(x, axis, [(i, i ^ stride) for i in range(count)])  20.9 us
    ppermute x1, starting transfers between devices, on_device(): from_east = lax.ppermute(west_pay, 'lon', west_ring)  4.44 us
    ppermute x2, starting transfers between devices, on_device(): lax.ppermute(pay, 'lat', lat_pairs(side))  3.6 us
    pallas_call x1, Pallas kernels, on_device(): pl.pallas_call(lambda *refs: pack_kernel(sides, *refs), out_shape=[sds(RO...  3.22 us
    ppermute x10, starting transfers between devices, pair_rounds(): x = x + lax.ppermute(x, axis, [(i, i ^ stride) for i in range(count)])  2.52 us
  transfers between devices with their start and end apart: 14, of which 9 were waited for; matrix products, arithmetic and copies ran while one was open for 1% of the time, Pallas kernels for 15%

profile of v4, /device:TPU:0, one launch (start us, length us, event | category | flops | bytes accessed | tf_op | source)
XLA Modules:
  0.0 71.9 jit_solution(15005232033606560321)
XLA Ops:
  1.4 3.2 %pack_halos.1 = (f32[16,56,128]{2,1,0:T(8,128)}, f32[16,40,128]{2,1,0:T(8,128)}, f32[152,128]{1,0:T(8,128)}, f32[152,128]{1,0:T(8,128)}, f32[8,128]{1,0:T(8,128)}, /*index=5*/f32[856,128]{1,0:T(8,128)}) custom-call(s32[7]{0:T(128)} %stack.39.refs_0_.scal, f32[640,128]{1,0:T(8,128)} %bitcast.24, s32[160,128]{1,0:T(8,128)} %bitcast.26, f32[16,128]{1,0:T(8,128)} %refs_3_.1, ...), custom_call_target="tpu_custom_call" | custom-call | flops 1000000000 | bytes 3000000 | tf_op jit(solution)/shard_map/pack_halos/pallas_call | solution.py:817
  4.6 3.0 %collective-permute-start.7 = (f32[856,128]{1,0:T(8,128)}, f32[856,128]{1,0:T(8,128)S(1)}, u32[]{:S(2)}, u32[]{:S(2)}) collective-permute-start(f32[856,128]{1,0:T(8,128)} %get-tuple-element.54), channel_id=1, source_target_pairs={{0,1},{1,0},{2,3},{3,2},{4,5},{5,4},{6,7},{7,6},{8,9},{9,8},{10,11... | collective-permute-start | bytes 1314824 | tf_op jit(solution)/shard_map/ppermute | solution.py:850
  7.6 4.4 %collective-permute-start.6 = (f32[152,128]{1,0:T(8,128)}, f32[152,128]{1,0:T(8,128)S(1)}, u32[]{:S(2)}, u32[]{:S(2)}) collective-permute-start(f32[152,128]{1,0:T(8,128)} %get-tuple-element.53), channel_id=1, source_target_pairs={{2,0},{4,2},{6,4},{8,6},{10,8},{12,10},{14,12},{16,14},{18,16},{20... | collective-permute-start | bytes 233480 | tf_op jit(solution)/shard_map/ppermute | solution.py:852
  12.1 1.4 %collective-permute-done = f32[8,128]{1,0:T(8,128)S(1)} collective-permute-done((f32[8,128]{1,0:T(8,128)}, f32[8,128]{1,0:T(8,128)S(1)}, u32[]{:S(2)}, u32[]{:S(2)}) %collective-permute-start) | collective-permute-done | bytes 4128 | tf_op jit(solution)/shard_map/ppermute | solution.py:781
  14.1 3.6 %collective-permute-done.1 = f32[8,128]{1,0:T(8,128)S(1)} collective-permute-done((f32[8,128]{1,0:T(8,128)S(1)}, f32[8,128]{1,0:T(8,128)S(1)}, u32[]{:S(2)}, u32[]{:S(2)}) %collective-permute-start.1) | collective-permute-done | bytes 4128 | tf_op jit(solution)/shard_map/ppermute | solution.py:781
  17.8 3.6 %collective-permute-done.2 = f32[8,128]{1,0:T(8,128)S(1)} collective-permute-done((f32[8,128]{1,0:T(8,128)S(1)}, f32[8,128]{1,0:T(8,128)S(1)}, u32[]{:S(2)}, u32[]{:S(2)}) %collective-permute-start.2) | collective-permute-done | bytes 4128 | tf_op jit(solution)/shard_map/ppermute | solution.py:781
  22.2 0.9 %pack_corners.1 = f32[192,128]{1,0:T(8,128)S(1)} custom-call(s32[7]{0:T(128)S(1)} %copy-done, f32[152,128]{1,0:T(8,128)S(1)} %collective-permute-done.5.refs_1_.refs_6_.refs_13_, f32[152,128]{1,0:T(8,128)S(1)} %collective-permute-done.6.refs_2_.refs_7_.refs_14_), custom_call_target="tpu_custom_call" | custom-call | flops 100000000 | bytes 1000000 | tf_op jit(solution)/shard_map/pack_corners/pallas_call | solution.py:853
  23.8 2.1 %collective-permute-done.3 = f32[8,128]{1,0:T(8,128)S(1)} collective-permute-done((f32[8,128]{1,0:T(8,128)S(1)}, f32[8,128]{1,0:T(8,128)S(1)}, u32[]{:S(2)}, u32[]{:S(2)}) %collective-permute-start.3) | collective-permute-done | bytes 4128 | tf_op jit(solution)/shard_map/ppermute | solution.py:781
  26.0 1.0 %copy-done.6 = f32[16,56,128]{2,1,0:T(8,128)S(1)} copy-done((f32[16,56,128]{2,1,0:T(8,128)S(1)}, f32[16,56,128]{2,1,0:T(8,128)}, u32[]{:S(2)}) %copy-start.6) | copy-done | bytes 458776
  27.0 1.2 %own_closure.1 = (f32[16,40,128]{2,1,0:T(8,128)S(1)}, f32[16,64,128]{2,1,0:T(8,128)S(1)}, f32[16,64,128]{2,1,0:T(8,128)S(1)}, bf16[64,144]{1,0:T(8,128)(2,1)S(1)...) custom-call(f32[16,56,128]{2,1,0:T(8,128)S(1)} %copy-done.6, ...), custom_call_target="tpu_custom_call" | custom-call | flops 1000000000 | bytes 2000000 | tf_op jit(solution)/shard_map/own_closure/pallas_call | solution.py:869
  28.2 1.2 %collective-permute-done.4 = f32[8,128]{1,0:T(8,128)S(1)} collective-permute-done((f32[8,128]{1,0:T(8,128)S(1)}, f32[8,128]{1,0:T(8,128)S(1)}, u32[]{:S(2)}, u32[]{:S(2)}) %collective-permute-start.4) | collective-permute-done | bytes 4128 | tf_op jit(solution)/shard_map/ppermute | solution.py:781
  29.5 2.1 %assemble.1 = (f32[48,72,256]{2,1,0:T(8,128)S(1)}, f32[48,16,256]{2,1,0:T(8,128)S(1)}, f32[48,8,256]{2,1,0:T(8,128)S(1)}, f32[48,40,256]{2,1,0:T(8,128)S(1)}) custom-call(s32[7]{0:T(128)S(1)} %copy-done, f32[48]{0:T(128)S(1)} %get-tuple-element.84.refs_1_.cs, f32[48]{0:T(128)S(1)} %get-tuple-element.85.refs_2_.fs, f32[8,128]{1,0:T(8,128)S(1)} %add.51.refs_3_, ...), custom_call_target="tpu_custom_call" | custom-call | flops 2000000000 | bytes 10000000 | tf_op jit(solution)/shard_map/assemble/pallas_call | solution.py:894
  31.6 2.2 %first_section.1.s1.state = f32[48,72,256]{2,1,0:T(8,128)S(1)} custom-call(s32[7]{0:T(128)S(1)} %copy-done, f32[48]{0:T(128)S(1)} %get-tuple-element.84.refs_1_.cs, f32[48]{0:T(128)S(1)} %get-tuple-element.85.refs_2_.fs, f32[48,72,256]{2,1,0:T(8,128)S(1)} %get-tuple-element.60.s0.refs_8_.state, f32[48,16,256]{2,1,0:T(8,128)S(1)} %get-tuple-element.61.masks.refs_10_), custom_call_target="tpu_custom_call" | custom-call | flops 1000000000 | bytes 10000000 | tf_op jit(solution)/shard_map/first_section/pallas_call | solution.py:894
  33.8 2.2 %second_section.1.refs_9_.state = f32[48,72,256]{2,1,0:T(8,128)S(1)} custom-call(s32[7]{0:T(128)S(1)} %copy-done, f32[48]{0:T(128)S(1)} %get-tuple-element.84.refs_1_.cs, f32[48]{0:T(128)S(1)} %get-tuple-element.85.refs_2_.fs, f32[48,72,256]{2,1,0:T(8,128)S(1)} %get-tuple-element.60.s0.refs_8_.state, f32[48,72,256]{2,1,0:T(8,128)S(1)} %first_section.1.s1.state, ...), custom_call_target="tpu_custom_call" | custom-call | flops 1000000000 | bytes 10000000 | tf_op jit(solution)/shard_map/second_section/pallas_call | solution.py:894
  36.0 15.6 %steps_and_adjoint.1 = (f32[80,128]{1,0:T(8,128)S(1)}, f32[48,40,256]{2,1,0:T(8,128)S(1)}, f32[48,40,256]{2,1,0:T(8,128)S(1)}, f32[16,40,128]{2,1,0:T(8,128)S(1)...) custom-call(s32[7]{0:T(128)S(1)} %copy-done, ...), custom_call_target="tpu_custom_call" | custom-call | flops 4000000000 | bytes 10000000 | tf_op jit(solution)/shard_map/steps_and_adjoint/pallas_call | solution.py:894
  52.4 3.3 %collective-permute-done.9 = f32[80,128]{1,0:T(8,128)S(1)} collective-permute-done((f32[80,128]{1,0:T(8,128)S(1)}, f32[80,128]{1,0:T(8,128)S(1)}, u32[]{:S(2)}, u32[]{:S(2)}) %collective-permute-start.9) | collective-permute-done | bytes 40992 | tf_op jit(solution)/shard_map/ppermute | solution.py:781
  55.6 2.1 %adjoint_third_section.1 = (f32[48,40,256]{2,1,0:T(8,128)S(1)}, f32[48,40,256]{2,1,0:T(8,128)S(1)}) custom-call(s32[7]{0:T(128)S(1)} %copy-done, f32[48]{0:T(128)S(1)} %get-tuple-element.84.refs_1_.cs, f32[48]{0:T(128)S(1)} %get-tuple-element.85.refs_2_.fs, f32[48,72,256]{2,1,0:T(8,128)S(1)} %second_section.1.refs_9_.state, ...), custom_call_target="tpu_custom_call" | custom-call | flops 1000000000 | bytes 10000000 | tf_op jit(solution)/shard_map/adjoint_third_section/pallas_call | solution.py:894
  57.9 2.2 %adjoint_second_section.1 = (f32[48,40,256]{2,1,0:T(8,128)S(1)}, f32[48,40,256]{2,1,0:T(8,128)S(1)}) custom-call(s32[7]{0:T(128)S(1)} %copy-done, f32[48]{0:T(128)S(1)} %get-tuple-element.84.refs_1_.cs, f32[48]{0:T(128)S(1)} %get-tuple-element.85.refs_2_.fs, f32[80,128]{1,0:T(8,128)S(1)} %add.53.gate, f32[48,72,256]{2,1,0:T(8,128)S(1)} %first_section.1.s1.state, ...), custom_call_target="tpu_custom_call" | custom-call | flops 1000000000 | bytes 10000000 | tf_op jit(solution)/shard_map/adjoint_second_section/pallas_call | solution.py:894
  60.0 1.8 %collective-permute-done.11 = f32[80,128]{1,0:T(8,128)S(1)} collective-permute-done((f32[80,128]{1,0:T(8,128)S(1)}, f32[80,128]{1,0:T(8,128)S(1)}, u32[]{:S(2)}, u32[]{:S(2)}) %collective-permute-start.11) | collective-permute-done | bytes 40992 | tf_op jit(solution)/shard_map/ppermute | solution.py:781
  61.9 2.4 %adjoint_first_section.1 = f32[640,128]{1,0:T(8,128)} custom-call(s32[7]{0:T(128)S(1)} %copy-done, f32[48]{0:T(128)S(1)} %get-tuple-element.84.refs_1_.cs, f32[48]{0:T(128)S(1)} %get-tuple-element.85.refs_2_.fs, f32[80,128]{1,0:T(8,128)S(1)} %add.54.gate, f32[48,72,256]{2,1,0:T(8,128)S(1)} %get-tuple-element.60.s0.refs_8_.state, ...), custom_call_target="tpu_custom_call" | custom-call | flops 1000000000 | bytes 10000000 | tf_op jit(solution)/shard_map/adjoint_first_section/pallas_call | solution.py:894
  64.3 1.6 %collective-permute-done.12 = f32[80,128]{1,0:T(8,128)S(1)} collective-permute-done((f32[80,128]{1,0:T(8,128)S(1)}, f32[80,128]{1,0:T(8,128)S(1)}, u32[]{:S(2)}, u32[]{:S(2)}) %collective-permute-start.12) | collective-permute-done | bytes 40992 | tf_op jit(solution)/shard_map/ppermute | solution.py:781
  65.9 0.8 %collective-permute-start.13 = (f32[80,128]{1,0:T(8,128)S(1)}, f32[80,128]{1,0:T(8,128)S(1)}, u32[]{:S(2)}, u32[]{:S(2)}) collective-permute-start(f32[80,128]{1,0:T(8,128)S(1)} %add.56), channel_id=1, source_target_pairs={{0,16},{2,18},{4,20},{6,22},{8,24},{10,26},{12,28},{14,30},{16,0},... | collective-permute-start | bytes 122888 | tf_op jit(solution)/shard_map/ppermute | solution.py:781
  66.7 2.1 %last_section.1 = f32[640,128]{1,0:T(8,128)} custom-call(s32[7]{0:T(128)S(1)} %copy-done, f32[48]{0:T(128)S(1)} %get-tuple-element.84.refs_1_.cs, f32[48]{0:T(128)S(1)} %get-tuple-element.85.refs_2_.fs, f32[80,128]{1,0:T(8,128)S(1)} %add.55.gate, f32[8,128]{1,0:T(8,128)S(1)} %add.52.refs_3_.sums, f32[48,72,256]{2,1,0:T(8,128)S(1)} %get-tuple-element.68.s3, ...), custom_call_target="tpu_custom_call" | custom-call | flops 1000000000 | bytes 10000000 | tf_op jit(solution)/shard_map/last_section/pallas_call | solution.py:894
  68.8 2.3 %collective-permute-done.13 = f32[80,128]{1,0:T(8,128)S(1)} collective-permute-done((f32[80,128]{1,0:T(8,128)S(1)}, f32[80,128]{1,0:T(8,128)S(1)}, u32[]{:S(2)}, u32[]{:S(2)}) %collective-permute-start.13) | collective-permute-done | bytes 40992 | tf_op jit(solution)/shard_map/ppermute | solution.py:781
  (49 shorter events, 4.6 us)
Async XLA Ops:
  1.3 20.8 %copy-start = (s32[7]{0:T(128)S(1)}, s32[7]{0:T(128)}, u32[]{:S(2)}) copy-start(s32[7]{0:T(128)} %stack.39.refs_0_.scal) | copy-start | bytes 88
  1.3 22.4 %copy-start.9 = (f32[64,40]{0,1:T(8,128)S(1)}, f32[64,40]{0,1:T(8,128)}, u32[]{:S(2)}) copy-start(f32[64,40]{0,1:T(8,128)} %param.17) | copy-start | bytes 30724
  1.3 24.6 %copy-start.1 = (f32[64,64]{1,0:T(8,128)S(1)}, f32[64,64]{1,0:T(8,128)}, u32[]{:S(2)}) copy-start(f32[64,64]{1,0:T(8,128)} %refs_1_.1) | copy-start | bytes 49156
  1.3 24.6 %copy-start.2 = (f32[40,64]{1,0:T(8,128)S(1)}, f32[40,64]{1,0:T(8,128)}, u32[]{:S(2)}) copy-start(f32[40,64]{1,0:T(8,128)} %refs_0_.1) | copy-start | bytes 30724
  1.3 24.6 %copy-start.3 = (f32[64]{0:T(128)S(1)}, f32[64]{0:T(128)}, u32[]{:S(2)}) copy-start(f32[64]{0:T(128)} %param.14) | copy-start | bytes 772
  1.3 24.6 %copy-start.4 = (f32[64]{0:T(128)S(1)}, f32[64]{0:T(128)}, u32[]{:S(2)}) copy-start(f32[64]{0:T(128)} %param.16) | copy-start | bytes 772
  1.4 24.6 %copy-start.5 = (f32[40]{0:T(128)S(1)}, f32[40]{0:T(128)}, u32[]{:S(2)}) copy-start(f32[40]{0:T(128)} %param.18) | copy-start | bytes 484
  4.6 24.9 %collective-permute-start.7 = (f32[856,128]{1,0:T(8,128)}, f32[856,128]{1,0:T(8,128)S(1)}, u32[]{:S(2)}, u32[]{:S(2)}) collective-permute-start(f32[856,128]{1,0:T(8,128)} %get-tuple-element.54), channel_id=1, source_target_pairs={{0,1},{1,0},{2,3},{3,2},{4,5},{5,4},{6,7},{7,6},{8,9},{9,8},{10,11... | collective-permute-start | bytes 1314824 | tf_op jit(solution)/shard_map/ppermute | solution.py:850
  7.6 14.5 %collective-permute-start.5 = (f32[152,128]{1,0:T(8,128)}, f32[152,128]{1,0:T(8,128)S(1)}, u32[]{:S(2)}, u32[]{:S(2)}) collective-permute-start(f32[152,128]{1,0:T(8,128)} %get-tuple-element.52), channel_id=1, source_target_pairs={{0,2},{2,4},{4,6},{6,8},{8,10},{10,12},{12,14},{14,16},{16,18},{18... | collective-permute-start | bytes 233480 | tf_op jit(solution)/shard_map/ppermute | solution.py:851
  7.6 14.5 %collective-permute-start.6 = (f32[152,128]{1,0:T(8,128)}, f32[152,128]{1,0:T(8,128)S(1)}, u32[]{:S(2)}, u32[]{:S(2)}) collective-permute-start(f32[152,128]{1,0:T(8,128)} %get-tuple-element.53), channel_id=1, source_target_pairs={{2,0},{4,2},{6,4},{8,6},{10,8},{12,10},{14,12},{16,14},{18,16},{20... | collective-permute-start | bytes 233480 | tf_op jit(solution)/shard_map/ppermute | solution.py:852
  12.1 1.4 %collective-permute-start = (f32[8,128]{1,0:T(8,128)}, f32[8,128]{1,0:T(8,128)S(1)}, u32[]{:S(2)}, u32[]{:S(2)}) collective-permute-start(f32[8,128]{1,0:T(8,128)} %get-tuple-element.46), channel_id=1, source_target_pairs={{0,2},{2,0},{4,6},{6,4},{8,10},{10,8},{12,14},{14,12},{16,18},{18,... | collective-permute-start | bytes 12296 | tf_op jit(solution)/shard_map/ppermute | solution.py:781
  14.1 3.6 %collective-permute-start.1 = (f32[8,128]{1,0:T(8,128)S(1)}, f32[8,128]{1,0:T(8,128)S(1)}, u32[]{:S(2)}, u32[]{:S(2)}) collective-permute-start(f32[8,128]{1,0:T(8,128)S(1)} %add.48), channel_id=1, source_target_pairs={{0,4},{2,6},{4,0},{6,2},{8,12},{10,14},{12,8},{14,10},{16,20},{18,... | collective-permute-start | bytes 12296 | tf_op jit(solution)/shard_map/ppermute | solution.py:781
  17.8 3.6 %collective-permute-start.2 = (f32[8,128]{1,0:T(8,128)S(1)}, f32[8,128]{1,0:T(8,128)S(1)}, u32[]{:S(2)}, u32[]{:S(2)}) collective-permute-start(f32[8,128]{1,0:T(8,128)S(1)} %add.49), channel_id=1, source_target_pairs={{0,8},{2,10},{4,12},{6,14},{8,0},{10,2},{12,4},{14,6},{16,24},{18,... | collective-permute-start | bytes 12296 | tf_op jit(solution)/shard_map/ppermute | solution.py:781
  21.4 4.5 %collective-permute-start.3 = (f32[8,128]{1,0:T(8,128)S(1)}, f32[8,128]{1,0:T(8,128)S(1)}, u32[]{:S(2)}, u32[]{:S(2)}) collective-permute-start(f32[8,128]{1,0:T(8,128)S(1)} %add.50), channel_id=1, source_target_pairs={{0,16},{2,18},{4,20},{6,22},{8,24},{10,26},{12,28},{14,30},{16,0},... | collective-permute-start | bytes 12296 | tf_op jit(solution)/shard_map/ppermute | solution.py:781
  23.1 6.4 %collective-permute-start.8 = (f32[192,128]{1,0:T(8,128)S(1)}, f32[192,128]{1,0:T(8,128)S(1)}, u32[]{:S(2)}, u32[]{:S(2)}) collective-permute-start(f32[192,128]{1,0:T(8,128)S(1)} %pack_corners.1), channel_id=1, source_target_pairs={{0,1},{1,0},{2,3},{3,2},{4,5},{5,4},{6,7},{7,6},{8,9},{9,8},{10,11... | collective-permute-start | bytes 294920 | tf_op jit(solution)/shard_map/ppermute | solution.py:862
  25.9 3.6 %collective-permute-start.4 = (f32[8,128]{1,0:T(8,128)S(1)}, f32[8,128]{1,0:T(8,128)S(1)}, u32[]{:S(2)}, u32[]{:S(2)}) collective-permute-start(f32[8,128]{1,0:T(8,128)S(1)} %add.51.refs_3_), channel_id=1, source_target_pairs={{0,1},{1,0},{2,3},{3,2},{4,5},{5,4},{6,7},{7,6},{8,9},{9,8},{10,11... | collective-permute-start | bytes 12296 | tf_op jit(solution)/shard_map/ppermute | solution.py:781
  26.0 1.0 %copy-start.6 = (f32[16,56,128]{2,1,0:T(8,128)S(1)}, f32[16,56,128]{2,1,0:T(8,128)}, u32[]{:S(2)}) copy-start(f32[16,56,128]{2,1,0:T(8,128)} %get-tuple-element.47.own.refs_4_) | copy-start | bytes 1376260
  33.8 2.2 %copy-start.7 = (f32[16,56,128]{2,1,0:T(8,128)S(1)}, f32[16,56,128]{2,1,0:T(8,128)}, u32[]{:S(2)}) copy-start(f32[16,56,128]{2,1,0:T(8,128)} %get-tuple-element.47.own.refs_4_) | copy-start | bytes 1376260
  33.8 2.2 %copy-start.8 = (f32[16,40,128]{2,1,0:T(8,128)S(1)}, f32[16,40,128]{2,1,0:T(8,128)}, u32[]{:S(2)}) copy-start(f32[16,40,128]{2,1,0:T(8,128)} %get-tuple-element.48.refs_5_) | copy-start | bytes 983044
  51.6 4.0 %collective-permute-start.9 = (f32[80,128]{1,0:T(8,128)S(1)}, f32[80,128]{1,0:T(8,128)S(1)}, u32[]{:S(2)}, u32[]{:S(2)}) collective-permute-start(f32[80,128]{1,0:T(8,128)S(1)} %get-tuple-element.67), channel_id=1, source_target_pairs={{0,1},{1,0},{2,3},{3,2},{4,5},{5,4},{6,7},{7,6},{8,9},{9,8},{10,11... | collective-permute-start | bytes 122888 | tf_op jit(solution)/shard_map/ppermute | solution.py:781
  55.6 2.1 %collective-permute-start.10 = (f32[80,128]{1,0:T(8,128)S(1)}, f32[80,128]{1,0:T(8,128)S(1)}, u32[]{:S(2)}, u32[]{:S(2)}) collective-permute-start(f32[80,128]{1,0:T(8,128)S(1)} %add.53.gate), channel_id=1, source_target_pairs={{0,2},{2,0},{4,6},{6,4},{8,10},{10,8},{12,14},{14,12},{16,18},{18,... | collective-permute-start | bytes 122888 | tf_op jit(solution)/shard_map/ppermute | solution.py:781
  57.8 4.1 %collective-permute-start.11 = (f32[80,128]{1,0:T(8,128)S(1)}, f32[80,128]{1,0:T(8,128)S(1)}, u32[]{:S(2)}, u32[]{:S(2)}) collective-permute-start(f32[80,128]{1,0:T(8,128)S(1)} %add.54.gate), channel_id=1, source_target_pairs={{0,4},{2,6},{4,0},{6,2},{8,12},{10,14},{12,8},{14,10},{16,20},{18,... | collective-permute-start | bytes 122888 | tf_op jit(solution)/shard_map/ppermute | solution.py:781
  61.9 4.0 %collective-permute-start.12 = (f32[80,128]{1,0:T(8,128)S(1)}, f32[80,128]{1,0:T(8,128)S(1)}, u32[]{:S(2)}, u32[]{:S(2)}) collective-permute-start(f32[80,128]{1,0:T(8,128)S(1)} %add.55.gate), channel_id=1, source_target_pairs={{0,8},{2,10},{4,12},{6,14},{8,0},{10,2},{12,4},{14,6},{16,24},{18,... | collective-permute-start | bytes 122888 | tf_op jit(solution)/shard_map/ppermute | solution.py:781
  65.9 5.3 %collective-permute-start.13 = (f32[80,128]{1,0:T(8,128)S(1)}, f32[80,128]{1,0:T(8,128)S(1)}, u32[]{:S(2)}, u32[]{:S(2)}) collective-permute-start(f32[80,128]{1,0:T(8,128)S(1)} %add.56), channel_id=1, source_target_pairs={{0,16},{2,18},{4,20},{6,22},{8,24},{10,26},{12,28},{14,30},{16,0},... | collective-permute-start | bytes 122888 | tf_op jit(solution)/shard_map/ppermute | solution.py:781

commit v5 on v4

--- a/solution.py
+++ b/solution.py
@@ -61,7 +61,7 @@
     return packed
 
 
-def pack_kernel(sides, scal, x_hbm, mask_hbm, flux_hbm, cot_hbm, *outs):
+def pack_kernel(sides, x_hbm, mask_hbm, flux_hbm, cot_hbm, *outs):
     x, mask, flux, cot, sems = outs[-5:]
     own, cown, east, west, sums = outs[:5]
     per_side = outs[5 : 5 + len(sides)]
@@ -102,9 +102,10 @@
         at = 2 * PACK + 8 * t
         east[at : at + 8, :] = slot_pack(rows, lambda s: 8 * (s + 1), 8)
         west[at : at + 8, :] = slot_pack(rows, lambda s: 8 * s, 8)
+    southern = (lax.axis_index("lat") == 0).astype(jnp.int32)
     for side, lat in zip(sides, per_side):
-        start = {"swap": scal[0], "north": ROWS - REACH, "south": 0}[side]
-        cstart = {"swap": scal[1], "north": ROWS - CREACH, "south": 0}[side]
+        start = {"swap": southern * (ROWS - REACH), "north": ROWS - REACH, "south": 0}[side]
+        cstart = {"swap": southern * (ROWS - CREACH), "north": ROWS - CREACH, "south": 0}[side]
         for n in range(REACH):
             lat[PACK * n : PACK * (n + 1), :] = own[start + n]
         for n in range(CREACH):
@@ -261,35 +262,32 @@
         self.k4 = jnp.where(group < 2, DIFFUSIVITY, VISCOSITY).astype(F32)
 
 
-def derived(k, temp, salt, mixed):
-    zero = jnp.zeros_like(temp)
-    press = 0.4 * salt - 0.1 * temp
-    for by in (1, 2, 4):
-        press = press + jnp.where(k.sub >= by, pltpu.roll(press, by, 0), zero)
-    deep = jnp.where(k.is_t, 0.4 * pltpu.roll(mixed, 7, 0) - 0.1 * mixed, zero)
-    deep = deep + jnp.where(k.low, pltpu.roll(deep, 4, 0), zero)
-    deep = deep + pltpu.roll(deep, 1, 0)
-    deep = deep + pltpu.roll(deep, 2, 0) + press[7:8, :]
-    u4, v4 = deep_velocity(k, mixed)
-    return press, deep, u4, v4
-
-
-def deep_velocity(k, mixed):
-    zero = jnp.zeros_like(mixed)
-    u4 = jnp.where(k.is_u, mixed, zero)
-    u4 = u4 + pltpu.roll(u4, 1, 0)
-    u4 = u4 + pltpu.roll(u4, 6, 0)
-    v4 = jnp.where(k.is_v, mixed, zero)
-    v4 = v4 + pltpu.roll(v4, 7, 0)
-    v4 = v4 + pltpu.roll(v4, 6, 0)
-    return u4, v4
-
-
 def put_state(k, ref, row, tiles):
     for t in range(5):
         ref[row, 8 * t : 8 * t + 8, :] = tiles[t]
-    for t, values in enumerate(derived(k, tiles[0], tiles[1], tiles[4])):
-        ref[row, 40 + 8 * t : 48 + 8 * t, :] = values
+    press = 0.4 * tiles[1] - 0.1 * tiles[0]
+    for by in (1, 2, 4):
+        press = press + jnp.where(k.sub >= by, pltpu.roll(press, by, 0), 0.0)
+    ref[row, 40:48, :] = press
+    deep_8 = ref[row, 47:48, :] + (0.4 * ref[row, 33:34, :] - 0.1 * ref[row, 32:33, :])
+    ref[row, 48:49, :] = deep_8
+    ref[row, 49:50, :] = deep_8 + (0.4 * ref[row, 37:38, :] - 0.1 * ref[row, 36:37, :])
+
+
+def deep_pair(k, ref, row, upper, lower):
+    return jnp.where(k.low, ref[row, lower : lower + 1, :], ref[row, upper : upper + 1, :])
+
+
+def deep_u(k, ref, row):
+    return deep_pair(k, ref, row, 34, 38)
+
+
+def deep_v(k, ref, row):
+    return deep_pair(k, ref, row, 35, 39)
+
+
+def deep_p(k, ref, row):
+    return deep_pair(k, ref, row, 48, 49)
 
 
 def east_of(q):
@@ -298,54 +296,63 @@
 
 def west_of(q):
     return pltpu.roll(q, 1, 1)
+
+
+def gain_of(k, t):
+    return k.k4 if t == 4 else (DIFFUSIVITY if t < 2 else VISCOSITY)
 
 
 def tendency_row(k, ref, row, c, f):
     half = 0.5 * c
     c2 = c * c
     u, v = tile(ref, row, 2), tile(ref, row, 3)
-    u4, v4 = tile(ref, row, 7), tile(ref, row, 8)
-    uh, vh = u * half, v * 0.5
-    u4h, v4h = u4 * half, v4 * 0.5
+    u4, v4 = deep_u(k, ref, row), deep_v(k, ref, row)
     change = []
     for t in range(5):
+        gain = gain_of(k, t)
+        if t in (0, 2, 4):
+            au, av = (half * u4, 0.5 * v4) if t == 4 else (half * u, 0.5 * v)
+            along = gain * c2
+            at_e, at_w, at_n, at_s = along - au, along + au, gain - av, gain + av
         q = tile(ref, row, t)
-        e, w = east_of(q), west_of(q)
-        n, s = tile(ref, row + 1, t), tile(ref, row - 1, t)
-        lap = c2 * (e + w) + (n + s) - (2.0 * c2 + 2.0) * q
-        gain = k.k4 if t == 4 else (DIFFUSIVITY if t < 2 else VISCOSITY)
-        au, av = (u4h, v4h) if t == 4 else (uh, vh)
-        change.append(gain * lap - (au * (e - w) + av * (n - s)))
+        east, west = at_e * east_of(q), at_w * west_of(q)
+        north, south = at_n * tile(ref, row + 1, t), at_s * tile(ref, row - 1, t)
+        change.append((east + west) + (north + south) - (gain * (2.0 * c2 + 2.0)) * q)
     p = tile(ref, row, 5)
     change[2] = change[2] + (f * v - half * (east_of(p) - west_of(p)))
     change[3] = change[3] - (f * u + 0.5 * (tile(ref, row + 1, 5) - tile(ref, row - 1, 5)))
-    p4 = tile(ref, row, 6)
-    zero = jnp.zeros_like(p4)
+    p4 = deep_p(k, ref, row)
     fx = f * v4 - half * (east_of(p4) - west_of(p4))
-    fy = f * u4 + 0.5 * (tile(ref, row + 1, 6) - tile(ref, row - 1, 6))
-    change[4] = change[4] + jnp.where(k.is_u, fx, jnp.where(k.is_v, -fy, zero))
+    fy = f * u4 + 0.5 * (deep_p(k, ref, row + 1) - deep_p(k, ref, row - 1))
+    change[4] = change[4] + jnp.where(k.is_u, fx, jnp.where(k.is_v, -fy, 0.0))
     return change
 
 
 def adjoint_row(k, ref, aref, row, c, f):
     half = 0.5 * c
     c2 = c * c
-    u4 = tile(ref, row, 7)
+    u4 = deep_u(k, ref, row)
     qe = [east_of(tile(ref, row, t)) for t in range(5)]
     qw = [west_of(tile(ref, row, t)) for t in range(5)]
-    u4e, u4w = east_of(u4), west_of(u4)
     out = []
     to_u = to_v = None
     for t in range(5):
         a = tile(aref, row, t)
         ae, aw = east_of(a), west_of(a)
         an, as_ = tile(aref, row + 1, t), tile(aref, row - 1, t)
-        gain = k.k4 if t == 4 else (DIFFUSIVITY if t < 2 else VISCOSITY)
-        ue, uw = (u4e, u4w) if t == 4 else (qe[2], qw[2])
-        which = 8 if t == 4 else 3
-        vn, vs = tile(ref, row + 1, which), tile(ref, row - 1, which)
-        lap = c2 * (ae + aw) + (an + as_) - (2.0 * c2 + 2.0) * a
-        out.append(gain * lap + half * (ue * ae - uw * aw) + 0.5 * (vn * an - vs * as_))
+        gain = gain_of(k, t)
+        if t == 0:
+            ue, uw = half * qe[2], half * qw[2]
+            vn, vs = 0.5 * tile(ref, row + 1, 3), 0.5 * tile(ref, row - 1, 3)
+        if t == 4:
+            ue, uw = half * east_of(u4), half * west_of(u4)
+            vn, vs = 0.5 * deep_v(k, ref, row + 1), 0.5 * deep_v(k, ref, row - 1)
+        if t in (0, 2, 4):
+            along = gain * c2
+            at_e, at_w, at_n, at_s = along + ue, along - uw, gain + vn, gain - vs
+        out.append(
+            (at_e * ae + at_w * aw) + (at_n * an + at_s * as_) - (gain * (2.0 * c2 + 2.0)) * a
+        )
         px = a * (qe[t] - qw[t])
         py = a * (tile(ref, row + 1, t) - tile(ref, row - 1, t))
         if t < 4:
@@ -361,18 +368,17 @@
             px4, py4 = px * half, py * 0.5
     out[2] = out[2] - half * to_u - f * a3
     out[3] = out[3] - 0.5 * to_v + f * a2
-    zero = jnp.zeros_like(a4)
     sx = px4 + pltpu.roll(px4, 7, 0)
     sx = sx + pltpu.roll(sx, 2, 0)
     sy = py4 + pltpu.roll(py4, 1, 0)
     sy = sy + pltpu.roll(sy, 2, 0)
     at_u = -sx - f * pltpu.roll(a4, 7, 0)
     at_v = f * pltpu.roll(a4, 1, 0) - sy
-    deep = jnp.where(k.is_t, pltpu.roll(deep_bx, 6, 0) + pltpu.roll(deep_by, 5, 0), zero)
-    deep = deep + jnp.where(k.low, zero, pltpu.roll(deep, 4, 0))
+    deep = jnp.where(k.is_t, pltpu.roll(deep_bx, 6, 0) + pltpu.roll(deep_by, 5, 0), 0.0)
+    deep = deep + jnp.where(k.low, 0.0, pltpu.roll(deep, 4, 0))
     press = bx + by
     for shift in (1, 2, 4):
-        press = press + jnp.where(k.sub < 8 - shift, pltpu.roll(press, 8 - shift, 0), zero)
+        press = press + jnp.where(k.sub < 8 - shift, pltpu.roll(press, 8 - shift, 0), 0.0)
     press = press + deep[0:1, :]
     out[0] = out[0] - 0.1 * press
     out[1] = out[1] + 0.4 * press
@@ -493,7 +499,7 @@
         ref[row] = jnp.zeros(ref.shape[1:], F32)
 
 
-def assemble_kernel(sides, scal, cs, fs, gate, own, own_m, east, west, *rest):
+def assemble_kernel(sides, scal, cs, fs, own, own_m, east, west, *rest):
     n = len(sides)
     side_refs = [rest[2 * i : 2 * i + 2] for i in range(n)]
     (k1, k2, k3, b2, b3), rest = rest[2 * n : 2 * n + 5], rest[2 * n + 5 :]
@@ -572,7 +578,7 @@
     for_rows(scal, 9, section_2(Row(WIDE), cs, fs, masks, s0, s1, s2))
 
 
-def last_section_kernel(scal, cs, fs, gate, sums, s3, t2, masks, fluxes, outs, final):
+def last_section_kernel(scal, cs, fs, sums, s3, t2, masks, fluxes, outs, final):
     k = Row(WIDE)
     mean = sums[0:1, 0:1] / sums[1:2, 0:1]
 
@@ -738,12 +744,12 @@
     adjoint_third(Row(WIDE), scal, cs, fs, 2, state, masks, abuf, top, hold, bbuf)
 
 
-def back_second_kernel(scal, cs, fs, gate, state, masks, bbuf, top, hold, left, abuf):
+def back_second_kernel(scal, cs, fs, state, masks, bbuf, top, hold, left, abuf):
     zero_walls(abuf)
     adjoint_second(Row(WIDE), scal, cs, fs, 1, state, masks, bbuf, top, hold, left, abuf)
 
 
-def back_first_kernel(scal, cs, fs, gate, state, masks, abuf, left, from_closure, grad):
+def back_first_kernel(scal, cs, fs, state, masks, abuf, left, from_closure, grad):
     def store(r, tiles):
         done = []
         for t in range(5):
@@ -770,18 +776,25 @@
         bout[:, 10 * t + 9 : 10 * t + 10] = packed[73:74, 36 + t : 37 + t] * scale
 
 
-def pair_rounds(x, axes):
-    rounds = []
+def pair_rounds(x, axes, beside=()):
+    results = []
+    beside = list(beside)
+
+    def wait_for(x):
+        if beside:
+            results.append(beside.pop(0)(results))
+            x, results[-1] = lax.optimization_barrier((x, results[-1]))
+        return x
+
     for axis, count in axes:
         if count & (count - 1):
-            rounds.append(x := lax.psum(x, axis))
+            x = wait_for(lax.psum(x, axis))
             continue
-        stride = 1
-        while stride < count:
-            x = x + lax.ppermute(x, axis, [(i, i ^ stride) for i in range(count)])
-            rounds.append(x)
-            stride *= 2
-    return rounds
+        for bit in range(count.bit_length() - 1):
+            x = x + wait_for(lax.ppermute(x, axis, [(i, i ^ (1 << bit)) for i in range(count)]))
+    while beside:
+        results.append(beside.pop(0)(results))
+    return x, results
 
 
 def latitude_terms(row_index, row_count):
@@ -820,7 +833,7 @@
             sds(ROWS, PACK, COLS), sds(ROWS, FEATS, COLS), sds(STRIP, COLS), sds(STRIP, COLS), sds(8, COLS),
         ]
         + [sds(LAT, COLS)] * len(sides),
-        in_specs=[SMEM] + [hbm] * 4,
+        in_specs=[hbm] * 4,
         out_specs=[VMEM] * (5 + len(sides)),
         scratch_shapes=[
             pltpu.VMEM((40 * ROWS, COLS), F32), pltpu.VMEM((10 * ROWS, COLS), jnp.int32),
@@ -830,7 +843,6 @@
         cost_estimate=pl.CostEstimate(flops=10**9, bytes_accessed=3 * 10**6, transcendentals=0),
         name="pack_halos",
     )(
-        scal,
         initial_state.reshape(40 * ROWS, COLS),
         land_mask.reshape(10 * ROWS, COLS),
         surface_flux,
@@ -850,23 +862,10 @@
     lats = [lax.ppermute(pay, "lat", lat_pairs(side)) for side, pay in zip(sides, packed[5:])]
     from_west = lax.ppermute(east_pay, "lon", east_ring)
     from_east = lax.ppermute(west_pay, "lon", west_ring)
-    corner_pays = pl.pallas_call(
-        lambda *refs: corner_kernel(sides, *refs),
-        out_shape=[sds(2 * PACK + 80, COLS)] * len(sides),
-        in_specs=[SMEM, VMEM, VMEM],
-        out_specs=[VMEM] * len(sides),
-        compiler_params=params(8),
-        cost_estimate=pl.CostEstimate(flops=10**8, bytes_accessed=10**6, transcendentals=0),
-        name="pack_corners",
-    )(scal, from_west, from_east)
-    corners = [lax.ppermute(pay, "lat", lat_pairs(side)) for side, pay in zip(sides, corner_pays)]
-    received = [ref for pair in zip(lats, corners) for ref in pair]
-    means = pair_rounds(sums, (("lon", lon_n), ("lat", lat_n)))
-
     row = lambda b: b.reshape(1, -1)
     raw = (weight_in, weight_mid, weight_out, row(bias_in), row(bias_mid), row(bias_out))
     half = lambda *shape: jax.ShapeDtypeStruct(shape, BF16)
-    own_m, own_h1, own_h2, k1, k2, k3, q1, q2, q3, b2, b3 = pl.pallas_call(
+    own_closure = pl.pallas_call(
         own_closure_kernel,
         out_shape=[
             sds(ROWS, FEATS, COLS), sds(ROWS, HID, COLS), sds(ROWS, HID, COLS),
@@ -881,10 +880,31 @@
         compiler_params=params(12),
         cost_estimate=pl.CostEstimate(flops=10**9, bytes_accessed=2 * 10**6, transcendentals=0),
         name="own_closure",
-    )(own, *raw)
+    )
+    pack_corners = pl.pallas_call(
+        lambda *refs: corner_kernel(sides, *refs),
+        out_shape=[sds(2 * PACK + 80, COLS)] * len(sides),
+        in_specs=[SMEM, VMEM, VMEM],
+        out_specs=[VMEM] * len(sides),
+        compiler_params=params(8),
+        cost_estimate=pl.CostEstimate(flops=10**8, bytes_accessed=10**6, transcendentals=0),
+        name="pack_corners",
+    )
+    total, results = pair_rounds(
+        sums,
+        (("lon", lon_n), ("lat", lat_n)),
+        [
+            lambda done: sums,
+            lambda done: own_closure(own, *raw),
+            lambda done: pack_corners(scal, from_west, from_east),
+        ],
+    )
+    corners = [lax.ppermute(pay, "lat", lat_pairs(side)) for side, pay in zip(sides, results[2])]
+    received = [ref for pair in zip(lats, corners) for ref in pair]
+    own_m, own_h1, own_h2, k1, k2, k3, q1, q2, q3, b2, b3 = results[1]
 
     geometry = (scal, cs, fs)
-    state = sds(EXT, 72, WIDE)
+    state = sds(EXT, 56, WIDE)
     plain = sds(EXT, FEATS, WIDE)
     marks = sds(EXT, 16, WIDE)
     vmem = lambda shape: pltpu.VMEM(shape.shape, F32)
@@ -905,7 +925,7 @@
     s0, masks, fluxes, net = call(
         lambda *refs: assemble_kernel(sides, *refs), "assemble",
         [state, marks, sds(EXT, 8, WIDE), plain], [],
-        [means[max(len(means) - 2, 0)], own, own_m, from_west, from_east] + received + [k1, k2, k3, b2, b3],
+        [own, own_m, from_west, from_east] + received + [k1, k2, k3, b2, b3],
         2 * 10**9, 8,
     )
     s1 = call(first_section_kernel, "first_section", state, [], [s0, masks], 10**9, 8)
@@ -914,26 +934,29 @@
         lambda *refs: late_kernel(sides, *refs), "steps_and_adjoint",
         [sds(80, COLS), plain, plain, sds(ROWS, FEATS, COLS), state, state, plain],
         [vmem(state)] + [vmem(plain)] * 5 + [pltpu.VMEM((192, HID), F32)],
-        [means[-1], own, cown, own_h1, own_h2, s0, s2, masks, fluxes, net, from_west, from_east]
+        [total, own, cown, own_h1, own_h2, s0, s2, masks, fluxes, net, from_west, from_east]
         + received + [k1, k2, k3, q1, q2, q3, b2, b3],
         4 * 10**9, 18,
     )
-    rounds = pair_rounds(grads, (("lat", lat_n), ("lon", lon_n)))
-    final = call(
-        last_section_kernel, "last_section", sds(40 * ROWS, COLS), [],
-        [rounds[min(2, len(rounds) - 1)], means[-1], s3, t2, masks, fluxes, net_2], 10**9, 8,
-    )
-    hold, bbuf = call(
-        back_third_kernel, "adjoint_third_section", [plain, plain], [], [s2, masks, abuf, top], 10**9, 8
-    )
-    left, abuf = call(
-        back_second_kernel, "adjoint_second_section", [plain, plain], [],
-        [rounds[0], s1, masks, bbuf, top, hold], 10**9, 8,
-    )
-    state_grad = call(
-        back_first_kernel, "adjoint_first_section", sds(40 * ROWS, COLS), [],
-        [rounds[1], s0, masks, abuf, left, from_closure], 10**9, 8,
-    )
+    beside = [
+        lambda done: call(
+            back_third_kernel, "adjoint_third_section", [plain, plain], [], [s2, masks, abuf, top], 10**9, 8
+        ),
+        lambda done: call(
+            back_second_kernel, "adjoint_second_section", [plain, plain], [],
+            [s1, masks, done[0][1], top, done[0][0]], 10**9, 8,
+        ),
+        lambda done: call(
+            back_first_kernel, "adjoint_first_section", sds(40 * ROWS, COLS), [],
+            [s0, masks, done[1][1], done[1][0], from_closure], 10**9, 8,
+        ),
+        lambda done: call(
+            last_section_kernel, "last_section", sds(40 * ROWS, COLS), [],
+            [total, s3, t2, masks, fluxes, net_2], 10**9, 8,
+        ),
+    ]
+    summed, results = pair_rounds(grads, (("lat", lat_n), ("lon", lon_n)), beside)
+    state_grad, final = results[2:]
 
     scale = 1.0 / math.sqrt(lat_total * lon_total)
     g_in, g_bin, g_mid, g_bmid, g_out, g_bout = pl.pallas_call(
@@ -943,7 +966,7 @@
         out_specs=[VMEM] * 6,
         compiler_params=params(8),
         name="unpack_weight_grads",
-    )(rounds[-1])
+    )(summed)
     shape = initial_state.shape
     return (
         final.reshape(shape),

time: 72.1 us -> 68.3 us (0.947)
  waiting for transfers between devices: 20.9 us -> 18.8 us
  Pallas kernels: 36.9 us -> 35.1 us
  starting transfers between devices: 10.6 us -> 11.4 us
    ppermute x10, waiting for transfers between devices: 20.9 us -> 18.8 us  [pair_rounds(): lax.ppermute(x, axis, [(i, i ^ 1 << bit) for i in range(count)])]
    pallas_call x8, Pallas kernels: 30.8 us -> 29.6 us  [call(): pl.pallas_call(kernel, out_shape=out_shape, in_specs=[SMEM] * 3 + [VMEM]...]
  transfers between devices with their start and end apart: 14 -> 14, of which waited for: 9 -> 8; matrix products, arithmetic and copies ran while one was open for 1% -> 1% of each run, Pallas kernels for 15% -> 16%
where the time goes in v5:
time: 68.3 us; the launch traced here: 68.1 us
  Pallas kernels  35.1 us (51%)
  waiting for transfers between devices  18.8 us (28%)
  starting transfers between devices  11.4 us (17%)
  local copies, waits for them, and re-layouts  1.21 us (2%)
  between operations  0.89 us (1%)
  other arithmetic  0.79 us (1%)
    pallas_call x8, Pallas kernels, call(): pl.pallas_call(kernel, out_shape=out_shape, in_specs=[SMEM] * 3 + [VMEM]...  29.6 us
    ppermute x10, waiting for transfers between devices, pair_rounds(): lax.ppermute(x, axis, [(i, i ^ 1 << bit) for i in range(count)])  18.8 us
    ppermute x1, starting transfers between devices, on_device(): from_east = lax.ppermute(west_pay, 'lon', west_ring)  4.14 us
    ppermute x2, starting transfers between devices, on_device(): lax.ppermute(pay, 'lat', lat_pairs(side))  3.54 us
    ppermute x10, starting transfers between devices, pair_rounds(): lax.ppermute(x, axis, [(i, i ^ 1 << bit) for i in range(count)])  3.22 us
    pallas_call x1, Pallas kernels, on_device(): pl.pallas_call(lambda *refs: pack_kernel(sides, *refs), out_shape=[sds(RO...  2.61 us
  transfers between devices with their start and end apart: 14, of which 8 were waited for; matrix products, arithmetic and copies ran while one was open for 1% of the time, Pallas kernels for 16%

profile of v5, /device:TPU:0, one launch (start us, length us, event | category | flops | bytes accessed | tf_op | source)
XLA Modules:
  0.0 68.1 jit_solution(13677011214276860940)
XLA Ops:
  0.7 2.6 %pack_halos.1 = (f32[16,56,128]{2,1,0:T(8,128)}, f32[16,40,128]{2,1,0:T(8,128)}, f32[152,128]{1,0:T(8,128)}, f32[152,128]{1,0:T(8,128)}, f32[8,128]{1,0:T(8,128)}, /*index=5*/f32[856,128]{1,0:T(8,128)}) custom-call(f32[640,128]{1,0:T(8,128)} %bitcast.24, s32[160,128]{1,0:T(8,128)} %bitcast.26, f32[16,128]{1,0:T(8,128)} %refs_2_.2, f32[640,128]{1,0:T(8,128)} %bitcast.25), custom_call_target="tpu_custom_call" | custom-call | flops 1000000000 | bytes 3000000 | tf_op jit(solution)/shard_map/pack_halos/pallas_call | solution.py:830
  3.3 3.0 %collective-permute-start.7 = (f32[856,128]{1,0:T(8,128)}, f32[856,128]{1,0:T(8,128)S(1)}, u32[]{:S(2)}, u32[]{:S(2)}) collective-permute-start(f32[856,128]{1,0:T(8,128)} %get-tuple-element.93), channel_id=1, source_target_pairs={{0,1},{1,0},{2,3},{3,2},{4,5},{5,4},{6,7},{7,6},{8,9},{9,8},{10,11... | collective-permute-start | bytes 1314824 | tf_op jit(solution)/shard_map/ppermute | solution.py:862
  6.8 4.1 %collective-permute-start.4 = (f32[152,128]{1,0:T(8,128)}, f32[152,128]{1,0:T(8,128)S(1)}, u32[]{:S(2)}, u32[]{:S(2)}) collective-permute-start(f32[152,128]{1,0:T(8,128)} %get-tuple-element.87), channel_id=1, source_target_pairs={{2,0},{4,2},{6,4},{8,6},{10,8},{12,10},{14,12},{16,14},{18,16},{20... | collective-permute-start | bytes 233480 | tf_op jit(solution)/shard_map/ppermute | solution.py:864
  11.8 1.0 %copy-done.5 = f32[16,56,128]{2,1,0:T(8,128)S(1)} copy-done((f32[16,56,128]{2,1,0:T(8,128)S(1)}, f32[16,56,128]{2,1,0:T(8,128)}, u32[]{:S(2)}) %copy-start.5) | copy-done | bytes 458776
  12.8 1.3 %own_closure.1 = (f32[16,40,128]{2,1,0:T(8,128)S(1)}, f32[16,64,128]{2,1,0:T(8,128)S(1)}, f32[16,64,128]{2,1,0:T(8,128)S(1)}, bf16[64,144]{1,0:T(8,128)(2,1)S(1)...) custom-call(f32[16,56,128]{2,1,0:T(8,128)S(1)} %copy-done.5, ...), custom_call_target="tpu_custom_call" | custom-call | flops 1000000000 | bytes 2000000 | tf_op jit(solution)/shard_map/own_closure/pallas_call | solution.py:898
  14.2 1.2 %collective-permute-done.1 = f32[8,128]{1,0:T(8,128)S(1)} collective-permute-done((f32[8,128]{1,0:T(8,128)S(1)}, f32[8,128]{1,0:T(8,128)S(1)}, u32[]{:S(2)}, u32[]{:S(2)}) %collective-permute-start.1) | collective-permute-done | bytes 4128 | tf_op jit(solution)/shard_map/ppermute | solution.py:794
  15.4 0.9 %pack_corners.1 = f32[192,128]{1,0:T(8,128)S(1)} custom-call(s32[7]{0:T(128)S(1)} %stack.39.refs_0_.scal, f32[152,128]{1,0:T(8,128)S(1)} %collective-permute-done.3.refs_1_.refs_5_.refs_13_, f32[152,128]{1,0:T(8,128)S(1)} %collective-permute-done.4.refs_2_.refs_6_.refs_14_), custom_call_target="tpu_custom_call" | custom-call | flops 100000000 | bytes 1000000 | tf_op jit(solution)/shard_map/pack_corners/pallas_call | solution.py:899
  16.3 2.7 %collective-permute-done.2 = f32[8,128]{1,0:T(8,128)S(1)} collective-permute-done((f32[8,128]{1,0:T(8,128)S(1)}, f32[8,128]{1,0:T(8,128)S(1)}, u32[]{:S(2)}, u32[]{:S(2)}) %collective-permute-start.2) | collective-permute-done | bytes 4128 | tf_op jit(solution)/shard_map/ppermute | solution.py:794
  20.1 3.4 %collective-permute-done.5 = f32[8,128]{1,0:T(8,128)S(1)} collective-permute-done((f32[8,128]{1,0:T(8,128)S(1)}, f32[8,128]{1,0:T(8,128)S(1)}, u32[]{:S(2)}, u32[]{:S(2)}) %collective-permute-start.5) | collective-permute-done | bytes 4128 | tf_op jit(solution)/shard_map/ppermute | solution.py:794
  24.1 3.0 %collective-permute-done.6 = f32[8,128]{1,0:T(8,128)S(1)} collective-permute-done((f32[8,128]{1,0:T(8,128)S(1)}, f32[8,128]{1,0:T(8,128)S(1)}, u32[]{:S(2)}, u32[]{:S(2)}) %collective-permute-start.6) | collective-permute-done | bytes 4128 | tf_op jit(solution)/shard_map/ppermute | solution.py:794
  27.1 2.0 %assemble.1 = (f32[48,56,256]{2,1,0:T(8,128)S(1)}, f32[48,16,256]{2,1,0:T(8,128)S(1)}, f32[48,8,256]{2,1,0:T(8,128)S(1)}, f32[48,40,256]{2,1,0:T(8,128)S(1)}) custom-call(s32[7]{0:T(128)S(1)} %stack.39.refs_0_.scal, f32[48]{0:T(128)S(1)} %get-tuple-element.134.refs_1_.cs, f32[48]{0:T(128)S(1)} %get-tuple-element.135.refs_2_.fs, ...), custom_call_target="tpu_custom_call" | custom-call | flops 2000000000 | bytes 10000000 | tf_op jit(solution)/shard_map/assemble/pallas_call | solution.py:914
  29.1 2.0 %first_section.1.s1.state = f32[48,56,256]{2,1,0:T(8,128)S(1)} custom-call(s32[7]{0:T(128)S(1)} %stack.39.refs_0_.scal, f32[48]{0:T(128)S(1)} %get-tuple-element.134.refs_1_.cs, f32[48]{0:T(128)S(1)} %get-tuple-element.135.refs_2_.fs, f32[48,56,256]{2,1,0:T(8,128)S(1)} %get-tuple-element.100.s0.refs_8_.state, ...), custom_call_target="tpu_custom_call" | custom-call | flops 1000000000 | bytes 10000000 | tf_op jit(solution)/shard_map/first_section/pallas_call | solution.py:914
  31.2 2.1 %second_section.1.refs_9_.state = f32[48,56,256]{2,1,0:T(8,128)S(1)} custom-call(s32[7]{0:T(128)S(1)} %stack.39.refs_0_.scal, f32[48]{0:T(128)S(1)} %get-tuple-element.134.refs_1_.cs, f32[48]{0:T(128)S(1)} %get-tuple-element.135.refs_2_.fs, f32[48,56,256]{2,1,0:T(8,128)S(1)} %get-tuple-element.100.s0.refs_8_.state, ...), custom_call_target="tpu_custom_call" | custom-call | flops 1000000000 | bytes 10000000 | tf_op jit(solution)/shard_map/second_section/pallas_call | solution.py:914
  33.3 14.9 %steps_and_adjoint.1 = (f32[80,128]{1,0:T(8,128)S(1)}, f32[48,40,256]{2,1,0:T(8,128)S(1)}, f32[48,40,256]{2,1,0:T(8,128)S(1)}, f32[16,40,128]{2,1,0:T(8,128)S(1)...) custom-call(s32[7]{0:T(128)S(1)} %stack.39.refs_0_.scal, ...), custom_call_target="tpu_custom_call" | custom-call | flops 4000000000 | bytes 10000000 | tf_op jit(solution)/shard_map/steps_and_adjoint/pallas_call | solution.py:914
  48.7 2.0 %adjoint_third_section.1 = (f32[48,40,256]{2,1,0:T(8,128)S(1)}, f32[48,40,256]{2,1,0:T(8,128)S(1)}) custom-call(s32[7]{0:T(128)S(1)} %stack.39.refs_0_.scal, f32[48]{0:T(128)S(1)} %get-tuple-element.134.refs_1_.cs, f32[48]{0:T(128)S(1)} %get-tuple-element.135.refs_2_.fs, f32[48,56,256]{2,1,0:T(8,128)S(1)} %second_section.1.refs_9_.state, ...), custom_call_target="tpu_custom_call" | custom-call | flops 1000000000 | bytes 10000000 | tf_op jit(solution)/shard_map/adjoint_third_section/pallas_call | solution.py:914
  50.8 1.5 %collective-permute-done.9 = f32[80,128]{1,0:T(8,128)S(1)} collective-permute-done((f32[80,128]{1,0:T(8,128)S(1)}, f32[80,128]{1,0:T(8,128)S(1)}, u32[]{:S(2)}, u32[]{:S(2)}) %collective-permute-start.9) | collective-permute-done | bytes 40992 | tf_op jit(solution)/shard_map/ppermute | solution.py:794
  52.2 2.1 %adjoint_second_section.1 = (f32[48,40,256]{2,1,0:T(8,128)S(1)}, f32[48,40,256]{2,1,0:T(8,128)S(1)}) custom-call(s32[7]{0:T(128)S(1)} %stack.39.refs_0_.scal, f32[48]{0:T(128)S(1)} %get-tuple-element.134.refs_1_.cs, f32[48]{0:T(128)S(1)} %get-tuple-element.135.refs_2_.fs, f32[48,56,256]{2,1,0:T(8,128)S(1)} %first_section.1.s1.state, ...), custom_call_target="tpu_custom_call" | custom-call | flops 1000000000 | bytes 10000000 | tf_op jit(solution)/shard_map/adjoint_second_section/pallas_call | solution.py:914
  54.4 1.0 %collective-permute-start.11 = (f32[80,128]{1,0:T(8,128)S(1)}, f32[80,128]{1,0:T(8,128)S(1)}, u32[]{:S(2)}, u32[]{:S(2)}) collective-permute-start(f32[80,128]{1,0:T(8,128)S(1)} %add.54), channel_id=1, source_target_pairs={{0,4},{2,6},{4,0},{6,2},{8,12},{10,14},{12,8},{14,10},{16,20},{18,... | collective-permute-start | bytes 122888 | tf_op jit(solution)/shard_map/ppermute | solution.py:794
  55.3 2.3 %adjoint_first_section.1 = f32[640,128]{1,0:T(8,128)} custom-call(s32[7]{0:T(128)S(1)} %stack.39.refs_0_.scal, f32[48]{0:T(128)S(1)} %get-tuple-element.134.refs_1_.cs, f32[48]{0:T(128)S(1)} %get-tuple-element.135.refs_2_.fs, f32[48,56,256]{2,1,0:T(8,128)S(1)} %get-tuple-element.100.s0.refs_8_.state, f32[48,16,256]{2,1,0:T(8,128)S(1)} %get-tuple-element.101.masks.refs_10_, ...), custom_call_target="tpu_custom_call" | custom-call | flops 1000000000 | bytes 10000000 | tf_op jit(solution)/shard_map/adjoint_first_section/pallas_call | solution.py:914
  57.7 0.8 %collective-permute-done.11 = f32[80,128]{1,0:T(8,128)S(1)} collective-permute-done((f32[80,128]{1,0:T(8,128)S(1)}, f32[80,128]{1,0:T(8,128)S(1)}, u32[]{:S(2)}, u32[]{:S(2)}) %collective-permute-start.11) | collective-permute-done | bytes 40992 | tf_op jit(solution)/shard_map/ppermute | solution.py:794
  58.5 2.1 %last_section.1 = f32[640,128]{1,0:T(8,128)} custom-call(s32[7]{0:T(128)S(1)} %stack.39.refs_0_.scal, f32[48]{0:T(128)S(1)} %get-tuple-element.134.refs_1_.cs, f32[48]{0:T(128)S(1)} %get-tuple-element.135.refs_2_.fs, f32[8,128]{1,0:T(8,128)S(1)} %add.52.refs_3_.sums, f32[48,56,256]{2,1,0:T(8,128)S(1)} %get-tuple-element.122.s3, ...), custom_call_target="tpu_custom_call" | custom-call | flops 1000000000 | bytes 10000000 | tf_op jit(solution)/shard_map/last_section/pallas_call | solution.py:914
  60.5 1.9 %collective-permute-done.12 = f32[80,128]{1,0:T(8,128)S(1)} collective-permute-done((f32[80,128]{1,0:T(8,128)S(1)}, f32[80,128]{1,0:T(8,128)S(1)}, u32[]{:S(2)}, u32[]{:S(2)}) %collective-permute-start.12) | collective-permute-done | bytes 40992 | tf_op jit(solution)/shard_map/ppermute | solution.py:794
  63.0 4.4 %collective-permute-done.13 = f32[80,128]{1,0:T(8,128)S(1)} collective-permute-done((f32[80,128]{1,0:T(8,128)S(1)}, f32[80,128]{1,0:T(8,128)S(1)}, u32[]{:S(2)}, u32[]{:S(2)}) %collective-permute-start.13) | collective-permute-done | bytes 40992 | tf_op jit(solution)/shard_map/ppermute | solution.py:794
  67.4 0.7 %unpack_weight_grads.1 = (f32[40,64]{1,0:T(8,128)}, f32[1,64]{1,0:T(1,128)}, f32[64,64]{1,0:T(8,128)}, f32[1,64]{1,0:T(1,128)}, f32[40,64]{1,0:T(8,128)}, /*index=5*/f32[1,40]{1,0:T(1,128)}) custom-call(f32[80,128]{1,0:T(8,128)S(1)} %add.57.refs_0_), custom_call_target="tpu_custom_call" | custom-call | tf_op jit(solution)/shard_map/unpack_weight_grads/pallas_call | solution.py:962
  (47 shorter events, 4.3 us)
Async XLA Ops:
  0.6 10.3 %copy-start.8 = (f32[64,40]{0,1:T(8,128)S(1)}, f32[64,40]{0,1:T(8,128)}, u32[]{:S(2)}) copy-start(f32[64,40]{0,1:T(8,128)} %param.17) | copy-start | bytes 30724
  0.6 11.1 %copy-start.4 = (f32[40]{0:T(128)S(1)}, f32[40]{0:T(128)}, u32[]{:S(2)}) copy-start(f32[40]{0:T(128)} %param.18) | copy-start | bytes 484
  0.7 11.1 %copy-start.3 = (f32[64]{0:T(128)S(1)}, f32[64]{0:T(128)}, u32[]{:S(2)}) copy-start(f32[64]{0:T(128)} %param.16) | copy-start | bytes 772
  0.7 11.1 %copy-start = (f32[64,64]{1,0:T(8,128)S(1)}, f32[64,64]{1,0:T(8,128)}, u32[]{:S(2)}) copy-start(f32[64,64]{1,0:T(8,128)} %refs_1_.1) | copy-start | bytes 49156
  0.7 11.1 %copy-start.2 = (f32[64]{0:T(128)S(1)}, f32[64]{0:T(128)}, u32[]{:S(2)}) copy-start(f32[64]{0:T(128)} %param.14) | copy-start | bytes 772
  0.7 11.1 %copy-start.1 = (f32[40,64]{1,0:T(8,128)S(1)}, f32[40,64]{1,0:T(8,128)}, u32[]{:S(2)}) copy-start(f32[40,64]{1,0:T(8,128)} %refs_0_.1) | copy-start | bytes 30724
  3.3 23.8 %collective-permute-start.7 = (f32[856,128]{1,0:T(8,128)}, f32[856,128]{1,0:T(8,128)S(1)}, u32[]{:S(2)}, u32[]{:S(2)}) collective-permute-start(f32[856,128]{1,0:T(8,128)} %get-tuple-element.93), channel_id=1, source_target_pairs={{0,1},{1,0},{2,3},{3,2},{4,5},{5,4},{6,7},{7,6},{8,9},{9,8},{10,11... | collective-permute-start | bytes 1314824 | tf_op jit(solution)/shard_map/ppermute | solution.py:862
  6.3 4.7 %collective-permute-start = (f32[8,128]{1,0:T(8,128)}, f32[8,128]{1,0:T(8,128)S(1)}, u32[]{:S(2)}, u32[]{:S(2)}) collective-permute-start(f32[8,128]{1,0:T(8,128)} %get-tuple-element.71), channel_id=1, source_target_pairs={{0,2},{2,0},{4,6},{6,4},{8,10},{10,8},{12,14},{14,12},{16,18},{18,... | collective-permute-start | bytes 12296 | tf_op jit(solution)/shard_map/ppermute | solution.py:794
  6.3 9.0 %collective-permute-start.3 = (f32[152,128]{1,0:T(8,128)}, f32[152,128]{1,0:T(8,128)S(1)}, u32[]{:S(2)}, u32[]{:S(2)}) collective-permute-start(f32[152,128]{1,0:T(8,128)} %get-tuple-element.86), channel_id=1, source_target_pairs={{0,2},{2,4},{4,6},{6,8},{8,10},{10,12},{12,14},{14,16},{16,18},{18... | collective-permute-start | bytes 233480 | tf_op jit(solution)/shard_map/ppermute | solution.py:863
  6.8 8.5 %collective-permute-start.4 = (f32[152,128]{1,0:T(8,128)}, f32[152,128]{1,0:T(8,128)S(1)}, u32[]{:S(2)}, u32[]{:S(2)}) collective-permute-start(f32[152,128]{1,0:T(8,128)} %get-tuple-element.87), channel_id=1, source_target_pairs={{2,0},{4,2},{6,4},{8,6},{10,8},{12,10},{14,12},{16,14},{18,16},{20... | collective-permute-start | bytes 233480 | tf_op jit(solution)/shard_map/ppermute | solution.py:864
  11.8 3.6 %collective-permute-start.1 = (f32[8,128]{1,0:T(8,128)S(1)}, f32[8,128]{1,0:T(8,128)S(1)}, u32[]{:S(2)}, u32[]{:S(2)}) collective-permute-start(f32[8,128]{1,0:T(8,128)S(1)} %add.48), channel_id=1, source_target_pairs={{0,4},{2,6},{4,0},{6,2},{8,12},{10,14},{12,8},{14,10},{16,20},{18,... | collective-permute-start | bytes 12296 | tf_op jit(solution)/shard_map/ppermute | solution.py:794
  11.8 1.0 %copy-start.5 = (f32[16,56,128]{2,1,0:T(8,128)S(1)}, f32[16,56,128]{2,1,0:T(8,128)}, u32[]{:S(2)}) copy-start(f32[16,56,128]{2,1,0:T(8,128)} %get-tuple-element.73.own.refs_3_.refs_4_) | copy-start | bytes 1376260
  12.8 14.3 %copy-start.6 = (f32[16,56,128]{2,1,0:T(8,128)S(1)}, f32[16,56,128]{2,1,0:T(8,128)}, u32[]{:S(2)}) copy-start(f32[16,56,128]{2,1,0:T(8,128)} %get-tuple-element.73.own.refs_3_.refs_4_) | copy-start | bytes 1376260
  15.4 3.6 %collective-permute-start.2 = (f32[8,128]{1,0:T(8,128)S(1)}, f32[8,128]{1,0:T(8,128)S(1)}, u32[]{:S(2)}, u32[]{:S(2)}) collective-permute-start(f32[8,128]{1,0:T(8,128)S(1)} %add.49), channel_id=1, source_target_pairs={{0,8},{2,10},{4,12},{6,14},{8,0},{10,2},{12,4},{14,6},{16,24},{18,... | collective-permute-start | bytes 12296 | tf_op jit(solution)/shard_map/ppermute | solution.py:794
  19.0 4.5 %collective-permute-start.5 = (f32[8,128]{1,0:T(8,128)S(1)}, f32[8,128]{1,0:T(8,128)S(1)}, u32[]{:S(2)}, u32[]{:S(2)}) collective-permute-start(f32[8,128]{1,0:T(8,128)S(1)} %add.50), channel_id=1, source_target_pairs={{0,16},{2,18},{4,20},{6,22},{8,24},{10,26},{12,28},{14,30},{16,0},... | collective-permute-start | bytes 12296 | tf_op jit(solution)/shard_map/ppermute | solution.py:794
  19.6 7.5 %collective-permute-start.8 = (f32[192,128]{1,0:T(8,128)S(1)}, f32[192,128]{1,0:T(8,128)S(1)}, u32[]{:S(2)}, u32[]{:S(2)}) collective-permute-start(f32[192,128]{1,0:T(8,128)S(1)} %pack_corners.1), channel_id=1, source_target_pairs={{0,1},{1,0},{2,3},{3,2},{4,5},{5,4},{6,7},{7,6},{8,9},{9,8},{10,11... | collective-permute-start | bytes 294920 | tf_op jit(solution)/shard_map/ppermute | solution.py:902
  23.5 3.6 %collective-permute-start.6 = (f32[8,128]{1,0:T(8,128)S(1)}, f32[8,128]{1,0:T(8,128)S(1)}, u32[]{:S(2)}, u32[]{:S(2)}) collective-permute-start(f32[8,128]{1,0:T(8,128)S(1)} %add.51), channel_id=1, source_target_pairs={{0,1},{1,0},{2,3},{3,2},{4,5},{5,4},{6,7},{7,6},{8,9},{9,8},{10,11... | collective-permute-start | bytes 12296 | tf_op jit(solution)/shard_map/ppermute | solution.py:794
  31.2 2.1 %copy-start.7 = (f32[16,40,128]{2,1,0:T(8,128)S(1)}, f32[16,40,128]{2,1,0:T(8,128)}, u32[]{:S(2)}) copy-start(f32[16,40,128]{2,1,0:T(8,128)} %get-tuple-element.89.refs_5_) | copy-start | bytes 983044
  48.2 4.0 %collective-permute-start.9 = (f32[80,128]{1,0:T(8,128)S(1)}, f32[80,128]{1,0:T(8,128)S(1)}, u32[]{:S(2)}, u32[]{:S(2)}) collective-permute-start(f32[80,128]{1,0:T(8,128)S(1)} %get-tuple-element.107), channel_id=1, source_target_pairs={{0,1},{1,0},{2,3},{3,2},{4,5},{5,4},{6,7},{7,6},{8,9},{9,8},{10,11... | collective-permute-start | bytes 122888 | tf_op jit(solution)/shard_map/ppermute | solution.py:794
  52.2 2.1 %collective-permute-start.10 = (f32[80,128]{1,0:T(8,128)S(1)}, f32[80,128]{1,0:T(8,128)S(1)}, u32[]{:S(2)}, u32[]{:S(2)}) collective-permute-start(f32[80,128]{1,0:T(8,128)S(1)} %add.53), channel_id=1, source_target_pairs={{0,2},{2,0},{4,6},{6,4},{8,10},{10,8},{12,14},{14,12},{16,18},{18,... | collective-permute-start | bytes 122888 | tf_op jit(solution)/shard_map/ppermute | solution.py:794
  54.4 4.1 %collective-permute-start.11 = (f32[80,128]{1,0:T(8,128)S(1)}, f32[80,128]{1,0:T(8,128)S(1)}, u32[]{:S(2)}, u32[]{:S(2)}) collective-permute-start(f32[80,128]{1,0:T(8,128)S(1)} %add.54), channel_id=1, source_target_pairs={{0,4},{2,6},{4,0},{6,2},{8,12},{10,14},{12,8},{14,10},{16,20},{18,... | collective-permute-start | bytes 122888 | tf_op jit(solution)/shard_map/ppermute | solution.py:794
  58.4 4.0 %collective-permute-start.12 = (f32[80,128]{1,0:T(8,128)S(1)}, f32[80,128]{1,0:T(8,128)S(1)}, u32[]{:S(2)}, u32[]{:S(2)}) collective-permute-start(f32[80,128]{1,0:T(8,128)S(1)} %add.55), channel_id=1, source_target_pairs={{0,8},{2,10},{4,12},{6,14},{8,0},{10,2},{12,4},{14,6},{16,24},{18,... | collective-permute-start | bytes 122888 | tf_op jit(solution)/shard_map/ppermute | solution.py:794
  62.5 4.9 %collective-permute-start.13 = (f32[80,128]{1,0:T(8,128)S(1)}, f32[80,128]{1,0:T(8,128)S(1)}, u32[]{:S(2)}, u32[]{:S(2)}) collective-permute-start(f32[80,128]{1,0:T(8,128)S(1)} %add.56), channel_id=1, source_target_pairs={{0,16},{2,18},{4,20},{6,22},{8,24},{10,26},{12,28},{14,30},{16,0},... | collective-permute-start | bytes 122888 | tf_op jit(solution)/shard_map/ppermute | solution.py:794

commit v6 on v5

--- a/solution.py
+++ b/solution.py
@@ -776,24 +776,22 @@
         bout[:, 10 * t + 9 : 10 * t + 10] = packed[73:74, 36 + t : 37 + t] * scale
 
 
-def pair_rounds(x, axes, beside=()):
+def far_first(axes):
+    return [(axis, n, 1 << bit) for axis, n in axes for bit in reversed(range(n.bit_length() - 1))]
+
+
+def pair_rounds(x, rounds, beside):
     results = []
-    beside = list(beside)
-
-    def wait_for(x):
-        if beside:
-            results.append(beside.pop(0)(results))
-            x, results[-1] = lax.optimization_barrier((x, results[-1]))
-        return x
-
-    for axis, count in axes:
-        if count & (count - 1):
-            x = wait_for(lax.psum(x, axis))
-            continue
-        for bit in range(count.bit_length() - 1):
-            x = x + wait_for(lax.ppermute(x, axis, [(i, i ^ (1 << bit)) for i in range(count)]))
-    while beside:
-        results.append(beside.pop(0)(results))
+    for i in range(max(len(rounds), len(beside))):
+        if i < len(rounds):
+            axis, n, step = rounds[i]
+            got = lax.ppermute(x, axis, [(j, j ^ step) for j in range(n)])
+        if i < len(beside):
+            results.append(beside[i](results))
+            if i < len(rounds):
+                got, results[-1] = lax.optimization_barrier((got, results[-1]))
+        if i < len(rounds):
+            x = x + got
     return x, results
 
 
@@ -859,7 +857,6 @@
 
     east_ring = [(i, (i + 1) % lon_n) for i in range(lon_n)]
     west_ring = [((i + 1) % lon_n, i) for i in range(lon_n)]
-    lats = [lax.ppermute(pay, "lat", lat_pairs(side)) for side, pay in zip(sides, packed[5:])]
     from_west = lax.ppermute(east_pay, "lon", east_ring)
     from_east = lax.ppermute(west_pay, "lon", west_ring)
     row = lambda b: b.reshape(1, -1)
@@ -892,13 +889,14 @@
     )
     total, results = pair_rounds(
         sums,
-        (("lon", lon_n), ("lat", lat_n)),
+        far_first((("lat", lat_n),)) + far_first((("lon", lon_n),))[::-1],
         [
-            lambda done: sums,
+            lambda done: packed[5:],
             lambda done: own_closure(own, *raw),
             lambda done: pack_corners(scal, from_west, from_east),
         ],
     )
+    lats = [lax.ppermute(pay, "lat", lat_pairs(side)) for side, pay in zip(sides, results[0])]
     corners = [lax.ppermute(pay, "lat", lat_pairs(side)) for side, pay in zip(sides, results[2])]
     received = [ref for pair in zip(lats, corners) for ref in pair]
     own_m, own_h1, own_h2, k1, k2, k3, q1, q2, q3, b2, b3 = results[1]
@@ -955,7 +953,8 @@
             [total, s3, t2, masks, fluxes, net_2], 10**9, 8,
         ),
     ]
-    summed, results = pair_rounds(grads, (("lat", lat_n), ("lon", lon_n)), beside)
+    by_lon, by_lat = far_first((("lon", lon_n),)), far_first((("lat", lat_n),))
+    summed, results = pair_rounds(grads, by_lon[:-2] + by_lat + by_lon[-2:], beside)
     state_grad, final = results[2:]
 
     scale = 1.0 / math.sqrt(lat_total * lon_total)

time: 68.3 us -> 69.9 us (1.023)
  waiting for transfers between devices: 18.8 us -> 19.7 us
  starting transfers between devices: 11.4 us -> 12.1 us
    ppermute x10, starting transfers between devices: 3.22 us -> 5.3 us  [pair_rounds(): got = lax.ppermute(x, axis, [(j, j ^ step) for j in range(n)])]
    ppermute x2, starting transfers between devices: 3.54 us -> 2.32 us  [on_device(): lax.ppermute(pay, 'lat', lat_pairs(side))]
    ppermute x10, waiting for transfers between devices: 18.8 us -> 19.7 us  [pair_rounds(): got = lax.ppermute(x, axis, [(j, j ^ step) for j in range(n)])]
  transfers between devices with their start and end apart: 14 -> 14, of which waited for: 8 -> 9; matrix products, arithmetic and copies ran while one was open for 1% -> 1% of each run, Pallas kernels for 16% -> 15%
where the time goes in v6:
time: 69.9 us; the launch traced here: 69.7 us
  Pallas kernels  35.1 us (50%)
  waiting for transfers between devices  19.7 us (28%)
  starting transfers between devices  12.1 us (17%)
  local copies, waits for them, and re-layouts  1.21 us (2%)
  between operations  0.88 us (1%)
  other arithmetic  0.79 us (1%)
    pallas_call x8, Pallas kernels, call(): pl.pallas_call(kernel, out_shape=out_shape, in_specs=[SMEM] * 3 + [VMEM]...  29.6 us
    ppermute x10, waiting for transfers between devices, pair_rounds(): got = lax.ppermute(x, axis, [(j, j ^ step) for j in range(n)])  19.7 us
    ppermute x10, starting transfers between devices, pair_rounds(): got = lax.ppermute(x, axis, [(j, j ^ step) for j in range(n)])  5.3 us
    ppermute x1, starting transfers between devices, on_device(): from_east = lax.ppermute(west_pay, 'lon', west_ring)  4.44 us
    pallas_call x1, Pallas kernels, on_device(): pl.pallas_call(lambda *refs: pack_kernel(sides, *refs), out_shape=[sds(RO...  2.61 us
    ppermute x2, starting transfers between devices, on_device(): lax.ppermute(pay, 'lat', lat_pairs(side))  2.32 us
  transfers between devices with their start and end apart: 14, of which 9 were waited for; matrix products, arithmetic and copies ran while one was open for 1% of the time, Pallas kernels for 15%

profile of v6, /device:TPU:0, one launch (start us, length us, event | category | flops | bytes accessed | tf_op | source)
XLA Modules:
  0.0 69.7 jit_solution(11410281401127926769)
XLA Ops:
  0.7 2.6 %pack_halos.1 = (f32[16,56,128]{2,1,0:T(8,128)}, f32[16,40,128]{2,1,0:T(8,128)}, f32[152,128]{1,0:T(8,128)}, f32[152,128]{1,0:T(8,128)}, f32[8,128]{1,0:T(8,128)}, /*index=5*/f32[856,128]{1,0:T(8,128)}) custom-call(f32[640,128]{1,0:T(8,128)} %bitcast.24, s32[160,128]{1,0:T(8,128)} %bitcast.26, f32[16,128]{1,0:T(8,128)} %refs_2_.2, f32[640,128]{1,0:T(8,128)} %bitcast.25), custom_call_target="tpu_custom_call" | custom-call | flops 1000000000 | bytes 3000000 | tf_op jit(solution)/shard_map/pack_halos/pallas_call | solution.py:828
  3.3 3.0 %collective-permute-start = (f32[8,128]{1,0:T(8,128)}, f32[8,128]{1,0:T(8,128)S(1)}, u32[]{:S(2)}, u32[]{:S(2)}) collective-permute-start(f32[8,128]{1,0:T(8,128)} %get-tuple-element.72), channel_id=1, source_target_pairs={{0,1},{1,0},{2,3},{3,2},{4,5},{5,4},{6,7},{7,6},{8,9},{9,8},{10,11... | collective-permute-start | bytes 12296 | tf_op jit(solution)/shard_map/ppermute | solution.py:788
  6.3 1.8 %collective-permute-done = f32[8,128]{1,0:T(8,128)S(1)} collective-permute-done((f32[8,128]{1,0:T(8,128)}, f32[8,128]{1,0:T(8,128)S(1)}, u32[]{:S(2)}, u32[]{:S(2)}) %collective-permute-start) | collective-permute-done | bytes 4128 | tf_op jit(solution)/shard_map/ppermute | solution.py:788
  8.1 2.0 %collective-permute-start.7 = (f32[856,128]{1,0:T(8,128)}, f32[856,128]{1,0:T(8,128)S(1)}, u32[]{:S(2)}, u32[]{:S(2)}) collective-permute-start(f32[856,128]{1,0:T(8,128)} %get-tuple-element.95), channel_id=1, source_target_pairs={{0,1},{1,0},{2,3},{3,2},{4,5},{5,4},{6,7},{7,6},{8,9},{9,8},{10,11... | collective-permute-start | bytes 1314824 | tf_op jit(solution)/shard_map/ppermute | solution.py:899
  10.1 4.4 %collective-permute-start.4 = (f32[152,128]{1,0:T(8,128)}, f32[152,128]{1,0:T(8,128)S(1)}, u32[]{:S(2)}, u32[]{:S(2)}) collective-permute-start(f32[152,128]{1,0:T(8,128)} %get-tuple-element.89), channel_id=1, source_target_pairs={{2,0},{4,2},{6,4},{8,6},{10,8},{12,10},{14,12},{16,14},{18,16},{20... | collective-permute-start | bytes 233480 | tf_op jit(solution)/shard_map/ppermute | solution.py:861
  15.4 1.0 %copy-done.5 = f32[16,56,128]{2,1,0:T(8,128)S(1)} copy-done((f32[16,56,128]{2,1,0:T(8,128)S(1)}, f32[16,56,128]{2,1,0:T(8,128)}, u32[]{:S(2)}) %copy-start.5) | copy-done | bytes 458776
  16.4 1.3 %own_closure.1 = (f32[16,40,128]{2,1,0:T(8,128)S(1)}, f32[16,64,128]{2,1,0:T(8,128)S(1)}, f32[16,64,128]{2,1,0:T(8,128)S(1)}, bf16[64,144]{1,0:T(8,128)(2,1)S(1)...) custom-call(f32[16,56,128]{2,1,0:T(8,128)S(1)} %copy-done.5, ...), custom_call_target="tpu_custom_call" | custom-call | flops 1000000000 | bytes 2000000 | tf_op jit(solution)/shard_map/own_closure/pallas_call | solution.py:895
  17.9 0.9 %pack_corners.1 = f32[192,128]{1,0:T(8,128)S(1)} custom-call(s32[7]{0:T(128)S(1)} %stack.39.refs_0_.scal, f32[152,128]{1,0:T(8,128)S(1)} %collective-permute-done.3.refs_1_.refs_5_.refs_13_, f32[152,128]{1,0:T(8,128)S(1)} %collective-permute-done.4.refs_2_.refs_6_.refs_14_), custom_call_target="tpu_custom_call" | custom-call | flops 100000000 | bytes 1000000 | tf_op jit(solution)/shard_map/pack_corners/pallas_call | solution.py:896
  18.8 2.6 %collective-permute-done.2 = f32[8,128]{1,0:T(8,128)S(1)} collective-permute-done((f32[8,128]{1,0:T(8,128)S(1)}, f32[8,128]{1,0:T(8,128)S(1)}, u32[]{:S(2)}, u32[]{:S(2)}) %collective-permute-start.2) | collective-permute-done | bytes 4128 | tf_op jit(solution)/shard_map/ppermute | solution.py:788
  21.8 3.3 %collective-permute-done.5 = f32[8,128]{1,0:T(8,128)S(1)} collective-permute-done((f32[8,128]{1,0:T(8,128)S(1)}, f32[8,128]{1,0:T(8,128)S(1)}, u32[]{:S(2)}, u32[]{:S(2)}) %collective-permute-start.5) | collective-permute-done | bytes 4128 | tf_op jit(solution)/shard_map/ppermute | solution.py:788
  25.9 3.7 %collective-permute-done.6 = f32[8,128]{1,0:T(8,128)S(1)} collective-permute-done((f32[8,128]{1,0:T(8,128)S(1)}, f32[8,128]{1,0:T(8,128)S(1)}, u32[]{:S(2)}, u32[]{:S(2)}) %collective-permute-start.6) | collective-permute-done | bytes 4128 | tf_op jit(solution)/shard_map/ppermute | solution.py:788
  29.6 2.0 %assemble.1 = (f32[48,56,256]{2,1,0:T(8,128)S(1)}, f32[48,16,256]{2,1,0:T(8,128)S(1)}, f32[48,8,256]{2,1,0:T(8,128)S(1)}, f32[48,40,256]{2,1,0:T(8,128)S(1)}) custom-call(s32[7]{0:T(128)S(1)} %stack.39.refs_0_.scal, f32[48]{0:T(128)S(1)} %get-tuple-element.136.refs_1_.cs, f32[48]{0:T(128)S(1)} %get-tuple-element.137.refs_2_.fs, ...), custom_call_target="tpu_custom_call" | custom-call | flops 2000000000 | bytes 10000000 | tf_op jit(solution)/shard_map/assemble/pallas_call | solution.py:912
  31.6 2.0 %first_section.1.s1.state = f32[48,56,256]{2,1,0:T(8,128)S(1)} custom-call(s32[7]{0:T(128)S(1)} %stack.39.refs_0_.scal, f32[48]{0:T(128)S(1)} %get-tuple-element.136.refs_1_.cs, f32[48]{0:T(128)S(1)} %get-tuple-element.137.refs_2_.fs, f32[48,56,256]{2,1,0:T(8,128)S(1)} %get-tuple-element.102.s0.refs_8_.state, ...), custom_call_target="tpu_custom_call" | custom-call | flops 1000000000 | bytes 10000000 | tf_op jit(solution)/shard_map/first_section/pallas_call | solution.py:912
  33.7 2.1 %second_section.1.refs_9_.state = f32[48,56,256]{2,1,0:T(8,128)S(1)} custom-call(s32[7]{0:T(128)S(1)} %stack.39.refs_0_.scal, f32[48]{0:T(128)S(1)} %get-tuple-element.136.refs_1_.cs, f32[48]{0:T(128)S(1)} %get-tuple-element.137.refs_2_.fs, f32[48,56,256]{2,1,0:T(8,128)S(1)} %get-tuple-element.102.s0.refs_8_.state, ...), custom_call_target="tpu_custom_call" | custom-call | flops 1000000000 | bytes 10000000 | tf_op jit(solution)/shard_map/second_section/pallas_call | solution.py:912
  35.8 14.9 %steps_and_adjoint.1 = (f32[80,128]{1,0:T(8,128)S(1)}, f32[48,40,256]{2,1,0:T(8,128)S(1)}, f32[48,40,256]{2,1,0:T(8,128)S(1)}, f32[16,40,128]{2,1,0:T(8,128)S(1)...) custom-call(s32[7]{0:T(128)S(1)} %stack.39.refs_0_.scal, ...), custom_call_target="tpu_custom_call" | custom-call | flops 4000000000 | bytes 10000000 | tf_op jit(solution)/shard_map/steps_and_adjoint/pallas_call | solution.py:912
  51.5 2.0 %adjoint_third_section.1 = (f32[48,40,256]{2,1,0:T(8,128)S(1)}, f32[48,40,256]{2,1,0:T(8,128)S(1)}) custom-call(s32[7]{0:T(128)S(1)} %stack.39.refs_0_.scal, f32[48]{0:T(128)S(1)} %get-tuple-element.136.refs_1_.cs, f32[48]{0:T(128)S(1)} %get-tuple-element.137.refs_2_.fs, f32[48,56,256]{2,1,0:T(8,128)S(1)} %second_section.1.refs_9_.state, ...), custom_call_target="tpu_custom_call" | custom-call | flops 1000000000 | bytes 10000000 | tf_op jit(solution)/shard_map/adjoint_third_section/pallas_call | solution.py:912
  53.5 2.2 %collective-permute-done.9 = f32[80,128]{1,0:T(8,128)S(1)} collective-permute-done((f32[80,128]{1,0:T(8,128)S(1)}, f32[80,128]{1,0:T(8,128)S(1)}, u32[]{:S(2)}, u32[]{:S(2)}) %collective-permute-start.9) | collective-permute-done | bytes 40992 | tf_op jit(solution)/shard_map/ppermute | solution.py:788
  55.9 2.1 %adjoint_second_section.1 = (f32[48,40,256]{2,1,0:T(8,128)S(1)}, f32[48,40,256]{2,1,0:T(8,128)S(1)}) custom-call(s32[7]{0:T(128)S(1)} %stack.39.refs_0_.scal, f32[48]{0:T(128)S(1)} %get-tuple-element.136.refs_1_.cs, f32[48]{0:T(128)S(1)} %get-tuple-element.137.refs_2_.fs, f32[48,56,256]{2,1,0:T(8,128)S(1)} %first_section.1.s1.state, ...), custom_call_target="tpu_custom_call" | custom-call | flops 1000000000 | bytes 10000000 | tf_op jit(solution)/shard_map/adjoint_second_section/pallas_call | solution.py:912
  58.0 1.7 %collective-permute-done.10 = f32[80,128]{1,0:T(8,128)S(1)} collective-permute-done((f32[80,128]{1,0:T(8,128)S(1)}, f32[80,128]{1,0:T(8,128)S(1)}, u32[]{:S(2)}, u32[]{:S(2)}) %collective-permute-start.10) | collective-permute-done | bytes 40992 | tf_op jit(solution)/shard_map/ppermute | solution.py:788
  60.0 2.3 %adjoint_first_section.1 = f32[640,128]{1,0:T(8,128)} custom-call(s32[7]{0:T(128)S(1)} %stack.39.refs_0_.scal, f32[48]{0:T(128)S(1)} %get-tuple-element.136.refs_1_.cs, f32[48]{0:T(128)S(1)} %get-tuple-element.137.refs_2_.fs, f32[48,56,256]{2,1,0:T(8,128)S(1)} %get-tuple-element.102.s0.refs_8_.state, f32[48,16,256]{2,1,0:T(8,128)S(1)} %get-tuple-element.103.masks.refs_10_, ...), custom_call_target="tpu_custom_call" | custom-call | flops 1000000000 | bytes 10000000 | tf_op jit(solution)/shard_map/adjoint_first_section/pallas_call | solution.py:912
  62.3 1.4 %collective-permute-done.11 = f32[80,128]{1,0:T(8,128)S(1)} collective-permute-done((f32[80,128]{1,0:T(8,128)S(1)}, f32[80,128]{1,0:T(8,128)S(1)}, u32[]{:S(2)}, u32[]{:S(2)}) %collective-permute-start.11) | collective-permute-done | bytes 40992 | tf_op jit(solution)/shard_map/ppermute | solution.py:788
  63.9 2.1 %last_section.1 = f32[640,128]{1,0:T(8,128)} custom-call(s32[7]{0:T(128)S(1)} %stack.39.refs_0_.scal, f32[48]{0:T(128)S(1)} %get-tuple-element.136.refs_1_.cs, f32[48]{0:T(128)S(1)} %get-tuple-element.137.refs_2_.fs, f32[8,128]{1,0:T(8,128)S(1)} %add.52.refs_3_.sums, f32[48,56,256]{2,1,0:T(8,128)S(1)} %get-tuple-element.124.s3, ...), custom_call_target="tpu_custom_call" | custom-call | flops 1000000000 | bytes 10000000 | tf_op jit(solution)/shard_map/last_section/pallas_call | solution.py:912
  66.0 1.8 %collective-permute-done.12 = f32[80,128]{1,0:T(8,128)S(1)} collective-permute-done((f32[80,128]{1,0:T(8,128)S(1)}, f32[80,128]{1,0:T(8,128)S(1)}, u32[]{:S(2)}, u32[]{:S(2)}) %collective-permute-start.12) | collective-permute-done | bytes 40992 | tf_op jit(solution)/shard_map/ppermute | solution.py:788
  67.7 1.2 %collective-permute-done.13 = f32[80,128]{1,0:T(8,128)S(1)} collective-permute-done((f32[80,128]{1,0:T(8,128)S(1)}, f32[80,128]{1,0:T(8,128)S(1)}, u32[]{:S(2)}, u32[]{:S(2)}) %collective-permute-start.13) | collective-permute-done | bytes 40992 | tf_op jit(solution)/shard_map/ppermute | solution.py:788
  (47 shorter events, 4.3 us)
Async XLA Ops:
  0.6 14.0 %copy-start.8 = (f32[64,40]{0,1:T(8,128)S(1)}, f32[64,40]{0,1:T(8,128)}, u32[]{:S(2)}) copy-start(f32[64,40]{0,1:T(8,128)} %param.17) | copy-start | bytes 30724
  0.6 14.7 %copy-start.4 = (f32[40]{0:T(128)S(1)}, f32[40]{0:T(128)}, u32[]{:S(2)}) copy-start(f32[40]{0:T(128)} %param.18) | copy-start | bytes 484
  0.7 14.7 %copy-start.3 = (f32[64]{0:T(128)S(1)}, f32[64]{0:T(128)}, u32[]{:S(2)}) copy-start(f32[64]{0:T(128)} %param.16) | copy-start | bytes 772
  0.7 14.7 %copy-start = (f32[64,64]{1,0:T(8,128)S(1)}, f32[64,64]{1,0:T(8,128)}, u32[]{:S(2)}) copy-start(f32[64,64]{1,0:T(8,128)} %refs_1_.1) | copy-start | bytes 49156
  0.7 14.7 %copy-start.2 = (f32[64]{0:T(128)S(1)}, f32[64]{0:T(128)}, u32[]{:S(2)}) copy-start(f32[64]{0:T(128)} %param.14) | copy-start | bytes 772
  0.7 14.7 %copy-start.1 = (f32[40,64]{1,0:T(8,128)S(1)}, f32[40,64]{1,0:T(8,128)}, u32[]{:S(2)}) copy-start(f32[40,64]{1,0:T(8,128)} %refs_0_.1) | copy-start | bytes 30724
  3.3 4.8 %collective-permute-start = (f32[8,128]{1,0:T(8,128)}, f32[8,128]{1,0:T(8,128)S(1)}, u32[]{:S(2)}, u32[]{:S(2)}) collective-permute-start(f32[8,128]{1,0:T(8,128)} %get-tuple-element.72), channel_id=1, source_target_pairs={{0,1},{1,0},{2,3},{3,2},{4,5},{5,4},{6,7},{7,6},{8,9},{9,8},{10,11... | collective-permute-start | bytes 12296 | tf_op jit(solution)/shard_map/ppermute | solution.py:788
  8.1 21.5 %collective-permute-start.7 = (f32[856,128]{1,0:T(8,128)}, f32[856,128]{1,0:T(8,128)S(1)}, u32[]{:S(2)}, u32[]{:S(2)}) collective-permute-start(f32[856,128]{1,0:T(8,128)} %get-tuple-element.95), channel_id=1, source_target_pairs={{0,1},{1,0},{2,3},{3,2},{4,5},{5,4},{6,7},{7,6},{8,9},{9,8},{10,11... | collective-permute-start | bytes 1314824 | tf_op jit(solution)/shard_map/ppermute | solution.py:899
  10.1 7.7 %collective-permute-start.3 = (f32[152,128]{1,0:T(8,128)}, f32[152,128]{1,0:T(8,128)S(1)}, u32[]{:S(2)}, u32[]{:S(2)}) collective-permute-start(f32[152,128]{1,0:T(8,128)} %get-tuple-element.88), channel_id=1, source_target_pairs={{0,2},{2,4},{4,6},{6,8},{8,10},{10,12},{12,14},{14,16},{16,18},{18... | collective-permute-start | bytes 233480 | tf_op jit(solution)/shard_map/ppermute | solution.py:860
  10.1 7.7 %collective-permute-start.4 = (f32[152,128]{1,0:T(8,128)}, f32[152,128]{1,0:T(8,128)S(1)}, u32[]{:S(2)}, u32[]{:S(2)}) collective-permute-start(f32[152,128]{1,0:T(8,128)} %get-tuple-element.89), channel_id=1, source_target_pairs={{2,0},{4,2},{6,4},{8,6},{10,8},{12,10},{14,12},{16,14},{18,16},{20... | collective-permute-start | bytes 233480 | tf_op jit(solution)/shard_map/ppermute | solution.py:861
  15.4 2.4 %collective-permute-start.1 = (f32[8,128]{1,0:T(8,128)S(1)}, f32[8,128]{1,0:T(8,128)S(1)}, u32[]{:S(2)}, u32[]{:S(2)}) collective-permute-start(f32[8,128]{1,0:T(8,128)S(1)} %add.48), channel_id=1, source_target_pairs={{0,2},{2,0},{4,6},{6,4},{8,10},{10,8},{12,14},{14,12},{16,18},{18,... | collective-permute-start | bytes 12296 | tf_op jit(solution)/shard_map/ppermute | solution.py:788
  15.4 1.0 %copy-start.5 = (f32[16,56,128]{2,1,0:T(8,128)S(1)}, f32[16,56,128]{2,1,0:T(8,128)}, u32[]{:S(2)}) copy-start(f32[16,56,128]{2,1,0:T(8,128)} %get-tuple-element.75.own.refs_3_.refs_4_) | copy-start | bytes 1376260
  16.4 13.2 %copy-start.6 = (f32[16,56,128]{2,1,0:T(8,128)S(1)}, f32[16,56,128]{2,1,0:T(8,128)}, u32[]{:S(2)}) copy-start(f32[16,56,128]{2,1,0:T(8,128)} %get-tuple-element.75.own.refs_3_.refs_4_) | copy-start | bytes 1376260
  17.8 3.7 %collective-permute-start.2 = (f32[8,128]{1,0:T(8,128)S(1)}, f32[8,128]{1,0:T(8,128)S(1)}, u32[]{:S(2)}, u32[]{:S(2)}) collective-permute-start(f32[8,128]{1,0:T(8,128)S(1)} %add.49), channel_id=1, source_target_pairs={{0,4},{2,6},{4,0},{6,2},{8,12},{10,14},{12,8},{14,10},{16,20},{18,... | collective-permute-start | bytes 12296 | tf_op jit(solution)/shard_map/ppermute | solution.py:788
  21.5 3.6 %collective-permute-start.5 = (f32[8,128]{1,0:T(8,128)S(1)}, f32[8,128]{1,0:T(8,128)S(1)}, u32[]{:S(2)}, u32[]{:S(2)}) collective-permute-start(f32[8,128]{1,0:T(8,128)S(1)} %add.50), channel_id=1, source_target_pairs={{0,8},{2,10},{4,12},{6,14},{8,0},{10,2},{12,4},{14,6},{16,24},{18,... | collective-permute-start | bytes 12296 | tf_op jit(solution)/shard_map/ppermute | solution.py:788
  21.5 8.1 %collective-permute-start.8 = (f32[192,128]{1,0:T(8,128)S(1)}, f32[192,128]{1,0:T(8,128)S(1)}, u32[]{:S(2)}, u32[]{:S(2)}) collective-permute-start(f32[192,128]{1,0:T(8,128)S(1)} %pack_corners.1), channel_id=1, source_target_pairs={{0,1},{1,0},{2,3},{3,2},{4,5},{5,4},{6,7},{7,6},{8,9},{9,8},{10,11... | collective-permute-start | bytes 294920 | tf_op jit(solution)/shard_map/ppermute | solution.py:900
  25.1 4.5 %collective-permute-start.6 = (f32[8,128]{1,0:T(8,128)S(1)}, f32[8,128]{1,0:T(8,128)S(1)}, u32[]{:S(2)}, u32[]{:S(2)}) collective-permute-start(f32[8,128]{1,0:T(8,128)S(1)} %add.51), channel_id=1, source_target_pairs={{0,16},{2,18},{4,20},{6,22},{8,24},{10,26},{12,28},{14,30},{16,0},... | collective-permute-start | bytes 12296 | tf_op jit(solution)/shard_map/ppermute | solution.py:788
  33.7 2.1 %copy-start.7 = (f32[16,40,128]{2,1,0:T(8,128)S(1)}, f32[16,40,128]{2,1,0:T(8,128)}, u32[]{:S(2)}) copy-start(f32[16,40,128]{2,1,0:T(8,128)} %get-tuple-element.91.refs_5_) | copy-start | bytes 983044
  50.7 5.0 %collective-permute-start.9 = (f32[80,128]{1,0:T(8,128)S(1)}, f32[80,128]{1,0:T(8,128)S(1)}, u32[]{:S(2)}, u32[]{:S(2)}) collective-permute-start(f32[80,128]{1,0:T(8,128)S(1)} %get-tuple-element.109), channel_id=1, source_target_pairs={{0,16},{2,18},{4,20},{6,22},{8,24},{10,26},{12,28},{14,30},{16,0},... | collective-permute-start | bytes 122888 | tf_op jit(solution)/shard_map/ppermute | solution.py:788
  55.7 4.0 %collective-permute-start.10 = (f32[80,128]{1,0:T(8,128)S(1)}, f32[80,128]{1,0:T(8,128)S(1)}, u32[]{:S(2)}, u32[]{:S(2)}) collective-permute-start(f32[80,128]{1,0:T(8,128)S(1)} %add.53), channel_id=1, source_target_pairs={{0,8},{2,10},{4,12},{6,14},{8,0},{10,2},{12,4},{14,6},{16,24},{18,... | collective-permute-start | bytes 122888 | tf_op jit(solution)/shard_map/ppermute | solution.py:788
  59.7 4.0 %collective-permute-start.11 = (f32[80,128]{1,0:T(8,128)S(1)}, f32[80,128]{1,0:T(8,128)S(1)}, u32[]{:S(2)}, u32[]{:S(2)}) collective-permute-start(f32[80,128]{1,0:T(8,128)S(1)} %add.54), channel_id=1, source_target_pairs={{0,1},{1,0},{2,3},{3,2},{4,5},{5,4},{6,7},{7,6},{8,9},{9,8},{10,11... | collective-permute-start | bytes 122888 | tf_op jit(solution)/shard_map/ppermute | solution.py:788
  63.7 4.0 %collective-permute-start.12 = (f32[80,128]{1,0:T(8,128)S(1)}, f32[80,128]{1,0:T(8,128)S(1)}, u32[]{:S(2)}, u32[]{:S(2)}) collective-permute-start(f32[80,128]{1,0:T(8,128)S(1)} %add.55), channel_id=1, source_target_pairs={{0,4},{2,6},{4,0},{6,2},{8,12},{10,14},{12,8},{14,10},{16,20},{18,... | collective-permute-start | bytes 122888 | tf_op jit(solution)/shard_map/ppermute | solution.py:788
  67.7 1.2 %collective-permute-start.13 = (f32[80,128]{1,0:T(8,128)S(1)}, f32[80,128]{1,0:T(8,128)S(1)}, u32[]{:S(2)}, u32[]{:S(2)}) collective-permute-start(f32[80,128]{1,0:T(8,128)S(1)} %add.56), channel_id=1, source_target_pairs={{0,2},{2,0},{4,6},{6,4},{8,10},{10,8},{12,14},{14,12},{16,18},{18,... | collective-permute-start | bytes 122888 | tf_op jit(solution)/shard_map/ppermute | solution.py:788

commit v7 on v6

--- a/solution.py
+++ b/solution.py
@@ -23,8 +23,10 @@
 FEATS = 40
 HID = 64
 PACK = 56
+SUMS = 51
 STRIP = 2 * PACK + 40
 LAT_X = REACH * PACK
+CORNER = 2 * PACK + 80
 LAT = LAT_X + CREACH * FEATS
 SLOT = 16
 F32 = jnp.float32
@@ -90,7 +92,7 @@
         own[r, 48:49, :] = m8
         own[r, 49:50, :] = m9
         own[r, 50:51, :] = flux[r : r + 1, :]
-        own[r, 51:56, :] = jnp.zeros((5, COLS), F32)
+        own[r, SUMS:PACK, :] = sums[0:5, :]
     for half in range(2):
         for t in range(7):
             rows = [own[8 * half + s, 8 * t : 8 * t + 8, :] for s in range(8)]
@@ -120,6 +122,7 @@
                 rows = slice(at + 8 * t, at + 8 * t + 8)
                 corner[rows, :] = shift_rows(strip, t, start, near)
             corner[at + PACK : at + PACK + 40, :] = strip[2 * PACK : 2 * PACK + 40, :]
+        corner[CORNER : CORNER + 8, :] = jnp.zeros((8, COLS), F32)
 
 
 def shift_rows(strip, t, start, near):
@@ -390,10 +393,9 @@
     return out
 
 
-def for_rows(scal, reach, body):
-    low, high = PAD - reach * scal[2], PAD + ROWS + reach * scal[3]
+def for_span(low, high, up, body):
     turns = lax.div(high - low + TURN - 1, TURN)
-    first = jnp.where(scal[3] == 1, low, high - TURN * turns)
+    first = jnp.where(up == 1, low, high - TURN * turns)
 
     def turn(i, _):
         for j in range(TURN):
@@ -401,6 +403,23 @@
         return 0
 
     lax.fori_loop(0, turns, turn, 0)
+
+
+def for_rows(scal, reach, body):
+    for_span(PAD - reach * scal[2], PAD + ROWS + reach * scal[3], scal[3], body)
+
+
+def for_inner(scal, inset, body):
+    for_span(PAD + inset * scal[2], PAD + ROWS - inset * scal[3], scal[3], body)
+
+
+def for_outer(sides, scal, inset, reach, body):
+    if sides == ["swap"]:
+        low = jnp.where(scal[3] == 1, PAD + ROWS - inset, PAD - reach)
+        for_span(low, low + reach + inset, scal[3], body)
+    else:
+        for_span(PAD - reach * scal[2], PAD + inset * scal[2], 0, body)
+        for_span(PAD + ROWS - inset * scal[3], PAD + ROWS + reach * scal[3], 1, body)
 
 
 def mask_tile(ref, row, t):
@@ -499,83 +518,94 @@
         ref[row] = jnp.zeros(ref.shape[1:], F32)
 
 
-def assemble_kernel(sides, scal, cs, fs, own, own_m, east, west, *rest):
-    n = len(sides)
-    side_refs = [rest[2 * i : 2 * i + 2] for i in range(n)]
-    (k1, k2, k3, b2, b3), rest = rest[2 * n : 2 * n + 5], rest[2 * n + 5 :]
-    s0, masks, fluxes, outs = rest
+class Block:
+    def __init__(self, k, s0, masks, fluxes):
+        self.k, self.s0, self.masks, self.fluxes = k, s0, masks, fluxes
+        self.near_e, self.near_w = edges(REACH)
+
+    def put(self, row, core, from_e, from_w):
+        def both(t):
+            halo = jnp.where(self.near_e, from_e(t), jnp.where(self.near_w, from_w(t), 0.0))
+            return jnp.concatenate([core(t), halo], axis=1)
+
+        put_state(self.k, self.s0, row, [both(t) for t in range(5)])
+        self.masks[row, 0:8, :] = both(5)
+        last = both(6)
+        self.masks[row, 8:16, :] = jnp.where(self.k.low, last[1:2, :], last[0:1, :])
+        self.fluxes[row] = last
+
+
+def assemble_own_kernel(scal, cs, fs, own, own_m, east, west, k1, k2, k3, b2, b3, s0, masks, fluxes, net):
     k = Row(WIDE)
-    has_south = scal[2]
-    lo = lambda h: PAD - h * has_south
-
     zero_walls(s0)
-
-    near_e, near_w = edges(REACH)
-
-    def put_packed(row, core, halo):
-        both = lambda t: jnp.concatenate([core(t), halo(t)], axis=1)
-        put_state(k, s0, row, [both(t) for t in range(5)])
-        masks[row, 0:8, :] = both(5)
-        last = both(6)
-        masks[row, 8:16, :] = jnp.where(k.low, last[1:2, :], last[0:1, :])
-        fluxes[row] = last
-
+    block = Block(k, s0, masks, fluxes)
     for r in range(ROWS):
         at = (r // 8) * PACK
         turn = SLOT * (r % 8)
-
-        def halo(t):
-            from_e = pltpu.roll(west[at + 8 * t : at + 8 * t + 8, :], -turn % COLS, 1)
-            from_w = pltpu.roll(east[at + 8 * t : at + 8 * t + 8, :], -(turn + SLOT) % COLS, 1)
-            return jnp.where(near_e, from_e, jnp.where(near_w, from_w, 0.0))
-
-        put_packed(PAD + r, lambda t: own[r, 8 * t : 8 * t + 8, :], halo)
+        block.put(
+            PAD + r,
+            lambda t: own[r, 8 * t : 8 * t + 8, :],
+            lambda t: pltpu.roll(west[at + 8 * t : at + 8 * t + 8, :], -turn % COLS, 1),
+            lambda t: pltpu.roll(east[at + 8 * t : at + 8 * t + 8, :], -(turn + SLOT) % COLS, 1),
+        )
+        net[PAD + r, :, 0:COLS] = own_m[r]
+    columns = jnp.concatenate([wide_pack(s0, PAD), wide_pack(s0, PAD + 8)], axis=1)
+    o = closure_of(columns, k1, k2, k3, b2, b3)
+    for g in range(2):
+        wide_unpack(net, PAD + 8 * g, o[:, g * COLS : (g + 1) * COLS])
+
+
+def closure_of(columns, k1, k2, k3, b2, b3):
+    _, _, h2 = hidden_layers(split(to_48(columns, 1.0)), k1, k2, b2)
+    return last_layer(h2, k3, b3)
+
+
+def first_own_kernel(scal, cs, fs, s0, masks, s1):
+    zero_walls(s1)
+    for_inner(scal, 1, section_1(Row(WIDE), cs, fs, masks, s0, s1))
+
+
+def second_own_kernel(scal, cs, fs, s0, s1, masks, s2):
+    for_inner(scal, 2, section_2(Row(WIDE), cs, fs, masks, s0, s1, s2))
+
+
+def halo_kernel(sides, scal, cs, fs, own_s0, own_s1, own_s2, own_masks, own_fluxes, own_net, *rest):
+    n = len(sides)
+    side_refs = [rest[2 * i : 2 * i + 2] for i in range(n)]
+    net_refs, (s0, s1, s2, masks, fluxes, net) = rest[2 * n : 2 * n + 5], rest[2 * n + 5 :]
+    k = Row(WIDE)
+    for r in range(PAD, PAD + ROWS):
+        for src, dst in (
+            (own_s0, s0), (own_s1, s1), (own_s2, s2), (own_masks, masks), (own_fluxes, fluxes), (own_net, net)
+        ):
+            dst[r] = src[r]
+    for ref in (s0, s1, s2):
+        zero_walls(ref)
+    block = Block(k, s0, masks, fluxes)
+    firsts = []
     for side, (lat, corner) in zip(sides, side_refs):
         base = {"swap": scal[4], "north": PAD - REACH, "south": PAD + ROWS}[side]
         for r in range(REACH):
-
-            def halo(t):
-                wrows = slice(8 * t, 8 * t + 8)
-                erows = slice(PACK + 40 + 8 * t, PACK + 48 + 8 * t)
-                from_e = pltpu.roll(corner[erows, :], -REACH * r % COLS, 1)
-                from_w = pltpu.roll(corner[wrows, :], -REACH * (r + 1) % COLS, 1)
-                return jnp.where(near_e, from_e, jnp.where(near_w, from_w, 0.0))
-
-            put_packed(base + r, lambda t: lat[PACK * r + 8 * t : PACK * r + 8 * t + 8, :], halo)
-
-    for r in range(ROWS):
-        outs[PAD + r, :, 0:COLS] = own_m[r]
-
-    def closure_of(columns):
-        _, _, h2 = hidden_layers(split(to_48(columns, 1.0)), k1, k2, b2)
-        return last_layer(h2, k3, b3)
-
-    def halo_rows(first):
-        o = closure_of(jnp.concatenate([s0[first + i, 0:FEATS, 0:COLS] for i in range(8)], axis=1))
+            block.put(
+                base + r,
+                lambda t: lat[PACK * r + 8 * t : PACK * r + 8 * t + 8, :],
+                lambda t: pltpu.roll(corner[PACK + 40 + 8 * t : PACK + 48 + 8 * t, :], -REACH * r % COLS, 1),
+                lambda t: pltpu.roll(corner[8 * t : 8 * t + 8, :], -REACH * (r + 1) % COLS, 1),
+            )
+        near = {"swap": jnp.where(scal[2] == 1, PAD - 8, PAD + ROWS), "north": PAD - 8, "south": PAD + ROWS}
+        firsts.append(near[side])
+    columns = []
+    for first in firsts:
+        columns += [s0[first + i, 0:FEATS, 0:COLS] for i in range(8)] + [wide_pack(s0, first)]
+    o = closure_of(jnp.concatenate(columns, axis=1), *net_refs)
+    for g, first in enumerate(firsts):
         for i in range(8):
-            outs[first + i, :, 0:COLS] = o[:, i * COLS : (i + 1) * COLS]
-
-    if sides == ["swap"]:
-        groups = 3
-        halo_rows(jnp.where(has_south == 1, PAD - 8, PAD + ROWS))
-    else:
-        groups = 4
-        halo_rows(PAD - 8)
-        halo_rows(PAD + ROWS)
-    first = lo(8)
-    o = closure_of(jnp.concatenate([wide_pack(s0, first + 8 * g) for g in range(groups)], axis=1))
-    for g in range(groups):
-        wide_unpack(outs, first + 8 * g, o[:, g * COLS : (g + 1) * COLS])
-
-
-def first_section_kernel(scal, cs, fs, s0, masks, s1):
-    zero_walls(s1)
-    for_rows(scal, 10, section_1(Row(WIDE), cs, fs, masks, s0, s1))
-
-
-def second_section_kernel(scal, cs, fs, s0, s1, masks, s2):
-    zero_walls(s2)
-    for_rows(scal, 9, section_2(Row(WIDE), cs, fs, masks, s0, s1, s2))
+            at = (9 * g + i) * COLS
+            net[first + i, :, 0:COLS] = o[:, at : at + COLS]
+        at = (9 * g + 8) * COLS
+        wide_unpack(net, first, o[:, at : at + COLS])
+    for_outer(sides, scal, 1, 10, section_1(k, cs, fs, masks, s0, s1))
+    for_outer(sides, scal, 2, 9, section_2(k, cs, fs, masks, s0, s1, s2))
 
 
 def last_section_kernel(scal, cs, fs, sums, s3, t2, masks, fluxes, outs, final):
@@ -880,27 +910,14 @@
     )
     pack_corners = pl.pallas_call(
         lambda *refs: corner_kernel(sides, *refs),
-        out_shape=[sds(2 * PACK + 80, COLS)] * len(sides),
+        out_shape=[sds(CORNER + 8, COLS)] * len(sides),
         in_specs=[SMEM, VMEM, VMEM],
         out_specs=[VMEM] * len(sides),
         compiler_params=params(8),
         cost_estimate=pl.CostEstimate(flops=10**8, bytes_accessed=10**6, transcendentals=0),
         name="pack_corners",
     )
-    total, results = pair_rounds(
-        sums,
-        far_first((("lat", lat_n),)) + far_first((("lon", lon_n),))[::-1],
-        [
-            lambda done: packed[5:],
-            lambda done: own_closure(own, *raw),
-            lambda done: pack_corners(scal, from_west, from_east),
-        ],
-    )
-    lats = [lax.ppermute(pay, "lat", lat_pairs(side)) for side, pay in zip(sides, results[0])]
-    corners = [lax.ppermute(pay, "lat", lat_pairs(side)) for side, pay in zip(sides, results[2])]
-    received = [ref for pair in zip(lats, corners) for ref in pair]
-    own_m, own_h1, own_h2, k1, k2, k3, q1, q2, q3, b2, b3 = results[1]
-
+    lats = [lax.ppermute(pay, "lat", lat_pairs(side)) for side, pay in zip(sides, packed[5:])]
     geometry = (scal, cs, fs)
     state = sds(EXT, 56, WIDE)
     plain = sds(EXT, FEATS, WIDE)
@@ -920,14 +937,48 @@
             name=name,
         )(*geometry, *args)
 
-    s0, masks, fluxes, net = call(
-        lambda *refs: assemble_kernel(sides, *refs), "assemble",
-        [state, marks, sds(EXT, 8, WIDE), plain], [],
-        [own, own_m, from_west, from_east] + received + [k1, k2, k3, b2, b3],
-        2 * 10**9, 8,
+    own_m, own_h1, own_h2, k1, k2, k3, q1, q2, q3, b2, b3 = own_closure(own, *raw)
+    net_weights = [k1, k2, k3, b2, b3]
+    is_even = lax.axis_index("lon") % 2 == 0
+    theirs = jnp.where(is_even, from_east[SUMS:PACK, 0:1], from_west[SUMS:PACK, 0:1])
+    pair = sums + jnp.pad(jnp.broadcast_to(theirs, (PACK - SUMS, COLS)), ((0, 8 - PACK + SUMS), (0, 0)))
+
+    def own_sections(done):
+        s0, masks, fluxes, _ = done[0]
+        return call(first_own_kernel, "first_section_own", state, [], [s0, masks], 10**9, 8)
+
+    def own_second(done):
+        s0, masks, fluxes, _ = done[0]
+        s2 = call(second_own_kernel, "second_section_own", state, [], [s0, done[1], masks], 10**9, 8)
+        return s2, pack_corners(scal, from_west, from_east)
+
+    row_total, results = pair_rounds(
+        pair,
+        far_first((("lon", lon_n),))[:-1][::-1],
+        [
+            lambda done: call(
+                assemble_own_kernel, "assemble_own", [state, marks, sds(EXT, 8, WIDE), plain], [],
+                [own, own_m, from_west, from_east] + net_weights, 10**9, 8,
+            ),
+            own_sections,
+            own_second,
+        ],
     )
-    s1 = call(first_section_kernel, "first_section", state, [], [s0, masks], 10**9, 8)
-    s2 = call(second_section_kernel, "second_section", state, [], [s0, s1, masks], 10**9, 8)
+    (s0, masks, fluxes, net), s1, (s2, corner_pays) = results
+    corners = []
+    for side, pay in zip(sides, corner_pays):
+        pay = lax.dynamic_update_slice(pay, row_total, (CORNER, 0))
+        corners.append(lax.ppermute(pay, "lat", lat_pairs(side)))
+    if sides == ["swap"]:
+        total = row_total + corners[0][CORNER : CORNER + 8]
+    else:
+        total = lax.psum(row_total, "lat")
+    received = [ref for pair in zip(lats, corners) for ref in pair]
+    s0, s1, s2, masks, fluxes, net = call(
+        lambda *refs: halo_kernel(sides, *refs), "halo_rows",
+        [state, state, state, marks, sds(EXT, 8, WIDE), plain], [],
+        [s0, s1, s2, masks, fluxes, net] + received + net_weights, 2 * 10**9, 8,
+    )
     grads, top, abuf, from_closure, s3, t2, net_2 = call(
         lambda *refs: late_kernel(sides, *refs), "steps_and_adjoint",
         [sds(80, COLS), plain, plain, sds(ROWS, FEATS, COLS), state, state, plain],

time: 69.9 us -> 69.4 us (level)
  Pallas kernels: 35.1 us -> 36.4 us
  starting transfers between devices: 12.1 us -> 10.9 us
    ppermute x10 -> x8, waiting for transfers between devices: 19.7 us -> 13.6 us  [pair_rounds(): got = lax.ppermute(x, axis, [(j, j ^ step) for j in range(n)])]
    ppermute x0 -> x1, waiting for transfers between devices: none -> 3.15 us  [on_device(): corners.append(lax.ppermute(pay, 'lat', lat_pairs(side)))]
    ppermute x10 -> x8, starting transfers between devices: 5.3 us -> 2.41 us  [pair_rounds(): got = lax.ppermute(x, axis, [(j, j ^ step) for j in range(n)])]
    ppermute x1, waiting for transfers between devices: 0.01 us -> 2.67 us  [on_device(): from_west = lax.ppermute(east_pay, 'lon', east_ring)]
    ppermute x0 -> x1, starting transfers between devices: none -> 1.51 us  [on_device(): corners.append(lax.ppermute(pay, 'lat', lat_pairs(side)))]
    pallas_call x8 -> x9, Pallas kernels: 29.6 us -> 30.9 us  [call(): pl.pallas_call(kernel, out_shape=out_shape, in_specs=[SMEM] * 3 + [VMEM]...]
    ppermute x1, starting transfers between devices: 4.44 us -> 5.47 us  [on_device(): from_east = lax.ppermute(west_pay, 'lon', west_ring)]
    ppermute x2 -> x1, starting transfers between devices: 2.32 us -> 1.51 us  [on_device(): lax.ppermute(pay, 'lat', lat_pairs(side))]
  transfers between devices with their start and end apart: 14 -> 12, of which waited for: 9 -> 10; matrix products, arithmetic and copies ran while one was open for 1% -> 1% of each run, Pallas kernels for 15% -> 22%
where the time goes in v7:
time: 69.4 us; the launch traced here: 69.2 us
  Pallas kernels  36.4 us (52%)
  waiting for transfers between devices  19.4 us (28%)
  starting transfers between devices  10.9 us (16%)
  local copies, waits for them, and re-layouts  1.22 us (2%)
  between operations  0.89 us (1%)
    pallas_call x9, Pallas kernels, call(): pl.pallas_call(kernel, out_shape=out_shape, in_specs=[SMEM] * 3 + [VMEM]...  30.9 us
    ppermute x8, waiting for transfers between devices, pair_rounds(): got = lax.ppermute(x, axis, [(j, j ^ step) for j in range(n)])  13.6 us
    ppermute x1, starting transfers between devices, on_device(): from_east = lax.ppermute(west_pay, 'lon', west_ring)  5.47 us
    ppermute x1, waiting for transfers between devices, on_device(): corners.append(lax.ppermute(pay, 'lat', lat_pairs(side)))  3.15 us
    ppermute x1, waiting for transfers between devices, on_device(): from_west = lax.ppermute(east_pay, 'lon', east_ring)  2.67 us
    pallas_call x1, Pallas kernels, on_device(): pl.pallas_call(lambda *refs: pack_kernel(sides, *refs), out_shape=[sds(RO...  2.59 us
    ppermute x8, starting transfers between devices, pair_rounds(): got = lax.ppermute(x, axis, [(j, j ^ step) for j in range(n)])  2.41 us
    ppermute x1, starting transfers between devices, on_device(): lax.ppermute(pay, 'lat', lat_pairs(side))  1.51 us
  transfers between devices with their start and end apart: 12, of which 10 were waited for; matrix products, arithmetic and copies ran while one was open for 1% of the time, Pallas kernels for 22%

profile of v7, /device:TPU:0, one launch (start us, length us, event | category | flops | bytes accessed | tf_op | source)
XLA Modules:
  0.0 69.2 jit_solution(3152943101091533440)
XLA Ops:
  0.7 2.6 %pack_halos.1 = (f32[16,56,128]{2,1,0:T(8,128)}, f32[16,40,128]{2,1,0:T(8,128)}, f32[152,128]{1,0:T(8,128)}, f32[152,128]{1,0:T(8,128)}, f32[8,128]{1,0:T(8,128)}, /*index=5*/f32[856,128]{1,0:T(8,128)}) custom-call(f32[640,128]{1,0:T(8,128)} %bitcast.24, s32[160,128]{1,0:T(8,128)} %bitcast.26, f32[16,128]{1,0:T(8,128)} %refs_2_.2, f32[640,128]{1,0:T(8,128)} %bitcast.25), custom_call_target="tpu_custom_call" | custom-call | flops 1000000000 | bytes 3000000 | tf_op jit(solution)/shard_map/pack_halos/pallas_call | solution.py:858
  3.3 5.5 %collective-permute-start = (f32[152,128]{1,0:T(8,128)}, f32[152,128]{1,0:T(8,128)S(1)}, u32[]{:S(2)}, u32[]{:S(2)}) collective-permute-start(f32[152,128]{1,0:T(8,128)} %get-tuple-element.73), channel_id=1, source_target_pairs={{2,0},{4,2},{6,4},{8,6},{10,8},{12,10},{14,12},{16,14},{18,16},{20... | collective-permute-start | bytes 233480 | tf_op jit(solution)/shard_map/ppermute | solution.py:891
  8.8 1.5 %collective-permute-start.6 = (f32[856,128]{1,0:T(8,128)}, f32[856,128]{1,0:T(8,128)S(1)}, u32[]{:S(2)}, u32[]{:S(2)}) collective-permute-start(f32[856,128]{1,0:T(8,128)} %get-tuple-element.99), channel_id=1, source_target_pairs={{0,1},{1,0},{2,3},{3,2},{4,5},{5,4},{6,7},{7,6},{8,9},{9,8},{10,11... | collective-permute-start | bytes 1314824 | tf_op jit(solution)/shard_map/ppermute | solution.py:920
  11.6 1.2 %own_closure.1 = (f32[16,40,128]{2,1,0:T(8,128)S(1)}, f32[16,64,128]{2,1,0:T(8,128)S(1)}, f32[16,64,128]{2,1,0:T(8,128)S(1)}, bf16[64,144]{1,0:T(8,128)(2,1)S(1)...) custom-call(f32[16,56,128]{2,1,0:T(8,128)S(1)} %copy-done.5, ...), custom_call_target="tpu_custom_call" | custom-call | flops 1000000000 | bytes 2000000 | tf_op jit(solution)/shard_map/own_closure/pallas_call | solution.py:940
  12.8 2.7 %collective-permute-done.1.east.refs_1_.refs_13_ = f32[152,128]{1,0:T(8,128)S(1)} collective-permute-done((f32[152,128]{1,0:T(8,128)}, f32[152,128]{1,0:T(8,128)S(1)}, u32[]{:S(2)}, u32[]{:S(2)}) %collective-permute-start.1) | collective-permute-done | bytes 77856 | tf_op jit(solution)/shard_map/ppermute | solution.py:890
  15.7 1.5 %assemble_own.1 = (f32[48,56,256]{2,1,0:T(8,128)S(1)}, f32[48,16,256]{2,1,0:T(8,128)S(1)}, f32[48,8,256]{2,1,0:T(8,128)S(1)}, f32[48,40,256]{2,1,0:T(8,128)S(1)}) custom-call(s32[7]{0:T(128)S(1)} %stack.39.scal.refs_0_, f32[48]{0:T(128)S(1)} %get-tuple-element.138.cs.refs_1_, f32[48]{0:T(128)S(1)} %get-tuple-element.139.fs.refs_2_, ...), custom_call_target="tpu_custom_call" | custom-call | flops 1000000000 | bytes 10000000 | tf_op jit(solution)/shard_map/assemble_own/pallas_call | solution.py:929
  18.1 1.2 %collective-permute-done.2 = f32[8,128]{1,0:T(8,128)S(1)} collective-permute-done((f32[8,128]{1,0:T(8,128)S(1)}, f32[8,128]{1,0:T(8,128)S(1)}, u32[]{:S(2)}, u32[]{:S(2)}) %collective-permute-start.2) | collective-permute-done | bytes 4128 | tf_op jit(solution)/shard_map/ppermute | solution.py:818
  19.4 1.4 %first_section_own.1.s1.refs_4_ = f32[48,56,256]{2,1,0:T(8,128)S(1)} custom-call(s32[7]{0:T(128)S(1)} %stack.39.scal.refs_0_, f32[48]{0:T(128)S(1)} %get-tuple-element.138.cs.refs_1_, f32[48]{0:T(128)S(1)} %get-tuple-element.139.fs.refs_2_, f32[48,56,256]{2,1,0:T(8,128)S(1)} %get-tuple-element.87.s0.refs_3_, f32[48,16,256]{2,1,0:T(8,128)S(1)} %get-tuple-element.88.masks.refs_6_), custom_call_target="tpu_custom_call" | custom-call | flops 1000000000 | bytes 10000000 | tf_op jit(solution)/shard_map/first_section_own/pallas_call | solution.py:929
  20.8 2.2 %collective-permute-done.3 = f32[8,128]{1,0:T(8,128)S(1)} collective-permute-done((f32[8,128]{1,0:T(8,128)S(1)}, f32[8,128]{1,0:T(8,128)S(1)}, u32[]{:S(2)}, u32[]{:S(2)}) %collective-permute-start.3) | collective-permute-done | bytes 4128 | tf_op jit(solution)/shard_map/ppermute | solution.py:818
  23.0 1.4 %second_section_own.1.refs_5_ = f32[48,56,256]{2,1,0:T(8,128)S(1)} custom-call(s32[7]{0:T(128)S(1)} %stack.39.scal.refs_0_, f32[48]{0:T(128)S(1)} %get-tuple-element.138.cs.refs_1_, f32[48]{0:T(128)S(1)} %get-tuple-element.139.fs.refs_2_, f32[48,56,256]{2,1,0:T(8,128)S(1)} %get-tuple-element.87.s0.refs_3_, f32[48,56,256]{2,1,0:T(8,128)S(1)} %first_section_own.1.s1.refs_4_, ...), custom_call_target="tpu_custom_call" | custom-call | flops 1000000000 | bytes 10000000 | tf_op jit(solution)/shard_map/second_section_own/pallas_call | solution.py:929
  24.4 3.1 %collective-permute-done.4 = f32[8,128]{1,0:T(8,128)S(1)} collective-permute-done((f32[8,128]{1,0:T(8,128)S(1)}, f32[8,128]{1,0:T(8,128)S(1)}, u32[]{:S(2)}, u32[]{:S(2)}) %collective-permute-start.4) | collective-permute-done | bytes 4128 | tf_op jit(solution)/shard_map/ppermute | solution.py:818
  27.5 1.5 %collective-permute-start.5 = (f32[200,128]{1,0:T(8,128)S(1)}, f32[200,128]{1,0:T(8,128)S(1)}, u32[]{:S(2)}, u32[]{:S(2)}) collective-permute-start(f32[200,128]{1,0:T(8,128)S(1)} %get-tuple-element.136), channel_id=1, source_target_pairs={{0,1},{1,0},{2,3},{3,2},{4,5},{5,4},{6,7},{7,6},{8,9},{9,8},{10,11... | collective-permute-start | bytes 307208 | tf_op jit(solution)/shard_map/ppermute | solution.py:971
  29.0 3.2 %collective-permute-done.5.refs_10_.refs_16_ = f32[200,128]{1,0:T(8,128)S(1)} collective-permute-done((f32[200,128]{1,0:T(8,128)S(1)}, f32[200,128]{1,0:T(8,128)S(1)}, u32[]{:S(2)}, u32[]{:S(2)}) %collective-permute-start.5) | collective-permute-done | bytes 102432 | tf_op jit(solution)/shard_map/ppermute | solution.py:971
  32.2 2.9 %halo_rows.1 = (f32[48,56,256]{2,1,0:T(8,128)S(1)}, f32[48,56,256]{2,1,0:T(8,128)S(1)}, f32[48,56,256]{2,1,0:T(8,128)S(1)}, f32[48,16,256]{2,1,0:T(8,128)S(1)}, ...) custom-call(s32[7]{0:T(128)S(1)} %stack.39.scal.refs_0_, f32[48]{0:T(128)S(1)} %get-tuple-element.138.cs.refs_1_, ...), custom_call_target="tpu_custom_call" | custom-call | flops 2000000000 | bytes 10000000 | tf_op jit(solution)/shard_map/halo_rows/pallas_call | solution.py:929
  35.1 15.2 %steps_and_adjoint.1 = (f32[80,128]{1,0:T(8,128)S(1)}, f32[48,40,256]{2,1,0:T(8,128)S(1)}, f32[48,40,256]{2,1,0:T(8,128)S(1)}, f32[16,40,128]{2,1,0:T(8,128)S(1)...) custom-call(s32[7]{0:T(128)S(1)} %stack.39.scal.refs_0_, ...), custom_call_target="tpu_custom_call" | custom-call | flops 4000000000 | bytes 10000000 | tf_op jit(solution)/shard_map/steps_and_adjoint/pallas_call | solution.py:929
  50.3 2.0 %adjoint_third_section.1 = (f32[48,40,256]{2,1,0:T(8,128)S(1)}, f32[48,40,256]{2,1,0:T(8,128)S(1)}) custom-call(s32[7]{0:T(128)S(1)} %stack.39.scal.refs_0_, f32[48]{0:T(128)S(1)} %get-tuple-element.138.cs.refs_1_, f32[48]{0:T(128)S(1)} %get-tuple-element.139.fs.refs_2_, f32[48,56,256]{2,1,0:T(8,128)S(1)} %get-tuple-element.101.refs_9_.state, ...), custom_call_target="tpu_custom_call" | custom-call | flops 1000000000 | bytes 10000000 | tf_op jit(solution)/shard_map/adjoint_third_section/pallas_call | solution.py:929
  52.3 2.9 %collective-permute-done.7 = f32[80,128]{1,0:T(8,128)S(1)} collective-permute-done((f32[80,128]{1,0:T(8,128)S(1)}, f32[80,128]{1,0:T(8,128)S(1)}, u32[]{:S(2)}, u32[]{:S(2)}) %collective-permute-start.7) | collective-permute-done | bytes 40992 | tf_op jit(solution)/shard_map/ppermute | solution.py:818
  55.2 2.1 %adjoint_second_section.1 = (f32[48,40,256]{2,1,0:T(8,128)S(1)}, f32[48,40,256]{2,1,0:T(8,128)S(1)}) custom-call(s32[7]{0:T(128)S(1)} %stack.39.scal.refs_0_, f32[48]{0:T(128)S(1)} %get-tuple-element.138.cs.refs_1_, f32[48]{0:T(128)S(1)} %get-tuple-element.139.fs.refs_2_, f32[48,56,256]{2,1,0:T(8,128)S(1)} %get-tuple-element.114.state, ...), custom_call_target="tpu_custom_call" | custom-call | flops 1000000000 | bytes 10000000 | tf_op jit(solution)/shard_map/adjoint_second_section/pallas_call | solution.py:929
  57.3 1.9 %collective-permute-done.8 = f32[80,128]{1,0:T(8,128)S(1)} collective-permute-done((f32[80,128]{1,0:T(8,128)S(1)}, f32[80,128]{1,0:T(8,128)S(1)}, u32[]{:S(2)}, u32[]{:S(2)}) %collective-permute-start.8) | collective-permute-done | bytes 40992 | tf_op jit(solution)/shard_map/ppermute | solution.py:818
  59.2 1.5 %collective-permute-start.9 = (f32[80,128]{1,0:T(8,128)S(1)}, f32[80,128]{1,0:T(8,128)S(1)}, u32[]{:S(2)}, u32[]{:S(2)}) collective-permute-start(f32[80,128]{1,0:T(8,128)S(1)} %add.61), channel_id=1, source_target_pairs={{0,1},{1,0},{2,3},{3,2},{4,5},{5,4},{6,7},{7,6},{8,9},{9,8},{10,11... | collective-permute-start | bytes 122888 | tf_op jit(solution)/shard_map/ppermute | solution.py:818
  60.7 2.4 %adjoint_first_section.1 = f32[640,128]{1,0:T(8,128)} custom-call(s32[7]{0:T(128)S(1)} %stack.39.scal.refs_0_, f32[48]{0:T(128)S(1)} %get-tuple-element.138.cs.refs_1_, f32[48]{0:T(128)S(1)} %get-tuple-element.139.fs.refs_2_, f32[48,56,256]{2,1,0:T(8,128)S(1)} %get-tuple-element.100.refs_8_.state, f32[48,16,256]{2,1,0:T(8,128)S(1)} %get-tuple-element.102.refs_10_.masks, ...), custom_call_target="tpu_custom_call" | custom-call | flops 1000000000 | bytes 10000000 | tf_op jit(solution)/shard_map/adjoint_first_section/pallas_call | solution.py:929
  64.1 2.1 %last_section.1 = f32[640,128]{1,0:T(8,128)} custom-call(s32[7]{0:T(128)S(1)} %stack.39.scal.refs_0_, f32[48]{0:T(128)S(1)} %get-tuple-element.138.cs.refs_1_, f32[48]{0:T(128)S(1)} %get-tuple-element.139.fs.refs_2_, f32[8,128]{1,0:T(8,128)S(1)} %slice_add_fusion.refs_3_.sums, f32[48,56,256]{2,1,0:T(8,128)S(1)} %get-tuple-element.124.s3, ...), custom_call_target="tpu_custom_call" | custom-call | flops 1000000000 | bytes 10000000 | tf_op jit(solution)/shard_map/last_section/pallas_call | solution.py:929
  66.1 1.1 %collective-permute-done.10 = f32[80,128]{1,0:T(8,128)S(1)} collective-permute-done((f32[80,128]{1,0:T(8,128)S(1)}, f32[80,128]{1,0:T(8,128)S(1)}, u32[]{:S(2)}, u32[]{:S(2)}) %collective-permute-start.10) | collective-permute-done | bytes 40992 | tf_op jit(solution)/shard_map/ppermute | solution.py:818
  67.2 1.2 %collective-permute-done.11 = f32[80,128]{1,0:T(8,128)S(1)} collective-permute-done((f32[80,128]{1,0:T(8,128)S(1)}, f32[80,128]{1,0:T(8,128)S(1)}, u32[]{:S(2)}, u32[]{:S(2)}) %collective-permute-start.11) | collective-permute-done | bytes 40992 | tf_op jit(solution)/shard_map/ppermute | solution.py:818
  (48 shorter events, 4.3 us)
Async XLA Ops:
  0.6 9.7 %copy-start.8 = (f32[64,40]{0,1:T(8,128)S(1)}, f32[64,40]{0,1:T(8,128)}, u32[]{:S(2)}) copy-start(f32[64,40]{0,1:T(8,128)} %param.17) | copy-start | bytes 30724
  0.6 9.9 %copy-start.4 = (f32[40]{0:T(128)S(1)}, f32[40]{0:T(128)}, u32[]{:S(2)}) copy-start(f32[40]{0:T(128)} %param.18) | copy-start | bytes 484
  0.7 9.9 %copy-start.3 = (f32[64]{0:T(128)S(1)}, f32[64]{0:T(128)}, u32[]{:S(2)}) copy-start(f32[64]{0:T(128)} %param.16) | copy-start | bytes 772
  0.7 9.9 %copy-start = (f32[64,64]{1,0:T(8,128)S(1)}, f32[64,64]{1,0:T(8,128)}, u32[]{:S(2)}) copy-start(f32[64,64]{1,0:T(8,128)} %refs_1_.1) | copy-start | bytes 49156
  0.7 9.9 %copy-start.2 = (f32[64]{0:T(128)S(1)}, f32[64]{0:T(128)}, u32[]{:S(2)}) copy-start(f32[64]{0:T(128)} %param.14) | copy-start | bytes 772
  0.7 9.9 %copy-start.1 = (f32[40,64]{1,0:T(8,128)S(1)}, f32[40,64]{1,0:T(8,128)}, u32[]{:S(2)}) copy-start(f32[40,64]{1,0:T(8,128)} %refs_0_.1) | copy-start | bytes 30724
  3.3 12.3 %copy-start.9 = (f32[8,128]{1,0:T(8,128)S(1)}, f32[8,128]{1,0:T(8,128)}, u32[]{:S(2)}) copy-start(f32[8,128]{1,0:T(8,128)} %get-tuple-element.72) | copy-start | bytes 12292
  3.3 9.5 %collective-permute-start = (f32[152,128]{1,0:T(8,128)}, f32[152,128]{1,0:T(8,128)S(1)}, u32[]{:S(2)}, u32[]{:S(2)}) collective-permute-start(f32[152,128]{1,0:T(8,128)} %get-tuple-element.73), channel_id=1, source_target_pairs={{2,0},{4,2},{6,4},{8,6},{10,8},{12,10},{14,12},{16,14},{18,16},{20... | collective-permute-start | bytes 233480 | tf_op jit(solution)/shard_map/ppermute | solution.py:891
  8.8 6.7 %collective-permute-start.1 = (f32[152,128]{1,0:T(8,128)}, f32[152,128]{1,0:T(8,128)S(1)}, u32[]{:S(2)}, u32[]{:S(2)}) collective-permute-start(f32[152,128]{1,0:T(8,128)} %get-tuple-element.74), channel_id=1, source_target_pairs={{0,2},{2,4},{4,6},{6,8},{8,10},{10,12},{12,14},{14,16},{16,18},{18... | collective-permute-start | bytes 233480 | tf_op jit(solution)/shard_map/ppermute | solution.py:890
  8.8 23.4 %collective-permute-start.6 = (f32[856,128]{1,0:T(8,128)}, f32[856,128]{1,0:T(8,128)S(1)}, u32[]{:S(2)}, u32[]{:S(2)}) collective-permute-start(f32[856,128]{1,0:T(8,128)} %get-tuple-element.99), channel_id=1, source_target_pairs={{0,1},{1,0},{2,3},{3,2},{4,5},{5,4},{6,7},{7,6},{8,9},{9,8},{10,11... | collective-permute-start | bytes 1314824 | tf_op jit(solution)/shard_map/ppermute | solution.py:920
  10.5 1.0 %copy-start.5 = (f32[16,56,128]{2,1,0:T(8,128)S(1)}, f32[16,56,128]{2,1,0:T(8,128)}, u32[]{:S(2)}) copy-start(f32[16,56,128]{2,1,0:T(8,128)} %get-tuple-element.75.own.refs_4_) | copy-start | bytes 1376260
  15.7 3.6 %collective-permute-start.2 = (f32[8,128]{1,0:T(8,128)S(1)}, f32[8,128]{1,0:T(8,128)S(1)}, u32[]{:S(2)}, u32[]{:S(2)}) collective-permute-start(f32[8,128]{1,0:T(8,128)S(1)} %broadcast_add_fusion), channel_id=1, source_target_pairs={{0,4},{2,6},{4,0},{6,2},{8,12},{10,14},{12,8},{14,10},{16,20},{18,... | collective-permute-start | bytes 12296 | tf_op jit(solution)/shard_map/ppermute | solution.py:818
  19.4 3.6 %collective-permute-start.3 = (f32[8,128]{1,0:T(8,128)S(1)}, f32[8,128]{1,0:T(8,128)S(1)}, u32[]{:S(2)}, u32[]{:S(2)}) collective-permute-start(f32[8,128]{1,0:T(8,128)S(1)} %fusion.2), channel_id=1, source_target_pairs={{0,8},{2,10},{4,12},{6,14},{8,0},{10,2},{12,4},{14,6},{16,24},{18,... | collective-permute-start | bytes 12296 | tf_op jit(solution)/shard_map/ppermute | solution.py:818
  23.0 4.5 %collective-permute-start.4 = (f32[8,128]{1,0:T(8,128)S(1)}, f32[8,128]{1,0:T(8,128)S(1)}, u32[]{:S(2)}, u32[]{:S(2)}) collective-permute-start(f32[8,128]{1,0:T(8,128)S(1)} %add.57), channel_id=1, source_target_pairs={{0,16},{2,18},{4,20},{6,22},{8,24},{10,26},{12,28},{14,30},{16,0},... | collective-permute-start | bytes 12296 | tf_op jit(solution)/shard_map/ppermute | solution.py:818
  27.5 4.7 %collective-permute-start.5 = (f32[200,128]{1,0:T(8,128)S(1)}, f32[200,128]{1,0:T(8,128)S(1)}, u32[]{:S(2)}, u32[]{:S(2)}) collective-permute-start(f32[200,128]{1,0:T(8,128)S(1)} %get-tuple-element.136), channel_id=1, source_target_pairs={{0,1},{1,0},{2,3},{3,2},{4,5},{5,4},{6,7},{7,6},{8,9},{9,8},{10,11... | collective-permute-start | bytes 307208 | tf_op jit(solution)/shard_map/ppermute | solution.py:971
  32.2 2.9 %copy-start.6 = (f32[16,56,128]{2,1,0:T(8,128)S(1)}, f32[16,56,128]{2,1,0:T(8,128)}, u32[]{:S(2)}) copy-start(f32[16,56,128]{2,1,0:T(8,128)} %get-tuple-element.75.own.refs_4_) | copy-start | bytes 1376260
  32.2 2.9 %copy-start.7 = (f32[16,40,128]{2,1,0:T(8,128)S(1)}, f32[16,40,128]{2,1,0:T(8,128)}, u32[]{:S(2)}) copy-start(f32[16,40,128]{2,1,0:T(8,128)} %get-tuple-element.93.refs_5_) | copy-start | bytes 983044
  50.3 4.9 %collective-permute-start.7 = (f32[80,128]{1,0:T(8,128)S(1)}, f32[80,128]{1,0:T(8,128)S(1)}, u32[]{:S(2)}, u32[]{:S(2)}) collective-permute-start(f32[80,128]{1,0:T(8,128)S(1)} %get-tuple-element.108), channel_id=1, source_target_pairs={{0,16},{2,18},{4,20},{6,22},{8,24},{10,26},{12,28},{14,30},{16,0},... | collective-permute-start | bytes 122888 | tf_op jit(solution)/shard_map/ppermute | solution.py:818
  55.2 4.0 %collective-permute-start.8 = (f32[80,128]{1,0:T(8,128)S(1)}, f32[80,128]{1,0:T(8,128)S(1)}, u32[]{:S(2)}, u32[]{:S(2)}) collective-permute-start(f32[80,128]{1,0:T(8,128)S(1)} %add.60), channel_id=1, source_target_pairs={{0,8},{2,10},{4,12},{6,14},{8,0},{10,2},{12,4},{14,6},{16,24},{18,... | collective-permute-start | bytes 122888 | tf_op jit(solution)/shard_map/ppermute | solution.py:818
  59.2 4.0 %collective-permute-start.9 = (f32[80,128]{1,0:T(8,128)S(1)}, f32[80,128]{1,0:T(8,128)S(1)}, u32[]{:S(2)}, u32[]{:S(2)}) collective-permute-start(f32[80,128]{1,0:T(8,128)S(1)} %add.61), channel_id=1, source_target_pairs={{0,1},{1,0},{2,3},{3,2},{4,5},{5,4},{6,7},{7,6},{8,9},{9,8},{10,11... | collective-permute-start | bytes 122888 | tf_op jit(solution)/shard_map/ppermute | solution.py:818
  63.2 4.0 %collective-permute-start.10 = (f32[80,128]{1,0:T(8,128)S(1)}, f32[80,128]{1,0:T(8,128)S(1)}, u32[]{:S(2)}, u32[]{:S(2)}) collective-permute-start(f32[80,128]{1,0:T(8,128)S(1)} %add.62), channel_id=1, source_target_pairs={{0,4},{2,6},{4,0},{6,2},{8,12},{10,14},{12,8},{14,10},{16,20},{18,... | collective-permute-start | bytes 122888 | tf_op jit(solution)/shard_map/ppermute | solution.py:818
  67.2 1.2 %collective-permute-start.11 = (f32[80,128]{1,0:T(8,128)S(1)}, f32[80,128]{1,0:T(8,128)S(1)}, u32[]{:S(2)}, u32[]{:S(2)}) collective-permute-start(f32[80,128]{1,0:T(8,128)S(1)} %add.63), channel_id=1, source_target_pairs={{0,2},{2,0},{4,6},{6,4},{8,10},{10,8},{12,14},{14,12},{16,18},{18,... | collective-permute-start | bytes 122888 | tf_op jit(solution)/shard_map/ppermute | solution.py:818

commit v8 on v7

--- a/solution.py
+++ b/solution.py
@@ -23,7 +23,6 @@
 FEATS = 40
 HID = 64
 PACK = 56
-SUMS = 51
 STRIP = 2 * PACK + 40
 LAT_X = REACH * PACK
 CORNER = 2 * PACK + 80
@@ -92,7 +91,7 @@
         own[r, 48:49, :] = m8
         own[r, 49:50, :] = m9
         own[r, 50:51, :] = flux[r : r + 1, :]
-        own[r, SUMS:PACK, :] = sums[0:5, :]
+        own[r, 51:PACK, :] = jnp.zeros((5, COLS), F32)
     for half in range(2):
         for t in range(7):
             rows = [own[8 * half + s, 8 * t : 8 * t + 8, :] for s in range(8)]
@@ -937,38 +936,33 @@
             name=name,
         )(*geometry, *args)
 
-    own_m, own_h1, own_h2, k1, k2, k3, q1, q2, q3, b2, b3 = own_closure(own, *raw)
+
+    def last_round(done):
+        own_m, _, _, k1, k2, k3, _, _, _, b2, b3 = done[1]
+        blocks = call(
+            assemble_own_kernel, "assemble_own", [state, marks, sds(EXT, 8, WIDE), plain], [],
+            [own, own_m, from_west, from_east, k1, k2, k3, b2, b3], 10**9, 8,
+        )
+        return blocks, pack_corners(scal, from_west, from_east)
+
+    rounds = far_first((("lon", lon_n),))[::-1]
+    row_total, results = pair_rounds(
+        sums,
+        rounds,
+        [lambda done: sums, lambda done: own_closure(own, *raw)]
+        + [lambda done: sums] * (len(rounds) - 3)
+        + [last_round],
+    )
+    own_m, own_h1, own_h2, k1, k2, k3, q1, q2, q3, b2, b3 = results[1]
     net_weights = [k1, k2, k3, b2, b3]
-    is_even = lax.axis_index("lon") % 2 == 0
-    theirs = jnp.where(is_even, from_east[SUMS:PACK, 0:1], from_west[SUMS:PACK, 0:1])
-    pair = sums + jnp.pad(jnp.broadcast_to(theirs, (PACK - SUMS, COLS)), ((0, 8 - PACK + SUMS), (0, 0)))
-
-    def own_sections(done):
-        s0, masks, fluxes, _ = done[0]
-        return call(first_own_kernel, "first_section_own", state, [], [s0, masks], 10**9, 8)
-
-    def own_second(done):
-        s0, masks, fluxes, _ = done[0]
-        s2 = call(second_own_kernel, "second_section_own", state, [], [s0, done[1], masks], 10**9, 8)
-        return s2, pack_corners(scal, from_west, from_east)
-
-    row_total, results = pair_rounds(
-        pair,
-        far_first((("lon", lon_n),))[:-1][::-1],
-        [
-            lambda done: call(
-                assemble_own_kernel, "assemble_own", [state, marks, sds(EXT, 8, WIDE), plain], [],
-                [own, own_m, from_west, from_east] + net_weights, 10**9, 8,
-            ),
-            own_sections,
-            own_second,
-        ],
-    )
-    (s0, masks, fluxes, net), s1, (s2, corner_pays) = results
+    (s0, masks, fluxes, net), corner_pays = results[-1]
     corners = []
     for side, pay in zip(sides, corner_pays):
         pay = lax.dynamic_update_slice(pay, row_total, (CORNER, 0))
         corners.append(lax.ppermute(pay, "lat", lat_pairs(side)))
+    s1 = call(first_own_kernel, "first_section_own", state, [], [s0, masks], 10**9, 8)
+    s2 = call(second_own_kernel, "second_section_own", state, [], [s0, s1, masks], 10**9, 8)
+    corners, s2 = lax.optimization_barrier((corners, s2))
     if sides == ["swap"]:
         total = row_total + corners[0][CORNER : CORNER + 8]
     else:

time: 69.4 us -> 65.4 us (0.942)
  waiting for transfers between devices: 19.4 us -> 14.7 us
    ppermute x1, waiting for transfers between devices: 2.67 us -> 0.01 us  [on_device(): from_west = lax.ppermute(east_pay, 'lon', east_ring)]
    ppermute x1, waiting for transfers between devices: 3.15 us -> 1.27 us  [on_device(): corners.append(lax.ppermute(pay, 'lat', lat_pairs(side)))]
    ppermute x8 -> x9, starting transfers between devices: 2.41 us -> 3.58 us  [pair_rounds(): got = lax.ppermute(x, axis, [(j, j ^ step) for j in range(n)])]
    ppermute x1, starting transfers between devices: 1.51 us -> 0.53 us  [on_device(): corners.append(lax.ppermute(pay, 'lat', lat_pairs(side)))]
    ppermute x8 -> x9, waiting for transfers between devices: 13.6 us -> 13.4 us  [pair_rounds(): got = lax.ppermute(x, axis, [(j, j ^ step) for j in range(n)])]
  transfers between devices with their start and end apart: 12 -> 13, of which waited for: 10 -> 9; matrix products, arithmetic and copies ran while one was open for 1% -> 1% of each run, Pallas kernels for 22% -> 23%
where the time goes in v8:
time: 65.4 us; the launch traced here: 65.2 us
  Pallas kernels  36.4 us (56%)
  waiting for transfers between devices  14.7 us (22%)
  starting transfers between devices  11.3 us (17%)
  local copies, waits for them, and re-layouts  1.21 us (2%)
  between operations  0.86 us (1%)
  other arithmetic  0.79 us (1%)
    pallas_call x9, Pallas kernels, call(): pl.pallas_call(kernel, out_shape=out_shape, in_specs=[SMEM] * 3 + [VMEM]...  30.9 us
    ppermute x9, waiting for transfers between devices, pair_rounds(): got = lax.ppermute(x, axis, [(j, j ^ step) for j in range(n)])  13.4 us
    ppermute x1, starting transfers between devices, on_device(): from_east = lax.ppermute(west_pay, 'lon', west_ring)  5.58 us
    ppermute x9, starting transfers between devices, pair_rounds(): got = lax.ppermute(x, axis, [(j, j ^ step) for j in range(n)])  3.58 us
    pallas_call x1, Pallas kernels, on_device(): pl.pallas_call(lambda *refs: pack_kernel(sides, *refs), out_shape=[sds(RO...  2.6 us
    ppermute x1, starting transfers between devices, on_device(): lax.ppermute(pay, 'lat', lat_pairs(side))  1.5 us
  transfers between devices with their start and end apart: 13, of which 9 were waited for; matrix products, arithmetic and copies ran while one was open for 1% of the time, Pallas kernels for 23%

profile of v8, /device:TPU:0, one launch (start us, length us, event | category | flops | bytes accessed | tf_op | source)
XLA Modules:
  0.0 65.2 jit_solution(9117938731158213527)
XLA Ops:
  0.7 2.6 %pack_halos.1 = (f32[16,56,128]{2,1,0:T(8,128)}, f32[16,40,128]{2,1,0:T(8,128)}, f32[152,128]{1,0:T(8,128)}, f32[152,128]{1,0:T(8,128)}, f32[8,128]{1,0:T(8,128)}, /*index=5*/f32[856,128]{1,0:T(8,128)}) custom-call(f32[640,128]{1,0:T(8,128)} %bitcast.24, s32[160,128]{1,0:T(8,128)} %bitcast.26, f32[16,128]{1,0:T(8,128)} %refs_2_.2, f32[640,128]{1,0:T(8,128)} %bitcast.25), custom_call_target="tpu_custom_call" | custom-call | flops 1000000000 | bytes 3000000 | tf_op jit(solution)/shard_map/pack_halos/pallas_call | solution.py:857
  3.9 5.6 %collective-permute-start.5 = (f32[152,128]{1,0:T(8,128)}, f32[152,128]{1,0:T(8,128)S(1)}, u32[]{:S(2)}, u32[]{:S(2)}) collective-permute-start(f32[152,128]{1,0:T(8,128)} %get-tuple-element.102), channel_id=1, source_target_pairs={{2,0},{4,2},{6,4},{8,6},{10,8},{12,10},{14,12},{16,14},{18,16},{20... | collective-permute-start | bytes 233480 | tf_op jit(solution)/shard_map/ppermute | solution.py:890
  9.5 1.5 %collective-permute-start.7 = (f32[856,128]{1,0:T(8,128)}, f32[856,128]{1,0:T(8,128)S(1)}, u32[]{:S(2)}, u32[]{:S(2)}) collective-permute-start(f32[856,128]{1,0:T(8,128)} %get-tuple-element.123), channel_id=1, source_target_pairs={{0,1},{1,0},{2,3},{3,2},{4,5},{5,4},{6,7},{7,6},{8,9},{9,8},{10,11... | collective-permute-start | bytes 1314824 | tf_op jit(solution)/shard_map/ppermute | solution.py:919
  11.8 1.0 %copy-done.5 = f32[16,56,128]{2,1,0:T(8,128)S(1)} copy-done((f32[16,56,128]{2,1,0:T(8,128)S(1)}, f32[16,56,128]{2,1,0:T(8,128)}, u32[]{:S(2)}) %copy-start.5) | copy-done | bytes 458776
  12.8 1.3 %own_closure.1 = (f32[16,40,128]{2,1,0:T(8,128)S(1)}, f32[16,64,128]{2,1,0:T(8,128)S(1)}, f32[16,64,128]{2,1,0:T(8,128)S(1)}, bf16[64,144]{1,0:T(8,128)(2,1)S(1)...) custom-call(f32[16,56,128]{2,1,0:T(8,128)S(1)} %copy-done.5, ...), custom_call_target="tpu_custom_call" | custom-call | flops 1000000000 | bytes 2000000 | tf_op jit(solution)/shard_map/own_closure/pallas_call | solution.py:952
  14.1 1.3 %collective-permute-done.1 = f32[8,128]{1,0:T(8,128)S(1)} collective-permute-done((f32[8,128]{1,0:T(8,128)S(1)}, f32[8,128]{1,0:T(8,128)S(1)}, u32[]{:S(2)}, u32[]{:S(2)}) %collective-permute-start.1) | collective-permute-done | bytes 4128 | tf_op jit(solution)/shard_map/ppermute | solution.py:817
  15.5 3.4 %collective-permute-done.2 = f32[8,128]{1,0:T(8,128)S(1)} collective-permute-done((f32[8,128]{1,0:T(8,128)S(1)}, f32[8,128]{1,0:T(8,128)S(1)}, u32[]{:S(2)}, u32[]{:S(2)}) %collective-permute-start.2) | collective-permute-done | bytes 4128 | tf_op jit(solution)/shard_map/ppermute | solution.py:817
  19.6 1.5 %assemble_own.1 = (f32[48,56,256]{2,1,0:T(8,128)S(1)}, f32[48,16,256]{2,1,0:T(8,128)S(1)}, f32[48,8,256]{2,1,0:T(8,128)S(1)}, f32[48,40,256]{2,1,0:T(8,128)S(1)}) custom-call(s32[7]{0:T(128)S(1)} %stack.39.scal.refs_0_, f32[48]{0:T(128)S(1)} %get-tuple-element.162.cs.refs_1_, f32[48]{0:T(128)S(1)} %get-tuple-element.163.fs.refs_2_, ...), custom_call_target="tpu_custom_call" | custom-call | flops 1000000000 | bytes 10000000 | tf_op jit(solution)/shard_map/assemble_own/pallas_call | solution.py:928
  22.0 1.4 %collective-permute-done.3 = f32[8,128]{1,0:T(8,128)S(1)} collective-permute-done((f32[8,128]{1,0:T(8,128)S(1)}, f32[8,128]{1,0:T(8,128)S(1)}, u32[]{:S(2)}, u32[]{:S(2)}) %collective-permute-start.3) | collective-permute-done | bytes 4128 | tf_op jit(solution)/shard_map/ppermute | solution.py:817
  24.0 1.4 %first_section_own.1.s1.refs_4_ = f32[48,56,256]{2,1,0:T(8,128)S(1)} custom-call(s32[7]{0:T(128)S(1)} %stack.39.scal.refs_0_, f32[48]{0:T(128)S(1)} %get-tuple-element.162.cs.refs_1_, f32[48]{0:T(128)S(1)} %get-tuple-element.163.fs.refs_2_, f32[48,56,256]{2,1,0:T(8,128)S(1)} %get-tuple-element.114.s0.refs_3_, f32[48,16,256]{2,1,0:T(8,128)S(1)} %get-tuple-element.115.masks.refs_6_), custom_call_target="tpu_custom_call" | custom-call | flops 1000000000 | bytes 10000000 | tf_op jit(solution)/shard_map/first_section_own/pallas_call | solution.py:928
  25.4 1.4 %second_section_own.1.refs_5_ = f32[48,56,256]{2,1,0:T(8,128)S(1)} custom-call(s32[7]{0:T(128)S(1)} %stack.39.scal.refs_0_, f32[48]{0:T(128)S(1)} %get-tuple-element.162.cs.refs_1_, f32[48]{0:T(128)S(1)} %get-tuple-element.163.fs.refs_2_, f32[48,56,256]{2,1,0:T(8,128)S(1)} %get-tuple-element.114.s0.refs_3_, f32[48,56,256]{2,1,0:T(8,128)S(1)} %first_section_own.1.s1.refs_4_, ...), custom_call_target="tpu_custom_call" | custom-call | flops 1000000000 | bytes 10000000 | tf_op jit(solution)/shard_map/second_section_own/pallas_call | solution.py:928
  26.9 1.3 %collective-permute-done.6.refs_10_.refs_16_ = f32[200,128]{1,0:T(8,128)S(1)} collective-permute-done((f32[200,128]{1,0:T(8,128)S(1)}, f32[200,128]{1,0:T(8,128)S(1)}, u32[]{:S(2)}, u32[]{:S(2)}) %collective-permute-start.6) | collective-permute-done | bytes 102432 | tf_op jit(solution)/shard_map/ppermute | solution.py:962
  28.2 2.9 %halo_rows.1 = (f32[48,56,256]{2,1,0:T(8,128)S(1)}, f32[48,56,256]{2,1,0:T(8,128)S(1)}, f32[48,56,256]{2,1,0:T(8,128)S(1)}, f32[48,16,256]{2,1,0:T(8,128)S(1)}, ...) custom-call(s32[7]{0:T(128)S(1)} %stack.39.scal.refs_0_, f32[48]{0:T(128)S(1)} %get-tuple-element.162.cs.refs_1_, ...), custom_call_target="tpu_custom_call" | custom-call | flops 2000000000 | bytes 10000000 | tf_op jit(solution)/shard_map/halo_rows/pallas_call | solution.py:928
  31.1 15.1 %steps_and_adjoint.1 = (f32[80,128]{1,0:T(8,128)S(1)}, f32[48,40,256]{2,1,0:T(8,128)S(1)}, f32[48,40,256]{2,1,0:T(8,128)S(1)}, f32[16,40,128]{2,1,0:T(8,128)S(1)...) custom-call(s32[7]{0:T(128)S(1)} %stack.39.scal.refs_0_, ...), custom_call_target="tpu_custom_call" | custom-call | flops 4000000000 | bytes 10000000 | tf_op jit(solution)/shard_map/steps_and_adjoint/pallas_call | solution.py:928
  46.2 0.9 %collective-permute-start.8 = (f32[80,128]{1,0:T(8,128)S(1)}, f32[80,128]{1,0:T(8,128)S(1)}, u32[]{:S(2)}, u32[]{:S(2)}) collective-permute-start(f32[80,128]{1,0:T(8,128)S(1)} %get-tuple-element.132), channel_id=1, source_target_pairs={{0,16},{2,18},{4,20},{6,22},{8,24},{10,26},{12,28},{14,30},{16,0},... | collective-permute-start | bytes 122888 | tf_op jit(solution)/shard_map/ppermute | solution.py:817
  47.1 2.0 %adjoint_third_section.1 = (f32[48,40,256]{2,1,0:T(8,128)S(1)}, f32[48,40,256]{2,1,0:T(8,128)S(1)}) custom-call(s32[7]{0:T(128)S(1)} %stack.39.scal.refs_0_, f32[48]{0:T(128)S(1)} %get-tuple-element.162.cs.refs_1_, f32[48]{0:T(128)S(1)} %get-tuple-element.163.fs.refs_2_, f32[48,56,256]{2,1,0:T(8,128)S(1)} %get-tuple-element.125.refs_9_.state, ...), custom_call_target="tpu_custom_call" | custom-call | flops 1000000000 | bytes 10000000 | tf_op jit(solution)/shard_map/adjoint_third_section/pallas_call | solution.py:928
  49.2 2.0 %collective-permute-done.8 = f32[80,128]{1,0:T(8,128)S(1)} collective-permute-done((f32[80,128]{1,0:T(8,128)S(1)}, f32[80,128]{1,0:T(8,128)S(1)}, u32[]{:S(2)}, u32[]{:S(2)}) %collective-permute-start.8) | collective-permute-done | bytes 40992 | tf_op jit(solution)/shard_map/ppermute | solution.py:817
  51.3 2.1 %adjoint_second_section.1 = (f32[48,40,256]{2,1,0:T(8,128)S(1)}, f32[48,40,256]{2,1,0:T(8,128)S(1)}) custom-call(s32[7]{0:T(128)S(1)} %stack.39.scal.refs_0_, f32[48]{0:T(128)S(1)} %get-tuple-element.162.cs.refs_1_, f32[48]{0:T(128)S(1)} %get-tuple-element.163.fs.refs_2_, f32[48,56,256]{2,1,0:T(8,128)S(1)} %get-tuple-element.138.state, ...), custom_call_target="tpu_custom_call" | custom-call | flops 1000000000 | bytes 10000000 | tf_op jit(solution)/shard_map/adjoint_second_section/pallas_call | solution.py:928
  53.4 1.8 %collective-permute-done.9 = f32[80,128]{1,0:T(8,128)S(1)} collective-permute-done((f32[80,128]{1,0:T(8,128)S(1)}, f32[80,128]{1,0:T(8,128)S(1)}, u32[]{:S(2)}, u32[]{:S(2)}) %collective-permute-start.9) | collective-permute-done | bytes 40992 | tf_op jit(solution)/shard_map/ppermute | solution.py:817
  55.7 2.4 %adjoint_first_section.1 = f32[640,128]{1,0:T(8,128)} custom-call(s32[7]{0:T(128)S(1)} %stack.39.scal.refs_0_, f32[48]{0:T(128)S(1)} %get-tuple-element.162.cs.refs_1_, f32[48]{0:T(128)S(1)} %get-tuple-element.163.fs.refs_2_, f32[48,56,256]{2,1,0:T(8,128)S(1)} %get-tuple-element.124.refs_8_.state, f32[48,16,256]{2,1,0:T(8,128)S(1)} %get-tuple-element.126.refs_10_.masks, ...), custom_call_target="tpu_custom_call" | custom-call | flops 1000000000 | bytes 10000000 | tf_op jit(solution)/shard_map/adjoint_first_section/pallas_call | solution.py:928
  58.1 1.1 %collective-permute-done.10 = f32[80,128]{1,0:T(8,128)S(1)} collective-permute-done((f32[80,128]{1,0:T(8,128)S(1)}, f32[80,128]{1,0:T(8,128)S(1)}, u32[]{:S(2)}, u32[]{:S(2)}) %collective-permute-start.10) | collective-permute-done | bytes 40992 | tf_op jit(solution)/shard_map/ppermute | solution.py:817
  60.0 2.1 %last_section.1 = f32[640,128]{1,0:T(8,128)} custom-call(s32[7]{0:T(128)S(1)} %stack.39.scal.refs_0_, f32[48]{0:T(128)S(1)} %get-tuple-element.162.cs.refs_1_, f32[48]{0:T(128)S(1)} %get-tuple-element.163.fs.refs_2_, f32[8,128]{1,0:T(8,128)S(1)} %slice_add_fusion.refs_3_.sums, f32[48,56,256]{2,1,0:T(8,128)S(1)} %get-tuple-element.148.s3, ...), custom_call_target="tpu_custom_call" | custom-call | flops 1000000000 | bytes 10000000 | tf_op jit(solution)/shard_map/last_section/pallas_call | solution.py:928
  62.1 1.1 %collective-permute-done.11 = f32[80,128]{1,0:T(8,128)S(1)} collective-permute-done((f32[80,128]{1,0:T(8,128)S(1)}, f32[80,128]{1,0:T(8,128)S(1)}, u32[]{:S(2)}, u32[]{:S(2)}) %collective-permute-start.11) | collective-permute-done | bytes 40992 | tf_op jit(solution)/shard_map/ppermute | solution.py:817
  63.2 1.2 %collective-permute-done.12 = f32[80,128]{1,0:T(8,128)S(1)} collective-permute-done((f32[80,128]{1,0:T(8,128)S(1)}, f32[80,128]{1,0:T(8,128)S(1)}, u32[]{:S(2)}, u32[]{:S(2)}) %collective-permute-start.12) | collective-permute-done | bytes 40992 | tf_op jit(solution)/shard_map/ppermute | solution.py:817
  (46 shorter events, 5.9 us)
Async XLA Ops:
  0.6 10.3 %copy-start.8 = (f32[64,40]{0,1:T(8,128)S(1)}, f32[64,40]{0,1:T(8,128)}, u32[]{:S(2)}) copy-start(f32[64,40]{0,1:T(8,128)} %param.17) | copy-start | bytes 30724
  0.6 11.1 %copy-start.4 = (f32[40]{0:T(128)S(1)}, f32[40]{0:T(128)}, u32[]{:S(2)}) copy-start(f32[40]{0:T(128)} %param.18) | copy-start | bytes 484
  0.7 11.1 %copy-start.3 = (f32[64]{0:T(128)S(1)}, f32[64]{0:T(128)}, u32[]{:S(2)}) copy-start(f32[64]{0:T(128)} %param.16) | copy-start | bytes 772
  0.7 11.1 %copy-start = (f32[64,64]{1,0:T(8,128)S(1)}, f32[64,64]{1,0:T(8,128)}, u32[]{:S(2)}) copy-start(f32[64,64]{1,0:T(8,128)} %refs_1_.1) | copy-start | bytes 49156
  0.7 11.1 %copy-start.2 = (f32[64]{0:T(128)S(1)}, f32[64]{0:T(128)}, u32[]{:S(2)}) copy-start(f32[64]{0:T(128)} %param.14) | copy-start | bytes 772
  0.7 11.1 %copy-start.1 = (f32[40,64]{1,0:T(8,128)S(1)}, f32[40,64]{1,0:T(8,128)}, u32[]{:S(2)}) copy-start(f32[40,64]{1,0:T(8,128)} %refs_0_.1) | copy-start | bytes 30724
  3.3 7.7 %collective-permute-start = (f32[8,128]{1,0:T(8,128)}, f32[8,128]{1,0:T(8,128)S(1)}, u32[]{:S(2)}, u32[]{:S(2)}) collective-permute-start(f32[8,128]{1,0:T(8,128)} %get-tuple-element.84), channel_id=1, source_target_pairs={{0,2},{2,0},{4,6},{6,4},{8,10},{10,8},{12,14},{14,12},{16,18},{18,... | collective-permute-start | bytes 12296 | tf_op jit(solution)/shard_map/ppermute | solution.py:817
  3.8 15.8 %collective-permute-start.4 = (f32[152,128]{1,0:T(8,128)}, f32[152,128]{1,0:T(8,128)S(1)}, u32[]{:S(2)}, u32[]{:S(2)}) collective-permute-start(f32[152,128]{1,0:T(8,128)} %get-tuple-element.101), channel_id=1, source_target_pairs={{0,2},{2,4},{4,6},{6,8},{8,10},{10,12},{12,14},{14,16},{16,18},{18... | collective-permute-start | bytes 233480 | tf_op jit(solution)/shard_map/ppermute | solution.py:889
  3.9 15.7 %collective-permute-start.5 = (f32[152,128]{1,0:T(8,128)}, f32[152,128]{1,0:T(8,128)S(1)}, u32[]{:S(2)}, u32[]{:S(2)}) collective-permute-start(f32[152,128]{1,0:T(8,128)} %get-tuple-element.102), channel_id=1, source_target_pairs={{2,0},{4,2},{6,4},{8,6},{10,8},{12,10},{14,12},{16,14},{18,16},{20... | collective-permute-start | bytes 233480 | tf_op jit(solution)/shard_map/ppermute | solution.py:890
  9.5 18.7 %collective-permute-start.7 = (f32[856,128]{1,0:T(8,128)}, f32[856,128]{1,0:T(8,128)S(1)}, u32[]{:S(2)}, u32[]{:S(2)}) collective-permute-start(f32[856,128]{1,0:T(8,128)} %get-tuple-element.123), channel_id=1, source_target_pairs={{0,1},{1,0},{2,3},{3,2},{4,5},{5,4},{6,7},{7,6},{8,9},{9,8},{10,11... | collective-permute-start | bytes 1314824 | tf_op jit(solution)/shard_map/ppermute | solution.py:919
  11.7 3.6 %collective-permute-start.1 = (f32[8,128]{1,0:T(8,128)S(1)}, f32[8,128]{1,0:T(8,128)S(1)}, u32[]{:S(2)}, u32[]{:S(2)}) collective-permute-start(f32[8,128]{1,0:T(8,128)S(1)} %add.48), channel_id=1, source_target_pairs={{0,4},{2,6},{4,0},{6,2},{8,12},{10,14},{12,8},{14,10},{16,20},{18,... | collective-permute-start | bytes 12296 | tf_op jit(solution)/shard_map/ppermute | solution.py:817
  11.8 1.0 %copy-start.5 = (f32[16,56,128]{2,1,0:T(8,128)S(1)}, f32[16,56,128]{2,1,0:T(8,128)}, u32[]{:S(2)}) copy-start(f32[16,56,128]{2,1,0:T(8,128)} %get-tuple-element.86.own.refs_4_) | copy-start | bytes 1376260
  12.8 6.8 %copy-start.6 = (f32[16,56,128]{2,1,0:T(8,128)S(1)}, f32[16,56,128]{2,1,0:T(8,128)}, u32[]{:S(2)}) copy-start(f32[16,56,128]{2,1,0:T(8,128)} %get-tuple-element.86.own.refs_4_) | copy-start | bytes 1376260
  15.4 3.6 %collective-permute-start.2 = (f32[8,128]{1,0:T(8,128)S(1)}, f32[8,128]{1,0:T(8,128)S(1)}, u32[]{:S(2)}, u32[]{:S(2)}) collective-permute-start(f32[8,128]{1,0:T(8,128)S(1)} %add.49), channel_id=1, source_target_pairs={{0,8},{2,10},{4,12},{6,14},{8,0},{10,2},{12,4},{14,6},{16,24},{18,... | collective-permute-start | bytes 12296 | tf_op jit(solution)/shard_map/ppermute | solution.py:817
  19.0 4.5 %collective-permute-start.3 = (f32[8,128]{1,0:T(8,128)S(1)}, f32[8,128]{1,0:T(8,128)S(1)}, u32[]{:S(2)}, u32[]{:S(2)}) collective-permute-start(f32[8,128]{1,0:T(8,128)S(1)} %add.50), channel_id=1, source_target_pairs={{0,16},{2,18},{4,20},{6,22},{8,24},{10,26},{12,28},{14,30},{16,0},... | collective-permute-start | bytes 12296 | tf_op jit(solution)/shard_map/ppermute | solution.py:817
  23.5 4.7 %collective-permute-start.6 = (f32[200,128]{1,0:T(8,128)S(1)}, f32[200,128]{1,0:T(8,128)S(1)}, u32[]{:S(2)}, u32[]{:S(2)}) collective-permute-start(f32[200,128]{1,0:T(8,128)S(1)} %get-tuple-element.160), channel_id=1, source_target_pairs={{0,1},{1,0},{2,3},{3,2},{4,5},{5,4},{6,7},{7,6},{8,9},{9,8},{10,11... | collective-permute-start | bytes 307208 | tf_op jit(solution)/shard_map/ppermute | solution.py:962
  28.1 2.9 %copy-start.7 = (f32[16,40,128]{2,1,0:T(8,128)S(1)}, f32[16,40,128]{2,1,0:T(8,128)}, u32[]{:S(2)}) copy-start(f32[16,40,128]{2,1,0:T(8,128)} %get-tuple-element.117.refs_5_) | copy-start | bytes 983044
  46.2 5.0 %collective-permute-start.8 = (f32[80,128]{1,0:T(8,128)S(1)}, f32[80,128]{1,0:T(8,128)S(1)}, u32[]{:S(2)}, u32[]{:S(2)}) collective-permute-start(f32[80,128]{1,0:T(8,128)S(1)} %get-tuple-element.132), channel_id=1, source_target_pairs={{0,16},{2,18},{4,20},{6,22},{8,24},{10,26},{12,28},{14,30},{16,0},... | collective-permute-start | bytes 122888 | tf_op jit(solution)/shard_map/ppermute | solution.py:817
  51.2 4.0 %collective-permute-start.9 = (f32[80,128]{1,0:T(8,128)S(1)}, f32[80,128]{1,0:T(8,128)S(1)}, u32[]{:S(2)}, u32[]{:S(2)}) collective-permute-start(f32[80,128]{1,0:T(8,128)S(1)} %add.53), channel_id=1, source_target_pairs={{0,8},{2,10},{4,12},{6,14},{8,0},{10,2},{12,4},{14,6},{16,24},{18,... | collective-permute-start | bytes 122888 | tf_op jit(solution)/shard_map/ppermute | solution.py:817
  55.2 4.0 %collective-permute-start.10 = (f32[80,128]{1,0:T(8,128)S(1)}, f32[80,128]{1,0:T(8,128)S(1)}, u32[]{:S(2)}, u32[]{:S(2)}) collective-permute-start(f32[80,128]{1,0:T(8,128)S(1)} %add.54), channel_id=1, source_target_pairs={{0,1},{1,0},{2,3},{3,2},{4,5},{5,4},{6,7},{7,6},{8,9},{9,8},{10,11... | collective-permute-start | bytes 122888 | tf_op jit(solution)/shard_map/ppermute | solution.py:817
  59.2 4.0 %collective-permute-start.11 = (f32[80,128]{1,0:T(8,128)S(1)}, f32[80,128]{1,0:T(8,128)S(1)}, u32[]{:S(2)}, u32[]{:S(2)}) collective-permute-start(f32[80,128]{1,0:T(8,128)S(1)} %add.55), channel_id=1, source_target_pairs={{0,4},{2,6},{4,0},{6,2},{8,12},{10,14},{12,8},{14,10},{16,20},{18,... | collective-permute-start | bytes 122888 | tf_op jit(solution)/shard_map/ppermute | solution.py:817
  63.2 1.2 %collective-permute-start.12 = (f32[80,128]{1,0:T(8,128)S(1)}, f32[80,128]{1,0:T(8,128)S(1)}, u32[]{:S(2)}, u32[]{:S(2)}) collective-permute-start(f32[80,128]{1,0:T(8,128)S(1)} %add.56), channel_id=1, source_target_pairs={{0,2},{2,0},{4,6},{6,4},{8,10},{10,8},{12,14},{14,12},{16,18},{18,... | collective-permute-start | bytes 122888 | tf_op jit(solution)/shard_map/ppermute | solution.py:817

commit v9 on v8

--- a/solution.py
+++ b/solution.py
@@ -271,9 +271,11 @@
     for by in (1, 2, 4):
         press = press + jnp.where(k.sub >= by, pltpu.roll(press, by, 0), 0.0)
     ref[row, 40:48, :] = press
-    deep_8 = ref[row, 47:48, :] + (0.4 * ref[row, 33:34, :] - 0.1 * ref[row, 32:33, :])
-    ref[row, 48:49, :] = deep_8
-    ref[row, 49:50, :] = deep_8 + (0.4 * ref[row, 37:38, :] - 0.1 * ref[row, 36:37, :])
+    mixed = tiles[4]
+    over = lambda values, n: jnp.broadcast_to(values[n : n + 1, :], values.shape)
+    deep_8 = over(press, 7) + (0.4 * over(mixed, 1) - 0.1 * over(mixed, 0))
+    deep_9 = deep_8 + (0.4 * over(mixed, 5) - 0.1 * over(mixed, 4))
+    ref[row, 48:56, :] = jnp.where(k.low, deep_9, deep_8)
 
 
 def deep_pair(k, ref, row, upper, lower):
@@ -286,10 +288,6 @@
 
 def deep_v(k, ref, row):
     return deep_pair(k, ref, row, 35, 39)
-
-
-def deep_p(k, ref, row):
-    return deep_pair(k, ref, row, 48, 49)
 
 
 def east_of(q):
@@ -323,9 +321,9 @@
     p = tile(ref, row, 5)
     change[2] = change[2] + (f * v - half * (east_of(p) - west_of(p)))
     change[3] = change[3] - (f * u + 0.5 * (tile(ref, row + 1, 5) - tile(ref, row - 1, 5)))
-    p4 = deep_p(k, ref, row)
+    p4 = tile(ref, row, 6)
     fx = f * v4 - half * (east_of(p4) - west_of(p4))
-    fy = f * u4 + 0.5 * (deep_p(k, ref, row + 1) - deep_p(k, ref, row - 1))
+    fy = f * u4 + 0.5 * (tile(ref, row + 1, 6) - tile(ref, row - 1, 6))
     change[4] = change[4] + jnp.where(k.is_u, fx, jnp.where(k.is_v, -fy, 0.0))
     return change
 
@@ -397,8 +395,9 @@
     first = jnp.where(up == 1, low, high - TURN * turns)
 
     def turn(i, _):
-        for j in range(TURN):
-            body(first + TURN * i + j)
+        stores = [body(first + TURN * i + j) for j in range(TURN)]
+        for store in stores:
+            store()
         return 0
 
     lax.fori_loop(0, turns, turn, 0)
@@ -425,13 +424,17 @@
     return tile(ref, row, 1 if t == 4 else 0)
 
 
+def put_tiles(ref, row, tiles):
+    for t in range(5):
+        ref[row, 8 * t : 8 * t + 8, :] = tiles[t]
+
+
 def adjoint_third(k, scal, cs, fs, reach, state, masks, abuf, top, hold, bbuf):
     def body(r):
         d = adjoint_row(k, state, abuf, r, cs[r], fs[r])
-        for t in range(5):
-            ts = (2.0 / 3.0) * tile(top, r, t) + d[t]
-            hold[r, 8 * t : 8 * t + 8, :] = ts
-            bbuf[r, 8 * t : 8 * t + 8, :] = 0.0625 * mask_tile(masks, r, t) * ts
+        ts = [(2.0 / 3.0) * tile(top, r, t) + d[t] for t in range(5)]
+        masked = [0.0625 * mask_tile(masks, r, t) * ts[t] for t in range(5)]
+        return lambda: (put_tiles(hold, r, ts), put_tiles(bbuf, r, masked))
 
     for_rows(scal, reach, body)
 
@@ -439,11 +442,11 @@
 def adjoint_second(k, scal, cs, fs, reach, state, masks, bbuf, top, hold, left, abuf):
     def body(r):
         d = adjoint_row(k, state, bbuf, r, cs[r], fs[r])
-        for t in range(5):
-            ts = tile(hold, r, t)
-            tf = 0.25 * ts + d[t]
-            left[r, 8 * t : 8 * t + 8, :] = (1.0 / 3.0) * tile(top, r, t) + 0.75 * ts + tf
-            abuf[r, 8 * t : 8 * t + 8, :] = 0.25 * mask_tile(masks, r, t) * tf
+        ts = [tile(hold, r, t) for t in range(5)]
+        tf = [0.25 * ts[t] + d[t] for t in range(5)]
+        new = [(1.0 / 3.0) * tile(top, r, t) + 0.75 * ts[t] + tf[t] for t in range(5)]
+        masked = [0.25 * mask_tile(masks, r, t) * tf[t] for t in range(5)]
+        return lambda: (put_tiles(left, r, new), put_tiles(abuf, r, masked))
 
     for_rows(scal, reach, body)
 
@@ -451,7 +454,7 @@
 def adjoint_first(k, scal, cs, fs, reach, state, abuf, left, store):
     def body(r):
         d = adjoint_row(k, state, abuf, r, cs[r], fs[r])
-        store(r, [tile(left, r, t) + d[t] for t in range(5)])
+        return store(r, [tile(left, r, t) + d[t] for t in range(5)])
 
     for_rows(scal, reach, body)
 
@@ -476,23 +479,21 @@
 def section_1(k, cs, fs, masks, src, dst):
     def body(r):
         d = tendency_row(k, src, r, cs[r], fs[r])
-        put_state(
-            k, dst, r,
-            [tile(src, r, t) + 0.25 * mask_tile(masks, r, t) * d[t] for t in range(5)],
-        )
+        new = [tile(src, r, t) + 0.25 * mask_tile(masks, r, t) * d[t] for t in range(5)]
+        return lambda: put_state(k, dst, r, new)
+
     return body
+
 
 def section_2(k, cs, fs, masks, src, mid, dst):
     def body(r):
         d = tendency_row(k, mid, r, cs[r], fs[r])
-        put_state(
-            k, dst, r,
-            [
-                0.75 * tile(src, r, t) + 0.25 * tile(mid, r, t)
-                + 0.0625 * mask_tile(masks, r, t) * d[t]
-                for t in range(5)
-            ],
-        )
+        new = [
+            0.75 * tile(src, r, t) + 0.25 * tile(mid, r, t) + 0.0625 * mask_tile(masks, r, t) * d[t]
+            for t in range(5)
+        ]
+        return lambda: put_state(k, dst, r, new)
+
     return body
 
 
@@ -613,7 +614,7 @@
 
     def last(r):
         new = section_3(k, cs, fs, masks, fluxes, mean, s3, t2, outs, r)
-        put_result(final, r - PAD, [x[:, 0:COLS] for x in new])
+        return lambda: put_result(final, r - PAD, [x[:, 0:COLS] for x in new])
 
     for_rows(scal, 0, last)
 
@@ -663,7 +664,8 @@
         put_state(k, s3, r, section_3(s0, s2, r))
 
     def step_1_end(r):
-        put_state(k, s3, r, section_3(k, cs, fs, masks, fluxes, mean, s0, s2, outs_in, r))
+        new = section_3(k, cs, fs, masks, fluxes, mean, s0, s2, outs_in, r)
+        return lambda: put_state(k, s3, r, new)
 
     for_rows(scal, 8, step_1_end)
 
@@ -693,9 +695,9 @@
         return jnp.concatenate(parts, axis=0)
 
     def mask_cot(r):
-        for t in range(5):
-            bbuf[r, 8 * t : 8 * t + 8, :] = 0.25 * mask_tile(masks, r, t) * tile(cot, r, t)
-            abuf[r, 8 * t : 8 * t + 8, :] = (1.0 / 6.0) * mask_tile(masks, r, t) * tile(cot, r, t)
+        seen = [mask_tile(masks, r, t) * tile(cot, r, t) for t in range(5)]
+        quarter, sixth = [0.25 * x for x in seen], [(1.0 / 6.0) * x for x in seen]
+        return lambda: (put_tiles(bbuf, r, quarter), put_tiles(abuf, r, sixth))
 
     for_rows(scal, 6, mask_cot)
 
@@ -727,8 +729,8 @@
     for_rows(scal, 6, section_2(k, cs, fs, masks, s3, t1, t2))
 
     def store(r, tiles):
-        for t in range(5):
-            s4[r, 8 * t : 8 * t + 8, :] = tiles[t] + tile(gz, r, t)
+        new = [tiles[t] + tile(gz, r, t) for t in range(5)]
+        return lambda: put_tiles(s4, r, new)
 
     adjoint_third(k, scal, cs, fs, 5, t2, masks, abuf, cot, hold, bbuf)
     adjoint_second(k, scal, cs, fs, 4, t1, masks, bbuf, cot, hold, left, abuf)
@@ -747,8 +749,8 @@
     zero_walls(abuf)
 
     def mask_top(r):
-        for t in range(5):
-            abuf[r, 8 * t : 8 * t + 8, :] = (1.0 / 6.0) * mask_tile(masks, r, t) * tile(s4, r, t)
+        new = [(1.0 / 6.0) * mask_tile(masks, r, t) * tile(s4, r, t) for t in range(5)]
+        return lambda: put_tiles(abuf, r, new)
 
     for_rows(scal, 3, mask_top)
     grads[...] = jnp.zeros(grads.shape, F32)
@@ -784,7 +786,7 @@
         for t in range(5):
             m = masks[r, 8:16, 0:COLS] if t == 4 else masks[r, 0:8, 0:COLS]
             done.append(m * (tiles[t][:, 0:COLS] + from_closure[r - PAD, 8 * t : 8 * t + 8, :]))
-        put_result(grad, r - PAD, done)
+        return lambda: put_result(grad, r - PAD, done)
 
     adjoint_first(Row(WIDE), scal, cs, fs, 0, state, abuf, left, store)
 

time: 65.4 us -> 65.2 us (level)
  no operation moved by 1% of the time
where the time goes in v9:
time: 65.2 us; the launch traced here: 65 us
  Pallas kernels  36.1 us (55%)
  waiting for transfers between devices  14.8 us (23%)
  starting transfers between devices  11.2 us (17%)
  local copies, waits for them, and re-layouts  1.21 us (2%)
  between operations  0.86 us (1%)
  other arithmetic  0.79 us (1%)
    pallas_call x9, Pallas kernels, call(): pl.pallas_call(kernel, out_shape=out_shape, in_specs=[SMEM] * 3 + [VMEM]...  30.6 us
    ppermute x9, waiting for transfers between devices, pair_rounds(): got = lax.ppermute(x, axis, [(j, j ^ step) for j in range(n)])  13.5 us
    ppermute x1, starting transfers between devices, on_device(): from_east = lax.ppermute(west_pay, 'lon', west_ring)  5.58 us
    ppermute x9, starting transfers between devices, pair_rounds(): got = lax.ppermute(x, axis, [(j, j ^ step) for j in range(n)])  3.57 us
    pallas_call x1, Pallas kernels, on_device(): pl.pallas_call(lambda *refs: pack_kernel(sides, *refs), out_shape=[sds(RO...  2.6 us
    ppermute x1, starting transfers between devices, on_device(): lax.ppermute(pay, 'lat', lat_pairs(side))  1.5 us
    ppermute x1, waiting for transfers between devices, on_device(): corners.append(lax.ppermute(pay, 'lat', lat_pairs(side)))  1.33 us
  transfers between devices with their start and end apart: 13, of which 9 were waited for; matrix products, arithmetic and copies ran while one was open for 1% of the time, Pallas kernels for 23%

profile of v9, /device:TPU:0, one launch (start us, length us, event | category | flops | bytes accessed | tf_op | source)
XLA Modules:
  0.0 65.0 jit_solution(2123253260014049029)
XLA Ops:
  0.7 2.6 %pack_halos.1 = (f32[16,56,128]{2,1,0:T(8,128)}, f32[16,40,128]{2,1,0:T(8,128)}, f32[152,128]{1,0:T(8,128)}, f32[152,128]{1,0:T(8,128)}, f32[8,128]{1,0:T(8,128)}, /*index=5*/f32[856,128]{1,0:T(8,128)}) custom-call(f32[640,128]{1,0:T(8,128)} %bitcast.24, s32[160,128]{1,0:T(8,128)} %bitcast.26, f32[16,128]{1,0:T(8,128)} %refs_2_.2, f32[640,128]{1,0:T(8,128)} %bitcast.25), custom_call_target="tpu_custom_call" | custom-call | flops 1000000000 | bytes 3000000 | tf_op jit(solution)/shard_map/pack_halos/pallas_call | solution.py:859
  3.9 5.6 %collective-permute-start.5 = (f32[152,128]{1,0:T(8,128)}, f32[152,128]{1,0:T(8,128)S(1)}, u32[]{:S(2)}, u32[]{:S(2)}) collective-permute-start(f32[152,128]{1,0:T(8,128)} %get-tuple-element.102), channel_id=1, source_target_pairs={{2,0},{4,2},{6,4},{8,6},{10,8},{12,10},{14,12},{16,14},{18,16},{20... | collective-permute-start | bytes 233480 | tf_op jit(solution)/shard_map/ppermute | solution.py:892
  9.5 1.5 %collective-permute-start.7 = (f32[856,128]{1,0:T(8,128)}, f32[856,128]{1,0:T(8,128)S(1)}, u32[]{:S(2)}, u32[]{:S(2)}) collective-permute-start(f32[856,128]{1,0:T(8,128)} %get-tuple-element.123), channel_id=1, source_target_pairs={{0,1},{1,0},{2,3},{3,2},{4,5},{5,4},{6,7},{7,6},{8,9},{9,8},{10,11... | collective-permute-start | bytes 1314824 | tf_op jit(solution)/shard_map/ppermute | solution.py:921
  11.8 1.0 %copy-done.5 = f32[16,56,128]{2,1,0:T(8,128)S(1)} copy-done((f32[16,56,128]{2,1,0:T(8,128)S(1)}, f32[16,56,128]{2,1,0:T(8,128)}, u32[]{:S(2)}) %copy-start.5) | copy-done | bytes 458776
  12.8 1.3 %own_closure.1 = (f32[16,40,128]{2,1,0:T(8,128)S(1)}, f32[16,64,128]{2,1,0:T(8,128)S(1)}, f32[16,64,128]{2,1,0:T(8,128)S(1)}, bf16[64,144]{1,0:T(8,128)(2,1)S(1)...) custom-call(f32[16,56,128]{2,1,0:T(8,128)S(1)} %copy-done.5, ...), custom_call_target="tpu_custom_call" | custom-call | flops 1000000000 | bytes 2000000 | tf_op jit(solution)/shard_map/own_closure/pallas_call | solution.py:954
  14.1 1.3 %collective-permute-done.1 = f32[8,128]{1,0:T(8,128)S(1)} collective-permute-done((f32[8,128]{1,0:T(8,128)S(1)}, f32[8,128]{1,0:T(8,128)S(1)}, u32[]{:S(2)}, u32[]{:S(2)}) %collective-permute-start.1) | collective-permute-done | bytes 4128 | tf_op jit(solution)/shard_map/ppermute | solution.py:819
  15.5 3.4 %collective-permute-done.2 = f32[8,128]{1,0:T(8,128)S(1)} collective-permute-done((f32[8,128]{1,0:T(8,128)S(1)}, f32[8,128]{1,0:T(8,128)S(1)}, u32[]{:S(2)}, u32[]{:S(2)}) %collective-permute-start.2) | collective-permute-done | bytes 4128 | tf_op jit(solution)/shard_map/ppermute | solution.py:819
  19.6 1.5 %assemble_own.1 = (f32[48,56,256]{2,1,0:T(8,128)S(1)}, f32[48,16,256]{2,1,0:T(8,128)S(1)}, f32[48,8,256]{2,1,0:T(8,128)S(1)}, f32[48,40,256]{2,1,0:T(8,128)S(1)}) custom-call(s32[7]{0:T(128)S(1)} %stack.39.scal.refs_0_, f32[48]{0:T(128)S(1)} %get-tuple-element.162.cs.refs_1_, f32[48]{0:T(128)S(1)} %get-tuple-element.163.fs.refs_2_, ...), custom_call_target="tpu_custom_call" | custom-call | flops 1000000000 | bytes 10000000 | tf_op jit(solution)/shard_map/assemble_own/pallas_call | solution.py:930
  21.1 0.9 %pack_corners.1 = f32[200,128]{1,0:T(8,128)S(1)} custom-call(s32[7]{0:T(128)S(1)} %stack.39.scal.refs_0_, f32[152,128]{1,0:T(8,128)S(1)} %collective-permute-done.4.east.refs_1_.refs_13_, f32[152,128]{1,0:T(8,128)S(1)} %collective-permute-done.5.west.refs_2_.refs_14_), custom_call_target="tpu_custom_call" | custom-call | flops 100000000 | bytes 1000000 | tf_op jit(solution)/shard_map/pack_corners/pallas_call | solution.py:948
  22.0 1.5 %collective-permute-done.3 = f32[8,128]{1,0:T(8,128)S(1)} collective-permute-done((f32[8,128]{1,0:T(8,128)S(1)}, f32[8,128]{1,0:T(8,128)S(1)}, u32[]{:S(2)}, u32[]{:S(2)}) %collective-permute-start.3) | collective-permute-done | bytes 4128 | tf_op jit(solution)/shard_map/ppermute | solution.py:819
  24.0 1.4 %first_section_own.1.s1.refs_4_ = f32[48,56,256]{2,1,0:T(8,128)S(1)} custom-call(s32[7]{0:T(128)S(1)} %stack.39.scal.refs_0_, f32[48]{0:T(128)S(1)} %get-tuple-element.162.cs.refs_1_, f32[48]{0:T(128)S(1)} %get-tuple-element.163.fs.refs_2_, f32[48,56,256]{2,1,0:T(8,128)S(1)} %get-tuple-element.114.s0.refs_3_, f32[48,16,256]{2,1,0:T(8,128)S(1)} %get-tuple-element.115.masks.refs_6_), custom_call_target="tpu_custom_call" | custom-call | flops 1000000000 | bytes 10000000 | tf_op jit(solution)/shard_map/first_section_own/pallas_call | solution.py:930
  25.4 1.4 %second_section_own.1.refs_5_ = f32[48,56,256]{2,1,0:T(8,128)S(1)} custom-call(s32[7]{0:T(128)S(1)} %stack.39.scal.refs_0_, f32[48]{0:T(128)S(1)} %get-tuple-element.162.cs.refs_1_, f32[48]{0:T(128)S(1)} %get-tuple-element.163.fs.refs_2_, f32[48,56,256]{2,1,0:T(8,128)S(1)} %get-tuple-element.114.s0.refs_3_, f32[48,56,256]{2,1,0:T(8,128)S(1)} %first_section_own.1.s1.refs_4_, ...), custom_call_target="tpu_custom_call" | custom-call | flops 1000000000 | bytes 10000000 | tf_op jit(solution)/shard_map/second_section_own/pallas_call | solution.py:930
  26.8 1.3 %collective-permute-done.6.refs_10_.refs_16_ = f32[200,128]{1,0:T(8,128)S(1)} collective-permute-done((f32[200,128]{1,0:T(8,128)S(1)}, f32[200,128]{1,0:T(8,128)S(1)}, u32[]{:S(2)}, u32[]{:S(2)}) %collective-permute-start.6) | collective-permute-done | bytes 102432 | tf_op jit(solution)/shard_map/ppermute | solution.py:964
  28.2 2.9 %halo_rows.1 = (f32[48,56,256]{2,1,0:T(8,128)S(1)}, f32[48,56,256]{2,1,0:T(8,128)S(1)}, f32[48,56,256]{2,1,0:T(8,128)S(1)}, f32[48,16,256]{2,1,0:T(8,128)S(1)}, ...) custom-call(s32[7]{0:T(128)S(1)} %stack.39.scal.refs_0_, f32[48]{0:T(128)S(1)} %get-tuple-element.162.cs.refs_1_, ...), custom_call_target="tpu_custom_call" | custom-call | flops 2000000000 | bytes 10000000 | tf_op jit(solution)/shard_map/halo_rows/pallas_call | solution.py:930
  31.0 15.0 %steps_and_adjoint.1 = (f32[80,128]{1,0:T(8,128)S(1)}, f32[48,40,256]{2,1,0:T(8,128)S(1)}, f32[48,40,256]{2,1,0:T(8,128)S(1)}, f32[16,40,128]{2,1,0:T(8,128)S(1)...) custom-call(s32[7]{0:T(128)S(1)} %stack.39.scal.refs_0_, ...), custom_call_target="tpu_custom_call" | custom-call | flops 4000000000 | bytes 10000000 | tf_op jit(solution)/shard_map/steps_and_adjoint/pallas_call | solution.py:930
  46.9 2.0 %adjoint_third_section.1 = (f32[48,40,256]{2,1,0:T(8,128)S(1)}, f32[48,40,256]{2,1,0:T(8,128)S(1)}) custom-call(s32[7]{0:T(128)S(1)} %stack.39.scal.refs_0_, f32[48]{0:T(128)S(1)} %get-tuple-element.162.cs.refs_1_, f32[48]{0:T(128)S(1)} %get-tuple-element.163.fs.refs_2_, f32[48,56,256]{2,1,0:T(8,128)S(1)} %get-tuple-element.125.refs_9_.state, ...), custom_call_target="tpu_custom_call" | custom-call | flops 1000000000 | bytes 10000000 | tf_op jit(solution)/shard_map/adjoint_third_section/pallas_call | solution.py:930
  48.9 2.1 %collective-permute-done.8 = f32[80,128]{1,0:T(8,128)S(1)} collective-permute-done((f32[80,128]{1,0:T(8,128)S(1)}, f32[80,128]{1,0:T(8,128)S(1)}, u32[]{:S(2)}, u32[]{:S(2)}) %collective-permute-start.8) | collective-permute-done | bytes 40992 | tf_op jit(solution)/shard_map/ppermute | solution.py:819
  51.1 2.1 %adjoint_second_section.1 = (f32[48,40,256]{2,1,0:T(8,128)S(1)}, f32[48,40,256]{2,1,0:T(8,128)S(1)}) custom-call(s32[7]{0:T(128)S(1)} %stack.39.scal.refs_0_, f32[48]{0:T(128)S(1)} %get-tuple-element.162.cs.refs_1_, f32[48]{0:T(128)S(1)} %get-tuple-element.163.fs.refs_2_, f32[48,56,256]{2,1,0:T(8,128)S(1)} %get-tuple-element.138.state, ...), custom_call_target="tpu_custom_call" | custom-call | flops 1000000000 | bytes 10000000 | tf_op jit(solution)/shard_map/adjoint_second_section/pallas_call | solution.py:930
  53.2 1.8 %collective-permute-done.9 = f32[80,128]{1,0:T(8,128)S(1)} collective-permute-done((f32[80,128]{1,0:T(8,128)S(1)}, f32[80,128]{1,0:T(8,128)S(1)}, u32[]{:S(2)}, u32[]{:S(2)}) %collective-permute-start.9) | collective-permute-done | bytes 40992 | tf_op jit(solution)/shard_map/ppermute | solution.py:819
  55.5 2.3 %adjoint_first_section.1 = f32[640,128]{1,0:T(8,128)} custom-call(s32[7]{0:T(128)S(1)} %stack.39.scal.refs_0_, f32[48]{0:T(128)S(1)} %get-tuple-element.162.cs.refs_1_, f32[48]{0:T(128)S(1)} %get-tuple-element.163.fs.refs_2_, f32[48,56,256]{2,1,0:T(8,128)S(1)} %get-tuple-element.124.refs_8_.state, f32[48,16,256]{2,1,0:T(8,128)S(1)} %get-tuple-element.126.refs_10_.masks, ...), custom_call_target="tpu_custom_call" | custom-call | flops 1000000000 | bytes 10000000 | tf_op jit(solution)/shard_map/adjoint_first_section/pallas_call | solution.py:930
  57.9 1.1 %collective-permute-done.10 = f32[80,128]{1,0:T(8,128)S(1)} collective-permute-done((f32[80,128]{1,0:T(8,128)S(1)}, f32[80,128]{1,0:T(8,128)S(1)}, u32[]{:S(2)}, u32[]{:S(2)}) %collective-permute-start.10) | collective-permute-done | bytes 40992 | tf_op jit(solution)/shard_map/ppermute | solution.py:819
  59.8 2.1 %last_section.1 = f32[640,128]{1,0:T(8,128)} custom-call(s32[7]{0:T(128)S(1)} %stack.39.scal.refs_0_, f32[48]{0:T(128)S(1)} %get-tuple-element.162.cs.refs_1_, f32[48]{0:T(128)S(1)} %get-tuple-element.163.fs.refs_2_, f32[8,128]{1,0:T(8,128)S(1)} %slice_add_fusion.refs_3_.sums, f32[48,56,256]{2,1,0:T(8,128)S(1)} %get-tuple-element.148.s3, ...), custom_call_target="tpu_custom_call" | custom-call | flops 1000000000 | bytes 10000000 | tf_op jit(solution)/shard_map/last_section/pallas_call | solution.py:930
  61.9 1.1 %collective-permute-done.11 = f32[80,128]{1,0:T(8,128)S(1)} collective-permute-done((f32[80,128]{1,0:T(8,128)S(1)}, f32[80,128]{1,0:T(8,128)S(1)}, u32[]{:S(2)}, u32[]{:S(2)}) %collective-permute-start.11) | collective-permute-done | bytes 40992 | tf_op jit(solution)/shard_map/ppermute | solution.py:819
  63.0 1.2 %collective-permute-done.12 = f32[80,128]{1,0:T(8,128)S(1)} collective-permute-done((f32[80,128]{1,0:T(8,128)S(1)}, f32[80,128]{1,0:T(8,128)S(1)}, u32[]{:S(2)}, u32[]{:S(2)}) %collective-permute-start.12) | collective-permute-done | bytes 40992 | tf_op jit(solution)/shard_map/ppermute | solution.py:819
  (46 shorter events, 5.9 us)
Async XLA Ops:
  0.6 10.3 %copy-start.8 = (f32[64,40]{0,1:T(8,128)S(1)}, f32[64,40]{0,1:T(8,128)}, u32[]{:S(2)}) copy-start(f32[64,40]{0,1:T(8,128)} %param.17) | copy-start | bytes 30724
  0.6 11.1 %copy-start.4 = (f32[40]{0:T(128)S(1)}, f32[40]{0:T(128)}, u32[]{:S(2)}) copy-start(f32[40]{0:T(128)} %param.18) | copy-start | bytes 484
  0.7 11.1 %copy-start.3 = (f32[64]{0:T(128)S(1)}, f32[64]{0:T(128)}, u32[]{:S(2)}) copy-start(f32[64]{0:T(128)} %param.16) | copy-start | bytes 772
  0.7 11.1 %copy-start = (f32[64,64]{1,0:T(8,128)S(1)}, f32[64,64]{1,0:T(8,128)}, u32[]{:S(2)}) copy-start(f32[64,64]{1,0:T(8,128)} %refs_1_.1) | copy-start | bytes 49156
  0.7 11.1 %copy-start.2 = (f32[64]{0:T(128)S(1)}, f32[64]{0:T(128)}, u32[]{:S(2)}) copy-start(f32[64]{0:T(128)} %param.14) | copy-start | bytes 772
  0.7 11.1 %copy-start.1 = (f32[40,64]{1,0:T(8,128)S(1)}, f32[40,64]{1,0:T(8,128)}, u32[]{:S(2)}) copy-start(f32[40,64]{1,0:T(8,128)} %refs_0_.1) | copy-start | bytes 30724
  3.3 7.7 %collective-permute-start = (f32[8,128]{1,0:T(8,128)}, f32[8,128]{1,0:T(8,128)S(1)}, u32[]{:S(2)}, u32[]{:S(2)}) collective-permute-start(f32[8,128]{1,0:T(8,128)} %get-tuple-element.84), channel_id=1, source_target_pairs={{0,2},{2,0},{4,6},{6,4},{8,10},{10,8},{12,14},{14,12},{16,18},{18,... | collective-permute-start | bytes 12296 | tf_op jit(solution)/shard_map/ppermute | solution.py:819
  3.8 15.8 %collective-permute-start.4 = (f32[152,128]{1,0:T(8,128)}, f32[152,128]{1,0:T(8,128)S(1)}, u32[]{:S(2)}, u32[]{:S(2)}) collective-permute-start(f32[152,128]{1,0:T(8,128)} %get-tuple-element.101), channel_id=1, source_target_pairs={{0,2},{2,4},{4,6},{6,8},{8,10},{10,12},{12,14},{14,16},{16,18},{18... | collective-permute-start | bytes 233480 | tf_op jit(solution)/shard_map/ppermute | solution.py:891
  3.9 15.7 %collective-permute-start.5 = (f32[152,128]{1,0:T(8,128)}, f32[152,128]{1,0:T(8,128)S(1)}, u32[]{:S(2)}, u32[]{:S(2)}) collective-permute-start(f32[152,128]{1,0:T(8,128)} %get-tuple-element.102), channel_id=1, source_target_pairs={{2,0},{4,2},{6,4},{8,6},{10,8},{12,10},{14,12},{16,14},{18,16},{20... | collective-permute-start | bytes 233480 | tf_op jit(solution)/shard_map/ppermute | solution.py:892
  9.5 18.7 %collective-permute-start.7 = (f32[856,128]{1,0:T(8,128)}, f32[856,128]{1,0:T(8,128)S(1)}, u32[]{:S(2)}, u32[]{:S(2)}) collective-permute-start(f32[856,128]{1,0:T(8,128)} %get-tuple-element.123), channel_id=1, source_target_pairs={{0,1},{1,0},{2,3},{3,2},{4,5},{5,4},{6,7},{7,6},{8,9},{9,8},{10,11... | collective-permute-start | bytes 1314824 | tf_op jit(solution)/shard_map/ppermute | solution.py:921
  11.7 3.6 %collective-permute-start.1 = (f32[8,128]{1,0:T(8,128)S(1)}, f32[8,128]{1,0:T(8,128)S(1)}, u32[]{:S(2)}, u32[]{:S(2)}) collective-permute-start(f32[8,128]{1,0:T(8,128)S(1)} %add.48), channel_id=1, source_target_pairs={{0,4},{2,6},{4,0},{6,2},{8,12},{10,14},{12,8},{14,10},{16,20},{18,... | collective-permute-start | bytes 12296 | tf_op jit(solution)/shard_map/ppermute | solution.py:819
  11.8 1.0 %copy-start.5 = (f32[16,56,128]{2,1,0:T(8,128)S(1)}, f32[16,56,128]{2,1,0:T(8,128)}, u32[]{:S(2)}) copy-start(f32[16,56,128]{2,1,0:T(8,128)} %get-tuple-element.86.own.refs_4_) | copy-start | bytes 1376260
  12.8 6.8 %copy-start.6 = (f32[16,56,128]{2,1,0:T(8,128)S(1)}, f32[16,56,128]{2,1,0:T(8,128)}, u32[]{:S(2)}) copy-start(f32[16,56,128]{2,1,0:T(8,128)} %get-tuple-element.86.own.refs_4_) | copy-start | bytes 1376260
  15.4 3.6 %collective-permute-start.2 = (f32[8,128]{1,0:T(8,128)S(1)}, f32[8,128]{1,0:T(8,128)S(1)}, u32[]{:S(2)}, u32[]{:S(2)}) collective-permute-start(f32[8,128]{1,0:T(8,128)S(1)} %add.49), channel_id=1, source_target_pairs={{0,8},{2,10},{4,12},{6,14},{8,0},{10,2},{12,4},{14,6},{16,24},{18,... | collective-permute-start | bytes 12296 | tf_op jit(solution)/shard_map/ppermute | solution.py:819
  19.0 4.5 %collective-permute-start.3 = (f32[8,128]{1,0:T(8,128)S(1)}, f32[8,128]{1,0:T(8,128)S(1)}, u32[]{:S(2)}, u32[]{:S(2)}) collective-permute-start(f32[8,128]{1,0:T(8,128)S(1)} %add.50), channel_id=1, source_target_pairs={{0,16},{2,18},{4,20},{6,22},{8,24},{10,26},{12,28},{14,30},{16,0},... | collective-permute-start | bytes 12296 | tf_op jit(solution)/shard_map/ppermute | solution.py:819
  23.5 4.7 %collective-permute-start.6 = (f32[200,128]{1,0:T(8,128)S(1)}, f32[200,128]{1,0:T(8,128)S(1)}, u32[]{:S(2)}, u32[]{:S(2)}) collective-permute-start(f32[200,128]{1,0:T(8,128)S(1)} %get-tuple-element.160), channel_id=1, source_target_pairs={{0,1},{1,0},{2,3},{3,2},{4,5},{5,4},{6,7},{7,6},{8,9},{9,8},{10,11... | collective-permute-start | bytes 307208 | tf_op jit(solution)/shard_map/ppermute | solution.py:964
  28.1 2.9 %copy-start.7 = (f32[16,40,128]{2,1,0:T(8,128)S(1)}, f32[16,40,128]{2,1,0:T(8,128)}, u32[]{:S(2)}) copy-start(f32[16,40,128]{2,1,0:T(8,128)} %get-tuple-element.117.refs_5_) | copy-start | bytes 983044
  46.0 5.0 %collective-permute-start.8 = (f32[80,128]{1,0:T(8,128)S(1)}, f32[80,128]{1,0:T(8,128)S(1)}, u32[]{:S(2)}, u32[]{:S(2)}) collective-permute-start(f32[80,128]{1,0:T(8,128)S(1)} %get-tuple-element.132), channel_id=1, source_target_pairs={{0,16},{2,18},{4,20},{6,22},{8,24},{10,26},{12,28},{14,30},{16,0},... | collective-permute-start | bytes 122888 | tf_op jit(solution)/shard_map/ppermute | solution.py:819
  51.0 4.0 %collective-permute-start.9 = (f32[80,128]{1,0:T(8,128)S(1)}, f32[80,128]{1,0:T(8,128)S(1)}, u32[]{:S(2)}, u32[]{:S(2)}) collective-permute-start(f32[80,128]{1,0:T(8,128)S(1)} %add.53), channel_id=1, source_target_pairs={{0,8},{2,10},{4,12},{6,14},{8,0},{10,2},{12,4},{14,6},{16,24},{18,... | collective-permute-start | bytes 122888 | tf_op jit(solution)/shard_map/ppermute | solution.py:819
  55.0 4.0 %collective-permute-start.10 = (f32[80,128]{1,0:T(8,128)S(1)}, f32[80,128]{1,0:T(8,128)S(1)}, u32[]{:S(2)}, u32[]{:S(2)}) collective-permute-start(f32[80,128]{1,0:T(8,128)S(1)} %add.54), channel_id=1, source_target_pairs={{0,1},{1,0},{2,3},{3,2},{4,5},{5,4},{6,7},{7,6},{8,9},{9,8},{10,11... | collective-permute-start | bytes 122888 | tf_op jit(solution)/shard_map/ppermute | solution.py:819
  59.0 4.0 %collective-permute-start.11 = (f32[80,128]{1,0:T(8,128)S(1)}, f32[80,128]{1,0:T(8,128)S(1)}, u32[]{:S(2)}, u32[]{:S(2)}) collective-permute-start(f32[80,128]{1,0:T(8,128)S(1)} %add.55), channel_id=1, source_target_pairs={{0,4},{2,6},{4,0},{6,2},{8,12},{10,14},{12,8},{14,10},{16,20},{18,... | collective-permute-start | bytes 122888 | tf_op jit(solution)/shard_map/ppermute | solution.py:819
  63.0 1.2 %collective-permute-start.12 = (f32[80,128]{1,0:T(8,128)S(1)}, f32[80,128]{1,0:T(8,128)S(1)}, u32[]{:S(2)}, u32[]{:S(2)}) collective-permute-start(f32[80,128]{1,0:T(8,128)S(1)} %add.56), channel_id=1, source_target_pairs={{0,2},{2,0},{4,6},{6,4},{8,10},{10,8},{12,14},{14,12},{16,18},{18,... | collective-permute-start | bytes 122888 | tf_op jit(solution)/shard_map/ppermute | solution.py:819

commit v10 on v9

--- a/solution.py
+++ b/solution.py
@@ -31,7 +31,6 @@
 F32 = jnp.float32
 BF16 = jnp.bfloat16
 VMEM = pl.BlockSpec(memory_space=pltpu.VMEM)
-SMEM = pl.BlockSpec(memory_space=pltpu.SMEM)
 
 
 def params(megabytes):
@@ -113,9 +112,10 @@
             lat[LAT_X + FEATS * n : LAT_X + FEATS * (n + 1), :] = cown[cstart + n]
 
 
-def corner_kernel(sides, scal, east, west, *outs):
+def corner_kernel(sides, east, west, *outs):
+    southern = (lax.axis_index("lat") == 0).astype(jnp.int32)
     for side, corner in zip(sides, outs):
-        start = {"swap": scal[0], "north": ROWS - REACH, "south": 0}[side]
+        start = {"swap": southern * (ROWS - REACH), "north": ROWS - REACH, "south": 0}[side]
         for at, strip, near in ((0, east, 1), (PACK + 40, west, 0)):
             for t in range(7):
                 rows = slice(at + 8 * t, at + 8 * t + 8)
@@ -807,6 +807,29 @@
         bout[:, 10 * t + 9 : 10 * t + 10] = packed[73:74, 36 + t : 37 + t] * scale
 
 
+def position(lat_n):
+    lat_i = lax.axis_index("lat")
+    low = (lat_i == 0).astype(jnp.int32)
+    return (
+        low * (ROWS - REACH),
+        low * (ROWS - CREACH),
+        (lat_i > 0).astype(jnp.int32),
+        (lat_i < lat_n - 1).astype(jnp.int32),
+        jnp.where(low == 1, PAD + ROWS, PAD - REACH),
+        jnp.where(low == 1, PAD + ROWS, PAD - CREACH),
+        jnp.where(low == 1, 0, ROWS - CREACH),
+    )
+
+
+class RowTable:
+    def __init__(self, ref, number):
+        self.ref, self.number = ref, number
+
+    def __getitem__(self, row):
+        part = tile(self.ref, row, self.number)
+        return jnp.concatenate([part, part], axis=1)
+
+
 def far_first(axes):
     return [(axis, n, 1 << bit) for axis, n in axes for bit in reversed(range(n.bit_length() - 1))]
 
@@ -838,22 +861,9 @@
     lat_i = lax.axis_index("lat")
     lat_total, lon_total = ROWS * lat_n, COLS * lon_n
     sides = ["swap"] if lat_n == 2 else ["north", "south"]
-    is_low = (lat_i == 0).astype(jnp.int32)
-    has_south = (lat_i > 0).astype(jnp.int32)
-    has_north = (lat_i < lat_n - 1).astype(jnp.int32)
-    scal = jnp.stack(
-        [
-            is_low * (ROWS - REACH),
-            is_low * (ROWS - CREACH),
-            has_south,
-            has_north,
-            jnp.where(is_low == 1, PAD + ROWS, PAD - REACH),
-            jnp.where(is_low == 1, PAD + ROWS, PAD - CREACH),
-            jnp.where(is_low == 1, 0, ROWS - CREACH),
-        ]
-    ).astype(jnp.int32)
     rows = (lat_i * ROWS - PAD + jnp.arange(EXT, dtype=jnp.int32)).astype(F32)
-    cs, fs = latitude_terms(rows, lat_total)
+    tiles = [jnp.broadcast_to(x[:, None, None], (EXT, 8, COLS)) for x in latitude_terms(rows, lat_total)]
+    geometry = jnp.concatenate(tiles, axis=1)
 
     hbm = pl.BlockSpec(memory_space=pltpu.HBM)
     packed = pl.pallas_call(
@@ -912,14 +922,13 @@
     pack_corners = pl.pallas_call(
         lambda *refs: corner_kernel(sides, *refs),
         out_shape=[sds(CORNER + 8, COLS)] * len(sides),
-        in_specs=[SMEM, VMEM, VMEM],
+        in_specs=[VMEM, VMEM],
         out_specs=[VMEM] * len(sides),
         compiler_params=params(8),
         cost_estimate=pl.CostEstimate(flops=10**8, bytes_accessed=10**6, transcendentals=0),
         name="pack_corners",
     )
     lats = [lax.ppermute(pay, "lat", lat_pairs(side)) for side, pay in zip(sides, packed[5:])]
-    geometry = (scal, cs, fs)
     state = sds(EXT, 56, WIDE)
     plain = sds(EXT, FEATS, WIDE)
     marks = sds(EXT, 16, WIDE)
@@ -928,15 +937,15 @@
     def call(kernel, name, out_shape, scratch, args, flops, limit):
         single = not isinstance(out_shape, list)
         return pl.pallas_call(
-            kernel,
+            lambda geo, *refs: kernel(position(lat_n), RowTable(geo, 0), RowTable(geo, 1), *refs),
             out_shape=out_shape,
-            in_specs=[SMEM] * 3 + [VMEM] * len(args),
+            in_specs=[VMEM] * (1 + len(args)),
             out_specs=VMEM if single else [VMEM] * len(out_shape),
             scratch_shapes=scratch,
             compiler_params=params(limit),
             cost_estimate=pl.CostEstimate(flops=flops, bytes_accessed=10**7, transcendentals=0),
             name=name,
-        )(*geometry, *args)
+        )(geometry, *args)
 
 
     def last_round(done):
@@ -945,7 +954,7 @@
             assemble_own_kernel, "assemble_own", [state, marks, sds(EXT, 8, WIDE), plain], [],
             [own, own_m, from_west, from_east, k1, k2, k3, b2, b3], 10**9, 8,
         )
-        return blocks, pack_corners(scal, from_west, from_east)
+        return blocks, pack_corners(from_west, from_east)
 
     rounds = far_first((("lon", lon_n),))[::-1]
     row_total, results = pair_rounds(

time: 65.2 us -> 64.3 us (0.986)
  Pallas kernels: 36.1 us -> 31 us
  waiting for transfers between devices: 14.8 us -> 19.2 us
    pallas_call x10, Pallas kernels: 31.5 us -> 26.4 us  [the longest x9 26 us: call(): pl.pallas_call(lambda geo, *refs: kernel(position(lat_n), RowTable(geo, 0...]
    ppermute x9, waiting for transfers between devices: 13.5 us -> 16.9 us  [pair_rounds(): got = lax.ppermute(x, axis, [(j, j ^ step) for j in range(n)])]
    ppermute x1, waiting for transfers between devices: 1.33 us -> 2.38 us  [on_device(): corners.append(lax.ppermute(pay, 'lat', lat_pairs(side)))]
  transfers between devices with their start and end apart: 13 -> 13, of which waited for: 9 -> 9; matrix products, arithmetic and copies ran while one was open for 1% -> 2% of each run, Pallas kernels for 23% -> 17%
where the time goes in v10:
time: 64.3 us; the launch traced here: 64.1 us
  Pallas kernels  31 us (48%)
  waiting for transfers between devices  19.2 us (30%)
  starting transfers between devices  10.9 us (17%)
  local copies, waits for them, and re-layouts  1.34 us (2%)
  between operations  0.87 us (1%)
  other arithmetic  0.82 us (1%)
    pallas_call x9, Pallas kernels, call(): pl.pallas_call(lambda geo, *refs: kernel(position(lat_n), RowTable(geo, 0...  26 us
    ppermute x9, waiting for transfers between devices, pair_rounds(): got = lax.ppermute(x, axis, [(j, j ^ step) for j in range(n)])  16.9 us
    ppermute x1, starting transfers between devices, on_device(): from_east = lax.ppermute(west_pay, 'lon', west_ring)  5.58 us
    ppermute x9, starting transfers between devices, pair_rounds(): got = lax.ppermute(x, axis, [(j, j ^ step) for j in range(n)])  3.2 us
    pallas_call x1, Pallas kernels, on_device(): pl.pallas_call(lambda *refs: pack_kernel(sides, *refs), out_shape=[sds(RO...  2.6 us
    ppermute x1, waiting for transfers between devices, on_device(): corners.append(lax.ppermute(pay, 'lat', lat_pairs(side)))  2.38 us
    ppermute x1, starting transfers between devices, on_device(): lax.ppermute(pay, 'lat', lat_pairs(side))  1.5 us
  transfers between devices with their start and end apart: 13, of which 9 were waited for; matrix products, arithmetic and copies ran while one was open for 2% of the time, Pallas kernels for 17%

profile of v10, /device:TPU:0, one launch (start us, length us, event | category | flops | bytes accessed | tf_op | source)
XLA Modules:
  0.0 64.1 jit_solution(2829669227374128823)
XLA Ops:
  0.7 2.6 %pack_halos.1 = (f32[16,56,128]{2,1,0:T(8,128)}, f32[16,40,128]{2,1,0:T(8,128)}, f32[152,128]{1,0:T(8,128)}, f32[152,128]{1,0:T(8,128)}, f32[8,128]{1,0:T(8,128)}, /*index=5*/f32[856,128]{1,0:T(8,128)}) custom-call(f32[640,128]{1,0:T(8,128)} %bitcast.17, s32[160,128]{1,0:T(8,128)} %bitcast.19, f32[16,128]{1,0:T(8,128)} %refs_2_.2, f32[640,128]{1,0:T(8,128)} %bitcast.18), custom_call_target="tpu_custom_call" | custom-call | flops 1000000000 | bytes 3000000 | tf_op jit(solution)/shard_map/pack_halos/pallas_call | solution.py:869
  3.9 5.6 %collective-permute-start.5 = (f32[152,128]{1,0:T(8,128)}, f32[152,128]{1,0:T(8,128)S(1)}, u32[]{:S(2)}, u32[]{:S(2)}) collective-permute-start(f32[152,128]{1,0:T(8,128)} %get-tuple-element.102), channel_id=1, source_target_pairs={{2,0},{4,2},{6,4},{8,6},{10,8},{12,10},{14,12},{16,14},{18,16},{20... | collective-permute-start | bytes 233480 | tf_op jit(solution)/shard_map/ppermute | solution.py:902
  9.5 1.5 %collective-permute-start.7 = (f32[856,128]{1,0:T(8,128)}, f32[856,128]{1,0:T(8,128)S(1)}, u32[]{:S(2)}, u32[]{:S(2)}) collective-permute-start(f32[856,128]{1,0:T(8,128)} %get-tuple-element.123), channel_id=1, source_target_pairs={{0,1},{1,0},{2,3},{3,2},{4,5},{5,4},{6,7},{7,6},{8,9},{9,8},{10,11... | collective-permute-start | bytes 1314824 | tf_op jit(solution)/shard_map/ppermute | solution.py:931
  11.9 1.0 %copy-done.5 = f32[16,56,128]{2,1,0:T(8,128)S(1)} copy-done((f32[16,56,128]{2,1,0:T(8,128)S(1)}, f32[16,56,128]{2,1,0:T(8,128)}, u32[]{:S(2)}) %copy-start.5) | copy-done | bytes 458776
  12.9 1.2 %own_closure.1 = (f32[16,40,128]{2,1,0:T(8,128)S(1)}, f32[16,64,128]{2,1,0:T(8,128)S(1)}, f32[16,64,128]{2,1,0:T(8,128)S(1)}, bf16[64,144]{1,0:T(8,128)(2,1)S(1)...) custom-call(f32[16,56,128]{2,1,0:T(8,128)S(1)} %copy-done.5, ...), custom_call_target="tpu_custom_call" | custom-call | flops 1000000000 | bytes 2000000 | tf_op jit(solution)/shard_map/own_closure/pallas_call | solution.py:963
  14.1 1.3 %collective-permute-done.1 = f32[8,128]{1,0:T(8,128)S(1)} collective-permute-done((f32[8,128]{1,0:T(8,128)S(1)}, f32[8,128]{1,0:T(8,128)S(1)}, u32[]{:S(2)}, u32[]{:S(2)}) %collective-permute-start.1) | collective-permute-done | bytes 4128 | tf_op jit(solution)/shard_map/ppermute | solution.py:842
  15.7 3.3 %collective-permute-done.2 = f32[8,128]{1,0:T(8,128)S(1)} collective-permute-done((f32[8,128]{1,0:T(8,128)S(1)}, f32[8,128]{1,0:T(8,128)S(1)}, u32[]{:S(2)}, u32[]{:S(2)}) %collective-permute-start.2) | collective-permute-done | bytes 4128 | tf_op jit(solution)/shard_map/ppermute | solution.py:842
  19.7 0.9 %assemble_own.1 = (f32[48,56,256]{2,1,0:T(8,128)S(1)}, f32[48,16,256]{2,1,0:T(8,128)S(1)}, f32[48,8,256]{2,1,0:T(8,128)S(1)}, f32[48,40,256]{2,1,0:T(8,128)S(1)}) custom-call(f32[48,16,128]{2,1,0:T(8,128)S(1)} %pad_maximum_fusion.geo, f32[16,56,128]{2,1,0:T(8,128)S(1)} %copy-done.5, f32[16,40,128]{2,1,0:T(8,128)S(1)} %get-tuple-element.100.refs_1_, ...), custom_call_target="tpu_custom_call" | custom-call | flops 1000000000 | bytes 10000000 | tf_op jit(solution)/shard_map/assemble_own/pallas_call | solution.py:939
  21.0 2.6 %collective-permute-done.3 = f32[8,128]{1,0:T(8,128)S(1)} collective-permute-done((f32[8,128]{1,0:T(8,128)S(1)}, f32[8,128]{1,0:T(8,128)S(1)}, u32[]{:S(2)}, u32[]{:S(2)}) %collective-permute-start.3) | collective-permute-done | bytes 4128 | tf_op jit(solution)/shard_map/ppermute | solution.py:842
  24.1 0.9 %first_section_own.1.refs_1_ = f32[48,56,256]{2,1,0:T(8,128)S(1)} custom-call(f32[48,16,128]{2,1,0:T(8,128)S(1)} %pad_maximum_fusion.geo, f32[48,56,256]{2,1,0:T(8,128)S(1)} %get-tuple-element.114.refs_0_, f32[48,16,256]{2,1,0:T(8,128)S(1)} %get-tuple-element.115.refs_1_.refs_2_.refs_3_), custom_call_target="tpu_custom_call" | custom-call | flops 1000000000 | bytes 10000000 | tf_op jit(solution)/shard_map/first_section_own/pallas_call | solution.py:939
  24.9 0.9 %second_section_own.1.refs_2_ = f32[48,56,256]{2,1,0:T(8,128)S(1)} custom-call(f32[48,16,128]{2,1,0:T(8,128)S(1)} %pad_maximum_fusion.geo, f32[48,56,256]{2,1,0:T(8,128)S(1)} %get-tuple-element.114.refs_0_, f32[48,56,256]{2,1,0:T(8,128)S(1)} %first_section_own.1.refs_1_, f32[48,16,256]{2,1,0:T(8,128)S(1)} %get-tuple-element.115.refs_1_.refs_2_.refs_3_), custom_call_target="tpu_custom_call" | custom-call | flops 1000000000 | bytes 10000000 | tf_op jit(solution)/shard_map/second_section_own/pallas_call | solution.py:939
  25.8 2.4 %collective-permute-done.6.refs_7_.refs_13_ = f32[200,128]{1,0:T(8,128)S(1)} collective-permute-done((f32[200,128]{1,0:T(8,128)S(1)}, f32[200,128]{1,0:T(8,128)S(1)}, u32[]{:S(2)}, u32[]{:S(2)}) %collective-permute-start.6) | collective-permute-done | bytes 102432 | tf_op jit(solution)/shard_map/ppermute | solution.py:973
  28.2 2.3 %halo_rows.1 = (f32[48,56,256]{2,1,0:T(8,128)S(1)}, f32[48,56,256]{2,1,0:T(8,128)S(1)}, f32[48,56,256]{2,1,0:T(8,128)S(1)}, f32[48,16,256]{2,1,0:T(8,128)S(1)}, ...) custom-call(f32[48,16,128]{2,1,0:T(8,128)S(1)} %pad_maximum_fusion.geo, ...), custom_call_target="tpu_custom_call" | custom-call | flops 2000000000 | bytes 10000000 | tf_op jit(solution)/shard_map/halo_rows/pallas_call | solution.py:939
  30.5 14.7 %steps_and_adjoint.1 = (f32[80,128]{1,0:T(8,128)S(1)}, f32[48,40,256]{2,1,0:T(8,128)S(1)}, f32[48,40,256]{2,1,0:T(8,128)S(1)}, f32[16,40,128]{2,1,0:T(8,128)S(1)...) custom-call(f32[48,16,128]{2,1,0:T(8,128)S(1)} %pad_maximum_fusion.geo, ...), custom_call_target="tpu_custom_call" | custom-call | flops 4000000000 | bytes 10000000 | tf_op jit(solution)/shard_map/steps_and_adjoint/pallas_call | solution.py:939
  45.9 1.5 %adjoint_third_section.1 = (f32[48,40,256]{2,1,0:T(8,128)S(1)}, f32[48,40,256]{2,1,0:T(8,128)S(1)}) custom-call(f32[48,16,128]{2,1,0:T(8,128)S(1)} %pad_maximum_fusion.geo, f32[48,56,256]{2,1,0:T(8,128)S(1)} %get-tuple-element.125.refs_6_.refs_0_, f32[48,16,256]{2,1,0:T(8,128)S(1)} %get-tuple-element.126.refs_7_.refs_1_.refs_3_, ...), custom_call_target="tpu_custom_call" | custom-call | flops 1000000000 | bytes 10000000 | tf_op jit(solution)/shard_map/adjoint_third_section/pallas_call | solution.py:939
  47.4 2.7 %collective-permute-done.8 = f32[80,128]{1,0:T(8,128)S(1)} collective-permute-done((f32[80,128]{1,0:T(8,128)S(1)}, f32[80,128]{1,0:T(8,128)S(1)}, u32[]{:S(2)}, u32[]{:S(2)}) %collective-permute-start.8) | collective-permute-done | bytes 40992 | tf_op jit(solution)/shard_map/ppermute | solution.py:842
  50.2 1.6 %adjoint_second_section.1 = (f32[48,40,256]{2,1,0:T(8,128)S(1)}, f32[48,40,256]{2,1,0:T(8,128)S(1)}) custom-call(f32[48,16,128]{2,1,0:T(8,128)S(1)} %pad_maximum_fusion.geo, f32[48,56,256]{2,1,0:T(8,128)S(1)} %get-tuple-element.138.refs_0_, f32[48,16,256]{2,1,0:T(8,128)S(1)} %get-tuple-element.126.refs_7_.refs_1_.refs_3_, ...), custom_call_target="tpu_custom_call" | custom-call | flops 1000000000 | bytes 10000000 | tf_op jit(solution)/shard_map/adjoint_second_section/pallas_call | solution.py:939
  51.7 2.4 %collective-permute-done.9 = f32[80,128]{1,0:T(8,128)S(1)} collective-permute-done((f32[80,128]{1,0:T(8,128)S(1)}, f32[80,128]{1,0:T(8,128)S(1)}, u32[]{:S(2)}, u32[]{:S(2)}) %collective-permute-start.9) | collective-permute-done | bytes 40992 | tf_op jit(solution)/shard_map/ppermute | solution.py:842
  54.7 1.8 %adjoint_first_section.1 = f32[640,128]{1,0:T(8,128)} custom-call(f32[48,16,128]{2,1,0:T(8,128)S(1)} %pad_maximum_fusion.geo, f32[48,56,256]{2,1,0:T(8,128)S(1)} %get-tuple-element.124.refs_5_.refs_0_, f32[48,16,256]{2,1,0:T(8,128)S(1)} %get-tuple-element.126.refs_7_.refs_1_.refs_3_, f32[48,40,256]{2,1,0:T(8,128)S(1)} %get-tuple-element.144.refs_2_, ...), custom_call_target="tpu_custom_call" | custom-call | flops 1000000000 | bytes 10000000 | tf_op jit(solution)/shard_map/adjoint_first_section/pallas_call | solution.py:939
  56.5 1.7 %collective-permute-done.10 = f32[80,128]{1,0:T(8,128)S(1)} collective-permute-done((f32[80,128]{1,0:T(8,128)S(1)}, f32[80,128]{1,0:T(8,128)S(1)}, u32[]{:S(2)}, u32[]{:S(2)}) %collective-permute-start.10) | collective-permute-done | bytes 40992 | tf_op jit(solution)/shard_map/ppermute | solution.py:842
  58.2 0.8 %collective-permute-start.11 = (f32[80,128]{1,0:T(8,128)S(1)}, f32[80,128]{1,0:T(8,128)S(1)}, u32[]{:S(2)}, u32[]{:S(2)}) collective-permute-start(f32[80,128]{1,0:T(8,128)S(1)} %add.76), channel_id=1, source_target_pairs={{0,4},{2,6},{4,0},{6,2},{8,12},{10,14},{12,8},{14,10},{16,20},{18,... | collective-permute-start | bytes 122888 | tf_op jit(solution)/shard_map/ppermute | solution.py:842
  59.0 1.5 %last_section.1 = f32[640,128]{1,0:T(8,128)} custom-call(f32[48,16,128]{2,1,0:T(8,128)S(1)} %pad_maximum_fusion.geo, f32[8,128]{1,0:T(8,128)S(1)} %slice_add_fusion.refs_0_, f32[48,56,256]{2,1,0:T(8,128)S(1)} %get-tuple-element.148.refs_1_, f32[48,56,256]{2,1,0:T(8,128)S(1)} %get-tuple-element.149.refs_2_, ...), custom_call_target="tpu_custom_call" | custom-call | flops 1000000000 | bytes 10000000 | tf_op jit(solution)/shard_map/last_section/pallas_call | solution.py:939
  60.5 1.7 %collective-permute-done.11 = f32[80,128]{1,0:T(8,128)S(1)} collective-permute-done((f32[80,128]{1,0:T(8,128)S(1)}, f32[80,128]{1,0:T(8,128)S(1)}, u32[]{:S(2)}, u32[]{:S(2)}) %collective-permute-start.11) | collective-permute-done | bytes 40992 | tf_op jit(solution)/shard_map/ppermute | solution.py:842
  62.2 1.2 %collective-permute-done.12 = f32[80,128]{1,0:T(8,128)S(1)} collective-permute-done((f32[80,128]{1,0:T(8,128)S(1)}, f32[80,128]{1,0:T(8,128)S(1)}, u32[]{:S(2)}, u32[]{:S(2)}) %collective-permute-start.12) | collective-permute-done | bytes 40992 | tf_op jit(solution)/shard_map/ppermute | solution.py:842
  (48 shorter events, 5.2 us)
Async XLA Ops:
  0.6 10.4 %copy-start.8 = (f32[64,40]{0,1:T(8,128)S(1)}, f32[64,40]{0,1:T(8,128)}, u32[]{:S(2)}) copy-start(f32[64,40]{0,1:T(8,128)} %param.17) | copy-start | bytes 30724
  0.6 11.2 %copy-start.4 = (f32[40]{0:T(128)S(1)}, f32[40]{0:T(128)}, u32[]{:S(2)}) copy-start(f32[40]{0:T(128)} %param.18) | copy-start | bytes 484
  0.7 11.2 %copy-start.3 = (f32[64]{0:T(128)S(1)}, f32[64]{0:T(128)}, u32[]{:S(2)}) copy-start(f32[64]{0:T(128)} %param.16) | copy-start | bytes 772
  0.7 11.1 %copy-start = (f32[64,64]{1,0:T(8,128)S(1)}, f32[64,64]{1,0:T(8,128)}, u32[]{:S(2)}) copy-start(f32[64,64]{1,0:T(8,128)} %refs_1_.1) | copy-start | bytes 49156
  0.7 11.1 %copy-start.2 = (f32[64]{0:T(128)S(1)}, f32[64]{0:T(128)}, u32[]{:S(2)}) copy-start(f32[64]{0:T(128)} %param.14) | copy-start | bytes 772
  0.7 11.1 %copy-start.1 = (f32[40,64]{1,0:T(8,128)S(1)}, f32[40,64]{1,0:T(8,128)}, u32[]{:S(2)}) copy-start(f32[40,64]{1,0:T(8,128)} %refs_0_.1) | copy-start | bytes 30724
  3.3 7.8 %collective-permute-start = (f32[8,128]{1,0:T(8,128)}, f32[8,128]{1,0:T(8,128)S(1)}, u32[]{:S(2)}, u32[]{:S(2)}) collective-permute-start(f32[8,128]{1,0:T(8,128)} %get-tuple-element.84), channel_id=1, source_target_pairs={{0,2},{2,0},{4,6},{6,4},{8,10},{10,8},{12,14},{14,12},{16,18},{18,... | collective-permute-start | bytes 12296 | tf_op jit(solution)/shard_map/ppermute | solution.py:842
  3.8 15.9 %collective-permute-start.4 = (f32[152,128]{1,0:T(8,128)}, f32[152,128]{1,0:T(8,128)S(1)}, u32[]{:S(2)}, u32[]{:S(2)}) collective-permute-start(f32[152,128]{1,0:T(8,128)} %get-tuple-element.101), channel_id=1, source_target_pairs={{0,2},{2,4},{4,6},{6,8},{8,10},{10,12},{12,14},{14,16},{16,18},{18... | collective-permute-start | bytes 233480 | tf_op jit(solution)/shard_map/ppermute | solution.py:901
  3.9 15.8 %collective-permute-start.5 = (f32[152,128]{1,0:T(8,128)}, f32[152,128]{1,0:T(8,128)S(1)}, u32[]{:S(2)}, u32[]{:S(2)}) collective-permute-start(f32[152,128]{1,0:T(8,128)} %get-tuple-element.102), channel_id=1, source_target_pairs={{2,0},{4,2},{6,4},{8,6},{10,8},{12,10},{14,12},{16,14},{18,16},{20... | collective-permute-start | bytes 233480 | tf_op jit(solution)/shard_map/ppermute | solution.py:902
  9.5 18.7 %collective-permute-start.7 = (f32[856,128]{1,0:T(8,128)}, f32[856,128]{1,0:T(8,128)S(1)}, u32[]{:S(2)}, u32[]{:S(2)}) collective-permute-start(f32[856,128]{1,0:T(8,128)} %get-tuple-element.123), channel_id=1, source_target_pairs={{0,1},{1,0},{2,3},{3,2},{4,5},{5,4},{6,7},{7,6},{8,9},{9,8},{10,11... | collective-permute-start | bytes 1314824 | tf_op jit(solution)/shard_map/ppermute | solution.py:931
  11.8 3.6 %collective-permute-start.1 = (f32[8,128]{1,0:T(8,128)S(1)}, f32[8,128]{1,0:T(8,128)S(1)}, u32[]{:S(2)}, u32[]{:S(2)}) collective-permute-start(f32[8,128]{1,0:T(8,128)S(1)} %add.69), channel_id=1, source_target_pairs={{0,4},{2,6},{4,0},{6,2},{8,12},{10,14},{12,8},{14,10},{16,20},{18,... | collective-permute-start | bytes 12296 | tf_op jit(solution)/shard_map/ppermute | solution.py:842
  11.8 1.0 %copy-start.5 = (f32[16,56,128]{2,1,0:T(8,128)S(1)}, f32[16,56,128]{2,1,0:T(8,128)}, u32[]{:S(2)}) copy-start(f32[16,56,128]{2,1,0:T(8,128)} %get-tuple-element.86.own.refs_0_.refs_1_) | copy-start | bytes 1376260
  15.4 3.6 %collective-permute-start.2 = (f32[8,128]{1,0:T(8,128)S(1)}, f32[8,128]{1,0:T(8,128)S(1)}, u32[]{:S(2)}, u32[]{:S(2)}) collective-permute-start(f32[8,128]{1,0:T(8,128)S(1)} %add.70), channel_id=1, source_target_pairs={{0,8},{2,10},{4,12},{6,14},{8,0},{10,2},{12,4},{14,6},{16,24},{18,... | collective-permute-start | bytes 12296 | tf_op jit(solution)/shard_map/ppermute | solution.py:842
  19.0 4.5 %collective-permute-start.3 = (f32[8,128]{1,0:T(8,128)S(1)}, f32[8,128]{1,0:T(8,128)S(1)}, u32[]{:S(2)}, u32[]{:S(2)}) collective-permute-start(f32[8,128]{1,0:T(8,128)S(1)} %add.71), channel_id=1, source_target_pairs={{0,16},{2,18},{4,20},{6,22},{8,24},{10,26},{12,28},{14,30},{16,0},... | collective-permute-start | bytes 12296 | tf_op jit(solution)/shard_map/ppermute | solution.py:842
  23.5 4.7 %collective-permute-start.6 = (f32[200,128]{1,0:T(8,128)S(1)}, f32[200,128]{1,0:T(8,128)S(1)}, u32[]{:S(2)}, u32[]{:S(2)}) collective-permute-start(f32[200,128]{1,0:T(8,128)S(1)} %get-tuple-element.160), channel_id=1, source_target_pairs={{0,1},{1,0},{2,3},{3,2},{4,5},{5,4},{6,7},{7,6},{8,9},{9,8},{10,11... | collective-permute-start | bytes 307208 | tf_op jit(solution)/shard_map/ppermute | solution.py:973
  28.2 2.3 %copy-start.6 = (f32[16,56,128]{2,1,0:T(8,128)S(1)}, f32[16,56,128]{2,1,0:T(8,128)}, u32[]{:S(2)}) copy-start(f32[16,56,128]{2,1,0:T(8,128)} %get-tuple-element.86.own.refs_0_.refs_1_) | copy-start | bytes 1376260
  28.2 2.3 %copy-start.7 = (f32[16,40,128]{2,1,0:T(8,128)S(1)}, f32[16,40,128]{2,1,0:T(8,128)}, u32[]{:S(2)}) copy-start(f32[16,40,128]{2,1,0:T(8,128)} %get-tuple-element.117.refs_2_) | copy-start | bytes 983044
  45.2 4.9 %collective-permute-start.8 = (f32[80,128]{1,0:T(8,128)S(1)}, f32[80,128]{1,0:T(8,128)S(1)}, u32[]{:S(2)}, u32[]{:S(2)}) collective-permute-start(f32[80,128]{1,0:T(8,128)S(1)} %get-tuple-element.132), channel_id=1, source_target_pairs={{0,16},{2,18},{4,20},{6,22},{8,24},{10,26},{12,28},{14,30},{16,0},... | collective-permute-start | bytes 122888 | tf_op jit(solution)/shard_map/ppermute | solution.py:842
  50.1 4.0 %collective-permute-start.9 = (f32[80,128]{1,0:T(8,128)S(1)}, f32[80,128]{1,0:T(8,128)S(1)}, u32[]{:S(2)}, u32[]{:S(2)}) collective-permute-start(f32[80,128]{1,0:T(8,128)S(1)} %add.74), channel_id=1, source_target_pairs={{0,8},{2,10},{4,12},{6,14},{8,0},{10,2},{12,4},{14,6},{16,24},{18,... | collective-permute-start | bytes 122888 | tf_op jit(solution)/shard_map/ppermute | solution.py:842
  54.2 4.0 %collective-permute-start.10 = (f32[80,128]{1,0:T(8,128)S(1)}, f32[80,128]{1,0:T(8,128)S(1)}, u32[]{:S(2)}, u32[]{:S(2)}) collective-permute-start(f32[80,128]{1,0:T(8,128)S(1)} %add.75), channel_id=1, source_target_pairs={{0,1},{1,0},{2,3},{3,2},{4,5},{5,4},{6,7},{7,6},{8,9},{9,8},{10,11... | collective-permute-start | bytes 122888 | tf_op jit(solution)/shard_map/ppermute | solution.py:842
  58.2 4.0 %collective-permute-start.11 = (f32[80,128]{1,0:T(8,128)S(1)}, f32[80,128]{1,0:T(8,128)S(1)}, u32[]{:S(2)}, u32[]{:S(2)}) collective-permute-start(f32[80,128]{1,0:T(8,128)S(1)} %add.76), channel_id=1, source_target_pairs={{0,4},{2,6},{4,0},{6,2},{8,12},{10,14},{12,8},{14,10},{16,20},{18,... | collective-permute-start | bytes 122888 | tf_op jit(solution)/shard_map/ppermute | solution.py:842
  62.2 1.2 %collective-permute-start.12 = (f32[80,128]{1,0:T(8,128)S(1)}, f32[80,128]{1,0:T(8,128)S(1)}, u32[]{:S(2)}, u32[]{:S(2)}) collective-permute-start(f32[80,128]{1,0:T(8,128)S(1)} %add.77), channel_id=1, source_target_pairs={{0,2},{2,0},{4,6},{6,4},{8,10},{10,8},{12,14},{14,12},{16,18},{18,... | collective-permute-start | bytes 122888 | tf_op jit(solution)/shard_map/ppermute | solution.py:842

commit v11 on v10

--- a/solution.py
+++ b/solution.py
@@ -948,29 +948,23 @@
         )(geometry, *args)
 
 
-    def last_round(done):
-        own_m, _, _, k1, k2, k3, _, _, _, b2, b3 = done[1]
-        blocks = call(
-            assemble_own_kernel, "assemble_own", [state, marks, sds(EXT, 8, WIDE), plain], [],
-            [own, own_m, from_west, from_east, k1, k2, k3, b2, b3], 10**9, 8,
-        )
-        return blocks, pack_corners(from_west, from_east)
-
     rounds = far_first((("lon", lon_n),))[::-1]
     row_total, results = pair_rounds(
         sums,
         rounds,
-        [lambda done: sums, lambda done: own_closure(own, *raw)]
-        + [lambda done: sums] * (len(rounds) - 3)
-        + [last_round],
-    )
-    own_m, own_h1, own_h2, k1, k2, k3, q1, q2, q3, b2, b3 = results[1]
+        [lambda done: sums] * (len(rounds) - 1)
+        + [lambda done: (own_closure(own, *raw), pack_corners(from_west, from_east))],
+    )
+    (own_m, own_h1, own_h2, k1, k2, k3, q1, q2, q3, b2, b3), corner_pays = results[-1]
     net_weights = [k1, k2, k3, b2, b3]
-    (s0, masks, fluxes, net), corner_pays = results[-1]
     corners = []
     for side, pay in zip(sides, corner_pays):
         pay = lax.dynamic_update_slice(pay, row_total, (CORNER, 0))
         corners.append(lax.ppermute(pay, "lat", lat_pairs(side)))
+    s0, masks, fluxes, net = call(
+        assemble_own_kernel, "assemble_own", [state, marks, sds(EXT, 8, WIDE), plain], [],
+        [own, own_m, from_west, from_east] + net_weights, 10**9, 8,
+    )
     s1 = call(first_own_kernel, "first_section_own", state, [], [s0, masks], 10**9, 8)
     s2 = call(second_own_kernel, "second_section_own", state, [], [s0, s1, masks], 10**9, 8)
     corners, s2 = lax.optimization_barrier((corners, s2))

time: 64.3 us -> 64.7 us (level)
    ppermute x1, waiting for transfers between devices: 2.38 us -> 1.48 us  [on_device(): corners.append(lax.ppermute(pay, 'lat', lat_pairs(side)))]
    ppermute x9, waiting for transfers between devices: 16.9 us -> 17.7 us  [pair_rounds(): got = lax.ppermute(x, axis, [(j, j ^ step) for j in range(n)])]
where the time goes in v11:
time: 64.7 us; the launch traced here: 64.5 us
  Pallas kernels  31 us (48%)
  waiting for transfers between devices  19.2 us (30%)
  starting transfers between devices  11.2 us (17%)
  local copies, waits for them, and re-layouts  1.34 us (2%)
  between operations  0.88 us (1%)
  other arithmetic  0.82 us (1%)
    pallas_call x9, Pallas kernels, call(): pl.pallas_call(lambda geo, *refs: kernel(position(lat_n), RowTable(geo, 0...  26.1 us
    ppermute x9, waiting for transfers between devices, pair_rounds(): got = lax.ppermute(x, axis, [(j, j ^ step) for j in range(n)])  17.7 us
    ppermute x1, starting transfers between devices, on_device(): from_east = lax.ppermute(west_pay, 'lon', west_ring)  5.58 us
    ppermute x9, starting transfers between devices, pair_rounds(): got = lax.ppermute(x, axis, [(j, j ^ step) for j in range(n)])  3.56 us
    pallas_call x1, Pallas kernels, on_device(): pl.pallas_call(lambda *refs: pack_kernel(sides, *refs), out_shape=[sds(RO...  2.6 us
    ppermute x1, starting transfers between devices, on_device(): lax.ppermute(pay, 'lat', lat_pairs(side))  1.5 us
    ppermute x1, waiting for transfers between devices, on_device(): corners.append(lax.ppermute(pay, 'lat', lat_pairs(side)))  1.48 us
  transfers between devices with their start and end apart: 13, of which 9 were waited for; matrix products, arithmetic and copies ran while one was open for 2% of the time, Pallas kernels for 17%

profile of v11, /device:TPU:0, one launch (start us, length us, event | category | flops | bytes accessed | tf_op | source)
XLA Modules:
  0.0 64.5 jit_solution(15409181444542927849)
XLA Ops:
  0.7 2.6 %pack_halos.1 = (f32[16,56,128]{2,1,0:T(8,128)}, f32[16,40,128]{2,1,0:T(8,128)}, f32[152,128]{1,0:T(8,128)}, f32[152,128]{1,0:T(8,128)}, f32[8,128]{1,0:T(8,128)}, /*index=5*/f32[856,128]{1,0:T(8,128)}) custom-call(f32[640,128]{1,0:T(8,128)} %bitcast.17, s32[160,128]{1,0:T(8,128)} %bitcast.19, f32[16,128]{1,0:T(8,128)} %refs_2_.2, f32[640,128]{1,0:T(8,128)} %bitcast.18), custom_call_target="tpu_custom_call" | custom-call | flops 1000000000 | bytes 3000000 | tf_op jit(solution)/shard_map/pack_halos/pallas_call | solution.py:869
  3.9 5.6 %collective-permute-start.5 = (f32[152,128]{1,0:T(8,128)}, f32[152,128]{1,0:T(8,128)S(1)}, u32[]{:S(2)}, u32[]{:S(2)}) collective-permute-start(f32[152,128]{1,0:T(8,128)} %get-tuple-element.97), channel_id=1, source_target_pairs={{2,0},{4,2},{6,4},{8,6},{10,8},{12,10},{14,12},{16,14},{18,16},{20... | collective-permute-start | bytes 233480 | tf_op jit(solution)/shard_map/ppermute | solution.py:902
  9.5 1.5 %collective-permute-start.7 = (f32[856,128]{1,0:T(8,128)}, f32[856,128]{1,0:T(8,128)S(1)}, u32[]{:S(2)}, u32[]{:S(2)}) collective-permute-start(f32[856,128]{1,0:T(8,128)} %get-tuple-element.115), channel_id=1, source_target_pairs={{0,1},{1,0},{2,3},{3,2},{4,5},{5,4},{6,7},{7,6},{8,9},{9,8},{10,11... | collective-permute-start | bytes 1314824 | tf_op jit(solution)/shard_map/ppermute | solution.py:931
  12.1 3.2 %collective-permute-done.1 = f32[8,128]{1,0:T(8,128)S(1)} collective-permute-done((f32[8,128]{1,0:T(8,128)S(1)}, f32[8,128]{1,0:T(8,128)S(1)}, u32[]{:S(2)}, u32[]{:S(2)}) %collective-permute-start.1) | collective-permute-done | bytes 4128 | tf_op jit(solution)/shard_map/ppermute | solution.py:842
  15.4 1.0 %copy-done.5 = f32[16,56,128]{2,1,0:T(8,128)S(1)} copy-done((f32[16,56,128]{2,1,0:T(8,128)S(1)}, f32[16,56,128]{2,1,0:T(8,128)}, u32[]{:S(2)}) %copy-start.5) | copy-done | bytes 458776
  16.4 1.3 %own_closure.1 = (f32[16,40,128]{2,1,0:T(8,128)S(1)}, f32[16,64,128]{2,1,0:T(8,128)S(1)}, f32[16,64,128]{2,1,0:T(8,128)S(1)}, bf16[64,144]{1,0:T(8,128)(2,1)S(1)...) custom-call(f32[16,56,128]{2,1,0:T(8,128)S(1)} %copy-done.5, ...), custom_call_target="tpu_custom_call" | custom-call | flops 1000000000 | bytes 2000000 | tf_op jit(solution)/shard_map/own_closure/pallas_call | solution.py:956
  17.7 1.3 %collective-permute-done.2 = f32[8,128]{1,0:T(8,128)S(1)} collective-permute-done((f32[8,128]{1,0:T(8,128)S(1)}, f32[8,128]{1,0:T(8,128)S(1)}, u32[]{:S(2)}, u32[]{:S(2)}) %collective-permute-start.2) | collective-permute-done | bytes 4128 | tf_op jit(solution)/shard_map/ppermute | solution.py:842
  18.9 1.0 %collective-permute-start.3 = (f32[8,128]{1,0:T(8,128)S(1)}, f32[8,128]{1,0:T(8,128)S(1)}, u32[]{:S(2)}, u32[]{:S(2)}) collective-permute-start(f32[8,128]{1,0:T(8,128)S(1)} %add.71), channel_id=1, source_target_pairs={{0,16},{2,18},{4,20},{6,22},{8,24},{10,26},{12,28},{14,30},{16,0},... | collective-permute-start | bytes 12296 | tf_op jit(solution)/shard_map/ppermute | solution.py:842
  20.3 3.1 %collective-permute-done.3 = f32[8,128]{1,0:T(8,128)S(1)} collective-permute-done((f32[8,128]{1,0:T(8,128)S(1)}, f32[8,128]{1,0:T(8,128)S(1)}, u32[]{:S(2)}, u32[]{:S(2)}) %collective-permute-start.3) | collective-permute-done | bytes 4128 | tf_op jit(solution)/shard_map/ppermute | solution.py:842
  24.0 0.9 %assemble_own.1 = (f32[48,56,256]{2,1,0:T(8,128)S(1)}, f32[48,16,256]{2,1,0:T(8,128)S(1)}, f32[48,8,256]{2,1,0:T(8,128)S(1)}, f32[48,40,256]{2,1,0:T(8,128)S(1)}) custom-call(f32[48,16,128]{2,1,0:T(8,128)S(1)} %pad_maximum_fusion.geo, f32[16,56,128]{2,1,0:T(8,128)S(1)} %copy-done.6, f32[16,40,128]{2,1,0:T(8,128)S(1)} %get-tuple-element.100.refs_1_, ...), custom_call_target="tpu_custom_call" | custom-call | flops 1000000000 | bytes 10000000 | tf_op jit(solution)/shard_map/assemble_own/pallas_call | solution.py:939
  25.7 0.9 %second_section_own.1.refs_2_ = f32[48,56,256]{2,1,0:T(8,128)S(1)} custom-call(f32[48,16,128]{2,1,0:T(8,128)S(1)} %pad_maximum_fusion.geo, f32[48,56,256]{2,1,0:T(8,128)S(1)} %get-tuple-element.106.refs_0_, f32[48,56,256]{2,1,0:T(8,128)S(1)} %first_section_own.1.refs_1_, f32[48,16,256]{2,1,0:T(8,128)S(1)} %get-tuple-element.107.refs_1_.refs_2_.refs_3_), custom_call_target="tpu_custom_call" | custom-call | flops 1000000000 | bytes 10000000 | tf_op jit(solution)/shard_map/second_section_own/pallas_call | solution.py:939
  26.6 1.5 %collective-permute-done.6.refs_7_.refs_13_ = f32[200,128]{1,0:T(8,128)S(1)} collective-permute-done((f32[200,128]{1,0:T(8,128)S(1)}, f32[200,128]{1,0:T(8,128)S(1)}, u32[]{:S(2)}, u32[]{:S(2)}) %collective-permute-start.6) | collective-permute-done | bytes 102432 | tf_op jit(solution)/shard_map/ppermute | solution.py:963
  28.1 2.3 %halo_rows.1 = (f32[48,56,256]{2,1,0:T(8,128)S(1)}, f32[48,56,256]{2,1,0:T(8,128)S(1)}, f32[48,56,256]{2,1,0:T(8,128)S(1)}, f32[48,16,256]{2,1,0:T(8,128)S(1)}, ...) custom-call(f32[48,16,128]{2,1,0:T(8,128)S(1)} %pad_maximum_fusion.geo, ...), custom_call_target="tpu_custom_call" | custom-call | flops 2000000000 | bytes 10000000 | tf_op jit(solution)/shard_map/halo_rows/pallas_call | solution.py:939
  30.4 14.7 %steps_and_adjoint.1 = (f32[80,128]{1,0:T(8,128)S(1)}, f32[48,40,256]{2,1,0:T(8,128)S(1)}, f32[48,40,256]{2,1,0:T(8,128)S(1)}, f32[16,40,128]{2,1,0:T(8,128)S(1)...) custom-call(f32[48,16,128]{2,1,0:T(8,128)S(1)} %pad_maximum_fusion.geo, ...), custom_call_target="tpu_custom_call" | custom-call | flops 4000000000 | bytes 10000000 | tf_op jit(solution)/shard_map/steps_and_adjoint/pallas_call | solution.py:939
  45.1 1.0 %collective-permute-start.8 = (f32[80,128]{1,0:T(8,128)S(1)}, f32[80,128]{1,0:T(8,128)S(1)}, u32[]{:S(2)}, u32[]{:S(2)}) collective-permute-start(f32[80,128]{1,0:T(8,128)S(1)} %get-tuple-element.124), channel_id=1, source_target_pairs={{0,16},{2,18},{4,20},{6,22},{8,24},{10,26},{12,28},{14,30},{16,0},... | collective-permute-start | bytes 122888 | tf_op jit(solution)/shard_map/ppermute | solution.py:842
  46.2 1.5 %adjoint_third_section.1 = (f32[48,40,256]{2,1,0:T(8,128)S(1)}, f32[48,40,256]{2,1,0:T(8,128)S(1)}) custom-call(f32[48,16,128]{2,1,0:T(8,128)S(1)} %pad_maximum_fusion.geo, f32[48,56,256]{2,1,0:T(8,128)S(1)} %get-tuple-element.117.refs_6_.refs_0_, f32[48,16,256]{2,1,0:T(8,128)S(1)} %get-tuple-element.118.refs_7_.refs_1_.refs_3_, ...), custom_call_target="tpu_custom_call" | custom-call | flops 1000000000 | bytes 10000000 | tf_op jit(solution)/shard_map/adjoint_third_section/pallas_call | solution.py:939
  47.7 2.8 %collective-permute-done.8 = f32[80,128]{1,0:T(8,128)S(1)} collective-permute-done((f32[80,128]{1,0:T(8,128)S(1)}, f32[80,128]{1,0:T(8,128)S(1)}, u32[]{:S(2)}, u32[]{:S(2)}) %collective-permute-start.8) | collective-permute-done | bytes 40992 | tf_op jit(solution)/shard_map/ppermute | solution.py:842
  51.0 1.6 %adjoint_second_section.1 = (f32[48,40,256]{2,1,0:T(8,128)S(1)}, f32[48,40,256]{2,1,0:T(8,128)S(1)}) custom-call(f32[48,16,128]{2,1,0:T(8,128)S(1)} %pad_maximum_fusion.geo, f32[48,56,256]{2,1,0:T(8,128)S(1)} %get-tuple-element.130.refs_0_, f32[48,16,256]{2,1,0:T(8,128)S(1)} %get-tuple-element.118.refs_7_.refs_1_.refs_3_, ...), custom_call_target="tpu_custom_call" | custom-call | flops 1000000000 | bytes 10000000 | tf_op jit(solution)/shard_map/adjoint_second_section/pallas_call | solution.py:939
  52.5 2.0 %collective-permute-done.9 = f32[80,128]{1,0:T(8,128)S(1)} collective-permute-done((f32[80,128]{1,0:T(8,128)S(1)}, f32[80,128]{1,0:T(8,128)S(1)}, u32[]{:S(2)}, u32[]{:S(2)}) %collective-permute-start.9) | collective-permute-done | bytes 40992 | tf_op jit(solution)/shard_map/ppermute | solution.py:842
  55.0 1.8 %adjoint_first_section.1 = f32[640,128]{1,0:T(8,128)} custom-call(f32[48,16,128]{2,1,0:T(8,128)S(1)} %pad_maximum_fusion.geo, f32[48,56,256]{2,1,0:T(8,128)S(1)} %get-tuple-element.116.refs_5_.refs_0_, f32[48,16,256]{2,1,0:T(8,128)S(1)} %get-tuple-element.118.refs_7_.refs_1_.refs_3_, f32[48,40,256]{2,1,0:T(8,128)S(1)} %get-tuple-element.136.refs_2_, ...), custom_call_target="tpu_custom_call" | custom-call | flops 1000000000 | bytes 10000000 | tf_op jit(solution)/shard_map/adjoint_first_section/pallas_call | solution.py:939
  56.8 1.7 %collective-permute-done.10 = f32[80,128]{1,0:T(8,128)S(1)} collective-permute-done((f32[80,128]{1,0:T(8,128)S(1)}, f32[80,128]{1,0:T(8,128)S(1)}, u32[]{:S(2)}, u32[]{:S(2)}) %collective-permute-start.10) | collective-permute-done | bytes 40992 | tf_op jit(solution)/shard_map/ppermute | solution.py:842
  58.5 1.5 %last_section.1 = f32[640,128]{1,0:T(8,128)} custom-call(f32[48,16,128]{2,1,0:T(8,128)S(1)} %pad_maximum_fusion.geo, f32[8,128]{1,0:T(8,128)S(1)} %slice_add_fusion.refs_0_, f32[48,56,256]{2,1,0:T(8,128)S(1)} %get-tuple-element.140.refs_1_, f32[48,56,256]{2,1,0:T(8,128)S(1)} %get-tuple-element.141.refs_2_, ...), custom_call_target="tpu_custom_call" | custom-call | flops 1000000000 | bytes 10000000 | tf_op jit(solution)/shard_map/last_section/pallas_call | solution.py:939
  60.1 2.5 %collective-permute-done.11 = f32[80,128]{1,0:T(8,128)S(1)} collective-permute-done((f32[80,128]{1,0:T(8,128)S(1)}, f32[80,128]{1,0:T(8,128)S(1)}, u32[]{:S(2)}, u32[]{:S(2)}) %collective-permute-start.11) | collective-permute-done | bytes 40992 | tf_op jit(solution)/shard_map/ppermute | solution.py:842
  62.5 1.2 %collective-permute-done.12 = f32[80,128]{1,0:T(8,128)S(1)} collective-permute-done((f32[80,128]{1,0:T(8,128)S(1)}, f32[80,128]{1,0:T(8,128)S(1)}, u32[]{:S(2)}, u32[]{:S(2)}) %collective-permute-start.12) | collective-permute-done | bytes 40992 | tf_op jit(solution)/shard_map/ppermute | solution.py:842
  (48 shorter events, 5.2 us)
Async XLA Ops:
  0.6 11.4 %copy-start.8 = (f32[64,40]{0,1:T(8,128)S(1)}, f32[64,40]{0,1:T(8,128)}, u32[]{:S(2)}) copy-start(f32[64,40]{0,1:T(8,128)} %param.17) | copy-start | bytes 30724
  0.6 14.7 %copy-start = (f32[64,64]{1,0:T(8,128)S(1)}, f32[64,64]{1,0:T(8,128)}, u32[]{:S(2)}) copy-start(f32[64,64]{1,0:T(8,128)} %refs_1_.1) | copy-start | bytes 49156
  0.7 14.7 %copy-start.1 = (f32[40,64]{1,0:T(8,128)S(1)}, f32[40,64]{1,0:T(8,128)}, u32[]{:S(2)}) copy-start(f32[40,64]{1,0:T(8,128)} %refs_0_.1) | copy-start | bytes 30724
  0.7 14.7 %copy-start.2 = (f32[64]{0:T(128)S(1)}, f32[64]{0:T(128)}, u32[]{:S(2)}) copy-start(f32[64]{0:T(128)} %param.14) | copy-start | bytes 772
  0.7 14.7 %copy-start.3 = (f32[64]{0:T(128)S(1)}, f32[64]{0:T(128)}, u32[]{:S(2)}) copy-start(f32[64]{0:T(128)} %param.16) | copy-start | bytes 772
  0.7 14.7 %copy-start.4 = (f32[40]{0:T(128)S(1)}, f32[40]{0:T(128)}, u32[]{:S(2)}) copy-start(f32[40]{0:T(128)} %param.18) | copy-start | bytes 484
  3.3 7.7 %collective-permute-start = (f32[8,128]{1,0:T(8,128)}, f32[8,128]{1,0:T(8,128)S(1)}, u32[]{:S(2)}, u32[]{:S(2)}) collective-permute-start(f32[8,128]{1,0:T(8,128)} %get-tuple-element.80), channel_id=1, source_target_pairs={{0,2},{2,0},{4,6},{6,4},{8,10},{10,8},{12,14},{14,12},{16,18},{18,... | collective-permute-start | bytes 12296 | tf_op jit(solution)/shard_map/ppermute | solution.py:842
  3.8 16.1 %collective-permute-start.4 = (f32[152,128]{1,0:T(8,128)}, f32[152,128]{1,0:T(8,128)S(1)}, u32[]{:S(2)}, u32[]{:S(2)}) collective-permute-start(f32[152,128]{1,0:T(8,128)} %get-tuple-element.96), channel_id=1, source_target_pairs={{0,2},{2,4},{4,6},{6,8},{8,10},{10,12},{12,14},{14,16},{16,18},{18... | collective-permute-start | bytes 233480 | tf_op jit(solution)/shard_map/ppermute | solution.py:901
  3.9 16.1 %collective-permute-start.5 = (f32[152,128]{1,0:T(8,128)}, f32[152,128]{1,0:T(8,128)S(1)}, u32[]{:S(2)}, u32[]{:S(2)}) collective-permute-start(f32[152,128]{1,0:T(8,128)} %get-tuple-element.97), channel_id=1, source_target_pairs={{2,0},{4,2},{6,4},{8,6},{10,8},{12,10},{14,12},{16,14},{18,16},{20... | collective-permute-start | bytes 233480 | tf_op jit(solution)/shard_map/ppermute | solution.py:902
  9.5 18.7 %collective-permute-start.7 = (f32[856,128]{1,0:T(8,128)}, f32[856,128]{1,0:T(8,128)S(1)}, u32[]{:S(2)}, u32[]{:S(2)}) collective-permute-start(f32[856,128]{1,0:T(8,128)} %get-tuple-element.115), channel_id=1, source_target_pairs={{0,1},{1,0},{2,3},{3,2},{4,5},{5,4},{6,7},{7,6},{8,9},{9,8},{10,11... | collective-permute-start | bytes 1314824 | tf_op jit(solution)/shard_map/ppermute | solution.py:931
  11.7 3.6 %collective-permute-start.1 = (f32[8,128]{1,0:T(8,128)S(1)}, f32[8,128]{1,0:T(8,128)S(1)}, u32[]{:S(2)}, u32[]{:S(2)}) collective-permute-start(f32[8,128]{1,0:T(8,128)S(1)} %add.69), channel_id=1, source_target_pairs={{0,4},{2,6},{4,0},{6,2},{8,12},{10,14},{12,8},{14,10},{16,20},{18,... | collective-permute-start | bytes 12296 | tf_op jit(solution)/shard_map/ppermute | solution.py:842
  15.3 3.6 %collective-permute-start.2 = (f32[8,128]{1,0:T(8,128)S(1)}, f32[8,128]{1,0:T(8,128)S(1)}, u32[]{:S(2)}, u32[]{:S(2)}) collective-permute-start(f32[8,128]{1,0:T(8,128)S(1)} %add.70), channel_id=1, source_target_pairs={{0,8},{2,10},{4,12},{6,14},{8,0},{10,2},{12,4},{14,6},{16,24},{18,... | collective-permute-start | bytes 12296 | tf_op jit(solution)/shard_map/ppermute | solution.py:842
  15.4 1.0 %copy-start.5 = (f32[16,56,128]{2,1,0:T(8,128)S(1)}, f32[16,56,128]{2,1,0:T(8,128)}, u32[]{:S(2)}) copy-start(f32[16,56,128]{2,1,0:T(8,128)} %get-tuple-element.84.own.refs_0_.refs_1_) | copy-start | bytes 1376260
  16.4 7.6 %copy-start.6 = (f32[16,56,128]{2,1,0:T(8,128)S(1)}, f32[16,56,128]{2,1,0:T(8,128)}, u32[]{:S(2)}) copy-start(f32[16,56,128]{2,1,0:T(8,128)} %get-tuple-element.84.own.refs_0_.refs_1_) | copy-start | bytes 1376260
  18.9 4.5 %collective-permute-start.3 = (f32[8,128]{1,0:T(8,128)S(1)}, f32[8,128]{1,0:T(8,128)S(1)}, u32[]{:S(2)}, u32[]{:S(2)}) collective-permute-start(f32[8,128]{1,0:T(8,128)S(1)} %add.71), channel_id=1, source_target_pairs={{0,16},{2,18},{4,20},{6,22},{8,24},{10,26},{12,28},{14,30},{16,0},... | collective-permute-start | bytes 12296 | tf_op jit(solution)/shard_map/ppermute | solution.py:842
  23.4 4.7 %collective-permute-start.6 = (f32[200,128]{1,0:T(8,128)S(1)}, f32[200,128]{1,0:T(8,128)S(1)}, u32[]{:S(2)}, u32[]{:S(2)}) collective-permute-start(f32[200,128]{1,0:T(8,128)S(1)} %get-tuple-element.152), channel_id=1, source_target_pairs={{0,1},{1,0},{2,3},{3,2},{4,5},{5,4},{6,7},{7,6},{8,9},{9,8},{10,11... | collective-permute-start | bytes 307208 | tf_op jit(solution)/shard_map/ppermute | solution.py:963
  28.1 2.3 %copy-start.7 = (f32[16,40,128]{2,1,0:T(8,128)S(1)}, f32[16,40,128]{2,1,0:T(8,128)}, u32[]{:S(2)}) copy-start(f32[16,40,128]{2,1,0:T(8,128)} %get-tuple-element.109.refs_2_) | copy-start | bytes 983044
  45.1 5.4 %collective-permute-start.8 = (f32[80,128]{1,0:T(8,128)S(1)}, f32[80,128]{1,0:T(8,128)S(1)}, u32[]{:S(2)}, u32[]{:S(2)}) collective-permute-start(f32[80,128]{1,0:T(8,128)S(1)} %get-tuple-element.124), channel_id=1, source_target_pairs={{0,16},{2,18},{4,20},{6,22},{8,24},{10,26},{12,28},{14,30},{16,0},... | collective-permute-start | bytes 122888 | tf_op jit(solution)/shard_map/ppermute | solution.py:842
  50.5 4.0 %collective-permute-start.9 = (f32[80,128]{1,0:T(8,128)S(1)}, f32[80,128]{1,0:T(8,128)S(1)}, u32[]{:S(2)}, u32[]{:S(2)}) collective-permute-start(f32[80,128]{1,0:T(8,128)S(1)} %add.74), channel_id=1, source_target_pairs={{0,8},{2,10},{4,12},{6,14},{8,0},{10,2},{12,4},{14,6},{16,24},{18,... | collective-permute-start | bytes 122888 | tf_op jit(solution)/shard_map/ppermute | solution.py:842
  54.5 4.0 %collective-permute-start.10 = (f32[80,128]{1,0:T(8,128)S(1)}, f32[80,128]{1,0:T(8,128)S(1)}, u32[]{:S(2)}, u32[]{:S(2)}) collective-permute-start(f32[80,128]{1,0:T(8,128)S(1)} %add.75), channel_id=1, source_target_pairs={{0,1},{1,0},{2,3},{3,2},{4,5},{5,4},{6,7},{7,6},{8,9},{9,8},{10,11... | collective-permute-start | bytes 122888 | tf_op jit(solution)/shard_map/ppermute | solution.py:842
  58.5 4.0 %collective-permute-start.11 = (f32[80,128]{1,0:T(8,128)S(1)}, f32[80,128]{1,0:T(8,128)S(1)}, u32[]{:S(2)}, u32[]{:S(2)}) collective-permute-start(f32[80,128]{1,0:T(8,128)S(1)} %add.76), channel_id=1, source_target_pairs={{0,4},{2,6},{4,0},{6,2},{8,12},{10,14},{12,8},{14,10},{16,20},{18,... | collective-permute-start | bytes 122888 | tf_op jit(solution)/shard_map/ppermute | solution.py:842
  62.5 1.2 %collective-permute-start.12 = (f32[80,128]{1,0:T(8,128)S(1)}, f32[80,128]{1,0:T(8,128)S(1)}, u32[]{:S(2)}, u32[]{:S(2)}) collective-permute-start(f32[80,128]{1,0:T(8,128)S(1)} %add.77), channel_id=1, source_target_pairs={{0,2},{2,0},{4,6},{6,4},{8,10},{10,8},{12,14},{14,12},{16,18},{18,... | collective-permute-start | bytes 122888 | tf_op jit(solution)/shard_map/ppermute | solution.py:842
